TPU v7x, 32 devices: a whole 2x2x4 slice. The times are simulated.
32 devices in a mesh: expert: 4 (over y, x), context: 4 (over z), dp: 2 (over core).
Axes of the slice: x: 2, y: 2, z: 4, core: 2. Of those that a mesh axis runs over, the one named last changes fastest.
Arguments:
- tokens: bfloat16 [8, 580, 768], P(('expert', 'dp'), 'context'), may hold values from -6 to 6
- cotangent: float32 [8, 580, 768], P(('expert', 'dp'), 'context'), may hold values from -6 to 6
- first_gain: bfloat16 [768], P(('expert', 'context', 'dp')), may hold values from 0.099609375 to 1.8984375
- first_attend: bfloat16 [768, 2304], P(('expert', 'context', 'dp')), may hold values from -0.21875 to 0.21875
- first_output: bfloat16 [768, 768], P(('expert', 'context', 'dp')), may hold values from -0.875 to 0.875
- second_gain: bfloat16 [768], P(('expert', 'context', 'dp')), may hold values from 0.099609375 to 1.8984375
- widen_in: bfloat16 [768, 3072], P(('expert', 'context', 'dp')), may hold values from -0.21875 to 0.21875
- widen_out: bfloat16 [3072, 768], P(('expert', 'context', 'dp')), may hold values from -0.15625 to 0.15625
- third_gain: bfloat16 [768], P(('expert', 'context', 'dp')), may hold values from 0.099609375 to 1.8984375
- second_attend: bfloat16 [768, 2304], P(('expert', 'context', 'dp')), may hold values from -0.21875 to 0.21875
- second_output: bfloat16 [768, 768], P(('expert', 'context', 'dp')), may hold values from -0.875 to 0.875
- fourth_gain: bfloat16 [768], P(('expert', 'context', 'dp')), may hold values from 0.099609375 to 1.8984375
- router: bfloat16 [768, 4], P(('expert', 'context', 'dp')), may hold values from -0.15625 to 0.15625
- expert_in: bfloat16 [4, 768, 3072], P('expert', None, 'dp'), may hold values from -0.21875 to 0.21875
- expert_out: bfloat16 [4, 3072, 768], P('expert', 'dp'), may hold values from -0.3125 to 0.3125
- routes: int32 [8, 580, 2], P(('expert', 'dp'), 'context'), may hold values from 0 to 3, as said below
- buffer_slot: int32 [8, 580, 2], P(('expert', 'dp'), 'context'), may hold values from 0 to 91, as said below
Outputs:
- activations: float32 [8, 580, 768], P(('expert', 'dp'), 'context')
- token_slope: float32 [8, 580, 768], P(('expert', 'dp'), 'context')
- first_gain_slope: float32 [768], P(('expert', 'context', 'dp'))
- first_attend_slope: float32 [768, 2304], P(('expert', 'context', 'dp'))
- first_output_slope: float32 [768, 768], P(('expert', 'context', 'dp'))
- second_gain_slope: float32 [768], P(('expert', 'context', 'dp'))
- widen_in_slope: float32 [768, 3072], P(('expert', 'context', 'dp'))
- widen_out_slope: float32 [3072, 768], P(('expert', 'context', 'dp'))
- third_gain_slope: float32 [768], P(('expert', 'context', 'dp'))
- second_attend_slope: float32 [768, 2304], P(('expert', 'context', 'dp'))
- second_output_slope: float32 [768, 768], P(('expert', 'context', 'dp'))
- fourth_gain_slope: float32 [768], P(('expert', 'context', 'dp'))
- router_slope: float32 [768, 4], P(('expert', 'context', 'dp'))
- expert_in_slope: float32 [4, 768, 3072], P('expert', None, 'dp')
- expert_out_slope: float32 [4, 3072, 768], P('expert', 'dp')
Inputs may be any that keep to these rules, and one draw needn't show every extreme that they name: `routes`: the 2 experts of a slot differ. `buffer_slot`: within the 145 slots of one device, the kept pairs of each expert hold the rows 0, 1, ... in turn, each once; padding slots and dropped pairs hold 91; in every draw some expert gets all 91 rows from every device.
All inputs are finite; a program needn't handle non-finite values.
Results may differ from a plain program's by a relative error of at most 0.02.
Values may be sent and summed in bfloat16 or wider, within the bound.
No kernel may reach another device: no remote copies, remote signals or barrier semaphores. Data moves between devices by JAX's collectives and lax.ppermute only.
A program may use at most 256 MiB of HBM per device.

v0:
```python
import functools

import jax
import jax.numpy as jnp
from jax import lax
from jax.sharding import PartitionSpec as P

HEADS = 12
HEAD_DIM = 64
LEN = 577
TOP = 2
ALL = ("expert", "context", "dp")
CHIPS = ("expert", "context")
BF = jnp.bfloat16
F32 = jnp.float32


def up16(n):
    return (n + 15) // 16 * 16


def dot(a, b):
    return jnp.dot(a, b, preferred_element_type=F32)


def dot_t(a, b):
    return lax.dot_general(a, b, (((1,), (1,)), ((), ())), preferred_element_type=F32)


def t_dot(a, b):
    return lax.dot_general(a, b, (((0,), (0,)), ((), ())), preferred_element_type=F32)


class Links:
    def __init__(self, mesh):
        self.E = mesh.shape["expert"]
        self.C = mesh.shape["context"]
        self.D = mesh.shape["dp"]
        assert self.C == 4 and self.D == 2 and self.E % 2 == 0
        self.fast = self.E == 4
        flat = lambda e, c, d: (e * self.C + c) * self.D + d
        self.team = [
            (flat(e, c, d), flat((e // 2) * 2 + c // 2, 2 * (e % 2) + d, c % 2))
            for e in range(self.E)
            for c in range(self.C)
            for d in range(self.D)
        ]

    def move(self, x):
        return lax.ppermute(x, ALL, self.team)

    def xor(self, x, axis, j):
        n = {"expert": self.E, "context": self.C, "dp": self.D}[axis]
        return lax.ppermute(x, axis, [(i, i ^ j) for i in range(n)])

    def sib(self, x):
        return self.xor(x, "dp", 1)

    def partner(self, x):
        return self.xor(x, "expert", 1)

    def gather(self, x, first):
        if not self.fast:
            return lax.all_gather(x, CHIPS, axis=0, tiled=True)
        c = lax.axis_index("context")
        e = lax.axis_index("expert")
        parts = jnp.stack([x] + [self.xor(x, "context", j) for j in range(1, 4)])
        own = jnp.concatenate(
            [lax.dynamic_index_in_dim(parts, c ^ k, 0, False) for k in range(4)], 0
        )
        second = 3 - first
        blocks = {0: own, first: self.xor(own, "expert", first)}
        blocks[second] = self.xor(own, "expert", second)
        blocks[3] = self.xor(blocks[first], "expert", second)
        stacked = jnp.stack([blocks[j] for j in range(4)])
        return jnp.concatenate(
            [lax.dynamic_index_in_dim(stacked, e ^ k, 0, False) for k in range(4)], 0
        )

    def scatter(self, g, first):
        if not self.fast:
            return lax.psum_scatter(g.astype(BF), CHIPS, scatter_dimension=0, tiled=True).astype(F32)
        c = lax.axis_index("context")
        e = lax.axis_index("expert")
        n = g.shape[1]
        g = g.astype(BF).reshape(4, -1, n)
        second = 3 - first
        blk = [lax.dynamic_index_in_dim(g, e ^ j, 0, False) for j in range(4)]
        r0 = self.xor(blk[first], "expert", first)
        r1 = self.xor(blk[3], "expert", first)
        s1 = (blk[second].astype(F32) + r1.astype(F32)).astype(BF)
        r2 = self.xor(s1, "expert", second)
        s0 = (blk[0].astype(F32) + r0.astype(F32) + r2.astype(F32)).astype(BF)
        s0 = s0.reshape(4, -1, n)
        total = lax.dynamic_index_in_dim(s0, c, 0, False).astype(F32)
        for j in range(1, 4):
            piece = lax.dynamic_index_in_dim(s0, c ^ j, 0, False)
            total = total + self.xor(piece, "context", j).astype(F32)
        return total

    def total(self, x):
        if not self.fast:
            return lax.psum(x, ALL)
        x = x + self.xor(x, "dp", 1)
        x = x + self.xor(x, "expert", 1)
        x = x + self.xor(x, "expert", 2)
        x = x + self.xor(x, "context", 1)
        return x + self.xor(x, "context", 2)

    def swap_blocks(self, x):
        if not self.fast:
            return lax.all_to_all(x, "expert", 0, 0, tiled=True)
        return jnp.stack([x[0]] + [self.xor(x[j], "expert", j) for j in range(1, 4)])


def norm_parts(x):
    mean = jnp.mean(x, -1, keepdims=True)
    centre = x - mean
    scale = lax.rsqrt(jnp.mean(centre * centre, -1, keepdims=True) + 1e-06)
    return centre * scale, scale


def layer_norm(x, gain):
    return (norm_parts(x)[0] * gain).astype(BF)


def layer_norm_back(x, gain, slope):
    unit, scale = norm_parts(x)
    gain_slope = jnp.sum(slope * unit, 0)
    inner = slope * gain
    inner = inner - jnp.mean(inner, -1, keepdims=True) - unit * jnp.mean(inner * unit, -1, keepdims=True)
    return inner * scale, gain_slope


def gelu_both(h):
    k = 0.7978845608028654
    t = jnp.tanh(k * (h + 0.044715 * h * h * h))
    return 0.5 * h * (1 + t), 0.5 * (1 + t) + 0.5 * h * (1 - t * t) * k * (1 + 3 * 0.044715 * h * h)


def lane_rows(links, mine, d):
    keep = lax.dynamic_index_in_dim(mine, d, 0, False)
    give = lax.dynamic_index_in_dim(mine, 1 - d, 0, False)
    got = links.sib(give)
    return jnp.where(d == 0, jnp.concatenate([keep, got], 0), jnp.concatenate([got, keep], 0))


def in_order(d, own, other):
    return jnp.where(d == 0, jnp.stack([own, other]), jnp.stack([other, own]))


def body(links, *args):
    (tokens, cotangent, g1, w1, p1, g2, win, wout, g3, w3, p3, g4, router, ein, eout, routes, slots) = args
    e = lax.axis_index("expert")
    d = lax.axis_index("dp")
    blk_len, feat = tokens.shape[1:]
    rows = up16(blk_len)
    half = feat // 2
    chips = links.E * links.C
    rdev = w1.shape[0]
    ff = win.shape[1]
    lane_ff = ff // 2
    longest = LEN - (blk_len - 1) * links.C
    experts = router.shape[1]
    cap = max(2, (5 * TOP * blk_len + 4 * experts - 1) // (4 * experts))
    cap_rows = up16(cap)
    blk = 2 * (e % 2) + d

    def pad(x):
        return jnp.pad(x, ((0, rows - blk_len), (0, 0)))

    small = jnp.concatenate([g1[:, None], g2[:, None], g3[:, None], g4[:, None], router], 1)
    small = in_order(d, small, links.sib(small)).reshape(2 * rdev, -1)
    small = links.gather(small, 1)
    gains = small[:, :4].T.astype(F32)
    router_all = small[:, 4:]

    x0 = pad(links.move(tokens[0])).astype(F32)

    def attend_weights(w, p):
        w = w.reshape(rdev, 3, 2, half).transpose(2, 0, 1, 3).reshape(2, rdev, 3 * half)
        w = lane_rows(links, w, d)
        qk = links.gather(w[:, : 2 * half], 1)
        v = links.gather(w[:, 2 * half :], 2)
        p = links.gather(p, 2).reshape(2, chips // 2, rdev, feat)
        own = lax.dynamic_index_in_dim(p, d, 0, False)
        other = links.sib(lax.dynamic_index_in_dim(p, 1 - d, 0, False))
        p = in_order(d, own, other).transpose(1, 0, 2, 3).reshape(half, feat)
        return qk, v, p

    def widen_weights():
        hid = ff // (2 * chips)
        w = win.reshape(rdev, chips, 2, hid).transpose(2, 0, 1, 3).reshape(2, rdev, lane_ff)
        return links.gather(lane_rows(links, w, d), 1), links.gather(wout, 2)

    wt1 = attend_weights(w1, p1)
    wt2 = widen_weights()
    wt3 = attend_weights(w3, p3)
    ein_own, eout_own = ein[0], eout[0]
    ein_sib, eout_sib = links.sib(ein_own), links.sib(eout_own)

    pos = jnp.arange(rows, dtype=jnp.int32)

    def valid(b):
        return (pos < blk_len) & ((b < longest) | (pos < blk_len - 1))

    key_ok = jnp.concatenate([valid(blk ^ j) for j in range(4)])
    present = valid(blk).astype(F32)[:, None]
    up = pad(links.move(cotangent[0])) * present
    index = links.move(jnp.concatenate([routes[0], slots[0]], 1))
    index = jnp.pad(index, ((0, rows - blk_len), (0, 0)), constant_values=cap)
    chosen, slot = index[:, :TOP], index[:, TOP:]

    heads = lambda t: t.reshape(t.shape[0], -1, HEAD_DIM)

    def both(t):
        return jnp.concatenate([t, links.sib(t)], 0)

    def reduce_pair(partial):
        return partial[:rows] + links.sib(partial[rows:].astype(BF)).astype(F32)

    def attend_forward(x, gain, wt):
        qk_w, v_w, p_w = wt
        normed = both(layer_norm(x, gain))
        qk = dot(normed, qk_w).astype(BF)
        v = dot(normed, v_w).astype(BF)
        q = qk[:, :half]
        kv = jnp.concatenate([qk[:, half:], v], 1)
        kv = jnp.concatenate([kv, links.partner(kv)], 0)
        s = jnp.einsum("qhd,khd->hqk", heads(q), heads(kv[:, :half]), preferred_element_type=F32) * 0.125
        s = jnp.where(key_ok[None, None, :], s, -1e9)
        top = jnp.max(s, -1, keepdims=True)
        ex = jnp.exp(s - top)
        total = jnp.sum(ex, -1, keepdims=True)
        lse = top + jnp.log(total)
        shares = (ex / total).astype(BF)
        blended = jnp.einsum("hqk,khd->qhd", shares, heads(kv[:, half:]), preferred_element_type=F32)
        blended = blended.reshape(2 * rows, half).astype(BF)
        return x + reduce_pair(dot(blended, p_w)), (x, normed, q, kv, lse, blended)

    def attend_backward(u, kept, gain, wt):
        x, normed, q, kv, lse, blended = kept
        qk_w, v_w, p_w = wt
        u_low = both(u.astype(BF))
        p_slope = t_dot(blended, u_low)
        b_slope = heads(dot_t(u_low, p_w).astype(BF))
        keys, values = heads(kv[:, :half]), heads(kv[:, half:])
        s = jnp.einsum("qhd,khd->hqk", heads(q), keys, preferred_element_type=F32) * 0.125
        s = jnp.where(key_ok[None, None, :], s, -1e9)
        shares = jnp.exp(s - lse)
        ss = jnp.einsum("qhd,khd->hqk", b_slope, values, preferred_element_type=F32)
        ss = (shares * (ss - jnp.sum(shares * ss, -1, keepdims=True))).astype(BF)
        q_slope = jnp.einsum("hqk,khd->qhd", ss, keys, preferred_element_type=F32) * 0.125
        k_slope = jnp.einsum("hqk,qhd->khd", ss, heads(q), preferred_element_type=F32) * 0.125
        v_slope = jnp.einsum("hqk,qhd->khd", shares.astype(BF), b_slope, preferred_element_type=F32)
        kv_slope = jnp.concatenate([k_slope.reshape(-1, half), v_slope.reshape(-1, half)], 1)
        got = links.partner(kv_slope[2 * rows :].astype(BF)).astype(F32)
        kv_slope = (kv_slope[: 2 * rows] + got).astype(BF)
        qk_slope = jnp.concatenate([q_slope.reshape(-1, half).astype(BF), kv_slope[:, :half]], 1)
        v_slope = kv_slope[:, half:]
        n_slope = dot_t(qk_slope, qk_w) + dot_t(v_slope, v_w)
        dx, g_slope = layer_norm_back(x, gain, reduce_pair(n_slope))
        return u + dx, g_slope, (t_dot(normed, qk_slope), t_dot(normed, v_slope), p_slope)

    def attend_owner(slopes):
        qk, v, p = slopes
        w = jnp.concatenate([links.scatter(qk, 1), links.scatter(v, 2)], 1)
        w = w.reshape(2, rdev, 3 * half)
        mine = lax.dynamic_index_in_dim(w, d, 0, False)
        got = links.sib(lax.dynamic_index_in_dim(w, 1 - d, 0, False))
        w = in_order(d, mine, got).reshape(2, rdev, 3, half).transpose(1, 2, 0, 3).reshape(rdev, 3 * feat)
        p = p.astype(BF).reshape(chips // 2, 2, rdev, feat)
        own = lax.dynamic_index_in_dim(p, d, 1, False)
        got = links.sib(lax.dynamic_index_in_dim(p, 1 - d, 1, False))
        p = in_order(d, own, got).reshape(chips * rdev, feat)
        return w, links.scatter(p, 2)

    def widen_owner(slope_in, slope_out):
        w = links.scatter(slope_in, 1).reshape(2, rdev, lane_ff)
        mine = lax.dynamic_index_in_dim(w, d, 0, False)
        got = links.sib(lax.dynamic_index_in_dim(w, 1 - d, 0, False))
        w = in_order(d, mine, got).reshape(2, rdev, chips, -1).transpose(1, 2, 0, 3).reshape(rdev, ff)
        return w, links.scatter(slope_out, 2)

    x1, kept1 = attend_forward(x0, gains[0], wt1)
    normed2 = both(layer_norm(x1, gains[1]))
    hidden = dot(normed2, wt2[0])
    active = gelu_both(hidden)[0].astype(BF)
    x2 = x1 + reduce_pair(dot(active, wt2[1]))
    x3, kept3 = attend_forward(x2, gains[2], wt3)

    moe = layer_norm(x3, gains[3])
    gates_all = jax.nn.softmax(dot(moe, router_all), axis=-1)
    expert_ids = jnp.arange(experts, dtype=jnp.int32)
    match = (chosen[:, :, None] == expert_ids).astype(F32)
    gate = jnp.sum(gates_all[:, None, :] * match, -1)
    place = chosen ^ e if links.fast else chosen
    target = jnp.where(slot < cap, place * cap_rows + slot, experts * cap_rows)
    pick = (target[:, :, None] == jnp.arange(experts * cap_rows, dtype=jnp.int32)).astype(BF)
    pick0, pick1 = pick[:, 0], pick[:, 1]
    sent = t_dot(pick0 + pick1, moe).astype(BF)
    slope0 = (gate[:, 0:1] * up).astype(BF)
    slope1 = (gate[:, 1:2] * up).astype(BF)
    sent_slope = (t_dot(pick0, slope0) + t_dot(pick1, slope1)).astype(BF)
    blocks = lambda a, b: jnp.stack([a.reshape(experts, cap_rows, feat), b.reshape(experts, cap_rows, feat)], 1)
    came = links.swap_blocks(blocks(sent, sent_slope))
    e_rows = came[:, 0].reshape(-1, feat)
    e_slope = came[:, 1].reshape(-1, feat)

    def expert_half(w_in, w_out):
        h = dot(e_rows, w_in)
        act, dact = gelu_both(h)
        act = act.astype(BF)
        result = dot(act, w_out)
        hs = (dact * dot_t(e_slope, w_out)).astype(BF)
        return result, dot_t(hs, w_in), t_dot(e_rows, hs), t_dot(act, e_slope)

    half_a = expert_half(ein_own, eout_own)
    half_b = expert_half(ein_sib, eout_sib)
    back = links.swap_blocks(blocks((half_a[0] + half_b[0]).astype(BF), (half_a[1] + half_b[1]).astype(BF)))
    result = back[:, 0].reshape(-1, feat)
    row_slope = back[:, 1].reshape(-1, feat)
    e_sums = []
    for k in (2, 3):
        mine = half_a[k] + links.sib(half_b[k].astype(BF)).astype(F32)
        e_sums.append(lax.psum(mine.astype(BF), "context").astype(F32))

    picked0, picked1 = dot(pick0, result), dot(pick1, result)
    acts = (x3 + gate[:, 0:1] * picked0 + gate[:, 1:2] * picked1) * present
    gate_slope = jnp.stack([jnp.sum(up * picked0, -1), jnp.sum(up * picked1, -1)], 1)
    all_slope = jnp.sum(gate_slope[:, :, None] * match, 1)
    logit_slope = gates_all * (all_slope - jnp.sum(gates_all * all_slope, -1, keepdims=True))
    logit_slope = logit_slope.astype(BF)
    router_slope = t_dot(moe, logit_slope)
    n_slope = dot(pick0 + pick1, row_slope) + dot_t(logit_slope, router_all)
    dx, g4_slope = layer_norm_back(x3, gains[3], n_slope)
    u = up + dx

    u, g3_slope, slopes3 = attend_backward(u, kept3, gains[2], wt3)
    u_low = both(u.astype(BF))
    wout_slope = t_dot(active, u_low)
    h_slope = (gelu_both(hidden)[1] * dot_t(u_low, wt2[1])).astype(BF)
    win_slope = t_dot(normed2, h_slope)
    dx, g2_slope = layer_norm_back(x1, gains[1], reduce_pair(dot_t(h_slope, wt2[0])))
    u = u + dx
    u, g1_slope, slopes1 = attend_backward(u, kept1, gains[0], wt1)

    w3_out, p3_out = attend_owner(slopes3)
    win_out, wout_out = widen_owner(win_slope, wout_slope)
    w1_out, p1_out = attend_owner(slopes1)
    small = jnp.concatenate([jnp.stack([g1_slope, g2_slope, g3_slope, g4_slope]), router_slope.T], 0)
    small = links.total(small)
    flat = (e * links.C + lax.axis_index("context")) * 2 + d
    small = small.reshape(-1, 2 * chips, rdev)
    small = lax.dynamic_index_in_dim(small, flat, 1, False)

    acts = links.move(acts[:blk_len])[None]
    token_slope = links.move(u[:blk_len])[None]
    return (
        acts, token_slope, small[0], w1_out, p1_out, small[1], win_out, wout_out,
        small[2], w3_out, p3_out, small[3], small[4:].T, e_sums[0][None], e_sums[1][None],
    )


def solution(mesh):
    links = Links(mesh)
    tok = P(("expert", "dp"), "context", None)
    vec, mat = P(ALL), P(ALL, None)
    ein, eout = P("expert", None, "dp"), P("expert", "dp", None)
    dense = (vec, mat, mat, vec, mat, mat, vec, mat, mat, vec, mat, ein, eout)
    return jax.shard_map(
        functools.partial(body, links),
        mesh=mesh,
        in_specs=(tok, tok) + dense + (tok, tok),
        out_specs=(tok, tok) + dense,
        check_vma=False,
    )
```

profile of v0, /device:TPU:10, one launch (start us, length us, event | category | flops | bytes accessed | tf_op | source)
XLA Modules:
  0.0 665.1 jit_solution(7065282390209406114)
XLA Ops:
  15.2 3.7 collective-permute-start.3
  46.8 3.4 collective-permute-start.11
  53.5 3.5 collective-permute-start.49
  58.2 3.8 collective-permute-done.49
  62.0 3.4 collective-permute-start.40
  67.5 5.9 collective-permute-start.26
  74.5 6.5 collective-permute-done.40
  82.1 6.7 %collective-permute-done.35 = bf16[48,1536]{1,0:T(8,128)(2,1)S(1)} collective-permute-done((bf16[48,1536]{1,0:T(8,128)(2,1)S(1)}, bf16[48,1536]{1,0:T(8,128)(2,1)S(1)}, u32[]{:S(2)}, u32[]{:S(2)}) %collective-permute-start.35) | collective-permute-done | bytes 147488 | tf_op jit(solution)/shard_map/ppermute | solution.py:54
  107.6 4.4 collective-permute-done.21
  116.9 4.9 collective-permute-done.15
  129.8 4.4 collective-permute-done.43
  139.6 9.3 %collective-permute-done.22 = bf16[320,768]{1,0:T(8,128)(2,1)} collective-permute-done((bf16[320,768]{1,0:T(8,128)(2,1)}, bf16[320,768]{1,0:T(8,128)(2,1)}, u32[]{:S(2)}, u32[]{:S(2)}) %collective-permute-start.22) | collective-permute-done | bytes 491552 | tf_op jit(solution)/shard_map/ppermute | solution.py:54
  162.8 9.7 %collective-permute-done.44 = bf16[384,768]{1,0:T(8,128)(2,1)} collective-permute-done((bf16[384,768]{1,0:T(8,128)(2,1)}, bf16[384,768]{1,0:T(8,128)(2,1)}, u32[]{:S(2)}, u32[]{:S(2)}) %collective-permute-start.44) | collective-permute-done | bytes 589856 | tf_op jit(solution)/shard_map/ppermute | solution.py:54
  187.3 7.3 %collective-permute-done.53 = bf16[192,768]{1,0:T(8,128)(2,1)S(1)} collective-permute-done((bf16[192,768]{1,0:T(8,128)(2,1)S(1)}, bf16[192,768]{1,0:T(8,128)(2,1)S(1)}, u32[]{:S(2)}, u32[]{:S(2)}) %collective-permute-start.53) | collective-permute-done | bytes 294944 | tf_op jit(solution)/shard_map/ppermute | solution.py:54
  204.6 3.5 collective-permute-start.70
  224.3 5.3 collective-permute-done.70
  231.1 3.5 collective-permute-start.73
  234.6 6.3 collective-permute-done.71
  241.0 5.5 collective-permute-done.73
  251.0 4.6 fusion.4
  265.6 3.7 fusion.25
  269.3 3.4 fusion.33
  284.0 5.5 collective-permute-done.78
  295.3 6.5 collective-permute-start.79
  303.3 3.4 fusion.8
  306.7 6.1 multiply_reduce_fusion.1
  315.5 4.9 multiply_convert_fusion.1
  354.9 4.9 collective-permute-done.134
  361.3 3.8 collective-permute-done.135
  396.4 4.2 multiply_reduce_fusion
  409.9 5.4 collective-permute-done.115
  424.0 4.7 fusion.27
  429.9 4.5 fusion.26
  434.6 8.5 %collective-permute-done.109 = bf16[96,768]{1,0:T(8,128)(2,1)} collective-permute-done((bf16[96,768]{1,0:T(8,128)(2,1)}, bf16[96,768]{1,0:T(8,128)(2,1)}, u32[]{:S(2)}, u32[]{:S(2)}) %collective-permute-start.109) | collective-permute-done | bytes 147488 | tf_op jit(solution)/shard_map/ppermute | solution.py:54
  458.1 3.5 collective-permute-done.113
  464.3 9.3 %collective-permute-done.101 = bf16[192,384]{1,0:T(8,128)(2,1)S(1)} collective-permute-done((bf16[192,384]{1,0:T(8,128)(2,1)S(1)}, bf16[192,384]{1,0:T(8,128)(2,1)S(1)}, u32[]{:S(2)}, u32[]{:S(2)}) %collective-permute-start.101) | collective-permute-done | bytes 147488 | tf_op jit(solution)/shard_map/ppermute | solution.py:54
  486.5 8.8 %collective-permute-done.102 = bf16[192,384]{1,0:T(8,128)(2,1)} collective-permute-done((bf16[192,384]{1,0:T(8,128)(2,1)}, bf16[192,384]{1,0:T(8,128)(2,1)}, u32[]{:S(2)}, u32[]{:S(2)}) %collective-permute-start.102) | collective-permute-done | bytes 147488 | tf_op jit(solution)/shard_map/ppermute | solution.py:54
  496.4 3.4 collective-permute-start.103
  512.1 8.0 %collective-permute-done.117 = bf16[48,1536]{1,0:T(8,128)(2,1)S(1)} collective-permute-done((bf16[48,1536]{1,0:T(8,128)(2,1)}, bf16[48,1536]{1,0:T(8,128)(2,1)S(1)}, u32[]{:S(2)}, u32[]{:S(2)}) %collective-permute-start.117) | collective-permute-done | bytes 147488 | tf_op jit(solution)/shard_map/ppermute | solution.py:54
  520.2 7.0 %collective-permute-done.119 = bf16[48,1536]{1,0:T(8,128)(2,1)S(1)} collective-permute-done((bf16[48,1536]{1,0:T(8,128)(2,1)}, bf16[48,1536]{1,0:T(8,128)(2,1)S(1)}, u32[]{:S(2)}, u32[]{:S(2)}) %collective-permute-start.119) | collective-permute-done | bytes 147488 | tf_op jit(solution)/shard_map/ppermute | solution.py:54
  527.1 11.9 %collective-permute-done.118 = bf16[48,1536]{1,0:T(8,128)(2,1)S(1)} collective-permute-done((bf16[48,1536]{1,0:T(8,128)(2,1)}, bf16[48,1536]{1,0:T(8,128)(2,1)S(1)}, u32[]{:S(2)}, u32[]{:S(2)}) %collective-permute-start.118) | collective-permute-done | bytes 147488 | tf_op jit(solution)/shard_map/ppermute | solution.py:54
  539.0 5.3 collective-permute-start.92
  552.3 43.1 %collective-permute-done.93 = f32[8,768]{1,0:T(8,128)S(1)} collective-permute-done((f32[8,768]{1,0:T(8,128)S(1)}, f32[8,768]{1,0:T(8,128)S(1)}, u32[]{:S(2)}, u32[]{:S(2)}) %collective-permute-start.93) | collective-permute-done | bytes 24608 | tf_op jit(solution)/shard_map/ppermute | solution.py:54
  597.4 4.0 collective-permute-start.99
  604.9 4.6 collective-permute-done.99
  609.5 5.6 collective-permute-done.98
  619.9 30.9 %all-reduce.6.cloned.1.call-done = (bf16[1,768,1536]{2,1,0:T(8,128)(2,1)}, bf16[1,1536,768]{2,1,0:T(8,128)(2,1)}) async-done(((bf16[1,768,1536]{2,1,0:T(8,128)(2,1)}, bf16[1,1536,768]{2,1,0:T(8,128)(2,1)}), (bf16[1,768,1536]{2,1,0:T(8,128)(2,1)}, bf16[1,1536,768]{2,1,0:T(8,128)(2,1)})) %all-reduce.6.cloned.1.call-update) | async-done | bytes 4718608 | tf_op jit(solution)/shard_map/psum | solution.py:326
  650.8 4.6 broadcast_in_dim.60
  (861 shorter events, 322.5 us)
Async XLA Ops:
  7.2 643.6 %all-reduce.6.cloned.1.call-start = ((), (), s32[]{:S(2)}) async-start(), calls=%async_computation | async-start | bytes 9437184 | tf_op jit(solution)/shard_map/psum | solution.py:326
  7.3 24.2 %collective-permute-start.23 = (bf16[24,768]{1,0:T(8,128)(2,1)}, bf16[24,768]{1,0:T(8,128)(2,1)S(1)}, u32[]{:S(2)}, u32[]{:S(2)}) collective-permute-start(bf16[24,768]{1,0:T(8,128)(2,1)} %param.21), channel_id=1, source_target_pairs={{0,2},{2,0},{4,6},{6,4},{1,3},{3,1},{5,7},{7,5},{8,10},{10,8},{12,... | collective-permute-start | bytes 110600 | tf_op jit(solution)/shard_map/ppermute | solution.py:54
  7.8 25.2 %collective-permute-start.25 = (bf16[24,768]{1,0:T(8,128)(2,1)}, bf16[24,768]{1,0:T(8,128)(2,1)S(1)}, u32[]{:S(2)}, u32[]{:S(2)}) collective-permute-start(bf16[24,768]{1,0:T(8,128)(2,1)} %param.21), channel_id=1, source_target_pairs={{0,6},{2,4},{4,2},{6,0},{1,7},{3,5},{5,3},{7,1},{8,14},{10,12},{12... | collective-permute-start | bytes 110600 | tf_op jit(solution)/shard_map/ppermute | solution.py:54
  33.0 41.4 %collective-permute-start.39 = (bf16[96,768]{1,0:T(8,128)(2,1)S(1)}, bf16[96,768]{1,0:T(8,128)(2,1)S(1)}, u32[]{:S(2)}, u32[]{:S(2)}) collective-permute-start(bf16[96,768]{1,0:T(8,128)(2,1)S(1)} %copy-done.85), channel_id=1, source_target_pairs={{0,2},{2,0},{4,6},{6,4},{1,3},{3,1},{5,7},{7,5},{8,10},{10,8},{12,... | collective-permute-start | bytes 442376 | tf_op jit(solution)/shard_map/ppermute | solution.py:54
  34.0 40.4 %collective-permute-start.41 = (bf16[96,768]{1,0:T(8,128)(2,1)S(1)}, bf16[96,768]{1,0:T(8,128)(2,1)S(1)}, u32[]{:S(2)}, u32[]{:S(2)}) collective-permute-start(bf16[96,768]{1,0:T(8,128)(2,1)S(1)} %copy-done.85), channel_id=1, source_target_pairs={{0,6},{2,4},{4,2},{6,0},{1,7},{3,5},{5,3},{7,1},{8,14},{10,12},{12... | collective-permute-start | bytes 442376 | tf_op jit(solution)/shard_map/ppermute | solution.py:54
  62.0 19.0 %collective-permute-start.40 = (bf16[96,768]{1,0:T(8,128)(2,1)S(1)}, bf16[96,768]{1,0:T(8,128)(2,1)S(1)}, u32[]{:S(2)}, u32[]{:S(2)}) collective-permute-start(bf16[96,768]{1,0:T(8,128)(2,1)S(1)} %copy-done.85), channel_id=1, source_target_pairs={{0,4},{2,6},{4,0},{6,2},{1,5},{3,7},{5,1},{7,3},{8,12},{10,14},{12... | collective-permute-start | bytes 442376 | tf_op jit(solution)/shard_map/ppermute | solution.py:54
  65.4 31.1 %collective-permute-start = (bf16[145,768]{1,0:T(8,128)(2,1)S(1)}, bf16[145,768]{1,0:T(8,128)(2,1)S(1)}, u32[]{:S(2)}, u32[]{:S(2)}) collective-permute-start(bf16[145,768]{1,0:T(8,128)(2,1)S(1)} %bitcast.839), channel_id=1, source_target_pairs={{0,0},{1,2},{2,1},{3,3},{4,8},{5,10},{6,9},{7,11},{8,4},{9,6},{10,... | collective-permute-start | bytes 668168 | tf_op jit(solution)/shard_map/ppermute | solution.py:50
  67.5 31.9 %collective-permute-start.26 = (bf16[96,768]{1,0:T(8,128)(2,1)S(1)}, bf16[96,768]{1,0:T(8,128)(2,1)S(1)}, u32[]{:S(2)}, u32[]{:S(2)}) collective-permute-start(bf16[96,768]{1,0:T(8,128)(2,1)S(1)} %get-tuple-element.269), channel_id=1, source_target_pairs={{0,8},{8,0},{16,24},{24,16},{1,9},{9,1},{17,25},{25,17},{2,10},{10... | collective-permute-start | bytes 442376 | tf_op jit(solution)/shard_map/ppermute | solution.py:54
  74.5 15.9 %collective-permute-start.34 = (bf16[48,1536]{1,0:T(8,128)(2,1)S(1)}, bf16[48,1536]{1,0:T(8,128)(2,1)S(1)}, u32[]{:S(2)}, u32[]{:S(2)}) collective-permute-start(bf16[48,1536]{1,0:T(8,128)(2,1)S(1)} %maximum_select_fusion.8), channel_id=1, source_target_pairs={{0,4},{2,6},{4,0},{6,2},{1,5},{3,7},{5,1},{7,3},{8,12},{10,14},{12... | collective-permute-start | bytes 442376 | tf_op jit(solution)/shard_map/ppermute | solution.py:54
  90.4 35.5 %collective-permute-start.64 = (bf16[96,768]{1,0:T(8,128)(2,1)S(1)}, bf16[96,768]{1,0:T(8,128)(2,1)S(1)}, u32[]{:S(2)}, u32[]{:S(2)}) collective-permute-start(bf16[96,768]{1,0:T(8,128)(2,1)S(1)} %get-tuple-element.255), channel_id=1, source_target_pairs={{0,8},{8,0},{16,24},{24,16},{1,9},{9,1},{17,25},{25,17},{2,10},{10... | collective-permute-start | bytes 442376 | tf_op jit(solution)/shard_map/ppermute | solution.py:54
  92.3 23.0 %collective-permute-start.65 = (bf16[96,768]{1,0:T(8,128)(2,1)S(1)}, bf16[96,768]{1,0:T(8,128)(2,1)S(1)}, u32[]{:S(2)}, u32[]{:S(2)}) collective-permute-start(bf16[96,768]{1,0:T(8,128)(2,1)S(1)} %get-tuple-element.255), channel_id=1, source_target_pairs={{0,16},{8,24},{16,0},{24,8},{1,17},{9,25},{17,1},{25,9},{2,18},{10... | collective-permute-start | bytes 442376 | tf_op jit(solution)/shard_map/ppermute | solution.py:54
  113.5 70.8 %collective-permute-start.57 = (bf16[192,384]{1,0:T(8,128)(2,1)}, bf16[192,384]{1,0:T(8,128)(2,1)}, u32[]{:S(2)}, u32[]{:S(2)}) collective-permute-start(bf16[192,384]{1,0:T(8,128)(2,1)} %get-tuple-element.261), channel_id=1, source_target_pairs={{0,8},{8,0},{16,24},{24,16},{1,9},{9,1},{17,25},{25,17},{2,10},{10... | collective-permute-start | bytes 442376 | tf_op jit(solution)/shard_map/ppermute | solution.py:54
  115.3 18.8 %collective-permute-start.43 = (bf16[384,768]{1,0:T(8,128)(2,1)}, bf16[384,768]{1,0:T(8,128)(2,1)}, u32[]{:S(2)}, u32[]{:S(2)}) collective-permute-start(bf16[384,768]{1,0:T(8,128)(2,1)} %get-tuple-element.198), channel_id=1, source_target_pairs={{0,16},{8,24},{16,0},{24,8},{1,17},{9,25},{17,1},{25,9},{2,18},{10... | collective-permute-start | bytes 1769480 | tf_op jit(solution)/shard_map/ppermute | solution.py:54
  121.8 16.6 %collective-permute-start.36 = (bf16[192,1536]{1,0:T(8,128)(2,1)}, bf16[192,1536]{1,0:T(8,128)(2,1)}, u32[]{:S(2)}, u32[]{:S(2)}) collective-permute-start(bf16[192,1536]{1,0:T(8,128)(2,1)} %get-tuple-element.192), channel_id=1, source_target_pairs={{0,8},{8,0},{16,24},{24,16},{1,9},{9,1},{17,25},{25,17},{2,10},{10... | collective-permute-start | bytes 1769480 | tf_op jit(solution)/shard_map/ppermute | solution.py:54
  125.9 23.0 %collective-permute-start.22 = (bf16[320,768]{1,0:T(8,128)(2,1)}, bf16[320,768]{1,0:T(8,128)(2,1)}, u32[]{:S(2)}, u32[]{:S(2)}) collective-permute-start(bf16[320,768]{1,0:T(8,128)(2,1)} %pad_maximum_fusion.27), channel_id=1, source_target_pairs={{0,8},{8,0},{16,24},{24,16},{1,9},{9,1},{17,25},{25,17},{2,10},{10... | collective-permute-start | bytes 1474568 | tf_op jit(solution)/shard_map/ppermute | solution.py:54
  127.4 34.1 %collective-permute-start.42 = (bf16[384,768]{1,0:T(8,128)(2,1)}, bf16[384,768]{1,0:T(8,128)(2,1)}, u32[]{:S(2)}, u32[]{:S(2)}) collective-permute-start(bf16[384,768]{1,0:T(8,128)(2,1)} %get-tuple-element.198), channel_id=1, source_target_pairs={{0,8},{8,0},{16,24},{24,16},{1,9},{9,1},{17,25},{25,17},{2,10},{10... | collective-permute-start | bytes 1769480 | tf_op jit(solution)/shard_map/ppermute | solution.py:54
  134.1 43.0 %collective-permute-start.37 = (bf16[192,1536]{1,0:T(8,128)(2,1)}, bf16[192,1536]{1,0:T(8,128)(2,1)}, u32[]{:S(2)}, u32[]{:S(2)}) collective-permute-start(bf16[192,1536]{1,0:T(8,128)(2,1)} %get-tuple-element.192), channel_id=1, source_target_pairs={{0,16},{8,24},{16,0},{24,8},{1,17},{9,25},{17,1},{25,9},{2,18},{10... | collective-permute-start | bytes 1769480 | tf_op jit(solution)/shard_map/ppermute | solution.py:54
  138.3 34.1 %collective-permute-start.44 = (bf16[384,768]{1,0:T(8,128)(2,1)}, bf16[384,768]{1,0:T(8,128)(2,1)}, u32[]{:S(2)}, u32[]{:S(2)}) collective-permute-start(bf16[384,768]{1,0:T(8,128)(2,1)} %collective-permute-done.43), channel_id=1, source_target_pairs={{0,8},{8,0},{16,24},{24,16},{1,9},{9,1},{17,25},{25,17},{2,10},{10... | collective-permute-start | bytes 1769480 | tf_op jit(solution)/shard_map/ppermute | solution.py:54
  148.9 28.5 %collective-permute-start.38 = (bf16[192,1536]{1,0:T(8,128)(2,1)}, bf16[192,1536]{1,0:T(8,128)(2,1)}, u32[]{:S(2)}, u32[]{:S(2)}) collective-permute-start(bf16[192,1536]{1,0:T(8,128)(2,1)} %collective-permute-done.36), channel_id=1, source_target_pairs={{0,16},{8,24},{16,0},{24,8},{1,17},{9,25},{17,1},{25,9},{2,18},{10... | collective-permute-start | bytes 1769480 | tf_op jit(solution)/shard_map/ppermute | solution.py:54
  200.5 21.5 %collective-permute-start.69 = (s32[145,4]{0,1:T(4,128)S(1)}, s32[145,4]{0,1:T(4,128)S(1)}, u32[]{:S(2)}, u32[]{:S(2)}) collective-permute-start(s32[145,4]{0,1:T(4,128)S(1)} %pad_add_fusion), channel_id=1, source_target_pairs={{0,0},{1,2},{2,1},{3,3},{4,8},{5,10},{6,9},{7,11},{8,4},{9,6},{10,... | collective-permute-start | bytes 6968 | tf_op jit(solution)/shard_map/ppermute | solution.py:50
  204.6 25.0 %collective-permute-start.70 = (f32[145,768]{1,0:T(8,128)}, f32[145,768]{1,0:T(8,128)S(1)}, u32[]{:S(2)}, u32[]{:S(2)}) collective-permute-start(f32[145,768]{1,0:T(8,128)} %bitcast.650), channel_id=1, source_target_pairs={{0,0},{1,2},{2,1},{3,3},{4,8},{5,10},{6,9},{7,11},{8,4},{9,6},{10,... | collective-permute-start | bytes 1336328 | tf_op jit(solution)/shard_map/ppermute | solution.py:50
  208.0 57.6 %collective-permute-start.75 = (bf16[1536,768]{1,0:T(8,128)(2,1)}, bf16[1536,768]{1,0:T(8,128)(2,1)}, u32[]{:S(2)}, u32[]{:S(2)}) collective-permute-start(bf16[1536,768]{1,0:T(8,128)(2,1)} %bitcast.197), channel_id=1, source_target_pairs={{0,1},{1,0},{2,3},{3,2},{4,5},{5,4},{6,7},{7,6},{8,9},{9,8},{10,11... | collective-permute-start | bytes 7077896 | tf_op jit(solution)/shard_map/ppermute | solution.py:54
  209.1 47.6 %collective-permute-start.74 = (bf16[768,1536]{1,0:T(8,128)(2,1)}, bf16[768,1536]{1,0:T(8,128)(2,1)}, u32[]{:S(2)}, u32[]{:S(2)}) collective-permute-start(bf16[768,1536]{1,0:T(8,128)(2,1)} %bitcast.838), channel_id=1, source_target_pairs={{0,1},{1,0},{2,3},{3,2},{4,5},{5,4},{6,7},{7,6},{8,9},{9,8},{10,11... | collective-permute-start | bytes 7077896 | tf_op jit(solution)/shard_map/ppermute | solution.py:54
  231.1 15.3 %collective-permute-start.73 = (bf16[2,96,768]{2,1,0:T(8,128)(2,1)S(1)}, bf16[2,96,768]{2,1,0:T(8,128)(2,1)S(1)}, u32[]{:S(2)}, u32[]{:S(2)}) collective-permute-start(bf16[2,96,768]{2,1,0:T(8,128)(2,1)S(1)} %get-tuple-element.149), channel_id=1, source_target_pairs={{0,24},{8,16},{16,8},{24,0},{1,25},{9,17},{17,9},{25,1},{2,26},{10... | collective-permute-start | bytes 884744 | tf_op jit(solution)/shard_map/ppermute | solution.py:54
  279.2 143.9 %collective-permute-start.148 = (bf16[1536,768]{1,0:T(8,128)(2,1)}, bf16[1536,768]{1,0:T(8,128)(2,1)}, u32[]{:S(2)}, u32[]{:S(2)}) collective-permute-start(bf16[1536,768]{1,0:T(8,128)(2,1)} %convolution_convert_fusion.2), channel_id=1, source_target_pairs={{0,1},{1,0},{2,3},{3,2},{4,5},{5,4},{6,7},{7,6},{8,9},{9,8},{10,11... | collective-permute-start | bytes 7077896 | tf_op jit(solution)/shard_map/ppermute | solution.py:54
  295.3 37.7 %collective-permute-start.79 = (f32[145,768]{1,0:T(8,128)}, f32[145,768]{1,0:T(8,128)}, u32[]{:S(2)}, u32[]{:S(2)}) collective-permute-start(f32[145,768]{1,0:T(8,128)} %fusion.70), channel_id=1, source_target_pairs={{0,0},{1,2},{2,1},{3,3},{4,8},{5,10},{6,9},{7,11},{8,4},{9,6},{10,... | collective-permute-start | bytes 1336328 | tf_op jit(solution)/shard_map/ppermute | solution.py:50
  344.0 15.9 %collective-permute-start.82 = (bf16[160,768]{1,0:T(8,128)(2,1)S(1)}, bf16[160,768]{1,0:T(8,128)(2,1)S(1)}, u32[]{:S(2)}, u32[]{:S(2)}) collective-permute-start(bf16[160,768]{1,0:T(8,128)(2,1)S(1)} %slice.527), channel_id=1, source_target_pairs={{0,1},{1,0},{2,3},{3,2},{4,5},{5,4},{6,7},{7,6},{8,9},{9,8},{10,11... | collective-permute-start | bytes 737288 | tf_op jit(solution)/shard_map/ppermute | solution.py:54
  370.5 58.2 %collective-permute-start.147 = (bf16[768,1536]{1,0:T(8,128)(2,1)}, bf16[768,1536]{1,0:T(8,128)(2,1)}, u32[]{:S(2)}, u32[]{:S(2)}) collective-permute-start(bf16[768,1536]{1,0:T(8,128)(2,1)} %convolution_convert_fusion.3), channel_id=1, source_target_pairs={{0,1},{1,0},{2,3},{3,2},{4,5},{5,4},{6,7},{7,6},{8,9},{9,8},{10,11... | collective-permute-start | bytes 7077896 | tf_op jit(solution)/shard_map/ppermute | solution.py:54
  387.8 86.5 %collective-permute-start.114 = (bf16[192,1536]{1,0:T(8,128)(2,1)}, bf16[192,1536]{1,0:T(8,128)(2,1)}, u32[]{:S(2)}, u32[]{:S(2)}) collective-permute-start(bf16[192,1536]{1,0:T(8,128)(2,1)} %get-tuple-element.125), channel_id=1, source_target_pairs={{0,8},{8,0},{16,24},{24,16},{1,9},{9,1},{17,25},{25,17},{2,10},{10... | collective-permute-start | bytes 1769480 | tf_op jit(solution)/shard_map/ppermute | solution.py:54
  391.3 24.0 %collective-permute-start.115 = (bf16[192,1536]{1,0:T(8,128)(2,1)}, bf16[192,1536]{1,0:T(8,128)(2,1)}, u32[]{:S(2)}, u32[]{:S(2)}) collective-permute-start(bf16[192,1536]{1,0:T(8,128)(2,1)} %get-tuple-element.126), channel_id=1, source_target_pairs={{0,8},{8,0},{16,24},{24,16},{1,9},{9,1},{17,25},{25,17},{2,10},{10... | collective-permute-start | bytes 1769480 | tf_op jit(solution)/shard_map/ppermute | solution.py:54
  394.0 23.7 %collective-permute-start.122 = (bf16[384,768]{1,0:T(8,128)(2,1)}, bf16[384,768]{1,0:T(8,128)(2,1)}, u32[]{:S(2)}, u32[]{:S(2)}) collective-permute-start(bf16[384,768]{1,0:T(8,128)(2,1)} %get-tuple-element.124), channel_id=1, source_target_pairs={{0,16},{8,24},{16,0},{24,8},{1,17},{9,25},{17,1},{25,9},{2,18},{10... | collective-permute-start | bytes 1769480 | tf_op jit(solution)/shard_map/ppermute | solution.py:54
  417.6 27.2 %collective-permute-start.86 = (bf16[320,768]{1,0:T(8,128)(2,1)}, bf16[320,768]{1,0:T(8,128)(2,1)}, u32[]{:S(2)}, u32[]{:S(2)}) collective-permute-start(bf16[320,768]{1,0:T(8,128)(2,1)} %fusion.52), channel_id=1, source_target_pairs={{0,8},{8,0},{16,24},{24,16},{1,9},{9,1},{17,25},{25,17},{2,10},{10... | collective-permute-start | bytes 1474568 | tf_op jit(solution)/shard_map/ppermute | solution.py:54
  421.1 55.0 %collective-permute-start.116 = (bf16[192,1536]{1,0:T(8,128)(2,1)}, bf16[192,1536]{1,0:T(8,128)(2,1)}, u32[]{:S(2)}, u32[]{:S(2)}) collective-permute-start(bf16[192,1536]{1,0:T(8,128)(2,1)} %fusion.43), channel_id=1, source_target_pairs={{0,16},{8,24},{16,0},{24,8},{1,17},{9,25},{17,1},{25,9},{2,18},{10... | collective-permute-start | bytes 1769480 | tf_op jit(solution)/shard_map/ppermute | solution.py:54
  423.1 27.5 %collective-permute-start.108 = (bf16[96,768]{1,0:T(8,128)(2,1)}, bf16[96,768]{1,0:T(8,128)(2,1)}, u32[]{:S(2)}, u32[]{:S(2)}) collective-permute-start(bf16[96,768]{1,0:T(8,128)(2,1)} %get-tuple-element.175), channel_id=1, source_target_pairs={{0,16},{8,24},{16,0},{24,8},{1,17},{9,25},{17,1},{25,9},{2,18},{10... | collective-permute-start | bytes 442376 | tf_op jit(solution)/shard_map/ppermute | solution.py:54
  456.9 21.4 %collective-permute-start.121 = (bf16[384,768]{1,0:T(8,128)(2,1)S(1)}, bf16[384,768]{1,0:T(8,128)(2,1)S(1)}, u32[]{:S(2)}, u32[]{:S(2)}) collective-permute-start(bf16[384,768]{1,0:T(8,128)(2,1)S(1)} %copy-done.49), channel_id=1, source_target_pairs={{0,16},{8,24},{16,0},{24,8},{1,17},{9,25},{17,1},{25,9},{2,18},{10... | collective-permute-start | bytes 1769480 | tf_op jit(solution)/shard_map/ppermute | solution.py:54
  461.6 18.3 %collective-permute-start.123 = (bf16[384,768]{1,0:T(8,128)(2,1)S(1)}, bf16[384,768]{1,0:T(8,128)(2,1)S(1)}, u32[]{:S(2)}, u32[]{:S(2)}) collective-permute-start(bf16[384,768]{1,0:T(8,128)(2,1)S(1)} %copy-done.50), channel_id=1, source_target_pairs={{0,8},{8,0},{16,24},{24,16},{1,9},{9,1},{17,25},{25,17},{2,10},{10... | collective-permute-start | bytes 1769480 | tf_op jit(solution)/shard_map/ppermute | solution.py:54
  476.1 120.0 %collective-permute-start.94 = (bf16[192,768]{1,0:T(8,128)(2,1)}, bf16[192,768]{1,0:T(8,128)(2,1)}, u32[]{:S(2)}, u32[]{:S(2)}) collective-permute-start(bf16[192,768]{1,0:T(8,128)(2,1)} %get-tuple-element.137), channel_id=1, source_target_pairs={{0,8},{8,0},{16,24},{24,16},{1,9},{9,1},{17,25},{25,17},{2,10},{10... | collective-permute-start | bytes 884744 | tf_op jit(solution)/shard_map/ppermute | solution.py:54
  478.3 24.0 %collective-permute-start.95 = (bf16[192,768]{1,0:T(8,128)(2,1)}, bf16[192,768]{1,0:T(8,128)(2,1)S(1)}, u32[]{:S(2)}, u32[]{:S(2)}) collective-permute-start(bf16[192,768]{1,0:T(8,128)(2,1)} %get-tuple-element.138), channel_id=1, source_target_pairs={{0,8},{8,0},{16,24},{24,16},{1,9},{9,1},{17,25},{25,17},{2,10},{10... | collective-permute-start | bytes 884744 | tf_op jit(solution)/shard_map/ppermute | solution.py:54
  479.9 15.4 %collective-permute-start.102 = (bf16[192,384]{1,0:T(8,128)(2,1)}, bf16[192,384]{1,0:T(8,128)(2,1)}, u32[]{:S(2)}, u32[]{:S(2)}) collective-permute-start(bf16[192,384]{1,0:T(8,128)(2,1)} %fusion.105), channel_id=1, source_target_pairs={{0,8},{8,0},{16,24},{24,16},{1,9},{9,1},{17,25},{25,17},{2,10},{10... | collective-permute-start | bytes 442376 | tf_op jit(solution)/shard_map/ppermute | solution.py:54
  507.2 19.9 %collective-permute-start.119 = (bf16[48,1536]{1,0:T(8,128)(2,1)}, bf16[48,1536]{1,0:T(8,128)(2,1)S(1)}, u32[]{:S(2)}, u32[]{:S(2)}) collective-permute-start(bf16[48,1536]{1,0:T(8,128)(2,1)} %get-tuple-element.173), channel_id=1, source_target_pairs={{0,6},{2,4},{4,2},{6,0},{1,7},{3,5},{5,3},{7,1},{8,14},{10,12},{12... | collective-permute-start | bytes 442376 | tf_op jit(solution)/shard_map/ppermute | solution.py:54
  509.1 29.9 %collective-permute-start.118 = (bf16[48,1536]{1,0:T(8,128)(2,1)}, bf16[48,1536]{1,0:T(8,128)(2,1)S(1)}, u32[]{:S(2)}, u32[]{:S(2)}) collective-permute-start(bf16[48,1536]{1,0:T(8,128)(2,1)} %get-tuple-element.174), channel_id=1, source_target_pairs={{0,4},{2,6},{4,0},{6,2},{1,5},{3,7},{5,1},{7,3},{8,12},{10,14},{12... | collective-permute-start | bytes 442376 | tf_op jit(solution)/shard_map/ppermute | solution.py:54
  510.6 37.6 %collective-permute-start.124 = (bf16[96,768]{1,0:T(8,128)(2,1)}, bf16[96,768]{1,0:T(8,128)(2,1)S(1)}, u32[]{:S(2)}, u32[]{:S(2)}) collective-permute-start(bf16[96,768]{1,0:T(8,128)(2,1)} %get-tuple-element.169), channel_id=1, source_target_pairs={{0,2},{2,0},{4,6},{6,4},{1,3},{3,1},{5,7},{7,5},{8,10},{10,8},{12,... | collective-permute-start | bytes 442376 | tf_op jit(solution)/shard_map/ppermute | solution.py:54
  520.2 28.2 %collective-permute-start.126 = (bf16[96,768]{1,0:T(8,128)(2,1)}, bf16[96,768]{1,0:T(8,128)(2,1)S(1)}, u32[]{:S(2)}, u32[]{:S(2)}) collective-permute-start(bf16[96,768]{1,0:T(8,128)(2,1)} %get-tuple-element.170), channel_id=1, source_target_pairs={{0,6},{2,4},{4,2},{6,0},{1,7},{3,5},{5,3},{7,1},{8,14},{10,12},{12... | collective-permute-start | bytes 442376 | tf_op jit(solution)/shard_map/ppermute | solution.py:54
  527.1 21.3 %collective-permute-start.125 = (bf16[96,768]{1,0:T(8,128)(2,1)}, bf16[96,768]{1,0:T(8,128)(2,1)S(1)}, u32[]{:S(2)}, u32[]{:S(2)}) collective-permute-start(bf16[96,768]{1,0:T(8,128)(2,1)} %get-tuple-element.171), channel_id=1, source_target_pairs={{0,4},{2,6},{4,0},{6,2},{1,5},{3,7},{5,1},{7,3},{8,12},{10,14},{12... | collective-permute-start | bytes 442376 | tf_op jit(solution)/shard_map/ppermute | solution.py:54
  546.1 71.3 %collective-permute-start.88 = (f32[145,768]{1,0:T(8,128)S(1)}, f32[145,768]{1,0:T(8,128)S(1)}, u32[]{:S(2)}, u32[]{:S(2)}) collective-permute-start(f32[145,768]{1,0:T(8,128)S(1)} %slice_add_fusion.6), channel_id=1, source_target_pairs={{0,0},{1,2},{2,1},{3,3},{4,8},{5,10},{6,9},{7,11},{8,4},{9,6},{10,... | collective-permute-start | bytes 1336328 | tf_op jit(solution)/shard_map/ppermute | solution.py:50
  548.2 47.8 %collective-permute-start.96 = (bf16[192,768]{1,0:T(8,128)(2,1)S(1)}, bf16[192,768]{1,0:T(8,128)(2,1)S(1)}, u32[]{:S(2)}, u32[]{:S(2)}) collective-permute-start(bf16[192,768]{1,0:T(8,128)(2,1)S(1)} %fusion.59), channel_id=1, source_target_pairs={{0,16},{8,24},{16,0},{24,8},{1,17},{9,25},{17,1},{25,9},{2,18},{10... | collective-permute-start | bytes 884744 | tf_op jit(solution)/shard_map/ppermute | solution.py:54
  548.3 53.9 %collective-permute-start.120 = (f32[24,1536]{1,0:T(8,128)S(1)}, f32[24,1536]{1,0:T(8,128)S(1)}, u32[]{:S(2)}, u32[]{:S(2)}) collective-permute-start(f32[24,1536]{1,0:T(8,128)S(1)} %get-tuple-element.221), channel_id=1, source_target_pairs={{0,1},{1,0},{2,3},{3,2},{4,5},{5,4},{6,7},{7,6},{8,9},{9,8},{10,11... | collective-permute-start | bytes 442376 | tf_op jit(solution)/shard_map/ppermute | solution.py:54
  548.4 46.9 %collective-permute-start.93 = (f32[8,768]{1,0:T(8,128)S(1)}, f32[8,768]{1,0:T(8,128)S(1)}, u32[]{:S(2)}, u32[]{:S(2)}) collective-permute-start(f32[8,768]{1,0:T(8,128)S(1)} %add.617), channel_id=1, source_target_pairs={{0,4},{2,6},{4,0},{6,2},{1,5},{3,7},{5,1},{7,3},{8,12},{10,14},{12... | collective-permute-start | bytes 73736 | tf_op jit(solution)/shard_map/ppermute | solution.py:54
  (250 other events, 1951.0 us)
Sparse Core Ops, SparseCore 0:
  434.6 216.1 all-reduce.5
where the time goes:
time: 676 us; the launch traced here: 665 us
  waiting for transfers between devices  274 us (41%)
  starting transfers between devices  169 us (25%)
  matrix products  84.7 us (13%)
  other arithmetic  63.6 us (9%)
  local copies, waits for them, and re-layouts  55.8 us (8%)
  between operations  17.9 us (3%)
    ppermute x144, waiting for transfers between devices, xor(): return lax.ppermute(x, axis, [(i, i ^ j) for i in range(n)])  238 us
    ppermute x144, starting transfers between devices, xor(): return lax.ppermute(x, axis, [(i, i ^ j) for i in range(n)])  151 us
    psum x1, waiting for transfers between devices, body(): e_sums.append(lax.psum(mine.astype(BF), 'context').astype(F32))  30.9 us
    dot_general x16, matrix products, t_dot(): lax.dot_general(a, b, (((0,), (0,)), ((), ())), preferred_element_type=F32)  23.3 us
    dot_general x13, matrix products, dot_t(): lax.dot_general(a, b, (((1,), (1,)), ((), ())), preferred_element_type=F32)  18.2 us
    ppermute x5, starting transfers between devices, move(): return lax.ppermute(x, ALL, self.team)  17.4 us
    dot_general x16, matrix products, dot(): return jnp.dot(a, b, preferred_element_type=F32)  16.5 us
    unnamed x299, local copies, waits for them, and re-layouts  14.5 us
  transfers between devices with their start and end apart: 150, of which 59 were waited for; matrix products, arithmetic and copies ran while one was open for 26% of the time, Pallas kernels for 0%

commit v1 on v0

v1 whole, which is shorter than its diff:
```python
import functools

import jax
import jax.numpy as jnp
from jax import lax
from jax.sharding import PartitionSpec as P

HEADS = 12
HEAD_DIM = 64
LEN = 577
TOP = 2
ALL = ("expert", "context", "dp")
CHIPS = ("expert", "context")
BF = jnp.bfloat16
F32 = jnp.float32


def up16(n):
    return (n + 15) // 16 * 16


def dot(a, b):
    return jnp.dot(a, b, preferred_element_type=F32)


def dot_t(a, b):
    return lax.dot_general(a, b, (((1,), (1,)), ((), ())), preferred_element_type=F32)


def t_dot(a, b):
    return lax.dot_general(a, b, (((0,), (0,)), ((), ())), preferred_element_type=F32)


class Links:
    def __init__(self, mesh):
        self.E = mesh.shape["expert"]
        self.C = mesh.shape["context"]
        self.D = mesh.shape["dp"]
        assert self.C == 4 and self.D == 2 and self.E % 2 == 0
        self.fast = self.E == 4
        self.chips = self.E * self.C
        flat = lambda e, c, d: (e * self.C + c) * self.D + d
        self.team = [
            (flat(e, c, d), flat((e // 2) * 2 + c // 2, 2 * (e % 2) + d, c % 2))
            for e in range(self.E)
            for c in range(self.C)
            for d in range(self.D)
        ]
        self.to_lane = [(f, (f % self.chips) * 2 + f // self.chips) for f in range(2 * self.chips)]
        self.from_lane = [(b, a) for a, b in self.to_lane]

    def move(self, x):
        return lax.ppermute(x, ALL, self.team)

    def xor(self, x, axis, j):
        n = {"expert": self.E, "context": self.C, "dp": self.D}[axis]
        return lax.ppermute(x, axis, [(i, i ^ j) for i in range(n)])

    def sib(self, x):
        return self.xor(x, "dp", 1)

    def partner(self, x):
        return self.xor(x, "expert", 1)

    def column(self, x):
        c = lax.axis_index("context")
        got = self.xor(x, "context", 1)
        x = jnp.where(c & 1 == 1, jnp.stack([got, x]), jnp.stack([x, got]))
        got = self.xor(x, "context", 2)
        return jnp.where(c & 2 == 2, jnp.concatenate([got, x]), jnp.concatenate([x, got]))

    def plane(self, x, first):
        second = 3 - first
        got = self.xor(x, "expert", first)
        far = self.xor(jnp.stack([x, got]), "expert", second)
        blocks = {0: x, first: got, second: far[0], 3: far[1]}
        return [blocks[j] for j in range(4)]

    def plane_sum(self, blk, first):
        second = 3 - first
        got = self.xor(jnp.stack([blk[first], blk[3]]), "expert", first).astype(F32)
        far = self.xor((blk[second].astype(F32) + got[1]).astype(BF), "expert", second)
        return blk[0].astype(F32) + got[0] + far.astype(F32)

    def column_sum(self, x):
        c = lax.axis_index("context")
        low, high = x[:2], x[2:]
        give = jnp.where(c & 2 == 2, low, high).astype(BF)
        x = jnp.where(c & 2 == 2, high, low) + self.xor(give, "context", 2).astype(F32)
        give = jnp.where(c & 1 == 1, x[0], x[1]).astype(BF)
        return jnp.where(c & 1 == 1, x[1], x[0]) + self.xor(give, "context", 1).astype(F32)

    def total(self, x):
        if not self.fast:
            return lax.psum(x, ALL)
        x = x + self.xor(x, "dp", 1)
        x = x + self.xor(x, "expert", 1)
        x = x + self.xor(x, "expert", 2)
        x = x + self.xor(x, "context", 1)
        return x + self.xor(x, "context", 2)

    def swap_blocks(self, x):
        if not self.fast:
            return list(lax.all_to_all(jnp.stack(x), "expert", 0, 0, tiled=True))
        return [x[0]] + [self.xor(x[j], "expert", j) for j in range(1, 4)]


def norm_parts(x):
    mean = jnp.mean(x, -1, keepdims=True)
    centre = x - mean
    scale = lax.rsqrt(jnp.mean(centre * centre, -1, keepdims=True) + 1e-06)
    return centre * scale, scale


def layer_norm(x, gain):
    return (norm_parts(x)[0] * gain).astype(BF)


def layer_norm_back(x, gain, slope, own):
    unit, scale = norm_parts(x)
    gain_slope = jnp.sum(slope[:own] * unit[:own], 0)
    inner = slope * gain
    inner = inner - jnp.mean(inner, -1, keepdims=True) - unit * jnp.mean(inner * unit, -1, keepdims=True)
    return inner * scale, gain_slope


def gelu_both(h):
    k = 0.7978845608028654
    t = jnp.tanh(k * (h + 0.044715 * h * h * h))
    return 0.5 * h * (1 + t), 0.5 * (1 + t) + 0.5 * h * (1 - t * t) * k * (1 + 3 * 0.044715 * h * h)


def lane_rows(links, mine, d):
    keep = lax.dynamic_index_in_dim(mine, d, 0, False)
    got = links.sib(lax.dynamic_index_in_dim(mine, 1 - d, 0, False))
    return jnp.where(d == 0, jnp.concatenate([keep, got], 0), jnp.concatenate([got, keep], 0))


def in_order(d, own, other):
    return jnp.where(d == 0, jnp.stack([own, other]), jnp.stack([other, own]))


class Weights:
    def __init__(self, links, rdev, feat, ff, experts):
        self.links, self.rdev, self.feat, self.ff, self.experts = links, rdev, feat, ff, experts
        self.e = lax.axis_index("expert")
        self.d = lax.axis_index("dp")
        self.half = feat // 2
        self.lane_ff = ff // 2

    def assemble(self, blocks):
        if not self.links.fast:
            return blocks
        stacked = jnp.stack(blocks)
        return jnp.concatenate(
            [lax.dynamic_index_in_dim(stacked, self.e ^ k, 0, False) for k in range(4)], 0
        )

    def split_attend(self, w):
        w = w.reshape(self.rdev, 3, 2, self.half).transpose(2, 0, 1, 3)
        return w.reshape(2, self.rdev, 3 * self.half)

    def split_widen(self, w):
        w = w.reshape(self.rdev, self.links.chips, 2, 2, -1).transpose(2, 0, 3, 1, 4)
        return w.reshape(2, self.rdev, self.lane_ff)

    def pack_attend(self, w, p, small):
        p = jnp.concatenate([p[:, : self.half], p[:, self.half :]], 0)
        parts = [w, p]
        if small is not None:
            parts.append(jnp.pad(small, ((0, 0), (0, 128 - small.shape[1]))))
        return jnp.concatenate(parts, 1)

    def pack_widen(self, w, wout):
        h = wout.shape[0] // 2
        return w, jnp.concatenate([wout[:h], wout[h:]], 1)

    def spread_attend(self, quad, first=1):
        f, h, r = self.feat, self.half, self.rdev
        n = quad.shape[0]
        qk = quad[..., :f].reshape(-1, f)
        v = quad[..., f : f + h].reshape(-1, h)
        p = quad[..., f + h : 2 * f].reshape(n, 2, r, h)
        left, right = p[:, 0].reshape(-1, h), p[:, 1].reshape(-1, h)
        rows = [v, left, right]
        has_small = quad.shape[2] > 2 * f
        if has_small:
            small = quad[..., 2 * f :].reshape(3, -1, 128)
            rows.append(jnp.concatenate([small[0], small[1], small[2]], 1))
        b = jnp.concatenate(rows, 0)
        if self.links.fast:
            a, b = self.links.plane(qk, first), self.links.plane(b, 3 - first)
            n1, n2 = v.shape[0], v.shape[0] + left.shape[0]
            n3 = n2 + left.shape[0]
            qk = self.assemble(a)
            v = self.assemble([t[:n1] for t in b])
            p = jnp.concatenate(
                [self.assemble([t[n1:n2] for t in b]), self.assemble([t[n2:n3] for t in b])], 1
            )
            if has_small:
                sm = [
                    jnp.concatenate([t[n3:, :128], t[n3:, 128:256], t[n3:, 256:]], 0) for t in b
                ]
                small = self.assemble(sm)
        else:
            p = jnp.concatenate([left, right], 1)
            if has_small:
                small = small.reshape(-1, 128)
        return (qk, v, p, small) if has_small else (qk, v, p)

    def spread_widen(self, quad_in, quad_out, first=1):
        f = self.feat
        out = []
        for i in range(2):
            a = quad_in[..., i * f : (i + 1) * f].reshape(-1, f)
            b = quad_out[..., i * f : (i + 1) * f].reshape(-1, f)
            if self.links.fast:
                n = a.shape[0]
                t = self.links.plane(jnp.concatenate([a, b], 0), first if i == 0 else 3 - first)
                out.append((self.assemble([x[:n] for x in t]), self.assemble([x[n:] for x in t])))
            else:
                out.append((a, b))
        return out

    def gather_column(self, buf):
        if self.links.fast:
            return self.links.column(buf)
        return lax.all_gather(buf, CHIPS, axis=0, tiled=False)

    def blocks(self, g):
        g = g.astype(BF).reshape(4, -1, g.shape[1])
        return [lax.dynamic_index_in_dim(g, self.e ^ j, 0, False) for j in range(4)]

    def owner_attend(self, qk, v, p, first=1):
        f, h, r, d = self.feat, self.half, self.rdev, self.d
        if self.links.fast:
            qk = self.links.plane_sum(self.blocks(qk), first)
            vb, lb, rb = self.blocks(v), self.blocks(p[:, :h]), self.blocks(p[:, h:])
            b = self.links.plane_sum(
                [jnp.concatenate(t, 0) for t in zip(vb, lb, rb)], 3 - first
            )
            n1 = 8 * r
            v, left, right = b[:n1], b[n1 : n1 + 4 * r], b[n1 + 4 * r :]
        else:
            left, right = p[:, :h], p[:, h:]
        qk, v = qk.reshape(-1, 2 * r, f), v.reshape(-1, 2 * r, h)
        p = jnp.concatenate([left.reshape(-1, r, h), right.reshape(-1, r, h)], 1)
        buf = jnp.concatenate([qk, v, p], 2)
        if self.links.fast:
            buf = self.links.column_sum(buf)
        else:
            buf = lax.psum_scatter(buf.astype(BF), CHIPS, scatter_dimension=0, tiled=False)
            buf = buf.astype(F32)
        w = buf[:, : f + h].reshape(2, r, f + h)
        p = jnp.concatenate([buf[:r, f + h :], buf[r:, f + h :]], 1)
        p = lax.ppermute(p, ALL, self.links.from_lane)
        mine = lax.dynamic_index_in_dim(w, d, 0, False)
        got = self.links.sib(lax.dynamic_index_in_dim(w, 1 - d, 0, False))
        w = in_order(d, mine, got).reshape(2, r, 3, h).transpose(1, 2, 0, 3).reshape(r, 3 * f)
        return w, p

    def owner_widen(self, halves, first=1):
        f, r, d = self.feat, self.rdev, self.d
        ins, outs = [], []
        for i, (a, b) in enumerate(halves):
            if self.links.fast:
                ab, bb = self.blocks(a), self.blocks(b)
                t = self.links.plane_sum(
                    [jnp.concatenate(x, 0) for x in zip(ab, bb)], first if i == 0 else 3 - first
                )
                a, b = t[: 8 * r], t[8 * r :]
            ins.append(a.reshape(-1, 2 * r, f))
            outs.append(b.reshape(-1, b.shape[0] // (4 if self.links.fast else self.links.chips), f))
        if self.links.fast:
            buf = self.links.column_sum(jnp.concatenate(ins + outs, 2))
            ins, outs = buf[:, : 2 * f], buf[:, 2 * f :]
        else:
            buf = [jnp.concatenate(ins, 2).astype(BF), jnp.concatenate(outs, 2).astype(BF)]
            ins, outs = [
                lax.psum_scatter(t, CHIPS, scatter_dimension=0, tiled=False).astype(F32) for t in buf
            ]
        w = ins.reshape(2, r, 2 * f)
        mine = lax.dynamic_index_in_dim(w, d, 0, False)
        got = self.links.sib(lax.dynamic_index_in_dim(w, 1 - d, 0, False))
        w = in_order(d, mine, got).reshape(2, r, 2, self.links.chips, -1)
        w = w.transpose(1, 3, 0, 2, 4).reshape(r, self.ff)
        return w, jnp.concatenate([outs[:, :f], outs[:, f:]], 0)


def body(links, *args):
    (tokens, cotangent, g1, w1, p1, g2, win, wout, g3, w3, p3, g4, router, ein, eout, routes, slots) = args
    e = lax.axis_index("expert")
    d = lax.axis_index("dp")
    blk_len, feat = tokens.shape[1:]
    rows = up16(blk_len)
    half = feat // 2
    rdev = w1.shape[0]
    ff = win.shape[1]
    longest = LEN - (blk_len - 1) * links.C
    experts = router.shape[1]
    cap = max(2, (5 * TOP * blk_len + 4 * experts - 1) // (4 * experts))
    cap_rows = up16(cap)
    blk = 2 * (e % 2) + d
    wt = Weights(links, rdev, feat, ff, experts)

    def pad(x):
        return jnp.pad(x, ((0, rows - blk_len), (0, 0)))

    def sib_cat(x):
        return jnp.concatenate([x, links.sib(x)], 0)

    small = jnp.concatenate([g1[:, None], g2[:, None], g3[:, None], g4[:, None], router], 1)
    gsm = small.shape[1]
    lane1 = jnp.concatenate(
        [wt.split_attend(w1), jnp.broadcast_to(small[None], (2, rdev, gsm))], 2
    )
    lane1 = lane_rows(links, lane1, d)
    ps = lax.ppermute(jnp.concatenate([p1, p3], 0), ALL, links.to_lane)
    x0 = sib_cat(pad(links.move(tokens[0]))).astype(F32)
    quad1 = wt.gather_column(
        wt.pack_attend(lane1[:, : 3 * half], ps[:rdev], lane1[:, 3 * half :])
    )
    wqk1, wv1, wp1, small = wt.spread_attend(quad1)
    gains = small[:, :4].T.astype(F32)
    router_all = small[:, 4:gsm]

    later = jnp.concatenate([wt.split_widen(win), wt.split_attend(w3)], 2)
    later = lane_rows(links, later, d)
    w_in, w_out = wt.pack_widen(later[:, : ff // 2], wout)
    if w_in.shape == w_out.shape:
        buf = jnp.concatenate([w_in, w_out, wt.pack_attend(later[:, ff // 2 :], ps[rdev:], None)], 1)
        buf, quad1 = lax.optimization_barrier((buf, quad1))
        quad = wt.gather_column(buf)
        quad2, quad3 = (quad[..., : ff // 2], quad[..., ff // 2 : ff]), quad[..., ff:]
    else:
        quad2 = wt.gather_column(w_in), wt.gather_column(w_out)
        quad3 = wt.gather_column(wt.pack_attend(later[:, ff // 2 :], ps[rdev:], None))
    wff = wt.spread_widen(*quad2)
    wqk3, wv3, wp3 = wt.spread_attend(quad3)

    ein_own, eout_own = ein[0], eout[0]
    ein_sib, eout_sib = links.sib(ein_own), links.sib(eout_own)

    pos = jnp.arange(rows, dtype=jnp.int32)

    def valid(b):
        return (pos < blk_len) & ((b < longest) | (pos < blk_len - 1))

    key_ok = jnp.concatenate([valid(blk ^ j) for j in range(4)])
    present = valid(blk).astype(F32)[:, None]
    up = pad(links.move(cotangent[0])) * present
    index = links.move(jnp.concatenate([routes[0], slots[0]], 1))
    index = jnp.pad(index, ((0, rows - blk_len), (0, 0)), constant_values=cap)
    chosen, slot = index[:, :TOP], index[:, TOP:]

    heads = lambda t: t.reshape(t.shape[0], -1, HEAD_DIM)

    def add_pair(x, partial, n):
        low = partial.astype(BF)
        if n == rows:
            return x[:rows] + partial[:rows] + links.sib(low[rows:]).astype(F32)
        got = links.sib(low)
        got = jnp.concatenate([got[rows:], got[:rows]], 0)
        return x + partial + got.astype(F32)

    def attend_forward(x, gain, wqk, wv, wp, n):
        normed = layer_norm(x, gain)
        qk = dot(normed, wqk).astype(BF)
        v = dot(normed, wv).astype(BF)
        q = qk[:, :half]
        kv = jnp.concatenate([qk[:, half:], v], 1)
        kv = jnp.concatenate([kv, links.partner(kv)], 0)
        s = jnp.einsum("qhd,khd->hqk", heads(q), heads(kv[:, :half]), preferred_element_type=F32) * 0.125
        s = jnp.where(key_ok[None, None, :], s, -1e9)
        top = jnp.max(s, -1, keepdims=True)
        ex = jnp.exp(s - top)
        total = jnp.sum(ex, -1, keepdims=True)
        lse = top + jnp.log(total)
        shares = (ex / total).astype(BF)
        blended = jnp.einsum("hqk,khd->qhd", shares, heads(kv[:, half:]), preferred_element_type=F32)
        blended = blended.reshape(2 * rows, half).astype(BF)
        return add_pair(x, dot(blended, wp), n), (x, normed, q, kv, lse, blended)

    def attend_backward(u, kept, gain, wqk, wv, wp, n):
        x, normed, q, kv, lse, blended = kept
        u_low = u.astype(BF)
        p_slope = t_dot(blended, u_low)
        b_slope = heads(dot_t(u_low, wp).astype(BF))
        keys, values = heads(kv[:, :half]), heads(kv[:, half:])
        s = jnp.einsum("qhd,khd->hqk", heads(q), keys, preferred_element_type=F32) * 0.125
        s = jnp.where(key_ok[None, None, :], s, -1e9)
        shares = jnp.exp(s - lse)
        ss = jnp.einsum("qhd,khd->hqk", b_slope, values, preferred_element_type=F32)
        ss = (shares * (ss - jnp.sum(shares * ss, -1, keepdims=True))).astype(BF)
        q_slope = jnp.einsum("hqk,khd->qhd", ss, keys, preferred_element_type=F32) * 0.125
        k_slope = jnp.einsum("hqk,qhd->khd", ss, heads(q), preferred_element_type=F32) * 0.125
        v_slope = jnp.einsum("hqk,qhd->khd", shares.astype(BF), b_slope, preferred_element_type=F32)
        kv_slope = jnp.concatenate([k_slope.reshape(-1, half), v_slope.reshape(-1, half)], 1)
        got = links.partner(kv_slope[2 * rows :].astype(BF)).astype(F32)
        kv_slope = (kv_slope[: 2 * rows] + got).astype(BF)
        qk_slope = jnp.concatenate([q_slope.reshape(-1, half).astype(BF), kv_slope[:, :half]], 1)
        v_slope = kv_slope[:, half:]
        n_slope = dot_t(qk_slope, wqk) + dot_t(v_slope, wv)
        dx, g_slope = norm_back(x, gain, n_slope, n)
        slopes = t_dot(normed, qk_slope), t_dot(normed, v_slope), p_slope
        return u[:n] + dx, g_slope, slopes

    def norm_back(x, gain, n_slope, n):
        n_slope = add_pair(jnp.zeros((2 * rows, 1), F32), n_slope, n)
        return layer_norm_back(x[:n], gain, n_slope, rows)

    x1, kept1 = attend_forward(x0, gains[0], wqk1, wv1, wp1, 2 * rows)
    normed2 = layer_norm(x1, gains[1])
    hidden = [dot(normed2, w) for w, _ in wff]
    active = [gelu_both(h)[0].astype(BF) for h in hidden]
    x2 = add_pair(x1, dot(active[0], wff[0][1]) + dot(active[1], wff[1][1]), 2 * rows)
    x3, kept3 = attend_forward(x2, gains[2], wqk3, wv3, wp3, rows)

    moe = layer_norm(x3, gains[3])
    gates_all = jax.nn.softmax(dot(moe, router_all), axis=-1)
    expert_ids = jnp.arange(experts, dtype=jnp.int32)
    match = (chosen[:, :, None] == expert_ids).astype(F32)
    gate = jnp.sum(gates_all[:, None, :] * match, -1)
    place = chosen ^ e if links.fast else chosen
    target = jnp.where(slot < cap, place * cap_rows + slot, experts * cap_rows)
    pick = (target[:, :, None] == jnp.arange(experts * cap_rows, dtype=jnp.int32)).astype(BF)
    pick0, pick1 = pick[:, 0], pick[:, 1]
    sent = t_dot(pick0 + pick1, moe).astype(BF)
    slope0 = (gate[:, 0:1] * up).astype(BF)
    slope1 = (gate[:, 1:2] * up).astype(BF)
    sent_slope = (t_dot(pick0, slope0) + t_dot(pick1, slope1)).astype(BF)

    def blocks(a, b):
        cut = lambda t, j: t[j * cap_rows : (j + 1) * cap_rows]
        return [jnp.concatenate([cut(a, j), cut(b, j)], 0) for j in range(experts)]

    def unblock(t):
        return jnp.concatenate([x[:cap_rows] for x in t]), jnp.concatenate([x[cap_rows:] for x in t])

    e_rows, e_slope = unblock(links.swap_blocks(blocks(sent, sent_slope)))

    def expert_half(w_in, w_out):
        h = dot(e_rows, w_in)
        act, dact = gelu_both(h)
        act = act.astype(BF)
        result = dot(act, w_out)
        hs = (dact * dot_t(e_slope, w_out)).astype(BF)
        return result, dot_t(hs, w_in), t_dot(e_rows, hs), t_dot(act, e_slope)

    half_a = expert_half(ein_own, eout_own)
    half_b = expert_half(ein_sib, eout_sib)
    back = blocks((half_a[0] + half_b[0]).astype(BF), (half_a[1] + half_b[1]).astype(BF))
    result, row_slope = unblock(links.swap_blocks(back))
    e_sums = []
    for k in (2, 3):
        mine = half_a[k] + links.sib(half_b[k].astype(BF)).astype(F32)
        e_sums.append(lax.psum(mine.astype(BF), "context").astype(F32))

    picked0, picked1 = dot(pick0, result), dot(pick1, result)
    acts = (x3 + gate[:, 0:1] * picked0 + gate[:, 1:2] * picked1) * present
    gate_slope = jnp.stack([jnp.sum(up * picked0, -1), jnp.sum(up * picked1, -1)], 1)
    all_slope = jnp.sum(gate_slope[:, :, None] * match, 1)
    logit_slope = gates_all * (all_slope - jnp.sum(gates_all * all_slope, -1, keepdims=True))
    logit_slope = logit_slope.astype(BF)
    router_slope = t_dot(moe, logit_slope)
    n_slope = dot(pick0 + pick1, row_slope) + dot_t(logit_slope, router_all)
    dx, g4_slope = layer_norm_back(x3, gains[3], n_slope, rows)
    u = up + dx
    u = jnp.concatenate([u, links.sib(u.astype(BF)).astype(F32)], 0)

    u, g3_slope, slopes3 = attend_backward(u, kept3, gains[2], wqk3, wv3, wp3, 2 * rows)
    w3_out, p3_out = wt.owner_attend(*slopes3)
    u_low = u.astype(BF)
    n_slope, slopes2 = 0.0, []
    for (wi, wo), h, a in zip(wff, hidden, active):
        h_slope = (gelu_both(h)[1] * dot_t(u_low, wo)).astype(BF)
        slopes2.append((t_dot(normed2, h_slope), t_dot(a, u_low)))
        n_slope = n_slope + dot_t(h_slope, wi)
    dx, g2_slope = norm_back(x1, gains[1], n_slope, 2 * rows)
    u = u + dx
    win_out, wout_out = wt.owner_widen(slopes2)
    u, g1_slope, slopes1 = attend_backward(u, kept1, gains[0], wqk1, wv1, wp1, rows)
    w1_out, p1_out = wt.owner_attend(*slopes1)

    small = jnp.concatenate([jnp.stack([g1_slope, g2_slope, g3_slope, g4_slope]), router_slope.T], 0)
    small = links.total(small)
    flat = (e * links.C + lax.axis_index("context")) * 2 + d
    small = small.reshape(-1, 2 * links.chips, rdev)
    small = lax.dynamic_index_in_dim(small, flat, 1, False)

    acts = links.move(acts[:blk_len])[None]
    token_slope = links.move(u[:blk_len])[None]
    return (
        acts, token_slope, small[0], w1_out, p1_out, small[1], win_out, wout_out,
        small[2], w3_out, p3_out, small[3], small[4:].T, e_sums[0][None], e_sums[1][None],
    )


def solution(mesh):
    links = Links(mesh)
    tok = P(("expert", "dp"), "context", None)
    vec, mat = P(ALL), P(ALL, None)
    ein, eout = P("expert", None, "dp"), P("expert", "dp", None)
    dense = (vec, mat, mat, vec, mat, mat, vec, mat, mat, vec, mat, ein, eout)
    return jax.shard_map(
        functools.partial(body, links),
        mesh=mesh,
        in_specs=(tok, tok) + dense + (tok, tok),
        out_specs=(tok, tok) + dense,
        check_vma=False,
    )
```

time: 676 us -> 703 us (1.040)
  the two profiles are of different devices: /device:TPU:10 before, /device:TPU:0 now
where the time goes in v1:
time: 703 us; the launch traced here: 692 us
  waiting for transfers between devices  342 us (49%)
  starting transfers between devices  104 us (15%)
  matrix products  91.2 us (13%)
  local copies, waits for them, and re-layouts  71.2 us (10%)
  other arithmetic  64.2 us (9%)
  between operations  18.7 us (3%)
    ppermute x66, waiting for transfers between devices, xor(): return lax.ppermute(x, axis, [(i, i ^ j) for i in range(n)])  330 us
    ppermute x66, starting transfers between devices, xor(): return lax.ppermute(x, axis, [(i, i ^ j) for i in range(n)])  88.5 us
    dot_general x18, matrix products, t_dot(): lax.dot_general(a, b, (((0,), (0,)), ((), ())), preferred_element_type=F32)  27.9 us
    unnamed x442, local copies, waits for them, and re-layouts  26.4 us
    dot_general x15, matrix products, dot_t(): lax.dot_general(a, b, (((1,), (1,)), ((), ())), preferred_element_type=F32)  19.3 us
    dot_general x18, matrix products, dot(): return jnp.dot(a, b, preferred_element_type=F32)  19.1 us
  transfers between devices with their start and end apart: 75, of which 35 were waited for; matrix products, arithmetic and copies ran while one was open for 27% of the time, Pallas kernels for 0%

profile of v1, /device:TPU:0, one launch (start us, length us, event | category | flops | bytes accessed | tf_op | source)
XLA Modules:
  0.0 691.6 jit_solution(430375496108988259)
XLA Ops:
  10.6 5.2 collective-permute-start.27
  20.3 3.1 collective-permute-start.12
  26.3 6.6 collective-permute-start.31
  33.3 8.0 %collective-permute-start.1 = (bf16[160,768]{1,0:T(8,128)(2,1)S(1)}, bf16[160,768]{1,0:T(8,128)(2,1)S(1)}, u32[]{:S(2)}, u32[]{:S(2)}) collective-permute-start(bf16[160,768]{1,0:T(8,128)(2,1)S(1)} %pad.16), channel_id=1, source_target_pairs={{0,1},{1,0},{2,3},{3,2},{4,5},{5,4},{6,7},{7,6},{8,9},{9,8},{10,11... | collective-permute-start | bytes 737288 | tf_op jit(solution)/shard_map/ppermute | solution.py:57
  41.3 3.5 collective-permute-done.4
  44.9 10.1 %collective-permute-start.5 = (bf16[2,48,1664]{2,1,0:T(8,128)(2,1)S(1)}, bf16[2,48,1664]{2,1,0:T(8,128)(2,1)S(1)}, u32[]{:S(2)}, u32[]{:S(2)}) collective-permute-start(bf16[2,48,1664]{2,1,0:T(8,128)(2,1)S(1)} %maximum_select_fusion.4), channel_id=1, source_target_pairs={{0,4},{2,6},{4,0},{6,2},{1,5},{3,7},{5,1},{7,3},{8,12},{10,14},{12... | collective-permute-start | bytes 958472 | tf_op jit(solution)/shard_map/ppermute | solution.py:57
  56.9 12.6 %collective-permute-done.5 = bf16[2,48,1664]{2,1,0:T(8,128)(2,1)S(1)} collective-permute-done((bf16[2,48,1664]{2,1,0:T(8,128)(2,1)S(1)}, bf16[2,48,1664]{2,1,0:T(8,128)(2,1)S(1)}, u32[]{:S(2)}, u32[]{:S(2)}) %collective-permute-start.5) | collective-permute-done | bytes 319520 | tf_op jit(solution)/shard_map/ppermute | solution.py:57
  69.8 5.6 collective-permute-start.8
  75.6 6.9 %collective-permute-done.8 = bf16[192,768]{1,0:T(8,128)(2,1)S(1)} collective-permute-done((bf16[192,768]{1,0:T(8,128)(2,1)S(1)}, bf16[192,768]{1,0:T(8,128)(2,1)S(1)}, u32[]{:S(2)}, u32[]{:S(2)}) %collective-permute-start.8) | collective-permute-done | bytes 294944 | tf_op jit(solution)/shard_map/ppermute | solution.py:57
  87.6 10.2 %collective-permute-done.9 = bf16[2,192,768]{2,1,0:T(8,128)(2,1)S(1)} collective-permute-done((bf16[2,192,768]{2,1,0:T(8,128)(2,1)S(1)}, bf16[2,192,768]{2,1,0:T(8,128)(2,1)S(1)}, u32[]{:S(2)}, u32[]{:S(2)}) %collective-permute-start.9) | collective-permute-done | bytes 589856 | tf_op jit(solution)/shard_map/ppermute | solution.py:57
  98.0 3.4 collective-permute-done.7
  107.5 20.4 %collective-permute-done.14 = bf16[2,48,4608]{2,1,0:T(8,128)(2,1)} collective-permute-done((bf16[2,48,4608]{2,1,0:T(8,128)(2,1)S(1)}, bf16[2,48,4608]{2,1,0:T(8,128)(2,1)}, u32[]{:S(2)}, u32[]{:S(2)}) %collective-permute-start.14) | collective-permute-done | bytes 884768 | tf_op jit(solution)/shard_map/ppermute | solution.py:57
  149.3 3.3 collective-permute-done.22
  157.2 4.0 collective-permute-done.15
  166.2 4.5 collective-permute-done.21
  171.8 23.8 %collective-permute-done.16 = bf16[2,384,768]{2,1,0:T(8,128)(2,1)S(1)} collective-permute-done((bf16[2,384,768]{2,1,0:T(8,128)(2,1)S(1)}, bf16[2,384,768]{2,1,0:T(8,128)(2,1)S(1)}, u32[]{:S(2)}, u32[]{:S(2)}) %collective-permute-start.16) | collective-permute-done | bytes 1179680 | tf_op jit(solution)/shard_map/ppermute | solution.py:57
  201.9 8.7 %collective-permute-done.23 = bf16[2,384,384]{2,1,0:T(8,128)(2,1)S(1)} collective-permute-done((bf16[2,384,384]{2,1,0:T(8,128)(2,1)S(1)}, bf16[2,384,384]{2,1,0:T(8,128)(2,1)S(1)}, u32[]{:S(2)}, u32[]{:S(2)}) %collective-permute-start.23) | collective-permute-done | bytes 589856 | tf_op jit(solution)/shard_map/ppermute | solution.py:57
  218.1 8.8 %collective-permute-done.24 = bf16[320,768]{1,0:T(8,128)(2,1)} collective-permute-done((bf16[320,768]{1,0:T(8,128)(2,1)}, bf16[320,768]{1,0:T(8,128)(2,1)}, u32[]{:S(2)}, u32[]{:S(2)}) %collective-permute-start.24) | collective-permute-done | bytes 491552 | tf_op jit(solution)/shard_map/ppermute | solution.py:57
  247.9 7.1 %collective-permute-done.30 = bf16[192,768]{1,0:T(8,128)(2,1)S(1)} collective-permute-done((bf16[192,768]{1,0:T(8,128)(2,1)S(1)}, bf16[192,768]{1,0:T(8,128)(2,1)S(1)}, u32[]{:S(2)}, u32[]{:S(2)}) %collective-permute-start.30) | collective-permute-done | bytes 294944 | tf_op jit(solution)/shard_map/ppermute | solution.py:57
  255.1 5.5 collective-permute-done.29
  261.7 3.6 fusion.182
  265.3 4.5 fusion.6
  271.0 3.0 convolution_convert_fusion
  274.0 3.2 fusion.164
  277.2 4.7 fusion.26
  284.7 3.2 fusion.27
  295.1 3.8 collective-permute-done.35
  298.9 5.3 collective-permute-done.34
  309.3 5.2 collective-permute-start.36
  317.4 4.5 multiply_reduce_fusion.1
  341.3 4.0 collective-permute-done.38
  373.1 5.4 collective-permute-done.67
  379.4 26.8 %collective-permute-done.65 = bf16[192,768]{1,0:T(8,128)(2,1)S(1)} collective-permute-done((bf16[192,768]{1,0:T(8,128)(2,1)S(1)}, bf16[192,768]{1,0:T(8,128)(2,1)S(1)}, u32[]{:S(2)}, u32[]{:S(2)}) %collective-permute-start.65) | collective-permute-done | bytes 294944 | tf_op jit(solution)/shard_map/ppermute | solution.py:57
  411.5 4.4 multiply_reduce_fusion
  425.1 3.2 collective-permute-start.69
  434.5 5.8 fusion.5
  441.2 4.5 fusion.4
  473.3 16.6 %collective-permute-done.45 = f32[8,768]{1,0:T(8,128)S(1)} collective-permute-done((f32[8,768]{1,0:T(8,128)S(1)}, f32[8,768]{1,0:T(8,128)S(1)}, u32[]{:S(2)}, u32[]{:S(2)}) %collective-permute-start.45) | collective-permute-done | bytes 24608 | tf_op jit(solution)/shard_map/ppermute | solution.py:57
  495.4 3.1 collective-permute-done.47
  498.5 3.6 collective-permute-start.48
  503.0 4.7 collective-permute-done.48
  523.2 2.8 collective-permute-start.53
  526.3 40.5 %collective-permute-done.53 = bf16[2,48,1536]{2,1,0:T(8,128)(2,1)S(1)} collective-permute-done((bf16[2,48,1536]{2,1,0:T(8,128)(2,1)S(1)}, bf16[2,48,1536]{2,1,0:T(8,128)(2,1)S(1)}, u32[]{:S(2)}, u32[]{:S(2)}) %collective-permute-start.53) | collective-permute-done | bytes 294944 | tf_op jit(solution)/shard_map/ppermute | solution.py:57
  567.2 7.9 %collective-permute-done.54 = bf16[48,1536]{1,0:T(8,128)(2,1)S(1)} collective-permute-done((bf16[48,1536]{1,0:T(8,128)(2,1)S(1)}, bf16[48,1536]{1,0:T(8,128)(2,1)S(1)}, u32[]{:S(2)}, u32[]{:S(2)}) %collective-permute-start.54) | collective-permute-done | bytes 147488 | tf_op jit(solution)/shard_map/ppermute | solution.py:57
  575.3 56.5 %collective-permute-done.61 = bf16[2,48,3072]{2,1,0:T(8,128)(2,1)S(1)} collective-permute-done((bf16[2,48,3072]{2,1,0:T(8,128)(2,1)S(1)}, bf16[2,48,3072]{2,1,0:T(8,128)(2,1)S(1)}, u32[]{:S(2)}, u32[]{:S(2)}) %collective-permute-start.61) | collective-permute-done | bytes 589856 | tf_op jit(solution)/shard_map/ppermute | solution.py:57
  636.2 21.6 %collective-permute-done.62 = bf16[48,3072]{1,0:T(8,128)(2,1)S(1)} collective-permute-done((bf16[48,3072]{1,0:T(8,128)(2,1)S(1)}, bf16[48,3072]{1,0:T(8,128)(2,1)S(1)}, u32[]{:S(2)}, u32[]{:S(2)}) %collective-permute-start.62) | collective-permute-done | bytes 294944 | tf_op jit(solution)/shard_map/ppermute | solution.py:57
  663.9 11.9 %all-reduce.7.cloned.1.call-done = (bf16[1,768,1536]{2,1,0:T(8,128)(2,1)}, bf16[1,1536,768]{2,1,0:T(8,128)(2,1)}) async-done(((bf16[1,768,1536]{2,1,0:T(8,128)(2,1)}, bf16[1,1536,768]{2,1,0:T(8,128)(2,1)}), (bf16[1,768,1536]{2,1,0:T(8,128)(2,1)}, bf16[1,1536,768]{2,1,0:T(8,128)(2,1)})) %all-reduce.7.cloned.1.call-update) | async-done | bytes 4718608 | tf_op jit(solution)/shard_map/psum | solution.py:457
  675.8 4.6 broadcast_in_dim.63
  (924 shorter events, 242.8 us)
Async XLA Ops:
  7.3 668.6 %all-reduce.7.cloned.1.call-start = ((), (), s32[]{:S(2)}) async-start(), calls=%async_computation | async-start | bytes 9437184 | tf_op jit(solution)/shard_map/psum | solution.py:457
  8.1 16.0 %collective-permute-start.26 = (s32[145,4]{0,1:T(4,128)S(1)}, s32[145,4]{0,1:T(4,128)S(1)}, u32[]{:S(2)}, u32[]{:S(2)}) collective-permute-start(s32[145,4]{0,1:T(4,128)S(1)} %pad_add_fusion), channel_id=1, source_target_pairs={{0,0},{1,2},{2,1},{3,3},{4,8},{5,10},{6,9},{7,11},{8,4},{9,6},{10,... | collective-permute-start | bytes 6968 | tf_op jit(solution)/shard_map/ppermute | solution.py:53
  10.6 229.9 %collective-permute-start.27 = (f32[145,768]{1,0:T(8,128)}, f32[145,768]{1,0:T(8,128)}, u32[]{:S(2)}, u32[]{:S(2)}) collective-permute-start(f32[145,768]{1,0:T(8,128)} %bitcast.554), channel_id=1, source_target_pairs={{0,0},{1,2},{2,1},{3,3},{4,8},{5,10},{6,9},{7,11},{8,4},{9,6},{10,... | collective-permute-start | bytes 1336328 | tf_op jit(solution)/shard_map/ppermute | solution.py:53
  18.3 14.6 %collective-permute-start.3 = (bf16[48,768]{1,0:T(8,128)(2,1)S(1)}, bf16[48,768]{1,0:T(8,128)(2,1)S(1)}, u32[]{:S(2)}, u32[]{:S(2)}) collective-permute-start(bf16[48,768]{1,0:T(8,128)(2,1)S(1)} %pad_maximum_fusion.80), channel_id=1, source_target_pairs={{0,0},{1,2},{2,4},{3,6},{4,8},{5,10},{6,12},{7,14},{8,16},{9,18},{... | collective-permute-start | bytes 221192 | tf_op jit(solution)/shard_map/ppermute | solution.py:318
  20.3 12.8 %collective-permute-start.12 = (bf16[24,2688]{1,0:T(8,128)(2,1)S(1)}, bf16[24,2688]{1,0:T(8,128)(2,1)S(1)}, u32[]{:S(2)}, u32[]{:S(2)}) collective-permute-start(bf16[24,2688]{1,0:T(8,128)(2,1)S(1)} %get-tuple-element.352), channel_id=1, source_target_pairs={{0,1},{1,0},{2,3},{3,2},{4,5},{5,4},{6,7},{7,6},{8,9},{9,8},{10,11... | collective-permute-start | bytes 387080 | tf_op jit(solution)/shard_map/ppermute | solution.py:57
  26.3 235.4 %collective-permute-start.31 = (bf16[768,1536]{1,0:T(8,128)(2,1)}, bf16[768,1536]{1,0:T(8,128)(2,1)}, u32[]{:S(2)}, u32[]{:S(2)}) collective-permute-start(bf16[768,1536]{1,0:T(8,128)(2,1)} %bitcast.685), channel_id=1, source_target_pairs={{0,1},{1,0},{2,3},{3,2},{4,5},{5,4},{6,7},{7,6},{8,9},{9,8},{10,11... | collective-permute-start | bytes 7077896 | tf_op jit(solution)/shard_map/ppermute | solution.py:57
  33.3 21.7 %collective-permute-start.1 = (bf16[160,768]{1,0:T(8,128)(2,1)S(1)}, bf16[160,768]{1,0:T(8,128)(2,1)S(1)}, u32[]{:S(2)}, u32[]{:S(2)}) collective-permute-start(bf16[160,768]{1,0:T(8,128)(2,1)S(1)} %pad.16), channel_id=1, source_target_pairs={{0,1},{1,0},{2,3},{3,2},{4,5},{5,4},{6,7},{7,6},{8,9},{9,8},{10,11... | collective-permute-start | bytes 737288 | tf_op jit(solution)/shard_map/ppermute | solution.py:57
  44.9 24.6 %collective-permute-start.5 = (bf16[2,48,1664]{2,1,0:T(8,128)(2,1)S(1)}, bf16[2,48,1664]{2,1,0:T(8,128)(2,1)S(1)}, u32[]{:S(2)}, u32[]{:S(2)}) collective-permute-start(bf16[2,48,1664]{2,1,0:T(8,128)(2,1)S(1)} %maximum_select_fusion.4), channel_id=1, source_target_pairs={{0,4},{2,6},{4,0},{6,2},{1,5},{3,7},{5,1},{7,3},{8,12},{10,14},{12... | collective-permute-start | bytes 958472 | tf_op jit(solution)/shard_map/ppermute | solution.py:57
  69.8 12.8 %collective-permute-start.8 = (bf16[192,768]{1,0:T(8,128)(2,1)S(1)}, bf16[192,768]{1,0:T(8,128)(2,1)S(1)}, u32[]{:S(2)}, u32[]{:S(2)}) collective-permute-start(bf16[192,768]{1,0:T(8,128)(2,1)S(1)} %bitcast.587), channel_id=1, source_target_pairs={{0,8},{8,0},{16,24},{24,16},{1,9},{9,1},{17,25},{25,17},{2,10},{10... | collective-permute-start | bytes 884744 | tf_op jit(solution)/shard_map/ppermute | solution.py:57
  82.6 15.2 %collective-permute-start.9 = (bf16[2,192,768]{2,1,0:T(8,128)(2,1)S(1)}, bf16[2,192,768]{2,1,0:T(8,128)(2,1)S(1)}, u32[]{:S(2)}, u32[]{:S(2)}) collective-permute-start(bf16[2,192,768]{2,1,0:T(8,128)(2,1)S(1)} %pad_maximum_fusion.23), channel_id=1, source_target_pairs={{0,16},{8,24},{16,0},{24,8},{1,17},{9,25},{17,1},{25,9},{2,18},{10... | collective-permute-start | bytes 1769480 | tf_op jit(solution)/shard_map/ppermute | solution.py:57
  85.6 15.9 %collective-permute-start.7 = (bf16[2,448,384]{2,1,0:T(8,128)(2,1)S(1)}, bf16[2,448,384]{2,1,0:T(8,128)(2,1)S(1)}, u32[]{:S(2)}, u32[]{:S(2)}) collective-permute-start(bf16[2,448,384]{2,1,0:T(8,128)(2,1)S(1)} %pad_maximum_fusion.22), channel_id=1, source_target_pairs={{0,8},{8,0},{16,24},{24,16},{1,9},{9,1},{17,25},{25,17},{2,10},{10... | collective-permute-start | bytes 2064392 | tf_op jit(solution)/shard_map/ppermute | solution.py:57
  87.5 40.4 %collective-permute-start.14 = (bf16[2,48,4608]{2,1,0:T(8,128)(2,1)S(1)}, bf16[2,48,4608]{2,1,0:T(8,128)(2,1)}, u32[]{:S(2)}, u32[]{:S(2)}) collective-permute-start(bf16[2,48,4608]{2,1,0:T(8,128)(2,1)S(1)} %maximum_select_fusion.1), channel_id=1, source_target_pairs={{0,4},{2,6},{4,0},{6,2},{1,5},{3,7},{5,1},{7,3},{8,12},{10,14},{12... | collective-permute-start | bytes 2654216 | tf_op jit(solution)/shard_map/ppermute | solution.py:57
  105.0 29.7 %collective-permute-start.10 = (bf16[320,768]{1,0:T(8,128)(2,1)}, bf16[320,768]{1,0:T(8,128)(2,1)}, u32[]{:S(2)}, u32[]{:S(2)}) collective-permute-start(bf16[320,768]{1,0:T(8,128)(2,1)} %pad_maximum_fusion.40), channel_id=1, source_target_pairs={{0,8},{8,0},{16,24},{24,16},{1,9},{9,1},{17,25},{25,17},{2,10},{10... | collective-permute-start | bytes 1474568 | tf_op jit(solution)/shard_map/ppermute | solution.py:57
  130.7 23.8 %collective-permute-start.17 = (bf16[384,768]{1,0:T(8,128)(2,1)}, bf16[384,768]{1,0:T(8,128)(2,1)}, u32[]{:S(2)}, u32[]{:S(2)}) collective-permute-start(bf16[384,768]{1,0:T(8,128)(2,1)} %get-tuple-element.265), channel_id=1, source_target_pairs={{0,16},{8,24},{16,0},{24,8},{1,17},{9,25},{17,1},{25,9},{2,18},{10... | collective-permute-start | bytes 1769480 | tf_op jit(solution)/shard_map/ppermute | solution.py:57
  132.0 14.2 %collective-permute-start.20 = (bf16[192,768]{1,0:T(8,128)(2,1)S(1)}, bf16[192,768]{1,0:T(8,128)(2,1)}, u32[]{:S(2)}, u32[]{:S(2)}) collective-permute-start(bf16[192,768]{1,0:T(8,128)(2,1)S(1)} %bitcast.584), channel_id=1, source_target_pairs={{0,8},{8,0},{16,24},{24,16},{1,9},{9,1},{17,25},{25,17},{2,10},{10... | collective-permute-start | bytes 884744 | tf_op jit(solution)/shard_map/ppermute | solution.py:57
  134.7 17.9 %collective-permute-start.22 = (bf16[384,384]{1,0:T(8,128)(2,1)}, bf16[384,384]{1,0:T(8,128)(2,1)}, u32[]{:S(2)}, u32[]{:S(2)}) collective-permute-start(bf16[384,384]{1,0:T(8,128)(2,1)} %get-tuple-element.342), channel_id=1, source_target_pairs={{0,16},{8,24},{16,0},{24,8},{1,17},{9,25},{17,1},{25,9},{2,18},{10... | collective-permute-start | bytes 884744 | tf_op jit(solution)/shard_map/ppermute | solution.py:57
  146.9 14.4 %collective-permute-start.15 = (bf16[384,768]{1,0:T(8,128)(2,1)S(1)}, bf16[384,768]{1,0:T(8,128)(2,1)S(1)}, u32[]{:S(2)}, u32[]{:S(2)}) collective-permute-start(bf16[384,768]{1,0:T(8,128)(2,1)S(1)} %copy-done.60), channel_id=1, source_target_pairs={{0,8},{8,0},{16,24},{24,16},{1,9},{9,1},{17,25},{25,17},{2,10},{10... | collective-permute-start | bytes 1769480 | tf_op jit(solution)/shard_map/ppermute | solution.py:57
  154.5 16.2 %collective-permute-start.21 = (bf16[2,192,768]{2,1,0:T(8,128)(2,1)S(1)}, bf16[2,192,768]{2,1,0:T(8,128)(2,1)S(1)}, u32[]{:S(2)}, u32[]{:S(2)}) collective-permute-start(bf16[2,192,768]{2,1,0:T(8,128)(2,1)S(1)} %pad_maximum_fusion.28), channel_id=1, source_target_pairs={{0,16},{8,24},{16,0},{24,8},{1,17},{9,25},{17,1},{25,9},{2,18},{10... | collective-permute-start | bytes 1769480 | tf_op jit(solution)/shard_map/ppermute | solution.py:57
  161.2 35.5 %collective-permute-start.18 = (bf16[2,384,768]{2,1,0:T(8,128)(2,1)S(1)}, bf16[2,384,768]{2,1,0:T(8,128)(2,1)S(1)}, u32[]{:S(2)}, u32[]{:S(2)}) collective-permute-start(bf16[2,384,768]{2,1,0:T(8,128)(2,1)S(1)} %pad_maximum_fusion.8), channel_id=1, source_target_pairs={{0,8},{8,0},{16,24},{24,16},{1,9},{9,1},{17,25},{25,17},{2,10},{10... | collective-permute-start | bytes 3538952 | tf_op jit(solution)/shard_map/ppermute | solution.py:57
  163.9 31.7 %collective-permute-start.16 = (bf16[2,384,768]{2,1,0:T(8,128)(2,1)S(1)}, bf16[2,384,768]{2,1,0:T(8,128)(2,1)S(1)}, u32[]{:S(2)}, u32[]{:S(2)}) collective-permute-start(bf16[2,384,768]{2,1,0:T(8,128)(2,1)S(1)} %pad_maximum_fusion.3), channel_id=1, source_target_pairs={{0,16},{8,24},{16,0},{24,8},{1,17},{9,25},{17,1},{25,9},{2,18},{10... | collective-permute-start | bytes 3538952 | tf_op jit(solution)/shard_map/ppermute | solution.py:57
  170.7 106.5 %collective-permute-start.32 = (bf16[1536,768]{1,0:T(8,128)(2,1)}, bf16[1536,768]{1,0:T(8,128)(2,1)}, u32[]{:S(2)}, u32[]{:S(2)}) collective-permute-start(bf16[1536,768]{1,0:T(8,128)(2,1)} %bitcast.143), channel_id=1, source_target_pairs={{0,1},{1,0},{2,3},{3,2},{4,5},{5,4},{6,7},{7,6},{8,9},{9,8},{10,11... | collective-permute-start | bytes 7077896 | tf_op jit(solution)/shard_map/ppermute | solution.py:57
  195.6 15.0 %collective-permute-start.23 = (bf16[2,384,384]{2,1,0:T(8,128)(2,1)S(1)}, bf16[2,384,384]{2,1,0:T(8,128)(2,1)S(1)}, u32[]{:S(2)}, u32[]{:S(2)}) collective-permute-start(bf16[2,384,384]{2,1,0:T(8,128)(2,1)S(1)} %pad_maximum_fusion.29), channel_id=1, source_target_pairs={{0,8},{8,0},{16,24},{24,16},{1,9},{9,1},{17,25},{25,17},{2,10},{10... | collective-permute-start | bytes 1769480 | tf_op jit(solution)/shard_map/ppermute | solution.py:57
  214.6 12.3 %collective-permute-start.24 = (bf16[320,768]{1,0:T(8,128)(2,1)}, bf16[320,768]{1,0:T(8,128)(2,1)}, u32[]{:S(2)}, u32[]{:S(2)}) collective-permute-start(bf16[320,768]{1,0:T(8,128)(2,1)} %pad_maximum_fusion.41), channel_id=1, source_target_pairs={{0,8},{8,0},{16,24},{24,16},{1,9},{9,1},{17,25},{25,17},{2,10},{10... | collective-permute-start | bytes 1474568 | tf_op jit(solution)/shard_map/ppermute | solution.py:57
  245.7 14.8 %collective-permute-start.29 = (bf16[192,768]{1,0:T(8,128)(2,1)S(1)}, bf16[192,768]{1,0:T(8,128)(2,1)S(1)}, u32[]{:S(2)}, u32[]{:S(2)}) collective-permute-start(bf16[192,768]{1,0:T(8,128)(2,1)S(1)} %pad_maximum_fusion.54), channel_id=1, source_target_pairs={{0,16},{8,24},{16,0},{24,8},{1,17},{9,25},{17,1},{25,9},{2,18},{10... | collective-permute-start | bytes 884744 | tf_op jit(solution)/shard_map/ppermute | solution.py:57
  246.5 14.1 %collective-permute-start.28 = (bf16[192,768]{1,0:T(8,128)(2,1)S(1)}, bf16[192,768]{1,0:T(8,128)(2,1)S(1)}, u32[]{:S(2)}, u32[]{:S(2)}) collective-permute-start(bf16[192,768]{1,0:T(8,128)(2,1)S(1)} %pad_maximum_fusion.53), channel_id=1, source_target_pairs={{0,8},{8,0},{16,24},{24,16},{1,9},{9,1},{17,25},{25,17},{2,10},{10... | collective-permute-start | bytes 884744 | tf_op jit(solution)/shard_map/ppermute | solution.py:57
  289.5 14.7 %collective-permute-start.34 = (bf16[192,768]{1,0:T(8,128)(2,1)S(1)}, bf16[192,768]{1,0:T(8,128)(2,1)S(1)}, u32[]{:S(2)}, u32[]{:S(2)}) collective-permute-start(bf16[192,768]{1,0:T(8,128)(2,1)S(1)} %pad_maximum_fusion.57), channel_id=1, source_target_pairs={{0,16},{8,24},{16,0},{24,8},{1,17},{9,25},{17,1},{25,9},{2,18},{10... | collective-permute-start | bytes 884744 | tf_op jit(solution)/shard_map/ppermute | solution.py:57
  294.6 145.7 %collective-permute-start.72 = (bf16[768,1536]{1,0:T(8,128)(2,1)}, bf16[768,1536]{1,0:T(8,128)(2,1)}, u32[]{:S(2)}, u32[]{:S(2)}) collective-permute-start(bf16[768,1536]{1,0:T(8,128)(2,1)} %convolution_convert_fusion.1), channel_id=1, source_target_pairs={{0,1},{1,0},{2,3},{3,2},{4,5},{5,4},{6,7},{7,6},{8,9},{9,8},{10,11... | collective-permute-start | bytes 7077896 | tf_op jit(solution)/shard_map/ppermute | solution.py:57
  294.6 139.8 %collective-permute-start.73 = (bf16[1536,768]{1,0:T(8,128)(2,1)}, bf16[1536,768]{1,0:T(8,128)(2,1)}, u32[]{:S(2)}, u32[]{:S(2)}) collective-permute-start(bf16[1536,768]{1,0:T(8,128)(2,1)} %convolution_convert_fusion), channel_id=1, source_target_pairs={{0,1},{1,0},{2,3},{3,2},{4,5},{5,4},{6,7},{7,6},{8,9},{9,8},{10,11... | collective-permute-start | bytes 7077896 | tf_op jit(solution)/shard_map/ppermute | solution.py:57
  309.3 29.7 %collective-permute-start.36 = (f32[145,768]{1,0:T(8,128)}, f32[145,768]{1,0:T(8,128)}, u32[]{:S(2)}, u32[]{:S(2)}) collective-permute-start(f32[145,768]{1,0:T(8,128)} %fusion.91), channel_id=1, source_target_pairs={{0,0},{1,2},{2,1},{3,3},{4,8},{5,10},{6,9},{7,11},{8,4},{9,6},{10,... | collective-permute-start | bytes 1336328 | tf_op jit(solution)/shard_map/ppermute | solution.py:53
  349.6 19.3 %collective-permute-start.66 = (bf16[2,384,384]{2,1,0:T(8,128)(2,1)S(1)}, bf16[2,384,384]{2,1,0:T(8,128)(2,1)S(1)}, u32[]{:S(2)}, u32[]{:S(2)}) collective-permute-start(bf16[2,384,384]{2,1,0:T(8,128)(2,1)S(1)} %pad_maximum_fusion.38), channel_id=1, source_target_pairs={{0,16},{8,24},{16,0},{24,8},{1,17},{9,25},{17,1},{25,9},{2,18},{10... | collective-permute-start | bytes 1769480 | tf_op jit(solution)/shard_map/ppermute | solution.py:57
  351.2 20.3 %collective-permute-start.64 = (bf16[2,192,768]{2,1,0:T(8,128)(2,1)S(1)}, bf16[2,192,768]{2,1,0:T(8,128)(2,1)S(1)}, u32[]{:S(2)}, u32[]{:S(2)}) collective-permute-start(bf16[2,192,768]{2,1,0:T(8,128)(2,1)S(1)} %pad_maximum_fusion.37), channel_id=1, source_target_pairs={{0,8},{8,0},{16,24},{24,16},{1,9},{9,1},{17,25},{25,17},{2,10},{10... | collective-permute-start | bytes 1769480 | tf_op jit(solution)/shard_map/ppermute | solution.py:57
  363.5 44.9 %collective-permute-start.40 = (bf16[320,768]{1,0:T(8,128)(2,1)S(1)}, bf16[320,768]{1,0:T(8,128)(2,1)S(1)}, u32[]{:S(2)}, u32[]{:S(2)}) collective-permute-start(bf16[320,768]{1,0:T(8,128)(2,1)S(1)} %get-tuple-element.400), channel_id=1, source_target_pairs={{0,1},{1,0},{2,3},{3,2},{4,5},{5,4},{6,7},{7,6},{8,9},{9,8},{10,11... | collective-permute-start | bytes 1474568 | tf_op jit(solution)/shard_map/ppermute | solution.py:57
  371.5 91.8 %collective-permute-start.59 = (bf16[2,384,768]{2,1,0:T(8,128)(2,1)}, bf16[2,384,768]{2,1,0:T(8,128)(2,1)}, u32[]{:S(2)}, u32[]{:S(2)}) collective-permute-start(bf16[2,384,768]{2,1,0:T(8,128)(2,1)} %pad_maximum_fusion.16), channel_id=1, source_target_pairs={{0,16},{8,24},{16,0},{24,8},{1,17},{9,25},{17,1},{25,9},{2,18},{10... | collective-permute-start | bytes 3538952 | tf_op jit(solution)/shard_map/ppermute | solution.py:57
  378.5 27.6 %collective-permute-start.65 = (bf16[192,768]{1,0:T(8,128)(2,1)S(1)}, bf16[192,768]{1,0:T(8,128)(2,1)S(1)}, u32[]{:S(2)}, u32[]{:S(2)}) collective-permute-start(bf16[192,768]{1,0:T(8,128)(2,1)S(1)} %fusion.99), channel_id=1, source_target_pairs={{0,16},{8,24},{16,0},{24,8},{1,17},{9,25},{17,1},{25,9},{2,18},{10... | collective-permute-start | bytes 884744 | tf_op jit(solution)/shard_map/ppermute | solution.py:57
  406.1 61.8 %collective-permute-start.57 = (bf16[2,384,768]{2,1,0:T(8,128)(2,1)}, bf16[2,384,768]{2,1,0:T(8,128)(2,1)}, u32[]{:S(2)}, u32[]{:S(2)}) collective-permute-start(bf16[2,384,768]{2,1,0:T(8,128)(2,1)} %pad_maximum_fusion.15), channel_id=1, source_target_pairs={{0,8},{8,0},{16,24},{24,16},{1,9},{9,1},{17,25},{25,17},{2,10},{10... | collective-permute-start | bytes 3538952 | tf_op jit(solution)/shard_map/ppermute | solution.py:57
  408.5 15.5 %collective-permute-start.68 = (bf16[2,48,1536]{2,1,0:T(8,128)(2,1)}, bf16[2,48,1536]{2,1,0:T(8,128)(2,1)}, u32[]{:S(2)}, u32[]{:S(2)}) collective-permute-start(bf16[2,48,1536]{2,1,0:T(8,128)(2,1)} %select_convert_fusion.1), channel_id=1, source_target_pairs={{0,4},{2,6},{4,0},{6,2},{1,5},{3,7},{5,1},{7,3},{8,12},{10,14},{12... | collective-permute-start | bytes 884744 | tf_op jit(solution)/shard_map/ppermute | solution.py:57
  431.6 17.0 %collective-permute-start.41 = (bf16[320,768]{1,0:T(8,128)(2,1)S(1)}, bf16[320,768]{1,0:T(8,128)(2,1)S(1)}, u32[]{:S(2)}, u32[]{:S(2)}) collective-permute-start(bf16[320,768]{1,0:T(8,128)(2,1)S(1)} %fusion.60), channel_id=1, source_target_pairs={{0,8},{8,0},{16,24},{24,16},{1,9},{9,1},{17,25},{25,17},{2,10},{10... | collective-permute-start | bytes 1474568 | tf_op jit(solution)/shard_map/ppermute | solution.py:57
  451.5 13.3 %collective-permute-start.42 = (bf16[160,768]{1,0:T(8,128)(2,1)S(1)}, bf16[160,768]{1,0:T(8,128)(2,1)S(1)}, u32[]{:S(2)}, u32[]{:S(2)}) collective-permute-start(bf16[160,768]{1,0:T(8,128)(2,1)S(1)} %slice.1313), channel_id=1, source_target_pairs={{0,1},{1,0},{2,3},{3,2},{4,5},{5,4},{6,7},{7,6},{8,9},{9,8},{10,11... | collective-permute-start | bytes 737288 | tf_op jit(solution)/shard_map/ppermute | solution.py:57
  456.4 53.7 %collective-permute-start.51 = (bf16[2,384,384]{2,1,0:T(8,128)(2,1)}, bf16[2,384,384]{2,1,0:T(8,128)(2,1)}, u32[]{:S(2)}, u32[]{:S(2)}) collective-permute-start(bf16[2,384,384]{2,1,0:T(8,128)(2,1)} %pad_maximum_fusion.36), channel_id=1, source_target_pairs={{0,16},{8,24},{16,0},{24,8},{1,17},{9,25},{17,1},{25,9},{2,18},{10... | collective-permute-start | bytes 1769480 | tf_op jit(solution)/shard_map/ppermute | solution.py:57
  461.6 51.3 %collective-permute-start.49 = (bf16[2,192,768]{2,1,0:T(8,128)(2,1)}, bf16[2,192,768]{2,1,0:T(8,128)(2,1)}, u32[]{:S(2)}, u32[]{:S(2)}) collective-permute-start(bf16[2,192,768]{2,1,0:T(8,128)(2,1)} %pad_maximum_fusion.35), channel_id=1, source_target_pairs={{0,8},{8,0},{16,24},{24,16},{1,9},{9,1},{17,25},{25,17},{2,10},{10... | collective-permute-start | bytes 1769480 | tf_op jit(solution)/shard_map/ppermute | solution.py:57
  467.6 48.4 %collective-permute-start.60 = (bf16[384,768]{1,0:T(8,128)(2,1)}, bf16[384,768]{1,0:T(8,128)(2,1)}, u32[]{:S(2)}, u32[]{:S(2)}) collective-permute-start(bf16[384,768]{1,0:T(8,128)(2,1)} %fusion.37), channel_id=1, source_target_pairs={{0,8},{8,0},{16,24},{24,16},{1,9},{9,1},{17,25},{25,17},{2,10},{10... | collective-permute-start | bytes 1769480 | tf_op jit(solution)/shard_map/ppermute | solution.py:57
  469.4 20.5 %collective-permute-start.45 = (f32[8,768]{1,0:T(8,128)S(1)}, f32[8,768]{1,0:T(8,128)S(1)}, u32[]{:S(2)}, u32[]{:S(2)}) collective-permute-start(f32[8,768]{1,0:T(8,128)S(1)} %add.518), channel_id=1, source_target_pairs={{0,8},{8,0},{16,24},{24,16},{1,9},{9,1},{17,25},{25,17},{2,10},{10... | collective-permute-start | bytes 73736 | tf_op jit(solution)/shard_map/ppermute | solution.py:57
  472.2 45.3 %collective-permute-start.58 = (bf16[384,768]{1,0:T(8,128)(2,1)}, bf16[384,768]{1,0:T(8,128)(2,1)}, u32[]{:S(2)}, u32[]{:S(2)}) collective-permute-start(bf16[384,768]{1,0:T(8,128)(2,1)} %fusion.41), channel_id=1, source_target_pairs={{0,16},{8,24},{16,0},{24,8},{1,17},{9,25},{17,1},{25,9},{2,18},{10... | collective-permute-start | bytes 1769480 | tf_op jit(solution)/shard_map/ppermute | solution.py:57
  507.8 125.8 %collective-permute-start.43 = (f32[145,768]{1,0:T(8,128)}, f32[145,768]{1,0:T(8,128)S(1)}, u32[]{:S(2)}, u32[]{:S(2)}) collective-permute-start(f32[145,768]{1,0:T(8,128)} %slice_add_fusion.6), channel_id=1, source_target_pairs={{0,0},{1,2},{2,1},{3,3},{4,8},{5,10},{6,9},{7,11},{8,4},{9,6},{10,... | collective-permute-start | bytes 1336328 | tf_op jit(solution)/shard_map/ppermute | solution.py:53
  523.2 43.6 %collective-permute-start.53 = (bf16[2,48,1536]{2,1,0:T(8,128)(2,1)S(1)}, bf16[2,48,1536]{2,1,0:T(8,128)(2,1)S(1)}, u32[]{:S(2)}, u32[]{:S(2)}) collective-permute-start(bf16[2,48,1536]{2,1,0:T(8,128)(2,1)S(1)} %select_convert_fusion.3), channel_id=1, source_target_pairs={{0,4},{2,6},{4,0},{6,2},{1,5},{3,7},{5,1},{7,3},{8,12},{10,14},{12... | collective-permute-start | bytes 884744 | tf_op jit(solution)/shard_map/ppermute | solution.py:57
  567.2 64.6 %collective-permute-start.61 = (bf16[2,48,3072]{2,1,0:T(8,128)(2,1)S(1)}, bf16[2,48,3072]{2,1,0:T(8,128)(2,1)S(1)}, u32[]{:S(2)}, u32[]{:S(2)}) collective-permute-start(bf16[2,48,3072]{2,1,0:T(8,128)(2,1)S(1)} %select_convert_fusion), channel_id=1, source_target_pairs={{0,4},{2,6},{4,0},{6,2},{1,5},{3,7},{5,1},{7,3},{8,12},{10,14},{12... | collective-permute-start | bytes 1769480 | tf_op jit(solution)/shard_map/ppermute | solution.py:57
  575.2 59.7 %collective-permute-start.55 = (f32[24,1152]{1,0:T(8,128)S(1)}, f32[24,1152]{1,0:T(8,128)S(1)}, u32[]{:S(2)}, u32[]{:S(2)}) collective-permute-start(f32[24,1152]{1,0:T(8,128)S(1)} %get-tuple-element.356), channel_id=1, source_target_pairs={{0,1},{1,0},{2,3},{3,2},{4,5},{5,4},{6,7},{7,6},{8,9},{9,8},{10,11... | collective-permute-start | bytes 331784 | tf_op jit(solution)/shard_map/ppermute | solution.py:57
  632.0 25.8 %collective-permute-start.62 = (bf16[48,3072]{1,0:T(8,128)(2,1)S(1)}, bf16[48,3072]{1,0:T(8,128)(2,1)S(1)}, u32[]{:S(2)}, u32[]{:S(2)}) collective-permute-start(bf16[48,3072]{1,0:T(8,128)(2,1)S(1)} %fusion.97), channel_id=1, source_target_pairs={{0,2},{2,0},{4,6},{6,4},{1,3},{3,1},{5,7},{7,5},{8,10},{10,8},{12,... | collective-permute-start | bytes 884744 | tf_op jit(solution)/shard_map/ppermute | solution.py:57
  (244 other events, 1560.0 us)
Sparse Core Ops, SparseCore 0:
  445.8 229.9 all-reduce.6

commit v2 on v0

v2 whole, which is shorter than its diff:
```python
import functools

import jax
import jax.numpy as jnp
from jax import lax
from jax.experimental import pallas as pl
from jax.experimental.pallas import tpu as pltpu
from jax.sharding import PartitionSpec as P

HEADS = 12
HEAD_DIM = 64
LEN = 577
TOP = 2
ALL = ("expert", "context", "dp")
CHIPS = ("expert", "context")
BF = jnp.bfloat16
F32 = jnp.float32
VM = pl.BlockSpec(memory_space=pltpu.VMEM)
HB = pl.BlockSpec(memory_space=pl.ANY)
SM = pl.BlockSpec(memory_space=pltpu.SMEM)


def up16(n):
    return (n + 15) // 16 * 16


def dot(a, b):
    return jnp.dot(a, b, preferred_element_type=F32)


def dot_t(a, b):
    return lax.dot_general(a, b, (((1,), (1,)), ((), ())), preferred_element_type=F32)


def t_dot(a, b):
    return lax.dot_general(a, b, (((0,), (0,)), ((), ())), preferred_element_type=F32)


def call(kernel, outs, ins, scratch=(), after=(), flops=0, bytes_accessed=0):
    n_in, n_after = len(ins), len(after)

    def run(*refs):
        kernel(*refs[:n_in], *refs[n_in + n_after :])

    return pl.pallas_call(
        run,
        out_shape=[jax.ShapeDtypeStruct(s, t) for s, t, _ in outs],
        in_specs=[s for _, s in ins] + [HB] * n_after,
        out_specs=[s for _, _, s in outs],
        scratch_shapes=list(scratch),
        compiler_params=pltpu.CompilerParams(vmem_limit_bytes=50 * 2**20),
        cost_estimate=pl.CostEstimate(
            flops=flops, bytes_accessed=bytes_accessed, transcendentals=0
        ),
    )(*[a for a, _ in ins], *after)


def norm_parts(x):
    mean = jnp.mean(x, -1, keepdims=True)
    centre = x - mean
    scale = lax.rsqrt(jnp.mean(centre * centre, -1, keepdims=True) + 1e-06)
    return centre * scale, scale


def layer_norm(x, gain):
    return (norm_parts(x)[0] * gain).astype(BF)


def norm_back(x, gain, slope, own):
    unit, scale = norm_parts(x)
    gain_slope = jnp.sum(slope[:own] * unit[:own], 0, keepdims=True)
    inner = slope * gain
    inner = inner - jnp.mean(inner, -1, keepdims=True) - unit * jnp.mean(inner * unit, -1, keepdims=True)
    return inner * scale, gain_slope


def gelu_both(h):
    k = 0.7978845608028654
    t = jnp.tanh(k * (h + 0.044715 * h * h * h))
    half = 0.5 * (1 + t)
    return h * half, half + 0.5 * h * (1 - t * t) * (k + (3 * 0.044715 * k) * h * h)


def add_both(mine, got, rows):
    return mine + jnp.concatenate([got[rows:], got[:rows]], 0).astype(F32)


def pair_masks():
    lane = lax.broadcasted_iota(jnp.int32, (1, 2 * HEAD_DIM), 1)
    return [(lane < HEAD_DIM).astype(BF), (lane >= HEAD_DIM).astype(BF)]


def key_mask(blk, rows, blk_len, longest):
    pos = lax.broadcasted_iota(jnp.int32, (rows, 1), 0)
    parts = []
    for j in range(4):
        last = jnp.where((blk ^ j) < longest, blk_len, blk_len - 1)
        parts.append(pos < last)
    return jnp.concatenate([jnp.where(p, 1.0, 0.0) for p in parts], 0) > 0.5


def attend_core(where, q, kv_own, kv_far, wp, rows, blk_len, longest, solo, after=()):
    half = q.shape[1]
    feat = wp.shape[1]
    pairs = half // (2 * HEAD_DIM)

    def kernel(where_ref, q_ref, ko_ref, kf_ref, wp_ref, part_ref, low_ref, blend_ref, lse_ref):
        ok = key_mask(where_ref[0], rows, blk_len, longest)
        masks = pair_masks()
        for p in range(pairs):
            at, vat = pl.ds(p * 128, 128), pl.ds(half + p * 128, 128)
            k = jnp.concatenate([ko_ref[:, at], kf_ref[:, at]], 0)
            v = jnp.concatenate([ko_ref[:, vat], kf_ref[:, vat]], 0)
            qp = q_ref[:, at]
            acc = None
            for h in range(2):
                s = dot_t(k, qp * masks[h]) * 0.125
                s = jnp.where(ok, s, -1e9)
                top = jnp.max(s, 0, keepdims=True)
                ex = jnp.exp(s - top)
                total = jnp.sum(ex, 0, keepdims=True)
                lse_ref[pl.ds(2 * p + h, 1), :] = top + jnp.log(total)
                shares = (ex * (1.0 / total)).astype(BF)
                out = t_dot(v * masks[h], shares)
                acc = out if acc is None else acc + out
            blend_ref[at, :] = acc.astype(BF)
        part = t_dot(blend_ref[...], wp_ref[...])
        part_ref[...] = part
        low_ref[...] = (part[rows:] if solo else part).astype(BF)

    r2 = 2 * rows
    return call(
        kernel,
        [((r2, feat), F32, VM), ((rows if solo else r2, feat), BF, VM), ((half, r2), BF, VM), ((8, r2), F32, VM)],
        [(where, SM), (q, VM), (kv_own, VM), (kv_far, VM), (wp, VM)],
        after=after,
        flops=2 * r2 * half * (8 * rows + feat),
        bytes_accessed=4 * 2**20,
    )


def attend_core_back(where, u_low, wp, blend, q, kv_own, kv_far, lse, rows, blk_len, longest, after=()):
    half = q.shape[1]
    feat = wp.shape[1]
    pairs = half // (2 * HEAD_DIM)
    r2 = 2 * rows

    def kernel(
        where_ref, u_ref, wp_ref, blend_ref, q_ref, ko_ref, kf_ref, lse_ref,
        dq_ref, own_ref, far_ref, wps_ref, bt_ref, dqt_ref,
    ):
        ok = key_mask(where_ref[0], rows, blk_len, longest)
        masks = pair_masks()
        sub = lax.broadcasted_iota(jnp.int32, (2 * HEAD_DIM, 1), 0)
        row_masks = [(sub < HEAD_DIM).astype(BF), (sub >= HEAD_DIM).astype(BF)]
        u = u_ref[...]
        bt_ref[...] = dot_t(wp_ref[...], u).astype(BF)
        for p in range(pairs):
            at, vat = pl.ds(p * 128, 128), pl.ds(half + p * 128, 128)
            k = jnp.concatenate([ko_ref[:, at], kf_ref[:, at]], 0)
            v = jnp.concatenate([ko_ref[:, vat], kf_ref[:, vat]], 0)
            qp = q_ref[:, at]
            bt = bt_ref[at, :]
            dqt = dk = dv = 0.0
            for h in range(2):
                qm = qp * masks[h]
                s = dot_t(k, qm) * 0.125
                shares = jnp.where(ok, jnp.exp(s - lse_ref[pl.ds(2 * p + h, 1), :]), 0.0)
                slope = dot(v * masks[h], bt)
                t = shares * slope
                ss = (t - shares * jnp.sum(t, 0, keepdims=True)).astype(BF)
                dqt += t_dot(k * masks[h], ss)
                dk += dot(ss, qm)
                dv += dot_t(shares.astype(BF), bt * row_masks[h])
            dqt_ref[at, :] = dqt * 0.125
            dk = dk * 0.125
            own_ref[:, at] = dk[:r2]
            own_ref[:, vat] = dv[:r2]
            far_ref[:, at] = dk[r2:].astype(BF)
            far_ref[:, vat] = dv[r2:].astype(BF)
        dq_ref[...] = dqt_ref[...].T.astype(BF)
        wps_ref[...] = dot(blend_ref[...], u).astype(BF)

    return call(
        kernel,
        [
            ((r2, half), BF, VM), ((r2, 2 * half), F32, VM), ((r2, 2 * half), BF, VM),
            ((half, feat), BF, VM),
        ],
        [
            (where, SM), (u_low, VM), (wp, VM), (blend, VM), (q, VM), (kv_own, VM), (kv_far, VM),
            (lse, VM),
        ],
        scratch=[pltpu.VMEM((half, r2), BF), pltpu.VMEM((half, r2), F32)],
        after=after,
        flops=2 * r2 * half * (20 * rows + 2 * feat),
        bytes_accessed=6 * 2**20,
    )


def block_refs(a0, a1, a23, first):
    second = 3 - first
    found = {0: a0, first: a1, second: a23.at[0], 3: a23.at[1]}
    return [found[j] for j in range(4)]


def start_all(copies):
    for c in copies:
        c.start()


def wait_all(copies):
    for c in copies:
        c.wait()


def attend_copies(e, a, b, w_ref, p_ref, small_ref, sems):
    copies = []

    def add(src, dst):
        copies.append(pltpu.make_async_copy(src, dst, sems.at[len(copies)]))

    n = w_ref.shape[0] // 4
    half = p_ref.shape[0]
    m = half // 4
    for j in range(4):
        to = e ^ j
        rows, prows = pl.ds(pl.multiple_of(to * n, 16), n), pl.ds(pl.multiple_of(to * m, 16), m)
        add(a[j], w_ref.at[rows, pl.ds(0, 2 * half)])
        add(b[j].at[pl.ds(0, n)], w_ref.at[rows, pl.ds(2 * half, half)])
        add(b[j].at[pl.ds(n, m)], p_ref.at[prows, pl.ds(0, half)])
        add(b[j].at[pl.ds(n + m, m)], p_ref.at[prows, pl.ds(half, half)])
        if small_ref is not None:
            for g in range(3):
                srows = pl.ds(pl.multiple_of(to * n + g * (n // 3), 16), n // 3)
                add(b[j].at[pl.ds(n + 2 * m, n // 3), pl.ds(128 * g, 128)], small_ref.at[srows])
    return copies


def attend_start(where, tokens, small_rows, gain_row, a, b, firsts, rows, after=()):
    opening = small_rows is not None
    feat = tokens[0].shape[1]
    half = feat // 2
    r2 = 2 * rows
    n_copy = 28 if opening else 16

    def kernel(where_ref, *refs):
        refs = list(refs)
        take = lambda n: [refs.pop(0) for _ in range(n)]
        tok = take(len(tokens))
        gain_ref = None if opening else take(1)[0]
        a_refs, b_refs = take(3), take(3)
        x_ref, normed_ref, q_ref, kv_ref, w_ref, p_ref = take(6)
        small_ref, rows_ref = take(2) if opening else (None, None)
        (sems,) = take(1)
        copies = attend_copies(
            where_ref[1], block_refs(*a_refs, firsts[0]), block_refs(*b_refs, firsts[1]),
            w_ref, p_ref, small_ref, sems,
        )
        start_all(copies)
        if opening:
            x_ref[...] = jnp.zeros_like(x_ref)
            n = tok[0].shape[0]
            x_ref[pl.ds(0, n), :] = tok[0][...].astype(F32)
            x_ref[pl.ds(rows, n), :] = tok[1][...].astype(F32)
            wait_all(copies)
            turned = small_ref[...].astype(F32).T
            rows_ref[...] = turned[: rows_ref.shape[0]]
            gain = turned[gain_row : gain_row + 1]
            x = x_ref[...]
            normed = layer_norm(x, gain)
        else:
            x = add_both(tok[0][...] + tok[1][...], tok[2][...], rows)
            x_ref[...] = x
            normed = layer_norm(x, gain_ref[pl.ds(gain_row, 1), :])
            wait_all(copies)
        normed_ref[...] = normed
        q_ref[...] = dot(normed, w_ref[:, :half]).astype(BF)
        kv_ref[...] = dot(normed, w_ref[:, half:]).astype(BF)

    outs = [
        ((r2, feat), F32, VM), ((r2, feat), BF, VM), ((r2, half), BF, VM), ((r2, feat), BF, VM),
        ((feat, 3 * half), BF, VM), ((half, feat), BF, VM),
    ]
    ins = [(where, SM)] + [(t, VM) for t in tokens]
    if opening:
        outs += [((feat, 128), BF, VM), ((small_rows, feat), F32, VM)]
    return ins, outs, kernel, n_copy


def attend_first(where, own, sib, small_rows, a, b, firsts, rows, after=()):
    ins, outs, kernel, n = attend_start(where, (own, sib), small_rows, 0, a, b, firsts, rows)
    ins += [(t, HB) for t in (*a, *b)]
    return call(
        kernel, outs, ins, scratch=[pltpu.SemaphoreType.DMA((n,))], after=after,
        flops=2 * 320 * 768 * 1152, bytes_accessed=6 * 2**20,
    )


def attend_next(where, x, part, got, gains, gain_row, a, b, firsts, rows, after=()):
    ins, outs, kernel, n = attend_start(where, (x, part, got), None, gain_row, a, b, firsts, rows)
    ins += [(gains, VM)] + [(t, HB) for t in (*a, *b)]
    return call(
        kernel, outs, ins, scratch=[pltpu.SemaphoreType.DMA((n,))], after=after,
        flops=2 * 320 * 768 * 1152, bytes_accessed=6 * 2**20,
    )


def widen_forward(where, x, part, got, gains, a, b, firsts, rows, after=()):
    r2, feat = x.shape
    wide = 2 * feat
    tile = 384

    def kernel(
        where_ref, x_ref, part_ref, got_ref, gains_ref, a0, a1, a23, b0, b1, b23,
        x1_ref, normed_ref, hidden_ref, out_ref, low_ref, wi_ref, wo_ref, sems,
    ):
        n = feat // 4
        copies = []
        for h, blocks in enumerate((block_refs(a0, a1, a23, firsts[0]), block_refs(b0, b1, b23, firsts[1]))):
            for j in range(4):
                at = (where_ref[1] ^ j) * n
                for src, dst in (
                    (blocks[j].at[0], wi_ref.at[pl.ds(pl.multiple_of(at, 16), n), pl.ds(h * feat, feat)]),
                    (blocks[j].at[1], wo_ref.at[pl.ds(pl.multiple_of(at + h * feat, 16), n)]),
                ):
                    copies.append(pltpu.make_async_copy(src, dst, sems.at[len(copies)]))
        start_all(copies)
        x1 = add_both(x_ref[...] + part_ref[...], got_ref[...], rows)
        x1_ref[...] = x1
        normed_ref[...] = layer_norm(x1, gains_ref[pl.ds(1, 1), :])
        wait_all(copies)
        out_ref[...] = jnp.zeros_like(out_ref)

        @pl.loop(0, wide // tile)
        def _(t):
            at = pl.ds(pl.multiple_of(t * tile, 128), tile)
            h = dot(normed_ref[...], wi_ref[:, at])
            hidden_ref[:, at] = h
            out_ref[...] += dot(gelu_both(h)[0].astype(BF), wo_ref[at, :])

        low_ref[...] = out_ref[...].astype(BF)

    return call(
        kernel,
        [
            ((r2, feat), F32, VM), ((r2, feat), BF, VM), ((r2, wide), F32, VM), ((r2, feat), F32, VM),
            ((r2, feat), BF, VM), ((feat, wide), BF, VM), ((wide, feat), BF, VM),
        ],
        [(where, SM), (x, VM), (part, VM), (got, VM), (gains, VM)] + [(t, HB) for t in (*a, *b)],
        scratch=[pltpu.SemaphoreType.DMA((16,))],
        after=after,
        flops=4 * r2 * feat * wide,
        bytes_accessed=16 * 2**20,
    )


def spread_out(e, firsts, pieces, sems):
    copies = []
    for src, n, h, place in pieces:
        first = firsts[h]
        for side, js in enumerate(((0, 3 - first), (first, 3))):
            for i, j in enumerate(js):
                at = pl.ds(pl.multiple_of((e ^ j) * n, 16), n)
                copies.append(
                    pltpu.make_async_copy(src(at), place(side, i), sems.at[len(copies)])
                )
    return copies


def widen_back(where, u, x, gains, part, got, normed, hidden, wi, wo, firsts, rows, after=()):
    r2, feat = u.shape
    wide = 2 * feat
    tile = 384
    n = feat // 4

    def kernel(
        where_ref, u_ref, x_ref, gains_ref, part_ref, got_ref, normed_ref, hidden_ref, wi_ref, wo_ref,
        u2_ref, gs_ref, out_ref, low_ref, keep_a, send_a, keep_b, send_b,
        ulow_ref, turned_ref, wis_ref, wos_ref, sems,
    ):
        slope = add_both(part_ref[...], got_ref[...], rows)
        dx, gain_slope = norm_back(x_ref[...], gains_ref[pl.ds(2, 1), :], slope, rows)
        gs_ref[...] = gain_slope
        u2 = u_ref[...] + dx
        u2_ref[...] = u2
        ulow_ref[...] = u2.astype(BF)
        turned_ref[...] = normed_ref[...].T
        out_ref[...] = jnp.zeros_like(out_ref)

        @pl.loop(0, wide // tile)
        def _(t):
            at = pl.ds(pl.multiple_of(t * tile, 128), tile)
            ulow = ulow_ref[...]
            act, dact = gelu_both(hidden_ref[:, at])
            hs = (dact * dot_t(ulow, wo_ref[at, :])).astype(BF)
            wos_ref[at, :] = t_dot(act.astype(BF), ulow).astype(BF)
            wis_ref[:, at] = dot(turned_ref[...], hs).astype(BF)
            out_ref[...] += dot_t(hs, wi_ref[:, at])

        outs = ((keep_a, send_a), (keep_b, send_b))
        pieces = []
        for h in range(2):
            pieces.append((
                lambda at, h=h: wis_ref.at[at, pl.ds(h * feat, feat)], n, h,
                lambda side, i, h=h: outs[h][side].at[i, 0],
            ))
            pieces.append((
                lambda at, h=h: wos_ref.at[pl.ds(h * feat, feat)].at[at], n, h,
                lambda side, i, h=h: outs[h][side].at[i, 1],
            ))
        copies = spread_out(where_ref[1], firsts, pieces, sems)
        start_all(copies)
        low_ref[...] = out_ref[...].astype(BF)
        wait_all(copies)

    block = ((2, 2, n, feat), BF, HB)
    return call(
        kernel,
        [((r2, feat), F32, VM), ((1, feat), F32, VM), ((r2, feat), F32, VM), ((r2, feat), BF, VM)]
        + [block] * 4,
        [
            (where, SM), (u, VM), (x, VM), (gains, VM), (part, VM), (got, VM), (normed, VM),
            (hidden, VM), (wi, VM), (wo, VM),
        ],
        scratch=[
            pltpu.VMEM((r2, feat), BF), pltpu.VMEM((feat, r2), BF), pltpu.VMEM((feat, wide), BF),
            pltpu.VMEM((wide, feat), BF), pltpu.SemaphoreType.DMA((16,)),
        ],
        after=after,
        flops=10 * r2 * feat * wide,
        bytes_accessed=24 * 2**20,
    )


def attend_proj_back(where, dq, own, got, normed, w, wps, firsts, rows, last, after=()):
    r2, feat = normed.shape
    half = feat // 2
    n, m = feat // 4, half // 4
    tile = 384

    def kernel(
        where_ref, dq_ref, own_ref, got_ref, normed_ref, w_ref, wps_ref,
        out_ref, low_ref, keep_a, send_a, keep_b, send_b, packed_ref, turned_ref, ws_ref, sems,
    ):
        packed_ref[:, :half] = dq_ref[...]
        packed_ref[:, half:] = (own_ref[...] + got_ref[...].astype(F32)).astype(BF)
        out = dot_t(packed_ref[...], w_ref[...])
        out_ref[...] = out[: out_ref.shape[0]]
        low_ref[...] = (out[rows:] if last else out).astype(BF)
        turned_ref[...] = normed_ref[...].T

        @pl.loop(0, 3 * half // tile)
        def _(t):
            at = pl.ds(pl.multiple_of(t * tile, 128), tile)
            ws_ref[:, at] = dot(turned_ref[...], packed_ref[:, at]).astype(BF)

        ab = ((keep_a, send_a), (keep_b, send_b))
        pieces = [
            (lambda at: ws_ref.at[at, pl.ds(0, feat)], n, 0, lambda side, i: ab[0][side].at[i]),
            (
                lambda at: ws_ref.at[at, pl.ds(feat, half)], n, 1,
                lambda side, i: ab[1][side].at[i, pl.ds(0, n)],
            ),
        ]
        for c in range(2):
            pieces.append((
                lambda at, c=c: wps_ref.at[at, pl.ds(c * half, half)], m, 1,
                lambda side, i, c=c: ab[1][side].at[i, pl.ds(n + c * m, m)],
            ))
        copies = spread_out(where_ref[1], firsts, pieces, sems)
        start_all(copies)
        wait_all(copies)

    n_out = rows if last else r2
    return call(
        kernel,
        [((n_out, feat), F32, VM), ((n_out, feat), BF, VM)]
        + [((2, n, feat), BF, HB)] * 2 + [((2, n + 2 * m, half), BF, HB)] * 2,
        [(where, SM), (dq, VM), (own, VM), (got, VM), (normed, VM), (w, VM), (wps, VM)],
        scratch=[
            pltpu.VMEM((r2, 3 * half), BF), pltpu.VMEM((feat, r2), BF), pltpu.VMEM((feat, 3 * half), BF),
            pltpu.SemaphoreType.DMA((16,)),
        ],
        after=after,
        flops=4 * r2 * feat * 3 * half,
        bytes_accessed=10 * 2**20,
    )


def join_upstream(u_own, u_sib, rows):
    feat = u_own.shape[1]

    def kernel(o_ref, s_ref, u_ref, low_ref):
        u_ref[pl.ds(0, rows), :] = o_ref[...]
        u_ref[pl.ds(rows, rows), :] = s_ref[...].astype(F32)
        low_ref[pl.ds(0, rows), :] = o_ref[...].astype(BF)
        low_ref[pl.ds(rows, rows), :] = s_ref[...]

    return call(
        kernel, [((2 * rows, feat), F32, VM), ((2 * rows, feat), BF, VM)], [(u_own, VM), (u_sib, VM)],
        bytes_accessed=2**21,
    )


def norm_step(u, x, gains, gain_row, part, got, rows, last, after=()):
    feat = x.shape[1]
    n = rows if last else 2 * rows

    def kernel(u_ref, x_ref, gains_ref, part_ref, got_ref, u2_ref, low_ref, gs_ref):
        if last:
            slope = part_ref[...] + got_ref[...].astype(F32)
        else:
            slope = add_both(part_ref[...], got_ref[...], rows)
        dx, gain_slope = norm_back(x_ref[:n], gains_ref[pl.ds(gain_row, 1), :], slope, rows)
        gs_ref[...] = gain_slope
        u2 = u_ref[:n] + dx
        u2_ref[...] = u2[: u2_ref.shape[0]]
        if not last:
            low_ref[...] = u2.astype(BF)

    n_out = last if last else n
    return call(
        kernel,
        [((n_out, feat), F32, VM), ((n if not last else 16, feat), BF, VM), ((1, feat), F32, VM)],
        [(u, VM), (x, VM), (gains, VM), (part, VM), (got, VM)],
        after=after,
        bytes_accessed=6 * 2**20,
    )


def picks(index, turn, cap, cap_rows, experts):
    at = lax.broadcasted_iota(jnp.int32, (1, experts * cap_rows), 1)
    out = []
    for k in range(TOP):
        chosen, slot = index[:, k : k + 1], index[:, TOP + k : TOP + k + 1]
        place = chosen if turn is None else chosen ^ turn
        target = jnp.where(slot < cap, place * cap_rows + slot, -1)
        out.append(jnp.where(at == target, 1.0, 0.0).astype(BF))
    return out


def lane_at(index, k):
    lane = lax.broadcasted_iota(jnp.int32, (1, 128), 1)
    return jnp.where(lane == index[:, k : k + 1] + 4, 1.0, 0.0)


def present_mask(blk, rows, blk_len, longest):
    pos = lax.broadcasted_iota(jnp.int32, (rows, 1), 0)
    last = jnp.where(blk < longest, blk_len, blk_len - 1)
    return jnp.where(pos < last, 1.0, 0.0)


def route(where, x, part, got, gains, small, cot, index, experts, cap, rows, blk_len, longest, fast, after=()):
    feat = x.shape[1]
    cap_rows = up16(cap)

    def kernel(where_ref, x_ref, part_ref, got_ref, gains_ref, small_ref, cot_ref, index_ref,
               x3_ref, moe_ref, gates_ref, up_ref, *blocks):
        x3 = x_ref[:rows] + part_ref[:rows] + got_ref[...].astype(F32)
        x3_ref[...] = x3
        moe = layer_norm(x3, gains_ref[pl.ds(3, 1), :])
        moe_ref[...] = moe
        lane = lax.broadcasted_iota(jnp.int32, (1, 128), 1)
        logits = dot(moe, small_ref[...])
        logits = jnp.where((lane >= 4) & (lane < 4 + experts), logits, -1e30)
        ex = jnp.exp(logits - jnp.max(logits, -1, keepdims=True))
        gates = ex / jnp.sum(ex, -1, keepdims=True)
        gates_ref[...] = gates
        up_ref[...] = jnp.zeros_like(up_ref)
        up_ref[pl.ds(0, blk_len), :] = cot_ref[...]
        up = up_ref[...] * present_mask(where_ref[0], rows, blk_len, longest)
        up_ref[...] = up
        index = index_ref[...]
        pick = picks(index, where_ref[1] if fast else None, cap, cap_rows, experts)
        sent = t_dot(pick[0] + pick[1], moe).astype(BF)
        slope = 0.0
        for k in range(TOP):
            gate = jnp.sum(gates * lane_at(index, k), -1, keepdims=True)
            slope += t_dot(pick[k], (gate * up).astype(BF))
        slope = slope.astype(BF)
        for j, ref in enumerate(blocks):
            ref[pl.ds(0, cap_rows), :] = sent[j * cap_rows : (j + 1) * cap_rows]
            ref[pl.ds(cap_rows, cap_rows), :] = slope[j * cap_rows : (j + 1) * cap_rows]

    return call(
        kernel,
        [((rows, feat), F32, VM), ((rows, feat), BF, VM), ((rows, 128), F32, VM), ((rows, feat), F32, VM)]
        + [((2 * cap_rows, feat), BF, VM)] * experts,
        [(where, SM), (x, VM), (part, VM), (got, VM), (gains, VM), (small, VM), (cot, VM), (index, VM)],
        after=after,
        flops=6 * rows * experts * cap_rows * feat,
        bytes_accessed=5 * 2**20,
    )


def expert_half(blocks, w_in, w_out, acc, cap_rows, after=()):
    feat = w_in.shape[0]
    wide = w_in.shape[1]
    tile = 512 if wide % 512 == 0 else wide
    n = len(blocks) * cap_rows
    steps = wide // tile
    final = acc is not None

    def kernel(*refs):
        refs = list(refs)
        take = lambda k: [refs.pop(0) for _ in range(k)]
        ins = take(len(blocks))
        wi_ref, wo_ref = take(2)
        before = take(2) if final else None
        take(len(after))
        outs = take(len(blocks)) if final else take(2)
        wis_ref, wos_ref = take(2)
        rows_ref, slope_ref, turned_ref, res_ref, back_ref = take(5)
        t = pl.program_id(0)

        @pl.when(t == 0)
        def _():
            for j, ref in enumerate(ins):
                at = pl.ds(j * cap_rows, cap_rows)
                rows_ref[at, :] = ref[pl.ds(0, cap_rows), :]
                slope_ref[at, :] = ref[pl.ds(cap_rows, cap_rows), :]
            turned_ref[...] = rows_ref[...].T
            if final:
                res_ref[...] = before[0][...]
                back_ref[...] = before[1][...]
            else:
                res_ref[...] = jnp.zeros_like(res_ref)
                back_ref[...] = jnp.zeros_like(back_ref)

        act, dact = gelu_both(dot(rows_ref[...], wi_ref[...]))
        act = act.astype(BF)
        hs = (dact * dot_t(slope_ref[...], wo_ref[...])).astype(BF)
        res_ref[...] += dot(act, wo_ref[...])
        back_ref[...] += dot_t(hs, wi_ref[...])
        wis_ref[...] = dot(turned_ref[...], hs).astype(BF)
        wos_ref[...] = t_dot(act, slope_ref[...]).astype(BF)

        @pl.when(t == steps - 1)
        def _():
            if final:
                for j, ref in enumerate(outs):
                    at = pl.ds(j * cap_rows, cap_rows)
                    ref[pl.ds(0, cap_rows), :] = res_ref[at, :].astype(BF)
                    ref[pl.ds(cap_rows, cap_rows), :] = back_ref[at, :].astype(BF)
            else:
                outs[0][...] = res_ref[...]
                outs[1][...] = back_ref[...]

    whole = lambda shape: pl.BlockSpec(shape, lambda t: (0,) * len(shape))
    wi_spec = pl.BlockSpec((feat, tile), lambda t: (0, t))
    wo_spec = pl.BlockSpec((tile, feat), lambda t: (t, 0))
    blk = (2 * cap_rows, feat)
    ins = [*blocks, w_in, w_out] + (list(acc) if final else []) + list(after)
    in_specs = [whole(blk)] * len(blocks) + [wi_spec, wo_spec] + [whole((n, feat))] * (2 if final else 0)
    in_specs += [HB] * len(after)
    if final:
        shapes, specs = [jax.ShapeDtypeStruct(blk, BF)] * len(blocks), [whole(blk)] * len(blocks)
    else:
        shapes, specs = [jax.ShapeDtypeStruct((n, feat), F32)] * 2, [whole((n, feat))] * 2
    shapes = shapes + [jax.ShapeDtypeStruct((feat, wide), BF), jax.ShapeDtypeStruct((wide, feat), BF)]
    return pl.pallas_call(
        kernel,
        grid=(steps,),
        out_shape=shapes,
        in_specs=in_specs,
        out_specs=specs + [wi_spec, wo_spec],
        scratch_shapes=[
            pltpu.VMEM((n, feat), BF), pltpu.VMEM((n, feat), BF), pltpu.VMEM((feat, n), BF),
            pltpu.VMEM((n, feat), F32), pltpu.VMEM((n, feat), F32),
        ],
        compiler_params=pltpu.CompilerParams(
            vmem_limit_bytes=50 * 2**20, dimension_semantics=("arbitrary",)
        ),
        cost_estimate=pl.CostEstimate(
            flops=12 * n * feat * wide, bytes_accessed=16 * 2**20, transcendentals=0
        ),
    )(*ins)


def combine(where, blocks, x3, moe, gates, up, index, small, gains, small_rows, experts, cap, rows, blk_len, longest, fast, after=()):
    feat = x3.shape[1]
    cap_rows = up16(cap)
    n = experts * cap_rows

    def kernel(where_ref, *refs):
        refs = list(refs)
        take = lambda k: [refs.pop(0) for _ in range(k)]
        ins = take(experts)
        x3_ref, moe_ref, gates_ref, up_ref, index_ref, small_ref, gains_ref = take(7)
        acts_ref, u_ref, low_ref, slopes_ref, result_ref, back_ref = take(6)
        for j, ref in enumerate(ins):
            at = pl.ds(j * cap_rows, cap_rows)
            result_ref[at, :] = ref[pl.ds(0, cap_rows), :]
            back_ref[at, :] = ref[pl.ds(cap_rows, cap_rows), :]
        index, gates, up, moe = index_ref[...], gates_ref[...], up_ref[...], moe_ref[...]
        pick = picks(index, where_ref[1] if fast else None, cap, cap_rows, experts)
        x3 = x3_ref[...]
        acts, all_slope = x3, 0.0
        for k in range(TOP):
            at_k = lane_at(index, k)
            gate = jnp.sum(gates * at_k, -1, keepdims=True)
            picked = dot(pick[k], result_ref[...])
            acts = acts + gate * picked
            all_slope += jnp.sum(up * picked, -1, keepdims=True) * at_k
        acts = acts * present_mask(where_ref[0], rows, blk_len, longest)
        acts_ref[...] = acts[:blk_len]
        logit = (gates * (all_slope - jnp.sum(gates * all_slope, -1, keepdims=True))).astype(BF)
        slope = dot(pick[0] + pick[1], back_ref[...]) + dot_t(logit, small_ref[...])
        dx, gain_slope = norm_back(x3, gains_ref[pl.ds(3, 1), :], slope, rows)
        u = up + dx
        u_ref[...] = u
        low_ref[...] = u.astype(BF)
        slopes_ref[...] = t_dot(logit, moe)[:small_rows]
        slopes_ref[pl.ds(3, 1), :] = gain_slope

    return call(
        kernel,
        [((blk_len, feat), F32, VM), ((rows, feat), F32, VM), ((rows, feat), BF, VM), ((small_rows, feat), F32, VM)],
        [(where, SM)] + [(b, VM) for b in blocks]
        + [(t, VM) for t in (x3, moe, gates, up, index, small, gains)],
        scratch=[pltpu.VMEM((n, feat), BF), pltpu.VMEM((n, feat), BF)],
        after=after,
        flops=6 * rows * n * feat,
        bytes_accessed=5 * 2**20,
    )


class Links:
    def __init__(self, mesh):
        self.E = mesh.shape["expert"]
        self.C = mesh.shape["context"]
        self.D = mesh.shape["dp"]
        assert self.C == 4 and self.D == 2 and self.E % 2 == 0
        self.fast = self.E == 4
        self.chips = self.E * self.C
        flat = lambda e, c, d: (e * self.C + c) * self.D + d
        self.team = [
            (flat(e, c, d), flat((e // 2) * 2 + c // 2, 2 * (e % 2) + d, c % 2))
            for e in range(self.E)
            for c in range(self.C)
            for d in range(self.D)
        ]
        self.to_lane = [(f, (f % self.chips) * 2 + f // self.chips) for f in range(2 * self.chips)]
        self.from_lane = [(b, a) for a, b in self.to_lane]

    def move(self, x):
        return lax.ppermute(x, ALL, self.team)

    def xor(self, x, axis, j):
        n = {"expert": self.E, "context": self.C, "dp": self.D}[axis]
        return lax.ppermute(x, axis, [(i, i ^ j) for i in range(n)])

    def sib(self, x):
        return self.xor(x, "dp", 1)

    def partner(self, x):
        return self.xor(x, "expert", 1)

    def column(self, x):
        c = lax.axis_index("context")
        got = self.xor(x, "context", 1)
        x = jnp.where(c & 1 == 1, jnp.stack([got, x]), jnp.stack([x, got]))
        got = self.xor(x, "context", 2)
        return jnp.where(c & 2 == 2, jnp.concatenate([got, x]), jnp.concatenate([x, got]))

    def plane(self, x, first):
        got = self.xor(x, "expert", first)
        return x, got, self.xor(jnp.stack([x, got]), "expert", 3 - first)

    def plane_sum(self, keep, send, first):
        got = self.xor(send, "expert", first).astype(F32)
        far = self.xor((keep[1].astype(F32) + got[1]).astype(BF), "expert", 3 - first)
        return keep[0].astype(F32) + got[0] + far.astype(F32)

    def column_sum(self, x):
        c = lax.axis_index("context")
        low, high = x[:2], x[2:]
        give = jnp.where(c & 2 == 2, low, high).astype(BF)
        x = jnp.where(c & 2 == 2, high, low) + self.xor(give, "context", 2).astype(F32)
        give = jnp.where(c & 1 == 1, x[0], x[1]).astype(BF)
        return jnp.where(c & 1 == 1, x[1], x[0]) + self.xor(give, "context", 1).astype(F32)

    def total(self, x):
        if not self.fast:
            return lax.psum(x, ALL)
        x = x + self.xor(x, "dp", 1)
        x = x + self.xor(x, "expert", 1)
        x = x + self.xor(x, "expert", 2)
        x = x + self.xor(x, "context", 1)
        return x + self.xor(x, "context", 2)

    def swap_blocks(self, x):
        if not self.fast:
            return list(lax.all_to_all(jnp.stack(x), "expert", 0, 0, tiled=True))
        return [x[0]] + [self.xor(x[j], "expert", j) for j in range(1, 4)]


def lane_rows(links, mine, d):
    keep = lax.dynamic_index_in_dim(mine, d, 0, False)
    got = links.sib(lax.dynamic_index_in_dim(mine, 1 - d, 0, False))
    return jnp.where(d == 0, jnp.concatenate([keep, got], 0), jnp.concatenate([got, keep], 0))


def in_order(d, own, other):
    return jnp.where(d == 0, jnp.stack([own, other]), jnp.stack([other, own]))


class Weights:
    def __init__(self, links, rdev, feat, ff):
        self.links, self.rdev, self.feat, self.ff = links, rdev, feat, ff
        self.d = lax.axis_index("dp")
        self.half = feat // 2
        self.firsts = (1, 2)

    def split_attend(self, w):
        w = w.reshape(self.rdev, 3, 2, self.half).transpose(2, 0, 1, 3)
        return w.reshape(2, self.rdev, 3 * self.half)

    def split_widen(self, w):
        w = w.reshape(self.rdev, self.links.chips, 2, 2, -1).transpose(2, 0, 3, 1, 4)
        return w.reshape(2, self.rdev, self.ff // 2)

    def pack_attend(self, w, p, small):
        parts = [w, jnp.concatenate([p[:, : self.half], p[:, self.half :]], 0)]
        if small is not None:
            parts.append(jnp.pad(small, ((0, 0), (0, 128 - small.shape[1]))))
        return jnp.concatenate(parts, 1)

    def pack_wide(self, wout):
        h = wout.shape[0] // 2
        return jnp.concatenate([wout[:h], wout[h:]], 1)

    def column(self, buf):
        if self.links.fast:
            return self.links.column(buf)
        return lax.all_gather(buf, CHIPS, axis=0, tiled=False)

    def plane(self, x, lane):
        first = self.firsts[lane]
        if self.links.fast:
            return self.links.plane(x, first)
        return x[0], x[first], jnp.stack([x[3 - first], x[3]])

    def cut(self, x):
        return x if self.links.fast else x.reshape(4, -1, x.shape[-1])

    def spread_attend(self, quad):
        f, h, r = self.feat, self.half, self.rdev
        n = quad.shape[0]
        p = quad[..., f + h : 2 * f].reshape(n, 2, r, h)
        v = quad[..., f : f + h]
        parts = [self.cut(t.reshape(-1, h)) for t in (v, p[:, 0], p[:, 1])]
        if quad.shape[2] > 2 * f:
            small = self.cut(quad[..., 2 * f :].reshape(-1, 128))
            small = small.reshape(small.shape[:-2] + (3, -1, 128))
            parts.append(jnp.concatenate([small[..., g, :, :] for g in range(3)], -1))
        a = self.plane(self.cut(quad[..., :f].reshape(-1, f)), 0)
        return a, self.plane(jnp.concatenate(parts, -2), 1)

    def spread_wide(self, quad_in, quad_out):
        out = []
        for i in range(2):
            pair = [self.cut(t[..., i * self.feat : (i + 1) * self.feat].reshape(-1, self.feat)) for t in (quad_in, quad_out)]
            out.append(self.plane(jnp.stack(pair, -3), i))
        return out

    def total(self, keep, send, lane):
        first = self.firsts[lane]
        if self.links.fast:
            return self.links.plane_sum(keep, send, first)
        blk = {0: keep[0], 3 - first: keep[1], first: send[0], 3: send[1]}
        return jnp.stack([blk[j] for j in range(4)])

    def column_sum(self, buf):
        if self.links.fast:
            return self.links.column_sum(buf)
        return lax.psum_scatter(buf.astype(BF), CHIPS, scatter_dimension=0, tiled=False).astype(F32)

    def exchange(self, w):
        w = w.reshape(2, self.rdev, -1)
        mine = lax.dynamic_index_in_dim(w, self.d, 0, False)
        got = self.links.sib(lax.dynamic_index_in_dim(w, 1 - self.d, 0, False))
        return in_order(self.d, mine, got)

    def owner_attend(self, keep_a, send_a, keep_b, send_b):
        f, h, r = self.feat, self.half, self.rdev
        a = self.total(keep_a, send_a, 0)
        b = self.total(keep_b, send_b, 1)
        n, m = f // 4, h // 4
        cut = lambda t, k: t.reshape(-1, k * r, t.shape[-1])
        p = [cut(b[..., n + i * m : n + (i + 1) * m, :], 1) for i in range(2)]
        buf = jnp.concatenate(
            [cut(a, 2), cut(b[..., :n, :], 2), jnp.concatenate(p, 1)], 2
        )
        buf = self.column_sum(buf)
        p = jnp.concatenate([buf[:r, f + h :], buf[r:, f + h :]], 1)
        p = lax.ppermute(p, ALL, self.links.from_lane)
        w = self.exchange(buf[:, : f + h])
        return w.reshape(2, r, 3, h).transpose(1, 2, 0, 3).reshape(r, 3 * f), p

    def owner_wide(self, keep_a, send_a, keep_b, send_b):
        f, r = self.feat, self.rdev
        a, b = self.total(keep_a, send_a, 0), self.total(keep_b, send_b, 1)
        hid = self.ff // (4 * self.links.chips)
        ins = [t[..., 0, :, :].reshape(-1, 2 * r, f) for t in (a, b)]
        outs = [t[..., 1, :, :].reshape(-1, hid, f) for t in (a, b)]
        if hid == 2 * r:
            buf = self.column_sum(jnp.concatenate(ins + outs, 2))
            ins, outs = buf[:, : 2 * f], buf[:, 2 * f :]
        else:
            ins, outs = [self.column_sum(jnp.concatenate(t, 2)) for t in (ins, outs)]
        w = self.exchange(ins).reshape(2, r, 2, self.links.chips, -1)
        w = w.transpose(1, 3, 0, 2, 4).reshape(r, self.ff)
        return w, jnp.concatenate([outs[:, :f], outs[:, f:]], 0)


def tie(x, *after):
    return lax.optimization_barrier((x, *after))[0]


def body(links, *args):
    (tokens, cotangent, g1, w1, p1, g2, win, wout, g3, w3, p3, g4, router, ein, eout, routes, slots) = args
    e = lax.axis_index("expert")
    d = lax.axis_index("dp")
    blk_len, feat = tokens.shape[1:]
    rows = up16(blk_len)
    half = feat // 2
    rdev = w1.shape[0]
    ff = win.shape[1]
    longest = LEN - (blk_len - 1) * links.C
    experts = router.shape[1]
    small_rows = (4 + experts + 7) // 8 * 8
    cap = max(2, (5 * TOP * blk_len + 4 * experts - 1) // (4 * experts))
    blk = 2 * (e % 2) + d
    where = jnp.stack([blk, e if links.fast else 0 * e]).astype(jnp.int32)
    wt = Weights(links, rdev, feat, ff)
    firsts = wt.firsts
    img = dict(rows=rows, blk_len=blk_len, longest=longest)

    small = jnp.concatenate([g1[:, None], g2[:, None], g3[:, None], g4[:, None], router], 1)
    gsm = small.shape[1]
    lane1 = jnp.concatenate(
        [wt.split_attend(w1), jnp.broadcast_to(small[None], (2, rdev, gsm))], 2
    )
    lane1 = lane_rows(links, lane1, d)
    ps = lax.ppermute(jnp.concatenate([p1, p3], 0), ALL, links.to_lane)
    tok = links.move(tokens[0])
    tok_sib = links.sib(tok)
    quad1 = wt.column(wt.pack_attend(lane1[:, : 3 * half], ps[:rdev], lane1[:, 3 * half :]))
    blocks1 = wt.spread_attend(quad1)

    later = jnp.concatenate([wt.split_widen(win), wt.split_attend(w3)], 2)
    later = lane_rows(links, later, d)
    w_in, w_out = later[:, : ff // 2], wt.pack_wide(wout)
    buf3 = wt.pack_attend(later[:, ff // 2 :], ps[rdev:], None)
    if w_in.shape == w_out.shape:
        quad = wt.column(tie(jnp.concatenate([w_in, w_out, buf3], 1), quad1))
        quad2, quad3 = (quad[..., : ff // 2], quad[..., ff // 2 : ff]), quad[..., ff:]
    else:
        quad2, quad3 = (wt.column(w_in), wt.column(w_out)), wt.column(buf3)
    blocks2 = wt.spread_wide(*quad2)
    blocks3 = wt.spread_attend(quad3)

    ein_own, eout_own = ein[0], eout[0]
    ein_sib, eout_sib = links.sib(ein_own), links.sib(eout_own)
    cot = links.move(cotangent[0])
    index = links.move(jnp.concatenate([routes[0], slots[0]], 1))
    index = jnp.pad(index, ((0, rows - blk_len), (0, 0)), constant_values=cap)

    x0, normed1, q1, kv1, wa1, wp1, small, gains = attend_first(
        where, tok, tok_sib, small_rows, *blocks1, firsts, rows
    )
    far1 = links.partner(kv1)
    part, low, blend1, lse1 = attend_core(where, q1, kv1, far1, wp1, solo=False, **img)
    x1, normed2, hidden, part2, low2, wi, wo = widen_forward(
        where, x0, part, links.sib(low), gains, *blocks2, firsts, rows
    )
    x2, normed3, q3, kv3, wa3, wp3 = attend_next(
        where, x1, part2, links.sib(low2), gains, 2, *blocks3, firsts, rows
    )
    far3 = links.partner(kv3)
    part3, low3, blend3, lse3 = attend_core(where, q3, kv3, far3, wp3, solo=True, **img)
    moe_args = dict(experts=experts, cap=cap, fast=links.fast, **img)
    x3, moe, gates, up, *sent = route(
        where, x2, part3, links.sib(low3), gains, small, cot, index, **moe_args
    )
    came = links.swap_blocks(sent)
    res, back, eis_sib, eos_sib = expert_half(came, ein_sib, eout_sib, None, up16(cap))
    *answer, eis, eos = expert_half(came, ein_own, eout_own, (res, back), up16(cap))
    answer = links.swap_blocks(answer)
    acts, u, u_low, small_slopes = combine(
        where, answer, x3, moe, gates, up, index, small, gains, small_rows, **moe_args
    )
    e_sums = [
        lax.psum((a.astype(F32) + links.sib(b).astype(F32)).astype(BF), "context").astype(F32)
        for a, b in ((eis, eis_sib), (eos, eos_sib))
    ]
    acts = links.move(acts)

    u, u_low = join_upstream(u, links.sib(u_low), rows)
    dq, own, far, wps = attend_core_back(where, u_low, wp3, blend3, q3, kv3, far3, lse3, **img)
    part, low, *slopes3 = attend_proj_back(
        where, dq, own, links.partner(far), normed3, wa3, wps, firsts, rows, False
    )
    u, g3_slope, part, low, *slopes2 = widen_back(
        where, u, x2, gains, part, links.sib(low), normed2, hidden, wi, wo, firsts, rows
    )
    w3_out, p3_out = wt.owner_attend(*slopes3)
    u, u_low, g2_slope = norm_step(u, x1, gains, 1, part, links.sib(low), rows, 0)
    win_out, wout_out = wt.owner_wide(*slopes2)
    dq, own, far, wps = attend_core_back(where, u_low, wp1, blend1, q1, kv1, far1, lse1, **img)
    part, low, *slopes1 = attend_proj_back(
        where, dq, own, links.partner(far), normed1, wa1, wps, firsts, rows, True
    )
    w1_out, p1_out = wt.owner_attend(*slopes1)
    u, _, g1_slope = norm_step(u, x0, gains, 0, part, links.sib(low), rows, blk_len)
    token_slope = links.move(u)

    small = jnp.concatenate([g1_slope, g2_slope, g3_slope, small_slopes[3:]], 0)
    small = links.total(small)
    flat = (e * links.C + lax.axis_index("context")) * 2 + d
    small = small.reshape(-1, 2 * links.chips, rdev)
    small = lax.dynamic_index_in_dim(small, flat, 1, False)
    return (
        acts[None], token_slope[None], small[0], w1_out, p1_out, small[1], win_out, wout_out,
        small[2], w3_out, p3_out, small[3], small[4 : 4 + experts].T, e_sums[0][None], e_sums[1][None],
    )


def solution(mesh):
    links = Links(mesh)
    tok = P(("expert", "dp"), "context", None)
    vec, mat = P(ALL), P(ALL, None)
    ein, eout = P("expert", None, "dp"), P("expert", "dp", None)
    dense = (vec, mat, mat, vec, mat, mat, vec, mat, mat, vec, mat, ein, eout)
    return jax.shard_map(
        functools.partial(body, links),
        mesh=mesh,
        in_specs=(tok, tok) + dense + (tok, tok),
        out_specs=(tok, tok) + dense,
        check_vma=False,
    )
```

time: 676 us -> 678 us (level)
  waiting for transfers between devices: 274 us -> 403 us
  Pallas kernels: 0 us -> 93.9 us
  matrix products: 84.7 us -> 0 us
  starting transfers between devices: 169 us -> 86.9 us
  other arithmetic: 63.6 us -> 35 us
  local copies, waits for them, and re-layouts: 55.8 us -> 35.5 us
    ppermute x144 -> x66, starting transfers between devices: 151 us -> 57.3 us  [xor(): return lax.ppermute(x, axis, [(i, i ^ j) for i in range(n)])]
    pallas_call x0 -> x17, Pallas kernels: none -> 93.9 us  [the longest x15 73.6 us: call(): pl.pallas_call(run, out_shape=[jax.ShapeDtypeStruct(s, t) for s, t, _ in...]
    dot_general x57 -> x0, matrix products: 84.7 us -> none  [the longest x16 23.3 us: t_dot(): lax.dot_general(a, b, (((0,), (0,)), ((), ())), preferred_element_type=F32)]
    ppermute x144 -> x66, waiting for transfers between devices: 238 us -> 321 us  [xor(): return lax.ppermute(x, axis, [(i, i ^ j) for i in range(n)])]
    psum x1, waiting for transfers between devices: 30.9 us -> 75.6 us  [body(): lax.psum((a.astype(F32) + links.sib(b).astype(F32)).astype(BF), 'context')]
    convert_element_type x30 -> x18, other arithmetic: 26.6 us -> 8.04 us  [the longest x6 5.59 us: plane_sum(): got = self.xor(send, 'expert', first).astype(F32)]
    ppermute x0 -> x3, starting transfers between devices: none -> 11.6 us  [the longest x2 7.17 us: owner_attend(): p = lax.ppermute(p, ALL, self.links.from_lane)]
    slice x23 -> x24, local copies, waits for them, and re-layouts: 12.7 us -> 3.04 us  [the longest x2 1.04 us: spread_attend(): v = quad[..., f:f + h]]
  transfers between devices with their start and end apart: 150 -> 75, of which waited for: 59 -> 38; matrix products, arithmetic and copies ran while one was open for 26% -> 6% of each run, Pallas kernels for 0% -> 9%
where the time goes in v2:
time: 678 us; the launch traced here: 670 us
  waiting for transfers between devices  403 us (59%)
  Pallas kernels  93.9 us (14%)
  starting transfers between devices  86.9 us (13%)
  local copies, waits for them, and re-layouts  35.5 us (5%)
  other arithmetic  35 us (5%)
  between operations  16 us (2%)
    ppermute x66, waiting for transfers between devices, xor(): return lax.ppermute(x, axis, [(i, i ^ j) for i in range(n)])  321 us
    psum x1, waiting for transfers between devices, body(): lax.psum((a.astype(F32) + links.sib(b).astype(F32)).astype(BF), 'context')  75.6 us
    pallas_call x15, Pallas kernels, call(): pl.pallas_call(run, out_shape=[jax.ShapeDtypeStruct(s, t) for s, t, _ in...  73.6 us
    ppermute x66, starting transfers between devices, xor(): return lax.ppermute(x, axis, [(i, i ^ j) for i in range(n)])  57.3 us
    unnamed x150, local copies, waits for them, and re-layouts  23 us
    pallas_call x2, Pallas kernels, expert_half(): pl.pallas_call(kernel, grid=(steps,), out_shape=shapes, in_specs=in_specs...  20.3 us
    ppermute x5, starting transfers between devices, move(): return lax.ppermute(x, ALL, self.team)  18.1 us
  transfers between devices with their start and end apart: 75, of which 38 were waited for; matrix products, arithmetic and copies ran while one was open for 6% of the time, Pallas kernels for 9%

profile of v2, /device:TPU:10, one launch (start us, length us, event | category | flops | bytes accessed | tf_op | source)
XLA Modules:
  0.0 670.4 jit_solution(18398788324877337)
XLA Ops:
  10.1 4.4 collective-permute-start.3
  19.2 5.0 collective-permute-done.4
  25.6 13.9 %collective-permute-done.5 = bf16[2,48,1664]{2,1,0:T(8,128)(2,1)S(1)} collective-permute-done((bf16[2,48,1664]{2,1,0:T(8,128)(2,1)S(1)}, bf16[2,48,1664]{2,1,0:T(8,128)(2,1)S(1)}, u32[]{:S(2)}, u32[]{:S(2)}) %collective-permute-start.5) | collective-permute-done | bytes 319520 | tf_op jit(solution)/shard_map/ppermute | solution.py:752
  43.2 10.3 %collective-permute-done.13 = bf16[48,4608]{1,0:T(8,128)(2,1)S(1)} collective-permute-done((bf16[48,4608]{1,0:T(8,128)(2,1)S(1)}, bf16[48,4608]{1,0:T(8,128)(2,1)S(1)}, u32[]{:S(2)}, u32[]{:S(2)}) %collective-permute-start.13) | collective-permute-done | bytes 442400 | tf_op jit(solution)/shard_map/ppermute | solution.py:752
  59.3 3.6 collective-permute-done.6.refs_4_
  67.1 30.5 %collective-permute-done.14 = bf16[2,48,4608]{2,1,0:T(8,128)(2,1)S(1)} collective-permute-done((bf16[2,48,4608]{2,1,0:T(8,128)(2,1)S(1)}, bf16[2,48,4608]{2,1,0:T(8,128)(2,1)S(1)}, u32[]{:S(2)}, u32[]{:S(2)}) %collective-permute-start.14) | collective-permute-done | bytes 884768 | tf_op jit(solution)/shard_map/ppermute | solution.py:752
  106.8 4.3 shard_map.280
  114.5 4.8 collective-permute-done.15.refs_6_
  121.8 8.1 %collective-permute-done.10.refs_3_.refs_6_ = bf16[320,768]{1,0:T(8,128)(2,1)S(1)} collective-permute-done((bf16[320,768]{1,0:T(8,128)(2,1)S(1)}, bf16[320,768]{1,0:T(8,128)(2,1)S(1)}, u32[]{:S(2)}, u32[]{:S(2)}) %collective-permute-start.10) | collective-permute-done | bytes 491552 | tf_op jit(solution)/shard_map/ppermute | solution.py:752
  129.9 23.2 %collective-permute-done.22.refs_9_ = bf16[384,384]{1,0:T(8,128)(2,1)S(1)} collective-permute-done((bf16[384,384]{1,0:T(8,128)(2,1)S(1)}, bf16[384,384]{1,0:T(8,128)(2,1)S(1)}, u32[]{:S(2)}, u32[]{:S(2)}) %collective-permute-start.22) | collective-permute-done | bytes 294944 | tf_op jit(solution)/shard_map/ppermute | solution.py:752
  153.1 4.2 shard_map.281
  157.3 3.8 collective-permute-done.20.refs_6_
  164.6 9.5 %shard_map.282 = (f32[320,768]{1,0:T(8,128)}, bf16[320,768]{1,0:T(8,128)(2,1)S(1)}, f32[320,1536]{1,0:T(8,128)}, f32[320,768]{1,0:T(8,128)}, bf16[320,768]{1,0:T...) custom-call(s32[2]{0:T(128)S(1)} %pad_add_fusion.1.refs_0_, ...), custom_call_target="tpu_custom_call" | custom-call | flops 1509949440 | bytes 16777216 | tf_op jit(solution)/shard_map/pallas_call | solution.py:45
  174.1 4.4 collective-permute-done.23.refs_10_
  179.4 4.8 shard_map.283
  187.8 15.6 %collective-permute-done.24.refs_3_.refs_6_ = bf16[320,768]{1,0:T(8,128)(2,1)S(1)} collective-permute-done((bf16[320,768]{1,0:T(8,128)(2,1)S(1)}, bf16[320,768]{1,0:T(8,128)(2,1)S(1)}, u32[]{:S(2)}, u32[]{:S(2)}) %collective-permute-start.24) | collective-permute-done | bytes 491552 | tf_op jit(solution)/shard_map/ppermute | solution.py:752
  203.3 4.2 shard_map.284
  209.4 4.4 collective-permute-start.27
  213.8 3.6 collective-permute-done.27
  223.9 6.4 collective-permute-done.28.refs_1_
  230.3 4.8 collective-permute-done.29.refs_2_
  235.2 9.9 %shard_map.286 = (f32[384,768]{1,0:T(8,128)S(1)}, f32[384,768]{1,0:T(8,128)S(1)}, bf16[768,1536]{1,0:T(8,128)(2,1)}, bf16[1536,768]{1,0:T(8,128)(2,1)}) custom-call(bf16[192,768]{1,0:T(8,128)(2,1)S(1)} %get-tuple-element.120.refs_0_, bf16[192,768]{1,0:T(8,128)(2,1)S(1)} %collective-permute-done.28.refs_1_, ...), custom_call_target="tpu_custom_call" | custom-call | flops 5435817984 | bytes 16777216 | tf_op jit(solution)/shard_map/pallas_call | solution.py:662
  246.1 10.4 %shard_map.287 = (bf16[192,768]{1,0:T(8,128)(2,1)S(1)}, bf16[192,768]{1,0:T(8,128)(2,1)S(1)}, bf16[192,768]{1,0:T(8,128)(2,1)S(1)}, bf16[192,768]{1,0:T(8,128)(2...) custom-call(bf16[192,768]{1,0:T(8,128)(2,1)S(1)} %get-tuple-element.120.refs_0_, ...), custom_call_target="tpu_custom_call" | custom-call | flops 5435817984 | bytes 16777216 | tf_op jit(solution)/shard_map/pallas_call | solution.py:662
  260.1 6.5 collective-permute-done.33.refs_2_
  266.5 4.9 collective-permute-done.34.refs_3_
  276.8 7.0 %shard_map.290 = (bf16[320,384]{1,0:T(8,128)(2,1)S(1)}, f32[320,768]{1,0:T(8,128)}, bf16[320,768]{1,0:T(8,128)(2,1)S(1)}, bf16[384,768]{1,0:T(8,128)(2,1)S(1)}) custom-call(s32[2]{0:T(128)S(1)} %pad_add_fusion.1.refs_0_, bf16[320,768]{1,0:T(8,128)(2,1)S(1)} %get-tuple-element.138.refs_1_, bf16[384,768]{1,0:T(8,128)(2,1)S(1)} %copy-done.25, ...), custom_call_target="tpu_custom_call" | custom-call | flops 1163919360 | bytes 6291456 | tf_op jit(solution)/shard_map/pallas_call | solution.py:45
  285.0 12.9 %collective-permute-done.38.refs_3_ = bf16[320,768]{1,0:T(8,128)(2,1)S(1)} collective-permute-done((bf16[320,768]{1,0:T(8,128)(2,1)S(1)}, bf16[320,768]{1,0:T(8,128)(2,1)S(1)}, u32[]{:S(2)}, u32[]{:S(2)}) %collective-permute-start.38) | collective-permute-done | bytes 491552 | tf_op jit(solution)/shard_map/ppermute | solution.py:752
  297.9 5.6 shard_map.291
  305.7 12.5 %collective-permute-done.66 = bf16[2,384,384]{2,1,0:T(8,128)(2,1)S(1)} collective-permute-done((bf16[2,384,384]{2,1,0:T(8,128)(2,1)S(1)}, bf16[2,384,384]{2,1,0:T(8,128)(2,1)S(1)}, u32[]{:S(2)}, u32[]{:S(2)}) %collective-permute-start.66) | collective-permute-done | bytes 589856 | tf_op jit(solution)/shard_map/ppermute | solution.py:752
  319.3 6.8 %collective-permute-start.36 = (f32[145,768]{1,0:T(8,128)}, f32[145,768]{1,0:T(8,128)}, u32[]{:S(2)}, u32[]{:S(2)}) collective-permute-start(f32[145,768]{1,0:T(8,128)} %get-tuple-element.134), channel_id=1, source_target_pairs={{0,0},{1,2},{2,1},{3,3},{4,8},{5,10},{6,9},{7,11},{8,4},{9,6},{10,... | collective-permute-start | bytes 1336328 | tf_op jit(solution)/shard_map/ppermute | solution.py:748
  327.9 7.9 %collective-permute-done.65 = bf16[192,768]{1,0:T(8,128)(2,1)S(1)} collective-permute-done((bf16[192,768]{1,0:T(8,128)(2,1)S(1)}, bf16[192,768]{1,0:T(8,128)(2,1)S(1)}, u32[]{:S(2)}, u32[]{:S(2)}) %collective-permute-start.65) | collective-permute-done | bytes 294944 | tf_op jit(solution)/shard_map/ppermute | solution.py:752
  337.5 12.8 %shard_map.292 = (f32[320,768]{1,0:T(8,128)S(1)}, f32[1,768]{1,0:T(1,128)S(1)}, f32[320,768]{1,0:T(8,128)S(1)}, bf16[320,768]{1,0:T(8,128)(2,1)S(1)}, bf16[2,2,1...) custom-call(s32[2]{0:T(128)S(1)} %pad_add_fusion.1.refs_0_, ...), custom_call_target="tpu_custom_call" | custom-call | flops 3774873600 | bytes 25165824 | tf_op jit(solution)/shard_map/pallas_call | solution.py:45
  350.4 5.5 collective-permute-done.68
  359.4 4.4 collective-permute-start.57
  369.3 7.0 %shard_map.294 = (bf16[320,384]{1,0:T(8,128)(2,1)S(1)}, f32[320,768]{1,0:T(8,128)}, bf16[320,768]{1,0:T(8,128)(2,1)S(1)}, bf16[384,768]{1,0:T(8,128)(2,1)S(1)}) custom-call(s32[2]{0:T(128)S(1)} %pad_add_fusion.1.refs_0_, bf16[320,768]{1,0:T(8,128)(2,1)S(1)} %get-tuple-element.157.refs_1_, bf16[384,768]{1,0:T(8,128)(2,1)S(1)} %copy-done.21, ...), custom_call_target="tpu_custom_call" | custom-call | flops 1163919360 | bytes 6291456 | tf_op jit(solution)/shard_map/pallas_call | solution.py:45
  378.0 21.4 %collective-permute-done.41.refs_3_ = bf16[320,768]{1,0:T(8,128)(2,1)S(1)} collective-permute-done((bf16[320,768]{1,0:T(8,128)(2,1)S(1)}, bf16[320,768]{1,0:T(8,128)(2,1)S(1)}, u32[]{:S(2)}, u32[]{:S(2)}) %collective-permute-start.41) | collective-permute-done | bytes 491552 | tf_op jit(solution)/shard_map/ppermute | solution.py:752
  402.3 5.5 shard_map.295
  413.4 3.9 fusion
  420.6 3.7 fusion.1
  437.4 5.0 collective-permute-start.60
  449.2 6.5 collective-permute-done.58
  456.9 5.5 collective-permute-done.60
  466.9 57.0 %collective-permute-done.53 = bf16[2,48,1536]{2,1,0:T(8,128)(2,1)S(1)} collective-permute-done((bf16[2,48,1536]{2,1,0:T(8,128)(2,1)S(1)}, bf16[2,48,1536]{2,1,0:T(8,128)(2,1)S(1)}, u32[]{:S(2)}, u32[]{:S(2)}) %collective-permute-start.53) | collective-permute-done | bytes 294944 | tf_op jit(solution)/shard_map/ppermute | solution.py:752
  527.7 3.7 collective-permute-done.54
  531.5 5.0 collective-permute-start.56
  536.5 30.6 %collective-permute-done.61 = bf16[2,48,3072]{2,1,0:T(8,128)(2,1)S(1)} collective-permute-done((bf16[2,48,3072]{2,1,0:T(8,128)(2,1)S(1)}, bf16[2,48,3072]{2,1,0:T(8,128)(2,1)S(1)}, u32[]{:S(2)}, u32[]{:S(2)}) %collective-permute-start.61) | collective-permute-done | bytes 589856 | tf_op jit(solution)/shard_map/ppermute | solution.py:752
  579.3 75.6 %all-reduce.5.cloned.1.call-done = (bf16[1,768,1536]{2,1,0:T(8,128)(2,1)}, bf16[1,1536,768]{2,1,0:T(8,128)(2,1)}) async-done(((bf16[1,768,1536]{2,1,0:T(8,128)(2,1)}, bf16[1,1536,768]{2,1,0:T(8,128)(2,1)}), (bf16[1,768,1536]{2,1,0:T(8,128)(2,1)}, bf16[1,1536,768]{2,1,0:T(8,128)(2,1)})) %all-reduce.5.cloned.1.call-update) | async-done | bytes 4718608 | tf_op jit(solution)/shard_map/psum | solution.py:996
  654.9 4.6 broadcast_in_dim.44
  (399 shorter events, 138.7 us)
Async XLA Ops:
  7.2 647.7 %all-reduce.5.cloned.1.call-start = ((), (), s32[]{:S(2)}) async-start(), calls=%async_computation | async-start | bytes 9437184 | tf_op jit(solution)/shard_map/psum | solution.py:996
  24.2 15.3 %collective-permute-start.5 = (bf16[2,48,1664]{2,1,0:T(8,128)(2,1)S(1)}, bf16[2,48,1664]{2,1,0:T(8,128)(2,1)S(1)}, u32[]{:S(2)}, u32[]{:S(2)}) collective-permute-start(bf16[2,48,1664]{2,1,0:T(8,128)(2,1)S(1)} %maximum_select_fusion.4), channel_id=1, source_target_pairs={{0,4},{2,6},{4,0},{6,2},{1,5},{3,7},{5,1},{7,3},{8,12},{10,14},{12... | collective-permute-start | bytes 958472 | tf_op jit(solution)/shard_map/ppermute | solution.py:752
  39.6 13.9 %collective-permute-start.13 = (bf16[48,4608]{1,0:T(8,128)(2,1)S(1)}, bf16[48,4608]{1,0:T(8,128)(2,1)S(1)}, u32[]{:S(2)}, u32[]{:S(2)}) collective-permute-start(bf16[48,4608]{1,0:T(8,128)(2,1)S(1)} %maximum_dynamic-update-slice_fusion), channel_id=1, source_target_pairs={{0,2},{2,0},{4,6},{6,4},{1,3},{3,1},{5,7},{7,5},{8,10},{10,8},{12,... | collective-permute-start | bytes 1327112 | tf_op jit(solution)/shard_map/ppermute | solution.py:752
  53.7 43.9 %collective-permute-start.14 = (bf16[2,48,4608]{2,1,0:T(8,128)(2,1)S(1)}, bf16[2,48,4608]{2,1,0:T(8,128)(2,1)S(1)}, u32[]{:S(2)}, u32[]{:S(2)}) collective-permute-start(bf16[2,48,4608]{2,1,0:T(8,128)(2,1)S(1)} %maximum_select_fusion.1), channel_id=1, source_target_pairs={{0,4},{2,6},{4,0},{6,2},{1,5},{3,7},{5,1},{7,3},{8,12},{10,14},{12... | collective-permute-start | bytes 2654216 | tf_op jit(solution)/shard_map/ppermute | solution.py:752
  57.0 45.2 %collective-permute-start = (bf16[145,768]{1,0:T(8,128)(2,1)S(1)}, bf16[145,768]{1,0:T(8,128)(2,1)S(1)}, u32[]{:S(2)}, u32[]{:S(2)}) collective-permute-start(bf16[145,768]{1,0:T(8,128)(2,1)S(1)} %bitcast.228), channel_id=1, source_target_pairs={{0,0},{1,2},{2,1},{3,3},{4,8},{5,10},{6,9},{7,11},{8,4},{9,6},{10,... | collective-permute-start | bytes 668168 | tf_op jit(solution)/shard_map/ppermute | solution.py:748
  63.8 40.1 %collective-permute-start.7 = (bf16[2,192,768]{2,1,0:T(8,128)(2,1)}, bf16[2,192,768]{2,1,0:T(8,128)(2,1)}, u32[]{:S(2)}, u32[]{:S(2)}) collective-permute-start(bf16[2,192,768]{2,1,0:T(8,128)(2,1)} %pad_maximum_fusion.4), channel_id=1, source_target_pairs={{0,16},{8,24},{16,0},{24,8},{1,17},{9,25},{17,1},{25,9},{2,18},{10... | collective-permute-start | bytes 1769480 | tf_op jit(solution)/shard_map/ppermute | solution.py:752
  67.1 36.8 %collective-permute-start.9 = (bf16[2,448,384]{2,1,0:T(8,128)(2,1)}, bf16[2,448,384]{2,1,0:T(8,128)(2,1)}, u32[]{:S(2)}, u32[]{:S(2)}) collective-permute-start(bf16[2,448,384]{2,1,0:T(8,128)(2,1)} %pad_maximum_fusion.3), channel_id=1, source_target_pairs={{0,8},{8,0},{16,24},{24,16},{1,9},{9,1},{17,25},{25,17},{2,10},{10... | collective-permute-start | bytes 2064392 | tf_op jit(solution)/shard_map/ppermute | solution.py:752
  99.9 13.7 %collective-permute-start.17 = (bf16[2,192,768]{2,1,0:T(8,128)(2,1)S(1)}, bf16[2,192,768]{2,1,0:T(8,128)(2,1)S(1)}, u32[]{:S(2)}, u32[]{:S(2)}) collective-permute-start(bf16[2,192,768]{2,1,0:T(8,128)(2,1)S(1)} %get-tuple-element.271.refs_8_), channel_id=1, source_target_pairs={{0,16},{8,24},{16,0},{24,8},{1,17},{9,25},{17,1},{25,9},{2,18},{10... | collective-permute-start | bytes 1769480 | tf_op jit(solution)/shard_map/ppermute | solution.py:752
  103.2 16.1 %collective-permute-start.15 = (bf16[2,192,768]{2,1,0:T(8,128)(2,1)S(1)}, bf16[2,192,768]{2,1,0:T(8,128)(2,1)S(1)}, u32[]{:S(2)}, u32[]{:S(2)}) collective-permute-start(bf16[2,192,768]{2,1,0:T(8,128)(2,1)S(1)} %get-tuple-element.273.refs_5_), channel_id=1, source_target_pairs={{0,8},{8,0},{16,24},{24,16},{1,9},{9,1},{17,25},{25,17},{2,10},{10... | collective-permute-start | bytes 1769480 | tf_op jit(solution)/shard_map/ppermute | solution.py:752
  111.1 18.7 %collective-permute-start.10 = (bf16[320,768]{1,0:T(8,128)(2,1)S(1)}, bf16[320,768]{1,0:T(8,128)(2,1)S(1)}, u32[]{:S(2)}, u32[]{:S(2)}) collective-permute-start(bf16[320,768]{1,0:T(8,128)(2,1)S(1)} %get-tuple-element.104.refs_2_.refs_5_), channel_id=1, source_target_pairs={{0,8},{8,0},{16,24},{24,16},{1,9},{9,1},{17,25},{25,17},{2,10},{10... | collective-permute-start | bytes 1474568 | tf_op jit(solution)/shard_map/ppermute | solution.py:752
  113.8 49.4 %collective-permute-start.18 = (bf16[2,2,192,768]{3,2,1,0:T(8,128)(2,1)S(1)}, bf16[2,2,192,768]{3,2,1,0:T(8,128)(2,1)S(1)}, u32[]{:S(2)}, u32[]{:S(2)}) collective-permute-start(bf16[2,2,192,768]{3,2,1,0:T(8,128)(2,1)S(1)} %pad_maximum_fusion.2), channel_id=1, source_target_pairs={{0,8},{8,0},{16,24},{24,16},{1,9},{9,1},{17,25},{25,17},{2,10},{10... | collective-permute-start | bytes 3538952 | tf_op jit(solution)/shard_map/ppermute | solution.py:752
  119.4 43.8 %collective-permute-start.16 = (bf16[2,2,192,768]{3,2,1,0:T(8,128)(2,1)S(1)}, bf16[2,2,192,768]{3,2,1,0:T(8,128)(2,1)S(1)}, u32[]{:S(2)}, u32[]{:S(2)}) collective-permute-start(bf16[2,2,192,768]{3,2,1,0:T(8,128)(2,1)S(1)} %pad_maximum_fusion.1), channel_id=1, source_target_pairs={{0,16},{8,24},{16,0},{24,8},{1,17},{9,25},{17,1},{25,9},{2,18},{10... | collective-permute-start | bytes 3538952 | tf_op jit(solution)/shard_map/ppermute | solution.py:752
  119.6 33.4 %collective-permute-start.22 = (bf16[384,384]{1,0:T(8,128)(2,1)S(1)}, bf16[384,384]{1,0:T(8,128)(2,1)S(1)}, u32[]{:S(2)}, u32[]{:S(2)}) collective-permute-start(bf16[384,384]{1,0:T(8,128)(2,1)S(1)} %get-tuple-element.281.refs_8_), channel_id=1, source_target_pairs={{0,16},{8,24},{16,0},{24,8},{1,17},{9,25},{17,1},{25,9},{2,18},{10... | collective-permute-start | bytes 884744 | tf_op jit(solution)/shard_map/ppermute | solution.py:752
  121.7 39.4 %collective-permute-start.20 = (bf16[192,768]{1,0:T(8,128)(2,1)S(1)}, bf16[192,768]{1,0:T(8,128)(2,1)S(1)}, u32[]{:S(2)}, u32[]{:S(2)}) collective-permute-start(bf16[192,768]{1,0:T(8,128)(2,1)S(1)} %bitcast.171), channel_id=1, source_target_pairs={{0,8},{8,0},{16,24},{24,16},{1,9},{9,1},{17,25},{25,17},{2,10},{10... | collective-permute-start | bytes 884744 | tf_op jit(solution)/shard_map/ppermute | solution.py:752
  129.9 94.0 %collective-permute-start.31 = (bf16[768,1536]{1,0:T(8,128)(2,1)}, bf16[768,1536]{1,0:T(8,128)(2,1)}, u32[]{:S(2)}, u32[]{:S(2)}) collective-permute-start(bf16[768,1536]{1,0:T(8,128)(2,1)} %bitcast.50.refs_4_), channel_id=1, source_target_pairs={{0,1},{1,0},{2,3},{3,2},{4,5},{5,4},{6,7},{7,6},{8,9},{9,8},{10,11... | collective-permute-start | bytes 7077896 | tf_op jit(solution)/shard_map/ppermute | solution.py:752
  153.0 70.8 %collective-permute-start.32 = (bf16[1536,768]{1,0:T(8,128)(2,1)}, bf16[1536,768]{1,0:T(8,128)(2,1)}, u32[]{:S(2)}, u32[]{:S(2)}) collective-permute-start(bf16[1536,768]{1,0:T(8,128)(2,1)} %bitcast.51.refs_5_), channel_id=1, source_target_pairs={{0,1},{1,0},{2,3},{3,2},{4,5},{5,4},{6,7},{7,6},{8,9},{9,8},{10,11... | collective-permute-start | bytes 7077896 | tf_op jit(solution)/shard_map/ppermute | solution.py:752
  162.9 15.6 %collective-permute-start.23 = (bf16[2,384,384]{2,1,0:T(8,128)(2,1)}, bf16[2,384,384]{2,1,0:T(8,128)(2,1)S(1)}, u32[]{:S(2)}, u32[]{:S(2)}) collective-permute-start(bf16[2,384,384]{2,1,0:T(8,128)(2,1)} %pad_maximum_fusion.8), channel_id=1, source_target_pairs={{0,8},{8,0},{16,24},{24,16},{1,9},{9,1},{17,25},{25,17},{2,10},{10... | collective-permute-start | bytes 1769480 | tf_op jit(solution)/shard_map/ppermute | solution.py:752
  163.2 15.3 %collective-permute-start.21 = (bf16[2,192,768]{2,1,0:T(8,128)(2,1)S(1)}, bf16[2,192,768]{2,1,0:T(8,128)(2,1)S(1)}, u32[]{:S(2)}, u32[]{:S(2)}) collective-permute-start(bf16[2,192,768]{2,1,0:T(8,128)(2,1)S(1)} %pad_maximum_fusion.7), channel_id=1, source_target_pairs={{0,16},{8,24},{16,0},{24,8},{1,17},{9,25},{17,1},{25,9},{2,18},{10... | collective-permute-start | bytes 1769480 | tf_op jit(solution)/shard_map/ppermute | solution.py:752
  184.2 19.2 %collective-permute-start.24 = (bf16[320,768]{1,0:T(8,128)(2,1)S(1)}, bf16[320,768]{1,0:T(8,128)(2,1)S(1)}, u32[]{:S(2)}, u32[]{:S(2)}) collective-permute-start(bf16[320,768]{1,0:T(8,128)(2,1)S(1)} %get-tuple-element.115.refs_2_.refs_5_), channel_id=1, source_target_pairs={{0,8},{8,0},{16,24},{24,16},{1,9},{9,1},{17,25},{25,17},{2,10},{10... | collective-permute-start | bytes 1474568 | tf_op jit(solution)/shard_map/ppermute | solution.py:752
  185.0 32.4 %collective-permute-start.26 = (f32[145,768]{1,0:T(8,128)S(1)}, f32[145,768]{1,0:T(8,128)S(1)}, u32[]{:S(2)}, u32[]{:S(2)}) collective-permute-start(f32[145,768]{1,0:T(8,128)S(1)} %bitcast.215), channel_id=1, source_target_pairs={{0,0},{1,2},{2,1},{3,3},{4,8},{5,10},{6,9},{7,11},{8,4},{9,6},{10,... | collective-permute-start | bytes 1336328 | tf_op jit(solution)/shard_map/ppermute | solution.py:748
  220.4 14.7 %collective-permute-start.29 = (bf16[192,768]{1,0:T(8,128)(2,1)S(1)}, bf16[192,768]{1,0:T(8,128)(2,1)S(1)}, u32[]{:S(2)}, u32[]{:S(2)}) collective-permute-start(bf16[192,768]{1,0:T(8,128)(2,1)S(1)} %get-tuple-element.122), channel_id=1, source_target_pairs={{0,16},{8,24},{16,0},{24,8},{1,17},{9,25},{17,1},{25,9},{2,18},{10... | collective-permute-start | bytes 884744 | tf_op jit(solution)/shard_map/ppermute | solution.py:752
  220.5 14.7 %collective-permute-start.30 = (bf16[192,768]{1,0:T(8,128)(2,1)S(1)}, bf16[192,768]{1,0:T(8,128)(2,1)S(1)}, u32[]{:S(2)}, u32[]{:S(2)}) collective-permute-start(bf16[192,768]{1,0:T(8,128)(2,1)S(1)} %get-tuple-element.123), channel_id=1, source_target_pairs={{0,24},{8,16},{16,8},{24,0},{1,25},{9,17},{17,9},{25,1},{2,26},{10... | collective-permute-start | bytes 884744 | tf_op jit(solution)/shard_map/ppermute | solution.py:752
  258.2 13.2 %collective-permute-start.34 = (bf16[192,768]{1,0:T(8,128)(2,1)S(1)}, bf16[192,768]{1,0:T(8,128)(2,1)S(1)}, u32[]{:S(2)}, u32[]{:S(2)}) collective-permute-start(bf16[192,768]{1,0:T(8,128)(2,1)S(1)} %get-tuple-element.128), channel_id=1, source_target_pairs={{0,16},{8,24},{16,0},{24,8},{1,17},{9,25},{17,1},{25,9},{2,18},{10... | collective-permute-start | bytes 884744 | tf_op jit(solution)/shard_map/ppermute | solution.py:752
  258.5 12.9 %collective-permute-start.35 = (bf16[192,768]{1,0:T(8,128)(2,1)S(1)}, bf16[192,768]{1,0:T(8,128)(2,1)S(1)}, u32[]{:S(2)}, u32[]{:S(2)}) collective-permute-start(bf16[192,768]{1,0:T(8,128)(2,1)S(1)} %get-tuple-element.129), channel_id=1, source_target_pairs={{0,24},{8,16},{16,8},{24,0},{1,25},{9,17},{17,9},{25,1},{2,26},{10... | collective-permute-start | bytes 884744 | tf_op jit(solution)/shard_map/ppermute | solution.py:752
  284.7 13.3 %collective-permute-start.38 = (bf16[320,768]{1,0:T(8,128)(2,1)S(1)}, bf16[320,768]{1,0:T(8,128)(2,1)S(1)}, u32[]{:S(2)}, u32[]{:S(2)}) collective-permute-start(bf16[320,768]{1,0:T(8,128)(2,1)S(1)} %get-tuple-element.143), channel_id=1, source_target_pairs={{0,8},{8,0},{16,24},{24,16},{1,9},{9,1},{17,25},{25,17},{2,10},{10... | collective-permute-start | bytes 1474568 | tf_op jit(solution)/shard_map/ppermute | solution.py:752
  303.6 14.6 %collective-permute-start.66 = (bf16[2,384,384]{2,1,0:T(8,128)(2,1)S(1)}, bf16[2,384,384]{2,1,0:T(8,128)(2,1)S(1)}, u32[]{:S(2)}, u32[]{:S(2)}) collective-permute-start(bf16[2,384,384]{2,1,0:T(8,128)(2,1)S(1)} %get-tuple-element.184), channel_id=1, source_target_pairs={{0,16},{8,24},{16,0},{24,8},{1,17},{9,25},{17,1},{25,9},{2,18},{10... | collective-permute-start | bytes 1769480 | tf_op jit(solution)/shard_map/ppermute | solution.py:752
  304.3 21.8 %collective-permute-start.64 = (bf16[2,192,768]{2,1,0:T(8,128)(2,1)S(1)}, bf16[2,192,768]{2,1,0:T(8,128)(2,1)S(1)}, u32[]{:S(2)}, u32[]{:S(2)}) collective-permute-start(bf16[2,192,768]{2,1,0:T(8,128)(2,1)S(1)} %get-tuple-element.182), channel_id=1, source_target_pairs={{0,8},{8,0},{16,24},{24,16},{1,9},{9,1},{17,25},{25,17},{2,10},{10... | collective-permute-start | bytes 1769480 | tf_op jit(solution)/shard_map/ppermute | solution.py:752
  318.8 93.7 %collective-permute-start.72 = (bf16[768,1536]{1,0:T(8,128)(2,1)}, bf16[768,1536]{1,0:T(8,128)(2,1)}, u32[]{:S(2)}, u32[]{:S(2)}) collective-permute-start(bf16[768,1536]{1,0:T(8,128)(2,1)} %get-tuple-element.186), channel_id=1, source_target_pairs={{0,1},{1,0},{2,3},{3,2},{4,5},{5,4},{6,7},{7,6},{8,9},{9,8},{10,11... | collective-permute-start | bytes 7077896 | tf_op jit(solution)/shard_map/ppermute | solution.py:752
  318.8 99.3 %collective-permute-start.73 = (bf16[1536,768]{1,0:T(8,128)(2,1)}, bf16[1536,768]{1,0:T(8,128)(2,1)}, u32[]{:S(2)}, u32[]{:S(2)}) collective-permute-start(bf16[1536,768]{1,0:T(8,128)(2,1)} %get-tuple-element.188), channel_id=1, source_target_pairs={{0,1},{1,0},{2,3},{3,2},{4,5},{5,4},{6,7},{7,6},{8,9},{9,8},{10,11... | collective-permute-start | bytes 7077896 | tf_op jit(solution)/shard_map/ppermute | solution.py:752
  319.3 37.8 %collective-permute-start.36 = (f32[145,768]{1,0:T(8,128)}, f32[145,768]{1,0:T(8,128)}, u32[]{:S(2)}, u32[]{:S(2)}) collective-permute-start(f32[145,768]{1,0:T(8,128)} %get-tuple-element.134), channel_id=1, source_target_pairs={{0,0},{1,2},{2,1},{3,3},{4,8},{5,10},{6,9},{7,11},{8,4},{9,6},{10,... | collective-permute-start | bytes 1336328 | tf_op jit(solution)/shard_map/ppermute | solution.py:748
  326.1 11.4 %collective-permute-start.39 = (bf16[320,768]{1,0:T(8,128)(2,1)S(1)}, bf16[320,768]{1,0:T(8,128)(2,1)S(1)}, u32[]{:S(2)}, u32[]{:S(2)}) collective-permute-start(bf16[320,768]{1,0:T(8,128)(2,1)S(1)} %get-tuple-element.148), channel_id=1, source_target_pairs={{0,1},{1,0},{2,3},{3,2},{4,5},{5,4},{6,7},{7,6},{8,9},{9,8},{10,11... | collective-permute-start | bytes 1474568 | tf_op jit(solution)/shard_map/ppermute | solution.py:752
  336.0 19.9 %collective-permute-start.68 = (bf16[2,48,1536]{2,1,0:T(8,128)(2,1)S(1)}, bf16[2,48,1536]{2,1,0:T(8,128)(2,1)S(1)}, u32[]{:S(2)}, u32[]{:S(2)}) collective-permute-start(bf16[2,48,1536]{2,1,0:T(8,128)(2,1)S(1)} %select_convert_fusion.1), channel_id=1, source_target_pairs={{0,4},{2,6},{4,0},{6,2},{1,5},{3,7},{5,1},{7,3},{8,12},{10,14},{12... | collective-permute-start | bytes 884744 | tf_op jit(solution)/shard_map/ppermute | solution.py:752
  350.3 13.4 %collective-permute-start.40 = (bf16[320,768]{1,0:T(8,128)(2,1)S(1)}, bf16[320,768]{1,0:T(8,128)(2,1)S(1)}, u32[]{:S(2)}, u32[]{:S(2)}) collective-permute-start(bf16[320,768]{1,0:T(8,128)(2,1)S(1)} %get-tuple-element.155), channel_id=1, source_target_pairs={{0,1},{1,0},{2,3},{3,2},{4,5},{5,4},{6,7},{7,6},{8,9},{9,8},{10,11... | collective-permute-start | bytes 1474568 | tf_op jit(solution)/shard_map/ppermute | solution.py:752
  356.9 19.4 %collective-permute-start.69 = (bf16[48,1536]{1,0:T(8,128)(2,1)S(1)}, bf16[48,1536]{1,0:T(8,128)(2,1)S(1)}, u32[]{:S(2)}, u32[]{:S(2)}) collective-permute-start(bf16[48,1536]{1,0:T(8,128)(2,1)S(1)} %fusion.33), channel_id=1, source_target_pairs={{0,2},{2,0},{4,6},{6,4},{1,3},{3,1},{5,7},{7,5},{8,10},{10,8},{12,... | collective-permute-start | bytes 442376 | tf_op jit(solution)/shard_map/ppermute | solution.py:752
  359.4 68.4 %collective-permute-start.57 = (bf16[2,2,192,768]{3,2,1,0:T(8,128)(2,1)}, bf16[2,2,192,768]{3,2,1,0:T(8,128)(2,1)}, u32[]{:S(2)}, u32[]{:S(2)}) collective-permute-start(bf16[2,2,192,768]{3,2,1,0:T(8,128)(2,1)} %get-tuple-element.178), channel_id=1, source_target_pairs={{0,8},{8,0},{16,24},{24,16},{1,9},{9,1},{17,25},{25,17},{2,10},{10... | collective-permute-start | bytes 3538952 | tf_op jit(solution)/shard_map/ppermute | solution.py:752
  364.5 67.1 %collective-permute-start.59 = (bf16[2,2,192,768]{3,2,1,0:T(8,128)(2,1)}, bf16[2,2,192,768]{3,2,1,0:T(8,128)(2,1)}, u32[]{:S(2)}, u32[]{:S(2)}) collective-permute-start(bf16[2,2,192,768]{3,2,1,0:T(8,128)(2,1)} %get-tuple-element.180), channel_id=1, source_target_pairs={{0,16},{8,24},{16,0},{24,8},{1,17},{9,25},{17,1},{25,9},{2,18},{10... | collective-permute-start | bytes 3538952 | tf_op jit(solution)/shard_map/ppermute | solution.py:752
  376.3 23.1 %collective-permute-start.41 = (bf16[320,768]{1,0:T(8,128)(2,1)S(1)}, bf16[320,768]{1,0:T(8,128)(2,1)S(1)}, u32[]{:S(2)}, u32[]{:S(2)}) collective-permute-start(bf16[320,768]{1,0:T(8,128)(2,1)S(1)} %get-tuple-element.162), channel_id=1, source_target_pairs={{0,8},{8,0},{16,24},{24,16},{1,9},{9,1},{17,25},{25,17},{2,10},{10... | collective-permute-start | bytes 1474568 | tf_op jit(solution)/shard_map/ppermute | solution.py:752
  409.3 14.9 %collective-permute-start.71 = (f32[24,768]{1,0:T(8,128)S(1)}, f32[24,768]{1,0:T(8,128)S(1)}, u32[]{:S(2)}, u32[]{:S(2)}) collective-permute-start(f32[24,768]{1,0:T(8,128)S(1)} %pad_maximum_fusion.13), channel_id=1, source_target_pairs={{0,0},{2,1},{4,2},{6,3},{8,4},{10,5},{12,6},{14,7},{16,8},{18,9},{... | collective-permute-start | bytes 221192 | tf_op jit(solution)/shard_map/ppermute | solution.py:898
  426.2 18.8 %collective-permute-start.49 = (bf16[2,192,768]{2,1,0:T(8,128)(2,1)S(1)}, bf16[2,192,768]{2,1,0:T(8,128)(2,1)}, u32[]{:S(2)}, u32[]{:S(2)}) collective-permute-start(bf16[2,192,768]{2,1,0:T(8,128)(2,1)S(1)} %copy-done.23), channel_id=1, source_target_pairs={{0,8},{8,0},{16,24},{24,16},{1,9},{9,1},{17,25},{25,17},{2,10},{10... | collective-permute-start | bytes 1769480 | tf_op jit(solution)/shard_map/ppermute | solution.py:752
  426.4 19.8 %collective-permute-start.51 = (bf16[2,384,384]{2,1,0:T(8,128)(2,1)}, bf16[2,384,384]{2,1,0:T(8,128)(2,1)}, u32[]{:S(2)}, u32[]{:S(2)}) collective-permute-start(bf16[2,384,384]{2,1,0:T(8,128)(2,1)} %get-tuple-element.176), channel_id=1, source_target_pairs={{0,16},{8,24},{16,0},{24,8},{1,17},{9,25},{17,1},{25,9},{2,18},{10... | collective-permute-start | bytes 1769480 | tf_op jit(solution)/shard_map/ppermute | solution.py:752
  431.5 24.1 %collective-permute-start.58 = (bf16[2,192,768]{2,1,0:T(8,128)(2,1)}, bf16[2,192,768]{2,1,0:T(8,128)(2,1)}, u32[]{:S(2)}, u32[]{:S(2)}) collective-permute-start(bf16[2,192,768]{2,1,0:T(8,128)(2,1)} %fusion.9), channel_id=1, source_target_pairs={{0,16},{8,24},{16,0},{24,8},{1,17},{9,25},{17,1},{25,9},{2,18},{10... | collective-permute-start | bytes 1769480 | tf_op jit(solution)/shard_map/ppermute | solution.py:752
  437.4 25.1 %collective-permute-start.60 = (bf16[2,192,768]{2,1,0:T(8,128)(2,1)}, bf16[2,192,768]{2,1,0:T(8,128)(2,1)}, u32[]{:S(2)}, u32[]{:S(2)}) collective-permute-start(bf16[2,192,768]{2,1,0:T(8,128)(2,1)} %fusion.10), channel_id=1, source_target_pairs={{0,8},{8,0},{16,24},{24,16},{1,9},{9,1},{17,25},{25,17},{2,10},{10... | collective-permute-start | bytes 1769480 | tf_op jit(solution)/shard_map/ppermute | solution.py:752
  442.3 125.8 %collective-permute-start.43 = (f32[145,768]{1,0:T(8,128)S(1)}, f32[145,768]{1,0:T(8,128)}, u32[]{:S(2)}, u32[]{:S(2)}) collective-permute-start(f32[145,768]{1,0:T(8,128)S(1)} %get-tuple-element.168), channel_id=1, source_target_pairs={{0,0},{1,2},{2,1},{3,3},{4,8},{5,10},{6,9},{7,11},{8,4},{9,6},{10,... | collective-permute-start | bytes 1336328 | tf_op jit(solution)/shard_map/ppermute | solution.py:748
  446.2 20.1 %collective-permute-start.50 = (bf16[192,768]{1,0:T(8,128)(2,1)S(1)}, bf16[192,768]{1,0:T(8,128)(2,1)S(1)}, u32[]{:S(2)}, u32[]{:S(2)}) collective-permute-start(bf16[192,768]{1,0:T(8,128)(2,1)S(1)} %fusion.25), channel_id=1, source_target_pairs={{0,16},{8,24},{16,0},{24,8},{1,17},{9,25},{17,1},{25,9},{2,18},{10... | collective-permute-start | bytes 884744 | tf_op jit(solution)/shard_map/ppermute | solution.py:752
  447.7 18.4 %collective-permute-start.52 = (bf16[384,384]{1,0:T(8,128)(2,1)S(1)}, bf16[384,384]{1,0:T(8,128)(2,1)S(1)}, u32[]{:S(2)}, u32[]{:S(2)}) collective-permute-start(bf16[384,384]{1,0:T(8,128)(2,1)S(1)} %fusion.26), channel_id=1, source_target_pairs={{0,8},{8,0},{16,24},{24,16},{1,9},{9,1},{17,25},{25,17},{2,10},{10... | collective-permute-start | bytes 884744 | tf_op jit(solution)/shard_map/ppermute | solution.py:752
  466.6 57.4 %collective-permute-start.53 = (bf16[2,48,1536]{2,1,0:T(8,128)(2,1)S(1)}, bf16[2,48,1536]{2,1,0:T(8,128)(2,1)S(1)}, u32[]{:S(2)}, u32[]{:S(2)}) collective-permute-start(bf16[2,48,1536]{2,1,0:T(8,128)(2,1)S(1)} %select_convert_fusion.3), channel_id=1, source_target_pairs={{0,4},{2,6},{4,0},{6,2},{1,5},{3,7},{5,1},{7,3},{8,12},{10,14},{12... | collective-permute-start | bytes 884744 | tf_op jit(solution)/shard_map/ppermute | solution.py:752
  524.3 42.9 %collective-permute-start.61 = (bf16[2,48,3072]{2,1,0:T(8,128)(2,1)S(1)}, bf16[2,48,3072]{2,1,0:T(8,128)(2,1)S(1)}, u32[]{:S(2)}, u32[]{:S(2)}) collective-permute-start(bf16[2,48,3072]{2,1,0:T(8,128)(2,1)S(1)} %select_convert_fusion), channel_id=1, source_target_pairs={{0,4},{2,6},{4,0},{6,2},{1,5},{3,7},{5,1},{7,3},{8,12},{10,14},{12... | collective-permute-start | bytes 1769480 | tf_op jit(solution)/shard_map/ppermute | solution.py:752
  531.5 39.4 %collective-permute-start.56 = (f32[24,768]{1,0:T(8,128)S(1)}, f32[24,768]{1,0:T(8,128)S(1)}, u32[]{:S(2)}, u32[]{:S(2)}) collective-permute-start(f32[24,768]{1,0:T(8,128)S(1)} %pad_maximum_fusion.12), channel_id=1, source_target_pairs={{0,0},{2,1},{4,2},{6,3},{8,4},{10,5},{12,6},{14,7},{16,8},{18,9},{... | collective-permute-start | bytes 221192 | tf_op jit(solution)/shard_map/ppermute | solution.py:898
  (97 other events, 714.7 us)
Sparse Core Ops, SparseCore 0:
  424.4 230.4 all-reduce.4

commit v3 on v2

v3 whole, which is shorter than its diff:
```python
import functools

import jax
import jax.numpy as jnp
from jax import lax
from jax.experimental import pallas as pl
from jax.experimental.pallas import tpu as pltpu
from jax.sharding import PartitionSpec as P

HEADS = 12
HEAD_DIM = 64
LEN = 577
TOP = 2
ALL = ("expert", "context", "dp")
CHIPS = ("expert", "context")
BF = jnp.bfloat16
F32 = jnp.float32
VM = pl.BlockSpec(memory_space=pltpu.VMEM)
HB = pl.BlockSpec(memory_space=pl.ANY)
SM = pl.BlockSpec(memory_space=pltpu.SMEM)


def up16(n):
    return (n + 15) // 16 * 16


def dot(a, b):
    return jnp.dot(a, b, preferred_element_type=F32)


def dot_t(a, b):
    return lax.dot_general(a, b, (((1,), (1,)), ((), ())), preferred_element_type=F32)


def t_dot(a, b):
    return lax.dot_general(a, b, (((0,), (0,)), ((), ())), preferred_element_type=F32)


def call(kernel, outs, ins, scratch=(), after=(), flops=0, bytes_accessed=0):
    n_in, n_after = len(ins), len(after)

    def run(*refs):
        kernel(*refs[:n_in], *refs[n_in + n_after :])

    return pl.pallas_call(
        run,
        out_shape=[jax.ShapeDtypeStruct(s, t) for s, t, _ in outs],
        in_specs=[s for _, s in ins] + [HB] * n_after,
        out_specs=[s for _, _, s in outs],
        scratch_shapes=list(scratch),
        compiler_params=pltpu.CompilerParams(vmem_limit_bytes=50 * 2**20),
        cost_estimate=pl.CostEstimate(
            flops=flops, bytes_accessed=bytes_accessed, transcendentals=0
        ),
    )(*[a for a, _ in ins], *after)


def norm_parts(x):
    mean = jnp.mean(x, -1, keepdims=True)
    centre = x - mean
    scale = lax.rsqrt(jnp.mean(centre * centre, -1, keepdims=True) + 1e-06)
    return centre * scale, scale


def layer_norm(x, gain):
    return (norm_parts(x)[0] * gain).astype(BF)


def norm_back(x, gain, slope):
    unit, scale = norm_parts(x)
    terms = slope * unit
    inner = slope * gain
    inner = inner - jnp.mean(inner, -1, keepdims=True) - unit * jnp.mean(inner * unit, -1, keepdims=True)
    return inner * scale, terms


def gelu_both(h):
    k = 0.7978845608028654
    t = jnp.tanh(k * (h + 0.044715 * h * h * h))
    half = 0.5 * (1 + t)
    return h * half, half + 0.5 * h * (1 - t * t) * (k + (3 * 0.044715 * k) * h * h)


def add_both(mine, got, rows):
    return mine + jnp.concatenate([got[rows:], got[:rows]], 0).astype(F32)


def pair_masks():
    lane = lax.broadcasted_iota(jnp.int32, (1, 2 * HEAD_DIM), 1)
    return [(lane < HEAD_DIM).astype(BF), (lane >= HEAD_DIM).astype(BF)]


def key_mask(blk, rows, blk_len, longest):
    pos = lax.broadcasted_iota(jnp.int32, (rows, 1), 0)
    parts = []
    for j in range(4):
        last = jnp.where((blk ^ j) < longest, blk_len, blk_len - 1)
        parts.append(pos < last)
    return jnp.concatenate([jnp.where(p, 1.0, 0.0) for p in parts], 0) > 0.5


def attend_core(where, q, kv_own, kv_far, wp, rows, blk_len, longest, solo, far=None, after=()):
    half = q.shape[1]
    feat = wp.shape[1]
    pairs = half // (2 * HEAD_DIM)
    r2 = 2 * rows

    def kernel(where_ref, q_ref, ko_ref, *refs):
        refs = list(refs)
        take = lambda n: [refs.pop(0) for _ in range(n)]
        given = take(1 if far is None else 3)
        wp_ref, part_ref, low_ref, blend_ref, lse_ref = take(5)
        if far is None:
            kf_ref = given[0]
        else:
            (kf_ref,) = take(1)
            for j in range(2):
                kf_ref[pl.ds(j * rows, rows), :] = dot(given[j][...], given[2][:, half:]).astype(BF)
        ok = key_mask(where_ref[0], rows, blk_len, longest)
        masks = pair_masks()
        for p in range(pairs):
            at, vat = pl.ds(p * 128, 128), pl.ds(half + p * 128, 128)
            k = jnp.concatenate([ko_ref[:, at], kf_ref[:, at]], 0)
            v = jnp.concatenate([ko_ref[:, vat], kf_ref[:, vat]], 0)
            qp = q_ref[:, at]
            acc = None
            for h in range(2):
                s = dot_t(k, qp * masks[h]) * 0.125
                s = jnp.where(ok, s, -1e9)
                top = jnp.max(s, 0, keepdims=True)
                ex = jnp.exp(s - top)
                total = jnp.sum(ex, 0, keepdims=True)
                lse_ref[pl.ds(2 * p + h, 1), :] = top + jnp.log(total)
                shares = (ex * (1.0 / total)).astype(BF)
                out = t_dot(v * masks[h], shares)
                acc = out if acc is None else acc + out
            blend_ref[at, :] = acc.astype(BF)
        part = t_dot(blend_ref[...], wp_ref[...])
        part_ref[...] = part
        low_ref[...] = (part[rows:] if solo else part).astype(BF)

    outs = [
        ((r2, feat), F32, VM), ((rows if solo else r2, feat), BF, VM), ((half, r2), BF, VM), ((8, r2), F32, VM),
    ]
    ins = [(where, SM), (q, VM), (kv_own, VM)]
    if far is None:
        ins.append((kv_far, VM))
    else:
        ins += [(t, VM) for t in far]
        outs.append(((r2, feat), BF, VM))
    return call(
        kernel,
        outs,
        ins + [(wp, VM)],
        after=after,
        flops=2 * r2 * half * (8 * rows + feat),
        bytes_accessed=4 * 2**20,
    )


def attend_core_back(where, u_low, wp, blend, q, kv_own, kv_far, lse, rows, blk_len, longest, after=()):
    half = q.shape[1]
    feat = wp.shape[1]
    pairs = half // (2 * HEAD_DIM)
    r2 = 2 * rows

    def kernel(
        where_ref, u_ref, wp_ref, blend_ref, q_ref, ko_ref, kf_ref, lse_ref,
        dq_ref, own_ref, far_ref, wps_ref, bt_ref, dqt_ref,
    ):
        ok = key_mask(where_ref[0], rows, blk_len, longest)
        masks = pair_masks()
        sub = lax.broadcasted_iota(jnp.int32, (2 * HEAD_DIM, 1), 0)
        row_masks = [(sub < HEAD_DIM).astype(BF), (sub >= HEAD_DIM).astype(BF)]
        u = u_ref[...]
        bt_ref[...] = dot_t(wp_ref[...], u).astype(BF)
        for p in range(pairs):
            at, vat = pl.ds(p * 128, 128), pl.ds(half + p * 128, 128)
            k = jnp.concatenate([ko_ref[:, at], kf_ref[:, at]], 0)
            v = jnp.concatenate([ko_ref[:, vat], kf_ref[:, vat]], 0)
            qp = q_ref[:, at]
            bt = bt_ref[at, :]
            dqt = dk = dv = 0.0
            for h in range(2):
                qm = qp * masks[h]
                s = dot_t(k, qm) * 0.125
                shares = jnp.where(ok, jnp.exp(s - lse_ref[pl.ds(2 * p + h, 1), :]), 0.0)
                slope = dot(v * masks[h], bt)
                t = shares * slope
                ss = (t - shares * jnp.sum(t, 0, keepdims=True)).astype(BF)
                dqt += t_dot(k * masks[h], ss)
                dk += dot(ss, qm)
                dv += dot_t(shares.astype(BF), bt * row_masks[h])
            dqt_ref[at, :] = dqt * 0.125
            dk = dk * 0.125
            own_ref[:, at] = dk[:r2]
            own_ref[:, vat] = dv[:r2]
            far_ref[:, at] = dk[r2:].astype(BF)
            far_ref[:, vat] = dv[r2:].astype(BF)
        dq_ref[...] = dqt_ref[...].T.astype(BF)
        wps_ref[...] = dot(blend_ref[...], u).astype(BF)

    return call(
        kernel,
        [
            ((r2, half), BF, VM), ((r2, 2 * half), F32, VM), ((r2, 2 * half), BF, VM),
            ((half, feat), BF, VM),
        ],
        [
            (where, SM), (u_low, VM), (wp, VM), (blend, VM), (q, VM), (kv_own, VM), (kv_far, VM),
            (lse, VM),
        ],
        scratch=[pltpu.VMEM((half, r2), BF), pltpu.VMEM((half, r2), F32)],
        after=after,
        flops=2 * r2 * half * (20 * rows + 2 * feat),
        bytes_accessed=6 * 2**20,
    )


def start_all(copies):
    for c in copies:
        c.start()


def wait_all(copies):
    for c in copies:
        c.wait()


def attend_copies(e, refs, w_ref, p_ref, small_ref, sems):
    copies = []

    def add(src, dst):
        copies.append(pltpu.make_async_copy(src, dst, sems.at[len(copies)]))

    n = w_ref.shape[0] // 4
    half = p_ref.shape[0]
    m = half // 4
    for j in range(4):
        to = e ^ j
        rows, prows = pl.ds(pl.multiple_of(to * n, 16), n), pl.ds(pl.multiple_of(to * m, 16), m)
        a, b, at = (refs[j], refs[j], 2 * n) if j < 3 else (refs[3], refs[4], 0)
        for g in range(2):
            add(a.at[pl.ds(g * n, n)], w_ref.at[rows, pl.ds(g * half, half)])
        add(b.at[pl.ds(at, n)], w_ref.at[rows, pl.ds(2 * half, half)])
        add(b.at[pl.ds(at + n, m)], p_ref.at[prows, pl.ds(0, half)])
        add(b.at[pl.ds(at + n + m, m)], p_ref.at[prows, pl.ds(half, half)])
        if small_ref is not None:
            for g in range(3):
                srows = pl.ds(pl.multiple_of(to * n + g * (n // 3), 16), n // 3)
                add(b.at[pl.ds(at + n + 2 * m, n // 3), pl.ds(128 * g, 128)], small_ref.at[srows])
    return copies


def attend_first(where, tokens, small_rows, blocks, rows, after=()):
    blk_len, feat = tokens[0].shape
    half = feat // 2
    r2 = 2 * rows

    def kernel(where_ref, *refs):
        refs = list(refs)
        take = lambda n: [refs.pop(0) for _ in range(n)]
        tok, block_refs = take(4), take(5)
        x_ref, normed_ref, q_ref, kv_ref, far_ref, w_ref, p_ref, small_ref, rows_ref, all_ref, sems = take(11)
        copies = attend_copies(where_ref[1], block_refs, w_ref, p_ref, small_ref, sems)
        start_all(copies)
        all_ref[...] = jnp.zeros_like(all_ref)
        for j in range(4):
            all_ref[pl.ds(j * rows, blk_len), :] = tok[j][...].astype(F32)
        x = all_ref[...]
        x_ref[...] = x[:r2]
        unit = norm_parts(x)[0]
        wait_all(copies)
        turned = small_ref[...].astype(F32).T
        rows_ref[...] = turned[: rows_ref.shape[0]]
        normed = (unit * turned[0:1]).astype(BF)
        normed_ref[...] = normed[:r2]
        q_ref[...] = dot(normed[:r2], w_ref[:, :half]).astype(BF)
        kv = dot(normed, w_ref[:, half:]).astype(BF)
        kv_ref[...] = kv[:r2]
        far_ref[...] = kv[r2:]

    return call(
        kernel,
        [
            ((r2, feat), F32, VM), ((r2, feat), BF, VM), ((r2, half), BF, VM), ((r2, feat), BF, VM),
            ((r2, feat), BF, VM), ((feat, 3 * half), BF, VM), ((half, feat), BF, VM),
            ((feat, 128), BF, VM), ((small_rows, feat), F32, VM),
        ],
        [(where, SM)] + [(t, VM) for t in tokens] + [(t, HB) for t in blocks],
        scratch=[pltpu.VMEM((2 * r2, feat), F32), pltpu.SemaphoreType.DMA((32,))],
        after=after,
        flops=2 * r2 * feat * 5 * half,
        bytes_accessed=6 * 2**20,
    )


def norm_next(x, part, got, gains, gain_row, rows, after=()):
    r2, feat = x.shape

    def kernel(x_ref, part_ref, got_ref, gains_ref, x2_ref, normed_ref, own_ref):
        x2 = add_both(x_ref[...] + part_ref[...], got_ref[...], rows)
        x2_ref[...] = x2
        normed = layer_norm(x2, gains_ref[pl.ds(gain_row, 1), :])
        normed_ref[...] = normed
        own_ref[...] = normed[:rows]

    return call(
        kernel,
        [((r2, feat), F32, VM), ((r2, feat), BF, VM), ((rows, feat), BF, VM)],
        [(x, VM), (part, VM), (got, VM), (gains, VM)],
        after=after,
        bytes_accessed=5 * 2**20,
    )


def attend_next(where, normed, blocks, after=()):
    r2, feat = normed.shape
    half = feat // 2

    def kernel(where_ref, normed_ref, *refs):
        refs = list(refs)
        take = lambda n: [refs.pop(0) for _ in range(n)]
        block_refs = take(5)
        q_ref, kv_ref, w_ref, p_ref, sems = take(5)
        copies = attend_copies(where_ref[1], block_refs, w_ref, p_ref, None, sems)
        start_all(copies)
        wait_all(copies)
        normed = normed_ref[...]
        q_ref[...] = dot(normed, w_ref[:, :half]).astype(BF)
        kv_ref[...] = dot(normed, w_ref[:, half:]).astype(BF)

    return call(
        kernel,
        [
            ((r2, half), BF, VM), ((r2, feat), BF, VM), ((feat, 3 * half), BF, VM), ((half, feat), BF, VM),
        ],
        [(where, SM), (normed, VM)] + [(t, HB) for t in blocks],
        scratch=[pltpu.SemaphoreType.DMA((20,))],
        after=after,
        flops=2 * r2 * feat * 3 * half,
        bytes_accessed=5 * 2**20,
    )


def widen_forward(where, x, part, got, gains, blocks, rows, after=()):
    r2, feat = x.shape
    wide = 2 * feat
    tile = 384

    def kernel(
        where_ref, x_ref, part_ref, got_ref, gains_ref, z0, z1, z2, a3, b3,
        x1_ref, normed_ref, hidden_ref, out_ref, low_ref, wi_ref, wo_ref, sems,
    ):
        n = feat // 4
        copies = []
        for h, last in enumerate((a3, b3)):
            pairs = [z0.at[h], z1.at[h], z2.at[h], last]
            for j in range(4):
                at = (where_ref[1] ^ j) * n
                for src, dst in (
                    (pairs[j].at[0], wi_ref.at[pl.ds(pl.multiple_of(at, 16), n), pl.ds(h * feat, feat)]),
                    (pairs[j].at[1], wo_ref.at[pl.ds(pl.multiple_of(at + h * feat, 16), n)]),
                ):
                    copies.append(pltpu.make_async_copy(src, dst, sems.at[len(copies)]))
        start_all(copies)
        x1 = add_both(x_ref[...] + part_ref[...], got_ref[...], rows)
        x1_ref[...] = x1
        normed_ref[...] = layer_norm(x1, gains_ref[pl.ds(1, 1), :])
        wait_all(copies)
        out_ref[...] = jnp.zeros_like(out_ref)

        @pl.loop(0, wide // tile)
        def _(t):
            at = pl.ds(pl.multiple_of(t * tile, 128), tile)
            h = dot(normed_ref[...], wi_ref[:, at])
            hidden_ref[:, at] = h
            out_ref[...] += dot(gelu_both(h)[0].astype(BF), wo_ref[at, :])

        low_ref[...] = out_ref[...].astype(BF)

    return call(
        kernel,
        [
            ((r2, feat), F32, VM), ((r2, feat), BF, VM), ((r2, wide), F32, VM), ((r2, feat), F32, VM),
            ((r2, feat), BF, VM), ((feat, wide), BF, VM), ((wide, feat), BF, VM),
        ],
        [(where, SM), (x, VM), (part, VM), (got, VM), (gains, VM)] + [(t, HB) for t in blocks],
        scratch=[pltpu.SemaphoreType.DMA((16,))],
        after=after,
        flops=4 * r2 * feat * wide,
        bytes_accessed=16 * 2**20,
    )


def widen_back(where, u, x, gains, part, got, normed, hidden, wi, wo, first, rows, columns, after=()):
    r2, feat = u.shape
    wide = 2 * feat
    tile = 384
    n = feat // 4

    def kernel(
        where_ref, u_ref, x_ref, gains_ref, part_ref, got_ref, normed_ref, hidden_ref, wi_ref, wo_ref,
        u2_ref, out_ref, low_ref, *more,
    ):
        outs, (ulow_ref, turned_ref, wis_ref, wos_ref, sems) = more[:-5], more[-5:]
        slope = add_both(part_ref[...], got_ref[...], rows)
        u2 = u_ref[...] + norm_back(x_ref[...], gains_ref[pl.ds(2, 1), :], slope)[0]
        u2_ref[...] = u2
        ulow_ref[...] = u2.astype(BF)
        turned_ref[...] = normed_ref[...].T
        out_ref[...] = jnp.zeros_like(out_ref)

        @pl.loop(0, wide // tile)
        def _(t):
            at = pl.ds(pl.multiple_of(t * tile, 128), tile)
            ulow = ulow_ref[...]
            act, dact = gelu_both(hidden_ref[:, at])
            hs = (dact * dot_t(ulow, wo_ref[at, :])).astype(BF)
            wos_ref[at, :] = t_dot(act.astype(BF), ulow).astype(BF)
            wis_ref[:, at] = dot(turned_ref[...], hs).astype(BF)
            out_ref[...] += dot_t(hs, wi_ref[:, at])

        copies = []
        slots = (0, 3 - first, first, 3)

        def add(h, at, size, dst):
            wide_at = pl.ds(pl.multiple_of(at, 16), size)
            deep_at = pl.ds(pl.multiple_of(at + h * feat, 16), size)
            for i, src in enumerate((wis_ref.at[wide_at, pl.ds(h * feat, feat)], wos_ref.at[deep_at])):
                copies.append(pltpu.make_async_copy(src, dst.at[i], sems.at[len(copies)]))

        for i, j in enumerate(slots):
            to = (where_ref[1] ^ j) * n
            add(0, to, n, outs[i // 2].at[i % 2])
            if columns:
                for c in range(4):
                    add(1, to + c * (n // 4), n // 4, outs[2].at[c, i])
            else:
                add(1, to, n, outs[2 + i // 2].at[i % 2])
        start_all(copies)
        low_ref[...] = out_ref[...].astype(BF)
        wait_all(copies)

    block = ((2, 2, n, feat), BF, HB)
    more = [((4, 4, 2, n // 4, feat), BF, HB)] if columns else [block] * 2
    return call(
        kernel,
        [((r2, feat), F32, VM), ((r2, feat), F32, VM), ((r2, feat), BF, VM)] + [block] * 2 + more,
        [
            (where, SM), (u, VM), (x, VM), (gains, VM), (part, VM), (got, VM), (normed, VM),
            (hidden, VM), (wi, VM), (wo, VM),
        ],
        scratch=[
            pltpu.VMEM((r2, feat), BF), pltpu.VMEM((feat, r2), BF), pltpu.VMEM((feat, wide), BF),
            pltpu.VMEM((wide, feat), BF), pltpu.SemaphoreType.DMA((40,)),
        ],
        after=after,
        flops=10 * r2 * feat * wide,
        bytes_accessed=24 * 2**20,
    )


def attend_proj_back(where, dq, own, got, normed, w, wps, small, first, rows, last, after=()):
    r2, feat = normed.shape
    half = feat // 2
    n, m = feat // 4, half // 4
    tile = 384
    extra = 0 if small is None else n // 3

    def kernel(where_ref, dq_ref, own_ref, got_ref, normed_ref, w_ref, wps_ref, *refs):
        refs = list(refs)
        take = lambda k: [refs.pop(0) for _ in range(k)]
        small_ref = take(1)[0] if extra else None
        out_ref, low_ref, keep_ref, send_ref, packed_ref, turned_ref, ws_ref, sm_ref, sems = take(9)
        packed_ref[:, :half] = dq_ref[...]
        packed_ref[:, half:] = (own_ref[...] + got_ref[...].astype(F32)).astype(BF)
        out = dot_t(packed_ref[...], w_ref[...])
        out_ref[...] = out[: out_ref.shape[0]]
        low_ref[...] = (out[rows:] if last else out).astype(BF)
        turned_ref[...] = normed_ref[...].T

        @pl.loop(0, 3 * half // tile)
        def _(t):
            at = pl.ds(pl.multiple_of(t * tile, 128), tile)
            ws_ref[:, at] = dot(turned_ref[...], packed_ref[:, at]).astype(BF)

        if extra:
            wide = jnp.concatenate(
                [small_ref[...], jnp.zeros((128 - small_ref.shape[0], feat), F32)], 0
            )
            sm_ref[...] = wide.T.astype(BF)
        copies = []

        def add(src, dst):
            copies.append(pltpu.make_async_copy(src, dst, sems.at[len(copies)]))

        for ref, js in ((keep_ref, (0, 3 - first)), (send_ref, (first, 3))):
            for i, j in enumerate(js):
                to = where_ref[1] ^ j
                at, pat = pl.ds(pl.multiple_of(to * n, 16), n), pl.ds(pl.multiple_of(to * m, 16), m)
                for g in range(3):
                    add(ws_ref.at[at, pl.ds(g * half, half)], ref.at[i, pl.ds(g * n, n)])
                for g in range(2):
                    add(wps_ref.at[pat, pl.ds(g * half, half)], ref.at[i, pl.ds(3 * n + g * m, m)])
                if extra:
                    for g in range(3):
                        sat = pl.ds(pl.multiple_of(to * n + g * extra, 16), extra)
                        add(sm_ref.at[sat], ref.at[i, pl.ds(3 * n + 2 * m, extra), pl.ds(128 * g, 128)])
        start_all(copies)
        wait_all(copies)

    n_out = rows if last else r2
    block = ((2, 3 * n + 2 * m + extra, half), BF, HB)
    return call(
        kernel,
        [((n_out, feat), F32, VM), ((n_out, feat), BF, VM), block, block],
        [(where, SM), (dq, VM), (own, VM), (got, VM), (normed, VM), (w, VM), (wps, VM)]
        + ([(small, VM)] if extra else []),
        scratch=[
            pltpu.VMEM((r2, 3 * half), BF), pltpu.VMEM((feat, r2), BF), pltpu.VMEM((feat, 3 * half), BF),
            pltpu.VMEM((feat, 128), BF), pltpu.SemaphoreType.DMA((32,)),
        ],
        after=after,
        flops=4 * r2 * feat * 3 * half,
        bytes_accessed=10 * 2**20,
    )


def join_upstream(u_own, u_sib, rows):
    feat = u_own.shape[1]

    def kernel(o_ref, s_ref, u_ref, low_ref):
        u_ref[pl.ds(0, rows), :] = o_ref[...]
        u_ref[pl.ds(rows, rows), :] = s_ref[...].astype(F32)
        low_ref[pl.ds(0, rows), :] = o_ref[...].astype(BF)
        low_ref[pl.ds(rows, rows), :] = s_ref[...]

    return call(
        kernel, [((2 * rows, feat), F32, VM), ((2 * rows, feat), BF, VM)], [(u_own, VM), (u_sib, VM)],
        bytes_accessed=2**21,
    )


def norm_step(u, x, gains, gain_row, part, got, rows, last, after=()):
    feat = x.shape[1]
    n = rows if last else 2 * rows

    def kernel(u_ref, x_ref, gains_ref, part_ref, got_ref, *outs):
        if last:
            slope = part_ref[...] + got_ref[...].astype(F32)
        else:
            slope = add_both(part_ref[...], got_ref[...], rows)
        u2 = u_ref[:n] + norm_back(x_ref[:n], gains_ref[pl.ds(gain_row, 1), :], slope)[0]
        low = outs[-1]
        low[...] = u2[: low.shape[0]].astype(BF)
        if not last:
            outs[0][...] = u2

    outs = [((last if last else n, feat), BF, VM)]
    return call(
        kernel,
        outs if last else [((n, feat), F32, VM)] + outs,
        [(u, VM), (x, VM), (gains, VM), (part, VM), (got, VM)],
        after=after,
        bytes_accessed=6 * 2**20,
    )


def picks(index, turn, cap, cap_rows, experts):
    at = lax.broadcasted_iota(jnp.int32, (1, experts * cap_rows), 1)
    out = []
    for k in range(TOP):
        chosen, slot = index[:, k : k + 1], index[:, TOP + k : TOP + k + 1]
        place = chosen if turn is None else chosen ^ turn
        target = jnp.where(slot < cap, place * cap_rows + slot, -1)
        out.append(jnp.where(at == target, 1.0, 0.0).astype(BF))
    return out


def lane_at(index, k):
    lane = lax.broadcasted_iota(jnp.int32, (1, 128), 1)
    return jnp.where(lane == index[:, k : k + 1] + 4, 1.0, 0.0)


def present_mask(blk, rows, blk_len, longest):
    pos = lax.broadcasted_iota(jnp.int32, (rows, 1), 0)
    last = jnp.where(blk < longest, blk_len, blk_len - 1)
    return jnp.where(pos < last, 1.0, 0.0)


def route(where, x, part, got, gains, small, cot, index, experts, cap, rows, blk_len, longest, fast, after=()):
    feat = x.shape[1]
    cap_rows = up16(cap)

    def kernel(where_ref, x_ref, part_ref, got_ref, gains_ref, small_ref, cot_ref, index_ref,
               x3_ref, moe_ref, gates_ref, up_ref, *blocks):
        x3 = x_ref[:rows] + part_ref[:rows] + got_ref[...].astype(F32)
        x3_ref[...] = x3
        moe = layer_norm(x3, gains_ref[pl.ds(3, 1), :])
        moe_ref[...] = moe
        lane = lax.broadcasted_iota(jnp.int32, (1, 128), 1)
        logits = dot(moe, small_ref[...])
        logits = jnp.where((lane >= 4) & (lane < 4 + experts), logits, -1e30)
        ex = jnp.exp(logits - jnp.max(logits, -1, keepdims=True))
        gates = ex / jnp.sum(ex, -1, keepdims=True)
        gates_ref[...] = gates
        up_ref[...] = jnp.zeros_like(up_ref)
        up_ref[pl.ds(0, blk_len), :] = cot_ref[...].astype(F32)
        up = up_ref[...] * present_mask(where_ref[0], rows, blk_len, longest)
        up_ref[...] = up
        index = index_ref[...]
        pick = picks(index, where_ref[1] if fast else None, cap, cap_rows, experts)
        sent = t_dot(pick[0] + pick[1], moe).astype(BF)
        slope = 0.0
        for k in range(TOP):
            gate = jnp.sum(gates * lane_at(index, k), -1, keepdims=True)
            slope += t_dot(pick[k], (gate * up).astype(BF))
        slope = slope.astype(BF)
        for j, ref in enumerate(blocks):
            ref[pl.ds(0, cap_rows), :] = sent[j * cap_rows : (j + 1) * cap_rows]
            ref[pl.ds(cap_rows, cap_rows), :] = slope[j * cap_rows : (j + 1) * cap_rows]

    return call(
        kernel,
        [((rows, feat), F32, VM), ((rows, feat), BF, VM), ((rows, 128), F32, VM), ((rows, feat), F32, VM)]
        + [((2 * cap_rows, feat), BF, VM)] * experts,
        [(where, SM), (x, VM), (part, VM), (got, VM), (gains, VM), (small, VM), (cot, VM), (index, VM)],
        after=after,
        flops=6 * rows * experts * cap_rows * feat,
        bytes_accessed=5 * 2**20,
    )


def expert_half(blocks, w_in, w_out, acc, cap_rows, after=()):
    feat = w_in.shape[0]
    wide = w_in.shape[1]
    tile = 512 if wide % 512 == 0 else wide
    n = len(blocks) * cap_rows
    steps = wide // tile
    final = acc is not None

    def kernel(*refs):
        refs = list(refs)
        take = lambda k: [refs.pop(0) for _ in range(k)]
        ins = take(len(blocks))
        wi_ref, wo_ref = take(2)
        before = take(2) if final else None
        take(len(after))
        outs = take(len(blocks)) if final else take(2)
        rows_ref, slope_ref, res_ref, back_ref = take(4)
        t = pl.program_id(0)

        @pl.when(t == 0)
        def _():
            for j, ref in enumerate(ins):
                at = pl.ds(j * cap_rows, cap_rows)
                rows_ref[at, :] = ref[pl.ds(0, cap_rows), :]
                slope_ref[at, :] = ref[pl.ds(cap_rows, cap_rows), :]
            if final:
                res_ref[...] = before[0][...]
                back_ref[...] = before[1][...]
            else:
                res_ref[...] = jnp.zeros_like(res_ref)
                back_ref[...] = jnp.zeros_like(back_ref)

        act, dact = gelu_both(dot(rows_ref[...], wi_ref[...]))
        hs = (dact * dot_t(slope_ref[...], wo_ref[...])).astype(BF)
        res_ref[...] += dot(act.astype(BF), wo_ref[...])
        back_ref[...] += dot_t(hs, wi_ref[...])

        @pl.when(t == steps - 1)
        def _():
            if final:
                for j, ref in enumerate(outs):
                    at = pl.ds(j * cap_rows, cap_rows)
                    ref[pl.ds(0, cap_rows), :] = res_ref[at, :].astype(BF)
                    ref[pl.ds(cap_rows, cap_rows), :] = back_ref[at, :].astype(BF)
            else:
                outs[0][...] = res_ref[...]
                outs[1][...] = back_ref[...]

    whole = lambda shape: pl.BlockSpec(shape, lambda t: (0,) * len(shape))
    blk = (2 * cap_rows, feat)
    ins = [*blocks, w_in, w_out] + (list(acc) if final else []) + list(after)
    in_specs = [whole(blk)] * len(blocks) + [
        pl.BlockSpec((feat, tile), lambda t: (0, t)), pl.BlockSpec((tile, feat), lambda t: (t, 0))
    ]
    in_specs += [whole((n, feat))] * (2 if final else 0) + [HB] * len(after)
    if final:
        shapes, specs = [jax.ShapeDtypeStruct(blk, BF)] * len(blocks), [whole(blk)] * len(blocks)
    else:
        shapes, specs = [jax.ShapeDtypeStruct((n, feat), F32)] * 2, [whole((n, feat))] * 2
    return pl.pallas_call(
        kernel,
        grid=(steps,),
        out_shape=shapes,
        in_specs=in_specs,
        out_specs=specs,
        scratch_shapes=[
            pltpu.VMEM((n, feat), BF), pltpu.VMEM((n, feat), BF),
            pltpu.VMEM((n, feat), F32), pltpu.VMEM((n, feat), F32),
        ],
        compiler_params=pltpu.CompilerParams(
            vmem_limit_bytes=50 * 2**20, dimension_semantics=("arbitrary",)
        ),
        cost_estimate=pl.CostEstimate(
            flops=8 * n * feat * wide, bytes_accessed=10 * 2**20, transcendentals=0
        ),
    )(*ins)


def expert_slopes(every, w_in, w_out, got, after=()):
    feat, wide = w_in.shape
    tile = 256 if wide % 256 == 0 else wide
    steps = wide // tile
    groups, experts, cap_rows = every.shape[0], every.shape[1], every.shape[2] // 2
    total = groups * experts * cap_rows
    kind = BF if got is None else F32

    def kernel(*refs):
        refs = list(refs)
        take = lambda k: [refs.pop(0) for _ in range(k)]
        every_ref, wi_ref, wo_ref = take(3)
        got_refs = take(2) if got is not None else None
        take(len(after))
        wis_ref, wos_ref, rows_ref, slope_ref, turned_ref, sems = take(6)

        @pl.when(pl.program_id(0) == 0)
        def _():
            copies = []
            for k in range(groups):
                for j in range(experts):
                    at = pl.ds((k * experts + j) * cap_rows, cap_rows)
                    for i, ref in enumerate((rows_ref, slope_ref)):
                        copies.append(pltpu.make_async_copy(
                            every_ref.at[k, j, pl.ds(i * cap_rows, cap_rows)], ref.at[at],
                            sems.at[len(copies)],
                        ))
            start_all(copies)
            wait_all(copies)
            turned_ref[...] = rows_ref[...].T

        act, dact = gelu_both(dot(rows_ref[...], wi_ref[...]))
        hs = (dact * dot_t(slope_ref[...], wo_ref[...])).astype(BF)
        wis = dot(turned_ref[...], hs)
        wos = t_dot(act.astype(BF), slope_ref[...])
        if got is not None:
            wis, wos = wis + got_refs[0][...].astype(F32), wos + got_refs[1][...].astype(F32)
        wis_ref[...] = wis.astype(kind)
        wos_ref[...] = wos.astype(kind)

    wi_spec = pl.BlockSpec((feat, tile), lambda t: (0, t))
    wo_spec = pl.BlockSpec((tile, feat), lambda t: (t, 0))
    return pl.pallas_call(
        kernel,
        grid=(steps,),
        out_shape=[jax.ShapeDtypeStruct((feat, wide), kind), jax.ShapeDtypeStruct((wide, feat), kind)],
        in_specs=[HB] + [wi_spec, wo_spec] * (1 if got is None else 2) + [HB] * len(after),
        out_specs=[wi_spec, wo_spec],
        scratch_shapes=[
            pltpu.VMEM((total, feat), BF), pltpu.VMEM((total, feat), BF), pltpu.VMEM((feat, total), BF),
            pltpu.SemaphoreType.DMA((2 * groups * experts,)),
        ],
        compiler_params=pltpu.CompilerParams(
            vmem_limit_bytes=56 * 2**20, dimension_semantics=("arbitrary",)
        ),
        cost_estimate=pl.CostEstimate(
            flops=8 * total * feat * wide, bytes_accessed=20 * 2**20, transcendentals=0
        ),
    )(every, w_in, w_out, *(got or ()), *after)


def combine(where, blocks, x3, moe, gates, up, index, small, gains, small_rows, experts, cap, rows, blk_len, longest, fast, after=()):
    feat = x3.shape[1]
    cap_rows = up16(cap)
    n = experts * cap_rows

    def kernel(where_ref, *refs):
        refs = list(refs)
        take = lambda k: [refs.pop(0) for _ in range(k)]
        ins = take(experts)
        x3_ref, moe_ref, gates_ref, up_ref, index_ref, small_ref, gains_ref = take(7)
        acts_ref, u_ref, low_ref, slopes_ref, result_ref, back_ref = take(6)
        for j, ref in enumerate(ins):
            at = pl.ds(j * cap_rows, cap_rows)
            result_ref[at, :] = ref[pl.ds(0, cap_rows), :]
            back_ref[at, :] = ref[pl.ds(cap_rows, cap_rows), :]
        index, gates, up, moe = index_ref[...], gates_ref[...], up_ref[...], moe_ref[...]
        pick = picks(index, where_ref[1] if fast else None, cap, cap_rows, experts)
        x3 = x3_ref[...]
        acts, all_slope = x3, 0.0
        for k in range(TOP):
            at_k = lane_at(index, k)
            gate = jnp.sum(gates * at_k, -1, keepdims=True)
            picked = dot(pick[k], result_ref[...])
            acts = acts + gate * picked
            all_slope += jnp.sum(up * picked, -1, keepdims=True) * at_k
        acts = acts * present_mask(where_ref[0], rows, blk_len, longest)
        acts_ref[...] = acts[:blk_len].astype(BF)
        logit = (gates * (all_slope - jnp.sum(gates * all_slope, -1, keepdims=True))).astype(BF)
        slope = dot(pick[0] + pick[1], back_ref[...]) + dot_t(logit, small_ref[...])
        dx, terms = norm_back(x3, gains_ref[pl.ds(3, 1), :], slope)
        u = up + dx
        u_ref[...] = u
        low_ref[...] = u.astype(BF)
        slopes_ref[...] = t_dot(logit, moe)[:small_rows]
        slopes_ref[pl.ds(3, 1), :] = jnp.sum(terms, 0, keepdims=True)

    return call(
        kernel,
        [((blk_len, feat), BF, VM), ((rows, feat), F32, VM), ((rows, feat), BF, VM), ((small_rows, feat), F32, VM)],
        [(where, SM)] + [(b, VM) for b in blocks]
        + [(t, VM) for t in (x3, moe, gates, up, index, small, gains)],
        scratch=[pltpu.VMEM((n, feat), BF), pltpu.VMEM((n, feat), BF)],
        after=after,
        flops=6 * rows * n * feat,
        bytes_accessed=5 * 2**20,
    )


def tie(xs, *after):
    return list(lax.optimization_barrier((*xs, *after)))[: len(xs)]


class Links:
    def __init__(self, mesh):
        self.E = mesh.shape["expert"]
        self.C = mesh.shape["context"]
        self.D = mesh.shape["dp"]
        assert self.C == 4 and self.D == 2 and self.E % 2 == 0
        self.fast = self.E == 4
        self.chips = self.E * self.C
        flat = lambda e, c, d: (e * self.C + c) * self.D + d
        self.team = [
            (flat(e, c, d), flat((e // 2) * 2 + c // 2, 2 * (e % 2) + d, c % 2))
            for e in range(self.E)
            for c in range(self.C)
            for d in range(self.D)
        ]
        self.to_lane = [(f, (f % self.chips) * 2 + f // self.chips) for f in range(2 * self.chips)]
        self.from_lane = [(b, a) for a, b in self.to_lane]

    def move(self, x):
        return lax.ppermute(x, ALL, self.team)

    def xor(self, x, axis, j):
        n = {"expert": self.E, "context": self.C, "dp": self.D}[axis]
        return lax.ppermute(x, axis, [(i, i ^ j) for i in range(n)])

    def sib(self, x):
        return self.xor(x, "dp", 1)

    def partner(self, x):
        return self.xor(x, "expert", 1)

    def column(self, x, *hold):
        c = lax.axis_index("context")
        got = tie([x] + [self.xor(x, "context", j) for j in range(1, 4)], *hold)
        pick = lambda k: jnp.where(
            c & 2 == 0, jnp.where(c & 1 == 0, got[k], got[k ^ 1]), jnp.where(c & 1 == 0, got[k ^ 2], got[k ^ 3])
        )
        return jnp.stack([pick(k) for k in range(4)])

    def plane_sum(self, keep, send, first, hold):
        (got,) = tie([self.xor(send, "expert", first)], *hold[0])
        got = got.astype(F32)
        give = (keep[1].astype(F32) + got[1]).astype(BF)
        (far,) = tie([self.xor(give, "expert", 3 - first)], *hold[1])
        return keep[0].astype(F32) + got[0] + far.astype(F32), give

    def column_sum(self, x, *hold):
        c = lax.axis_index("context")
        low = x.astype(BF)
        got = [self.xor(lax.dynamic_index_in_dim(low, c ^ j, 0, False), "context", j) for j in range(1, 4)]
        got = tie(got, *hold)
        total = lax.dynamic_index_in_dim(x, c, 0, False)
        for t in got:
            total = total + t.astype(F32)
        return total

    def swap_blocks(self, x):
        if not self.fast:
            return list(lax.all_to_all(jnp.stack(x), "expert", 0, 0, tiled=True))
        return [x[0]] + [self.xor(x[j], "expert", j) for j in range(1, 4)]


def lane_rows(links, mine, d):
    keep = lax.dynamic_index_in_dim(mine, d, 0, False)
    got = links.sib(lax.dynamic_index_in_dim(mine, 1 - d, 0, False))
    return jnp.where(d == 0, jnp.concatenate([keep, got], 0), jnp.concatenate([got, keep], 0))


def in_order(d, own, other):
    return jnp.where(d == 0, jnp.stack([own, other]), jnp.stack([other, own]))


class Weights:
    def __init__(self, links, rdev, feat, ff):
        self.links, self.rdev, self.feat, self.ff = links, rdev, feat, ff
        self.d = lax.axis_index("dp")
        self.given = []
        self.half = feat // 2

    def split_attend(self, w):
        w = w.reshape(self.rdev, 3, 2, self.half).transpose(2, 0, 1, 3)
        return w.reshape(2, self.rdev, 3 * self.half)

    def split_widen(self, w):
        w = w.reshape(self.rdev, self.links.chips, 2, 2, -1).transpose(2, 0, 3, 1, 4)
        return w.reshape(2, self.rdev, self.ff // 2)

    def pack_attend(self, w, p, small):
        parts = [w, jnp.concatenate([p[:, : self.half], p[:, self.half :]], 0)]
        if small is not None:
            parts.append(jnp.pad(small, ((0, 0), (0, 128 - small.shape[1]))))
        return jnp.concatenate(parts, 1)

    def pack_wide(self, wout):
        h = wout.shape[0] // 2
        return jnp.concatenate([wout[:h], wout[h:]], 1)

    def column(self, buf, *hold):
        if self.links.fast:
            return self.links.column(buf, *hold)
        return lax.all_gather(buf, CHIPS, axis=0, tiled=False)

    def cut(self, x):
        return x if self.links.fast else x.reshape(4, -1, x.shape[-1])

    def pack_block(self, quad):
        f, h, r = self.feat, self.half, self.rdev
        n = quad.shape[0]
        p = quad[..., f + h : 2 * f].reshape(n, 2, r, h)
        parts = [quad[..., i * h : (i + 1) * h] for i in range(3)] + [p[:, 0], p[:, 1]]
        parts = [self.cut(t.reshape(-1, h)) for t in parts]
        if quad.shape[2] > 2 * f:
            small = self.cut(quad[..., 2 * f :].reshape(-1, 128))
            small = small.reshape(small.shape[:-2] + (3, -1, 128))
            parts.append(jnp.concatenate([small[..., g, :, :] for g in range(3)], -1))
        return jnp.concatenate(parts, -2)

    def pack_pair(self, quad_in, quad_out):
        f = self.feat
        halves = []
        for i in range(2):
            pair = [self.cut(t[..., i * f : (i + 1) * f].reshape(-1, f)) for t in (quad_in, quad_out)]
            halves.append(jnp.stack(pair, -3))
        return jnp.stack(halves, -4)

    def spread(self, x, cuts, *hold):
        if not self.links.fast:
            return [x[0], x[1], x[2], cuts[0](x[3]), cuts[1](x[3])]
        to = lambda t, j: self.links.xor(t, "expert", j)
        x1, x2 = tie([to(x, 1), to(x, 2)], *hold)
        return [x, x1, x2, to(cuts[0](x1), 2), to(cuts[1](x2), 1)]

    def spread_attend(self, x, *hold):
        n = self.feat // 2
        return self.spread(x, (lambda t: t[:n], lambda t: t[n:]), *hold)

    def spread_pair(self, x, *hold):
        return self.spread(x, (lambda t: t[0], lambda t: t[1]), *hold)

    def total(self, keep, send, first, hold):
        if self.links.fast:
            out, give = self.links.plane_sum(keep, send, first, hold)
            self.given.append(give)
            return out
        blk = {0: keep[0], 3 - first: keep[1], first: send[0], 3: send[1]}
        return jnp.stack([blk[j] for j in range(4)])

    def column_sum(self, buf, hold):
        if self.links.fast and hold is not None:
            return self.links.column_sum(buf, *hold)
        axes = "context" if self.links.fast else CHIPS
        return lax.psum_scatter(buf.astype(BF), axes, scatter_dimension=0, tiled=False).astype(F32)

    def exchange(self, w):
        w = w.reshape(2, self.rdev, -1)
        mine = lax.dynamic_index_in_dim(w, self.d, 0, False)
        got = self.links.sib(lax.dynamic_index_in_dim(w, 1 - self.d, 0, False))
        return in_order(self.d, mine, got)

    def owner_attend(self, keep, send, first, hold, after=()):
        f, h, r = self.feat, self.half, self.rdev
        t = self.total(keep, send, first, hold)
        n, m = f // 4, h // 4
        cut = lambda t, k: t.reshape(-1, k * r, t.shape[-1])
        parts = [cut(t[..., g * n : (g + 1) * n, :], 2) for g in range(3)]
        p = [cut(t[..., 3 * n + g * m : 3 * n + (g + 1) * m, :], 1) for g in range(2)]
        parts.append(jnp.concatenate(p, 1))
        small = t.shape[-2] > 3 * n + 2 * m
        if small:
            sm = t[..., 3 * n + 2 * m :, :]
            sm = jnp.stack([sm[..., 128 * g : 128 * (g + 1)] for g in range(3)], -3)
            parts.append(sm.reshape(-1, 2 * r, 128))
        (buf,) = tie([jnp.concatenate(parts, 2)], *after)
        buf = self.column_sum(buf, hold[2])
        p = jnp.concatenate([buf[:r, f + h : 2 * f], buf[r:, f + h : 2 * f]], 1)
        p = lax.ppermute(p, ALL, self.links.from_lane)
        w = buf[:, : f + h]
        if small:
            w = jnp.concatenate([w, buf[:, 2 * f :]], 1)
        w = self.exchange(w)
        extra = w[0, :, f + h :] + w[1, :, f + h :]
        w = w[..., : f + h].reshape(2, r, 3, h).transpose(1, 2, 0, 3).reshape(r, 3 * f)
        return w, p, extra

    def reduce_column(self, by_context):
        t = lax.psum_scatter(by_context, "context", scatter_dimension=0, tiled=False)
        return t[:2], t[2:]

    def owner_wide(self, slopes, first, hold):
        f, r = self.feat, self.rdev
        a = self.total(*slopes[:2], first, hold[0])
        if self.links.fast:
            a = jnp.moveaxis(a.reshape(2, 4, 2 * r, f), 1, 0)
            a = self.column_sum(a, hold[0][2])
            b = self.total(*slopes[2:], first, hold[1])
            w = jnp.concatenate([a[0], b[0]], 1)
            w_out = jnp.concatenate([a[1], b[1]], 0)
        else:
            b = self.total(*slopes[2:], first, hold[1])
            hid = self.ff // (4 * self.links.chips)
            w = [t[..., 0, :, :].reshape(-1, 2 * r, f) for t in (a, b)]
            w_out = [t[..., 1, :, :].reshape(-1, hid, f) for t in (a, b)]
            w, w_out = [self.column_sum(jnp.concatenate(t, 2), None) for t in (w, w_out)]
            w_out = jnp.concatenate([w_out[:, :f], w_out[:, f:]], 0)
        w = self.exchange(w).reshape(2, r, 2, self.links.chips, -1)
        return w.transpose(1, 3, 0, 2, 4).reshape(r, self.ff), w_out


def body(links, *args):
    (tokens, cotangent, g1, w1, p1, g2, win, wout, g3, w3, p3, g4, router, ein, eout, routes, slots) = args
    e = lax.axis_index("expert")
    d = lax.axis_index("dp")
    blk_len, feat = tokens.shape[1:]
    rows = up16(blk_len)
    half = feat // 2
    rdev = w1.shape[0]
    ff = win.shape[1]
    longest = LEN - (blk_len - 1) * links.C
    experts = router.shape[1]
    small_rows = (4 + experts + 7) // 8 * 8
    cap = max(2, (5 * TOP * blk_len + 4 * experts - 1) // (4 * experts))
    blk = 2 * (e % 2) + d
    where = jnp.stack([blk, e if links.fast else 0 * e]).astype(jnp.int32)
    wt = Weights(links, rdev, feat, ff)
    img = dict(rows=rows, blk_len=blk_len, longest=longest)

    tok = links.move(tokens[0])
    ps = lax.ppermute(jnp.concatenate([p1, p3], 0), ALL, links.to_lane)
    small = jnp.concatenate([g1[:, None], g2[:, None], g3[:, None], g4[:, None], router], 1)
    gsm = small.shape[1]
    lane1 = jnp.concatenate(
        [wt.split_attend(w1), jnp.broadcast_to(small[None], (2, rdev, gsm))], 2
    )
    lane1 = lane_rows(links, lane1, d)
    buf1 = wt.pack_attend(lane1[:, : 3 * half], ps[:rdev], lane1[:, 3 * half :])
    quad1 = wt.column(buf1)
    tok_pair = jnp.stack([tok, links.partner(tok)])
    tok_sib = links.sib(tok_pair)
    toks = [tok_pair[0], tok_sib[0], tok_pair[1], tok_sib[1]]
    blocks1 = wt.spread_attend(wt.pack_block(quad1))

    later = jnp.concatenate([wt.split_widen(win), wt.split_attend(w3)], 2)
    later = lane_rows(links, later, d)
    w_in, w_out = later[:, : ff // 2], wt.pack_wide(wout)
    buf3 = wt.pack_attend(later[:, ff // 2 :], ps[rdev:], None)

    x0, normed1, q1, kv1, far1, wa1, wp1, small, gains = attend_first(where, toks, small_rows, blocks1, rows)
    part, low, blend1, lse1 = attend_core(where, q1, kv1, far1, wp1, solo=False, **img)
    if links.fast:
        (buf2,) = tie([jnp.concatenate([w_in, w_out], 1)], quad1)
        quad2 = wt.column(buf2, part)
        quad2 = quad2[..., : ff // 2], quad2[..., ff // 2 :]
    else:
        quad2 = wt.column(w_in), wt.column(w_out)
    pair2 = wt.pack_pair(*quad2)
    blocks2 = wt.spread_pair(pair2)
    quad3 = wt.column(tie([buf3], pair2)[0], *blocks2[1:3])
    cot, raw = tie([cotangent[0].astype(BF), jnp.concatenate([routes[0], slots[0]], 1)], quad3)
    raw, cot = tie([links.move(raw), links.move(cot)], blocks2[3])
    index = jnp.pad(raw, ((0, rows - blk_len), (0, 0)), constant_values=cap)
    x1, normed2, hidden, part2, low2, wi, wo = widen_forward(
        where, x0, part, links.sib(low), gains, blocks2, rows
    )
    blocks3 = wt.spread_attend(tie([wt.pack_block(quad3)], *blocks2[3:])[0], x1)
    x2, normed3, own3 = norm_next(x1, part2, links.sib(low2), gains, 2, rows)
    far_own = links.partner(own3)
    q3, kv3, wa3, wp3 = attend_next(where, normed3, blocks3, after=(cot, index))
    (far_own,) = tie([far_own], q3)
    part3, low3, blend3, lse3, far3 = attend_core(
        where, q3, kv3, None, wp3, solo=True, far=(far_own, links.sib(far_own), wa3), **img
    )
    moe_args = dict(experts=experts, cap=cap, fast=links.fast, **img)
    x3, moe, gates, up, *sent = route(
        where, x2, part3, links.sib(low3), gains, small, cot, index, **moe_args
    )
    ein_own, eout_own = ein[0], eout[0]
    ein_sib, eout_sib = [links.sib(t) for t in tie([ein_own, eout_own], low3)]
    came = links.swap_blocks(sent)
    every = lax.all_gather(jnp.stack(came), "context", axis=0, tiled=False)
    sums = expert_half(came, ein_sib, eout_sib, None, up16(cap))
    answer = links.swap_blocks(expert_half(came, ein_own, eout_own, sums, up16(cap)))
    acts, u, u_low, small_slopes = combine(
        where, answer, x3, moe, gates, up, index, small, gains, small_rows, **moe_args
    )

    u, u_low = join_upstream(u, links.sib(u_low), rows)
    dq, own, far, wps = attend_core_back(where, u_low, wp3, blend3, q3, kv3, far3, lse3, **img)
    first3, first2, first1 = 2, 2, 1
    part, low, *slopes3 = attend_proj_back(
        where, dq, own, links.partner(far), normed3, wa3, wps, small_slopes, first3, rows, False
    )
    u, part, low, *slopes2 = widen_back(
        where, u, x2, gains, part, links.sib(low), normed2, hidden, wi, wo, first2, rows, links.fast
    )
    u1, u_low = norm_step(u, x1, gains, 1, part, links.sib(low), rows, 0)
    dq1, own, far, wps = attend_core_back(where, u_low, wp1, blend1, q1, kv1, far1, lse1, **img)
    part, low, *slopes1 = attend_proj_back(
        where, dq1, own, links.partner(far), normed1, wa1, wps, None, first1, rows, True
    )
    (u2,) = norm_step(u1, x0, gains, 0, part, links.sib(low), rows, blk_len)
    moved = links.move(jnp.stack([acts, u2]))
    acts, token_slope = moved[0], moved[1]
    if links.fast:
        (by_context,) = tie(slopes2[2:], every)
        slopes2 = slopes2[:2] + list(wt.reduce_column(by_context))
        after3 = slopes2[2:]
    else:
        after3 = ()
    e_sib = expert_slopes(every, ein_sib, eout_sib, None, after=(u2,))
    w3_out, p3_out, extra = wt.owner_attend(*slopes3, first3, ((u,), (dq1,), None), after=after3)
    wt.given = []
    win_out, wout_out = wt.owner_wide(slopes2, first2, (((dq1,), (e_sib[0],), ()), ((e_sib[0],), (), ())))
    w1_out, p1_out, _ = wt.owner_attend(*slopes1, first1, ((e_sib[0],), (), ()))
    e_slopes = expert_slopes(every, ein_own, eout_own, [links.sib(t) for t in e_sib], after=wt.given)

    def gain_slope(w, slope, gain):
        return jnp.sum(w.astype(F32) * slope, 1) / gain.astype(F32)

    return (
        acts.astype(F32)[None], token_slope.astype(F32)[None],
        gain_slope(w1, w1_out, g1), w1_out, p1_out, gain_slope(win, win_out, g2), win_out, wout_out,
        gain_slope(w3, w3_out, g3), w3_out, p3_out, extra[:, 3], extra[:, 4 : 4 + experts],
        e_slopes[0][None], e_slopes[1][None],
    )


def solution(mesh):
    links = Links(mesh)
    tok = P(("expert", "dp"), "context", None)
    vec, mat = P(ALL), P(ALL, None)
    ein, eout = P("expert", None, "dp"), P("expert", "dp", None)
    dense = (vec, mat, mat, vec, mat, mat, vec, mat, mat, vec, mat, ein, eout)
    return jax.shard_map(
        functools.partial(body, links),
        mesh=mesh,
        in_specs=(tok, tok) + dense + (tok, tok),
        out_specs=(tok, tok) + dense,
        check_vma=False,
    )
```

time: 678 us -> 503 us (0.74)
  waiting for transfers between devices: 403 us -> 215 us
  Pallas kernels: 93.9 us -> 140 us
  other arithmetic: 35 us -> 16.1 us
  starting transfers between devices: 86.9 us -> 75.8 us
    ppermute x66 -> x63, waiting for transfers between devices: 321 us -> 183 us  [xor(): return lax.ppermute(x, axis, [(i, i ^ j) for i in range(n)])]
    psum x1 -> x0, waiting for transfers between devices: 75.6 us -> none  [body(): lax.psum((a.astype(F32) + links.sib(b).astype(F32)).astype(BF), 'context')]
    pallas_call x0 -> x2, Pallas kernels: none -> 48.9 us  [expert_slopes(): pl.pallas_call(kernel, grid=(steps,), out_shape=[jax.ShapeDtypeStruct((fe...]
    broadcast_in_dim x4 -> x0, other arithmetic: 14.8 us -> none  [the longest x2 8.55 us: body(): e_sums[0][None]]
    ppermute x5 -> x4, waiting for transfers between devices: 5.86 us -> 18.6 us  [move(): return lax.ppermute(x, ALL, self.team)]
    ppermute x2, waiting for transfers between devices: 0.47 us -> 8.27 us  [owner_attend(): p = lax.ppermute(p, ALL, self.links.from_lane)]
    ppermute x66 -> x63, starting transfers between devices: 57.3 us -> 49.9 us  [xor(): return lax.ppermute(x, axis, [(i, i ^ j) for i in range(n)])]
    ppermute x5 -> x4, starting transfers between devices: 18.1 us -> 12.1 us  [move(): return lax.ppermute(x, ALL, self.team)]
  transfers between devices with their start and end apart: 75 -> 73, of which waited for: 38 -> 40; matrix products, arithmetic and copies ran while one was open for 6% -> 6% of each run, Pallas kernels for 9% -> 27%
where the time goes in v3:
time: 503 us; the launch traced here: 499 us
  waiting for transfers between devices  215 us (43%)
  Pallas kernels  140 us (28%)
  starting transfers between devices  75.8 us (15%)
  local copies, waits for them, and re-layouts  35.9 us (7%)
  other arithmetic  16.1 us (3%)
  between operations  15.8 us (3%)
    ppermute x63, waiting for transfers between devices, xor(): return lax.ppermute(x, axis, [(i, i ^ j) for i in range(n)])  183 us
    pallas_call x16, Pallas kernels, call(): pl.pallas_call(run, out_shape=[jax.ShapeDtypeStruct(s, t) for s, t, _ in...  77.1 us
    ppermute x63, starting transfers between devices, xor(): return lax.ppermute(x, axis, [(i, i ^ j) for i in range(n)])  49.9 us
    pallas_call x2, Pallas kernels, expert_slopes(): pl.pallas_call(kernel, grid=(steps,), out_shape=[jax.ShapeDtypeStruct((fe...  48.9 us
    unnamed x169, local copies, waits for them, and re-layouts  23.8 us
    ppermute x4, waiting for transfers between devices, move(): return lax.ppermute(x, ALL, self.team)  18.6 us
    pallas_call x2, Pallas kernels, expert_half(): pl.pallas_call(kernel, grid=(steps,), out_shape=shapes, in_specs=in_specs...  13.7 us
    ppermute x4, starting transfers between devices, move(): return lax.ppermute(x, ALL, self.team)  12.1 us
  transfers between devices with their start and end apart: 73, of which 40 were waited for; matrix products, arithmetic and copies ran while one was open for 6% of the time, Pallas kernels for 27%

profile of v3, /device:TPU:10, one launch (start us, length us, event | category | flops | bytes accessed | tf_op | source)
XLA Modules:
  0.0 498.9 jit_solution(1162852548694788666)
XLA Ops:
  7.2 3.0 collective-permute-start
  14.3 3.8 collective-permute-start.4
  19.4 5.2 %collective-permute-done.4 = bf16[48,768]{1,0:T(8,128)(2,1)S(1)} collective-permute-done((bf16[48,768]{1,0:T(8,128)(2,1)S(1)}, bf16[48,768]{1,0:T(8,128)(2,1)S(1)}, u32[]{:S(2)}, u32[]{:S(2)}) %collective-permute-start.4) | collective-permute-done | bytes 73760 | tf_op jit(solution)/shard_map/ppermute | solution.py:1053
  28.5 3.6 collective-permute-done.5
  32.1 5.7 %collective-permute-done.6 = bf16[48,1664]{1,0:T(8,128)(2,1)S(1)} collective-permute-done((bf16[48,1664]{1,0:T(8,128)(2,1)S(1)}, bf16[48,1664]{1,0:T(8,128)(2,1)S(1)}, u32[]{:S(2)}, u32[]{:S(2)}) %collective-permute-start.6) | collective-permute-done | bytes 159776 | tf_op jit(solution)/shard_map/ppermute | solution.py:849
  37.8 5.4 %collective-permute-done.7 = bf16[48,1664]{1,0:T(8,128)(2,1)S(1)} collective-permute-done((bf16[48,1664]{1,0:T(8,128)(2,1)S(1)}, bf16[48,1664]{1,0:T(8,128)(2,1)S(1)}, u32[]{:S(2)}, u32[]{:S(2)}) %collective-permute-start.7) | collective-permute-done | bytes 159776 | tf_op jit(solution)/shard_map/ppermute | solution.py:849
  49.1 15.0 %collective-permute-done.8.refs_6_ = bf16[832,384]{1,0:T(8,128)(2,1)} collective-permute-done((bf16[832,384]{1,0:T(8,128)(2,1)}, bf16[832,384]{1,0:T(8,128)(2,1)}, u32[]{:S(2)}, u32[]{:S(2)}) %collective-permute-start.8) | collective-permute-done | bytes 639008 | tf_op jit(solution)/shard_map/ppermute | solution.py:849
  75.2 4.6 shard_map.280
  80.6 4.2 shard_map.281
  84.9 5.5 %collective-permute-done.15 = bf16[48,3072]{1,0:T(8,128)(2,1)S(1)} collective-permute-done((bf16[48,3072]{1,0:T(8,128)(2,1)S(1)}, bf16[48,3072]{1,0:T(8,128)(2,1)S(1)}, u32[]{:S(2)}, u32[]{:S(2)}) %collective-permute-start.15) | collective-permute-done | bytes 294944 | tf_op jit(solution)/shard_map/ppermute | solution.py:849
  90.3 5.6 %collective-permute-done.16 = bf16[48,3072]{1,0:T(8,128)(2,1)S(1)} collective-permute-done((bf16[48,3072]{1,0:T(8,128)(2,1)S(1)}, bf16[48,3072]{1,0:T(8,128)(2,1)S(1)}, u32[]{:S(2)}, u32[]{:S(2)}) %collective-permute-start.16) | collective-permute-done | bytes 294944 | tf_op jit(solution)/shard_map/ppermute | solution.py:849
  102.2 20.1 %collective-permute-done.17.refs_6_ = bf16[2,2,192,768]{3,2,1,0:T(8,128)(2,1)S(1)} collective-permute-done((bf16[2,2,192,768]{3,2,1,0:T(8,128)(2,1)S(1)}, bf16[2,2,192,768]{3,2,1,0:T(8,128)(2,1)S(1)}, u32[]{:S(2)}, u32[]{:S(2)}) %collective-permute-start.17) | collective-permute-done | bytes 1179680 | tf_op jit(solution)/shard_map/ppermute | solution.py:849
  125.7 12.4 %collective-permute-done.19.refs_8_ = bf16[2,192,768]{2,1,0:T(8,128)(2,1)S(1)} collective-permute-done((bf16[2,192,768]{2,1,0:T(8,128)(2,1)S(1)}, bf16[2,192,768]{2,1,0:T(8,128)(2,1)S(1)}, u32[]{:S(2)}, u32[]{:S(2)}) %collective-permute-start.19) | collective-permute-done | bytes 589856 | tf_op jit(solution)/shard_map/ppermute | solution.py:849
  140.6 9.9 %shard_map.282 = (f32[320,768]{1,0:T(8,128)S(1)}, bf16[320,768]{1,0:T(8,128)(2,1)S(1)}, f32[320,1536]{1,0:T(8,128)}, f32[320,768]{1,0:T(8,128)}, bf16[320,768]{1...) custom-call(s32[2]{0:T(128)S(1)} %pad_add_fusion.1.refs_0_, ...), custom_call_target="tpu_custom_call" | custom-call | flops 1509949440 | bytes 16777216 | tf_op jit(solution)/shard_map/pallas_call | solution.py:45
  163.3 4.3 collective-permute-start.29
  167.6 2.9 collective-permute-done.29
  171.4 4.1 shard_map.284
  177.3 5.7 %shard_map.285 = (f32[320,768]{1,0:T(8,128)S(1)}, bf16[160,768]{1,0:T(8,128)(2,1)S(1)}, bf16[384,320]{1,0:T(8,128)(2,1)S(1)}, f32[8,320]{1,0:T(8,128)S(1)}, bf16[320,768]{1,0:T(8,128)(2,1)S(1)}) custom-call(s32[2]{0:T(128)S(1)} %pad_add_fusion.1.refs_0_, bf16[320,384]{1,0:T(8,128)(2,1)S(1)} %get-tuple-element.175.refs_1_.refs_4_, ...), custom_call_target="tpu_custom_call" | custom-call | flops 503316480 | bytes 4194304 | tf_op jit(solution)/shard_map/pallas_call | solution.py:45
  186.2 4.6 collective-permute-done.33.refs_3_
  190.8 2.9 shard_map.286
  198.7 6.4 %collective-permute-done.34.refs_1_ = bf16[192,768]{1,0:T(8,128)(2,1)S(1)} collective-permute-done((bf16[192,768]{1,0:T(8,128)(2,1)S(1)}, bf16[192,768]{1,0:T(8,128)(2,1)S(1)}, u32[]{:S(2)}, u32[]{:S(2)}) %collective-permute-start.34) | collective-permute-done | bytes 294944 | tf_op jit(solution)/shard_map/ppermute | solution.py:849
  205.1 5.7 %collective-permute-done.36.refs_3_ = bf16[192,768]{1,0:T(8,128)(2,1)S(1)} collective-permute-done((bf16[192,768]{1,0:T(8,128)(2,1)S(1)}, bf16[192,768]{1,0:T(8,128)(2,1)S(1)}, u32[]{:S(2)}, u32[]{:S(2)}) %collective-permute-start.36) | collective-permute-done | bytes 294944 | tf_op jit(solution)/shard_map/ppermute | solution.py:849
  213.8 6.7 %shard_map.287 = (f32[384,768]{1,0:T(8,128)S(1)}, f32[384,768]{1,0:T(8,128)S(1)}) custom-call(bf16[192,768]{1,0:T(8,128)(2,1)S(1)} %get-tuple-element.184.refs_0_, bf16[192,768]{1,0:T(8,128)(2,1)S(1)} %collective-permute-done.34.refs_1_, bf16[192,768]{1,0:T(8,128)(2,1)S(1)} %collective-permute-done.35.refs_2_, bf16[192,768]{1,0:T(8,128)(2,1)S(1)} %copy-done.16, ...), custom_call_target="tpu_custom_call" | custom-call | flops 3623878656 | bytes 10485760 | tf_op jit(solution)/shard_map/pallas_call | solution.py:694
  222.5 6.9 %shard_map.288 = (bf16[192,768]{1,0:T(8,128)(2,1)S(1)}, bf16[192,768]{1,0:T(8,128)(2,1)S(1)}, bf16[192,768]{1,0:T(8,128)(2,1)S(1)}, bf16[192,768]{1,0:T(8,128)(2,1)S(1)}) custom-call(bf16[192,768]{1,0:T(8,128)(2,1)S(1)} %get-tuple-element.184.refs_0_, bf16[192,768]{1,0:T(8,128)(2,1)S(1)} %collective-permute-done.34.refs_1_, ...), custom_call_target="tpu_custom_call" | custom-call | flops 3623878656 | bytes 10485760 | tf_op jit(solution)/shard_map/pallas_call | solution.py:694
  233.0 6.5 %collective-permute-done.39.refs_2_ = bf16[192,768]{1,0:T(8,128)(2,1)S(1)} collective-permute-done((bf16[192,768]{1,0:T(8,128)(2,1)S(1)}, bf16[192,768]{1,0:T(8,128)(2,1)S(1)}, u32[]{:S(2)}, u32[]{:S(2)}) %collective-permute-start.39) | collective-permute-done | bytes 294944 | tf_op jit(solution)/shard_map/ppermute | solution.py:849
  239.5 5.6 %collective-permute-done.40.refs_3_ = bf16[192,768]{1,0:T(8,128)(2,1)S(1)} collective-permute-done((bf16[192,768]{1,0:T(8,128)(2,1)S(1)}, bf16[192,768]{1,0:T(8,128)(2,1)S(1)}, u32[]{:S(2)}, u32[]{:S(2)}) %collective-permute-start.40) | collective-permute-done | bytes 294944 | tf_op jit(solution)/shard_map/ppermute | solution.py:849
  249.9 7.0 %shard_map.291 = (bf16[320,384]{1,0:T(8,128)(2,1)S(1)}, f32[320,768]{1,0:T(8,128)}, bf16[320,768]{1,0:T(8,128)(2,1)S(1)}, bf16[384,768]{1,0:T(8,128)(2,1)S(1)}) custom-call(s32[2]{0:T(128)S(1)} %pad_add_fusion.1.refs_0_, bf16[320,768]{1,0:T(8,128)(2,1)S(1)} %get-tuple-element.204.refs_1_, bf16[384,768]{1,0:T(8,128)(2,1)S(1)} %copy-done.8, ...), custom_call_target="tpu_custom_call" | custom-call | flops 1163919360 | bytes 6291456 | tf_op jit(solution)/shard_map/pallas_call | solution.py:45
  257.8 12.4 %collective-permute-done.43.refs_3_ = bf16[320,768]{1,0:T(8,128)(2,1)S(1)} collective-permute-done((bf16[320,768]{1,0:T(8,128)(2,1)S(1)}, bf16[320,768]{1,0:T(8,128)(2,1)S(1)}, u32[]{:S(2)}, u32[]{:S(2)}) %collective-permute-start.43) | collective-permute-done | bytes 491552 | tf_op jit(solution)/shard_map/ppermute | solution.py:849
  270.2 6.2 %shard_map.292 = (f32[320,768]{1,0:T(8,128)S(1)}, bf16[320,768]{1,0:T(8,128)(2,1)S(1)}, bf16[2,832,384]{2,1,0:T(8,128)(2,1)}, bf16[2,832,384]{2,1,0:T(8,128)(2,1)}) custom-call(s32[2]{0:T(128)S(1)} %pad_add_fusion.1.refs_0_, bf16[320,384]{1,0:T(8,128)(2,1)S(1)} %get-tuple-element.208.refs_1_, f32[320,768]{1,0:T(8,128)} %get-tuple-element.209.refs_2_, ...), custom_call_target="tpu_custom_call" | custom-call | flops 1132462080 | bytes 10485760 | tf_op jit(solution)/shard_map/pallas_call | solution.py:45
  279.2 12.8 %shard_map.293 = (f32[320,768]{1,0:T(8,128)S(1)}, f32[320,768]{1,0:T(8,128)S(1)}, bf16[320,768]{1,0:T(8,128)(2,1)S(1)}, bf16[2,2,192,768]{3,2,1,0:T(8,128)(2,1)}...) custom-call(s32[2]{0:T(128)S(1)} %pad_add_fusion.1.refs_0_, f32[320,768]{1,0:T(8,128)} %copy-done.24, ...), custom_call_target="tpu_custom_call" | custom-call | flops 3774873600 | bytes 25165824 | tf_op jit(solution)/shard_map/pallas_call | solution.py:45
  297.0 7.2 %shard_map.295 = (bf16[320,384]{1,0:T(8,128)(2,1)S(1)}, f32[320,768]{1,0:T(8,128)}, bf16[320,768]{1,0:T(8,128)(2,1)}, bf16[384,768]{1,0:T(8,128)(2,1)S(1)}) custom-call(s32[2]{0:T(128)S(1)} %pad_add_fusion.1.refs_0_, bf16[320,768]{1,0:T(8,128)(2,1)S(1)} %get-tuple-element.223.refs_1_, bf16[384,768]{1,0:T(8,128)(2,1)S(1)} %copy-done.33, ...), custom_call_target="tpu_custom_call" | custom-call | flops 1163919360 | bytes 6291456 | tf_op jit(solution)/shard_map/pallas_call | solution.py:45
  305.0 3.4 collective-permute-done.64
  311.1 7.5 %collective-permute-done.46.refs_3_ = bf16[320,768]{1,0:T(8,128)(2,1)} collective-permute-done((bf16[320,768]{1,0:T(8,128)(2,1)}, bf16[320,768]{1,0:T(8,128)(2,1)}, u32[]{:S(2)}, u32[]{:S(2)}) %collective-permute-start.46) | collective-permute-done | bytes 491552 | tf_op jit(solution)/shard_map/ppermute | solution.py:849
  318.6 5.7 %shard_map.296 = (f32[160,768]{1,0:T(8,128)S(1)}, bf16[160,768]{1,0:T(8,128)(2,1)S(1)}, bf16[2,768,384]{2,1,0:T(8,128)(2,1)}, bf16[2,768,384]{2,1,0:T(8,128)(2,1)}) custom-call(s32[2]{0:T(128)S(1)} %pad_add_fusion.1.refs_0_, bf16[320,384]{1,0:T(8,128)(2,1)S(1)} %get-tuple-element.226.refs_1_, f32[320,768]{1,0:T(8,128)S(1)} %copy-done.1, ...), custom_call_target="tpu_custom_call" | custom-call | flops 1132462080 | bytes 10485760 | tf_op jit(solution)/shard_map/pallas_call | solution.py:45
  325.3 8.1 %collective-permute-done.56 = bf16[2,2,192,768]{3,2,1,0:T(8,128)(2,1)} collective-permute-done((bf16[2,2,192,768]{3,2,1,0:T(8,128)(2,1)}, bf16[2,2,192,768]{3,2,1,0:T(8,128)(2,1)}, u32[]{:S(2)}, u32[]{:S(2)}) %collective-permute-start.56) | collective-permute-done | bytes 1179680 | tf_op jit(solution)/shard_map/ppermute | solution.py:849
  339.1 2.9 collective-permute-start.48
  344.5 24.1 %shard_map.298 = (bf16[768,1536]{1,0:T(8,128)(2,1)}, bf16[1536,768]{1,0:T(8,128)(2,1)}) custom-call(bf16[4,4,192,768]{3,2,1,0:T(8,128)(2,1)} %bitcast.269, bf16[768,1536]{1,0:T(8,128)(2,1)} %collective-permute-done.37.refs_4_.refs_1_, bf16[1536,768]{1,0:T(8,128)(2,1)} %collective-permute-done.38.refs_5_.refs_2_, bf16[145,768]{1,0:T(8,128)(2,1)} %copy-done.6), custom_call_target="tpu_custom_call" | custom-call | flops 14495514624 | bytes 20971520 | tf_op jit(solution)/shard_map/pallas_call | solution.py:755
  371.4 5.6 %collective-permute-done.57 = bf16[2,192,768]{2,1,0:T(8,128)(2,1)S(1)} collective-permute-done((bf16[2,192,768]{2,1,0:T(8,128)(2,1)}, bf16[2,192,768]{2,1,0:T(8,128)(2,1)S(1)}, u32[]{:S(2)}, u32[]{:S(2)}) %collective-permute-start.57) | collective-permute-done | bytes 589856 | tf_op jit(solution)/shard_map/ppermute | solution.py:849
  381.2 15.7 %collective-permute-done.48 = bf16[2,145,768]{2,1,0:T(8,128)(2,1)S(1)} collective-permute-done((bf16[2,145,768]{2,1,0:T(8,128)(2,1)}, bf16[2,145,768]{2,1,0:T(8,128)(2,1)S(1)}, u32[]{:S(2)}, u32[]{:S(2)}) %collective-permute-start.48) | collective-permute-done | bytes 445472 | tf_op jit(solution)/shard_map/ppermute | solution.py:845
  402.8 6.2 %collective-permute-done.60 = bf16[2,48,768]{2,1,0:T(8,128)(2,1)S(1)} collective-permute-done((bf16[2,48,768]{2,1,0:T(8,128)(2,1)S(1)}, bf16[2,48,768]{2,1,0:T(8,128)(2,1)S(1)}, u32[]{:S(2)}, u32[]{:S(2)}) %collective-permute-start.60) | collective-permute-done | bytes 147488 | tf_op jit(solution)/shard_map/ppermute | solution.py:849
  409.7 3.9 collective-permute-start.52
  416.3 6.7 %collective-permute-done.52 = bf16[48,1536]{1,0:T(8,128)(2,1)S(1)} collective-permute-done((bf16[48,1536]{1,0:T(8,128)(2,1)S(1)}, bf16[48,1536]{1,0:T(8,128)(2,1)S(1)}, u32[]{:S(2)}, u32[]{:S(2)}) %collective-permute-start.52) | collective-permute-done | bytes 147488 | tf_op jit(solution)/shard_map/ppermute | solution.py:849
  426.1 6.2 %collective-permute-start.55 = (f32[24,768]{1,0:T(8,128)S(1)}, f32[24,768]{1,0:T(8,128)S(1)}, u32[]{:S(2)}, u32[]{:S(2)}) collective-permute-start(f32[24,768]{1,0:T(8,128)S(1)} %pad_maximum_fusion.12), channel_id=1, source_target_pairs={{0,0},{2,1},{4,2},{6,3},{8,4},{10,5},{12,6},{14,7},{16,8},{18,9},{... | collective-permute-start | bytes 221192 | tf_op jit(solution)/shard_map/ppermute | solution.py:1001
  437.3 5.7 %collective-permute-done.61 = bf16[2,2,48,768]{3,2,1,0:T(8,128)(2,1)S(1)} collective-permute-done((bf16[2,2,48,768]{3,2,1,0:T(8,128)(2,1)S(1)}, bf16[2,2,48,768]{3,2,1,0:T(8,128)(2,1)S(1)}, u32[]{:S(2)}, u32[]{:S(2)}) %collective-permute-start.61) | collective-permute-done | bytes 294944 | tf_op jit(solution)/shard_map/ppermute | solution.py:849
  444.4 4.4 collective-permute-done.62
  449.0 24.8 %shard_map.299 = (f32[768,1536]{1,0:T(8,128)}, f32[1536,768]{1,0:T(8,128)}) custom-call(bf16[4,4,192,768]{3,2,1,0:T(8,128)(2,1)} %bitcast.270, bf16[768,1536]{1,0:T(8,128)(2,1)} %bitcast.57.refs_4_.refs_1_, bf16[1536,768]{1,0:T(8,128)(2,1)} %bitcast.58.refs_5_.refs_2_, bf16[768,1536]{1,0:T(8,128)(2,1)} %collective-permute-done.68.refs_3_, ...), custom_call_target="tpu_custom_call" | custom-call | flops 14495514624 | bytes 20971520 | tf_op jit(solution)/shard_map/pallas_call | solution.py:755
  478.4 3.8 collective-permute-start.67
  482.8 5.4 %collective-permute-done.67 = f32[24,768]{1,0:T(8,128)S(1)} collective-permute-done((f32[24,768]{1,0:T(8,128)S(1)}, f32[24,768]{1,0:T(8,128)S(1)}, u32[]{:S(2)}, u32[]{:S(2)}) %collective-permute-start.67) | collective-permute-done | bytes 73760 | tf_op jit(solution)/shard_map/ppermute | solution.py:1001
  (414 shorter events, 131.0 us)
Async XLA Ops:
  7.2 336.5 %all-gather.3.cloned.1.call-start = ((), (), s32[]{:S(2)}) async-start(), calls=%async_computation.4 | async-start | bytes 5898240 | tf_op jit(solution)/shard_map/all_gather | solution.py:1104
  7.2 21.2 %collective-permute-start = (bf16[145,768]{1,0:T(8,128)(2,1)}, bf16[145,768]{1,0:T(8,128)(2,1)S(1)}, u32[]{:S(2)}, u32[]{:S(2)}) collective-permute-start(bf16[145,768]{1,0:T(8,128)(2,1)} %bitcast.271), channel_id=1, source_target_pairs={{0,0},{1,2},{2,1},{3,3},{4,8},{5,10},{6,9},{7,11},{8,4},{9,6},{10,... | collective-permute-start | bytes 668168 | tf_op jit(solution)/shard_map/ppermute | solution.py:845
  26.6 16.6 %collective-permute-start.7 = (bf16[48,1664]{1,0:T(8,128)(2,1)S(1)}, bf16[48,1664]{1,0:T(8,128)(2,1)S(1)}, u32[]{:S(2)}, u32[]{:S(2)}) collective-permute-start(bf16[48,1664]{1,0:T(8,128)(2,1)S(1)} %fusion.24), channel_id=1, source_target_pairs={{0,6},{2,4},{4,2},{6,0},{1,7},{3,5},{5,3},{7,1},{8,14},{10,12},{12... | collective-permute-start | bytes 479240 | tf_op jit(solution)/shard_map/ppermute | solution.py:849
  28.2 20.8 %collective-permute-start.13 = (bf16[24,2688]{1,0:T(8,128)(2,1)S(1)}, bf16[24,2688]{1,0:T(8,128)(2,1)S(1)}, u32[]{:S(2)}, u32[]{:S(2)}) collective-permute-start(bf16[24,2688]{1,0:T(8,128)(2,1)S(1)} %get-tuple-element.392), channel_id=1, source_target_pairs={{0,1},{1,0},{2,3},{3,2},{4,5},{5,4},{6,7},{7,6},{8,9},{9,8},{10,11... | collective-permute-start | bytes 387080 | tf_op jit(solution)/shard_map/ppermute | solution.py:849
  28.5 20.4 %collective-permute-start.1 = (bf16[145,768]{1,0:T(8,128)(2,1)S(1)}, bf16[145,768]{1,0:T(8,128)(2,1)S(1)}, u32[]{:S(2)}, u32[]{:S(2)}) collective-permute-start(bf16[145,768]{1,0:T(8,128)(2,1)S(1)} %collective-permute-done.refs_1_), channel_id=1, source_target_pairs={{0,8},{8,0},{16,24},{24,16},{1,9},{9,1},{17,25},{25,17},{2,10},{10... | collective-permute-start | bytes 668168 | tf_op jit(solution)/shard_map/ppermute | solution.py:849
  47.5 16.5 %collective-permute-start.8 = (bf16[832,384]{1,0:T(8,128)(2,1)}, bf16[832,384]{1,0:T(8,128)(2,1)}, u32[]{:S(2)}, u32[]{:S(2)}) collective-permute-start(bf16[832,384]{1,0:T(8,128)(2,1)} %maximum_dynamic-update-slice_fusion.1.refs_5_), channel_id=1, source_target_pairs={{0,8},{8,0},{16,24},{24,16},{1,9},{9,1},{17,25},{25,17},{2,10},{10... | collective-permute-start | bytes 1916936 | tf_op jit(solution)/shard_map/ppermute | solution.py:849
  47.5 16.5 %collective-permute-start.9 = (bf16[832,384]{1,0:T(8,128)(2,1)}, bf16[832,384]{1,0:T(8,128)(2,1)}, u32[]{:S(2)}, u32[]{:S(2)}) collective-permute-start(bf16[832,384]{1,0:T(8,128)(2,1)} %maximum_dynamic-update-slice_fusion.1.refs_5_), channel_id=1, source_target_pairs={{0,16},{8,24},{16,0},{24,8},{1,17},{9,25},{17,1},{25,9},{2,18},{10... | collective-permute-start | bytes 1916936 | tf_op jit(solution)/shard_map/ppermute | solution.py:849
  48.9 21.3 %collective-permute-start.2 = (bf16[2,145,768]{2,1,0:T(8,128)(2,1)S(1)}, bf16[2,145,768]{2,1,0:T(8,128)(2,1)S(1)}, u32[]{:S(2)}, u32[]{:S(2)}) collective-permute-start(bf16[2,145,768]{2,1,0:T(8,128)(2,1)S(1)} %pad_maximum_fusion.5), channel_id=1, source_target_pairs={{0,1},{1,0},{2,3},{3,2},{4,5},{5,4},{6,7},{7,6},{8,9},{9,8},{10,11... | collective-permute-start | bytes 1336328 | tf_op jit(solution)/shard_map/ppermute | solution.py:849
  68.3 16.6 %collective-permute-start.14 = (bf16[48,3072]{1,0:T(8,128)(2,1)S(1)}, bf16[48,3072]{1,0:T(8,128)(2,1)S(1)}, u32[]{:S(2)}, u32[]{:S(2)}) collective-permute-start(bf16[48,3072]{1,0:T(8,128)(2,1)S(1)} %pad_maximum_fusion.7), channel_id=1, source_target_pairs={{0,2},{2,0},{4,6},{6,4},{1,3},{3,1},{5,7},{7,5},{8,10},{10,8},{12,... | collective-permute-start | bytes 884744 | tf_op jit(solution)/shard_map/ppermute | solution.py:849
  68.3 22.0 %collective-permute-start.15 = (bf16[48,3072]{1,0:T(8,128)(2,1)S(1)}, bf16[48,3072]{1,0:T(8,128)(2,1)S(1)}, u32[]{:S(2)}, u32[]{:S(2)}) collective-permute-start(bf16[48,3072]{1,0:T(8,128)(2,1)S(1)} %pad_maximum_fusion.7), channel_id=1, source_target_pairs={{0,4},{2,6},{4,0},{6,2},{1,5},{3,7},{5,1},{7,3},{8,12},{10,14},{12... | collective-permute-start | bytes 884744 | tf_op jit(solution)/shard_map/ppermute | solution.py:849
  70.2 25.7 %collective-permute-start.16 = (bf16[48,3072]{1,0:T(8,128)(2,1)S(1)}, bf16[48,3072]{1,0:T(8,128)(2,1)S(1)}, u32[]{:S(2)}, u32[]{:S(2)}) collective-permute-start(bf16[48,3072]{1,0:T(8,128)(2,1)S(1)} %pad_maximum_fusion.7), channel_id=1, source_target_pairs={{0,6},{2,4},{4,2},{6,0},{1,7},{3,5},{5,3},{7,1},{8,14},{10,12},{12... | collective-permute-start | bytes 884744 | tf_op jit(solution)/shard_map/ppermute | solution.py:849
  96.6 25.7 %collective-permute-start.17 = (bf16[2,2,192,768]{3,2,1,0:T(8,128)(2,1)S(1)}, bf16[2,2,192,768]{3,2,1,0:T(8,128)(2,1)S(1)}, u32[]{:S(2)}, u32[]{:S(2)}) collective-permute-start(bf16[2,2,192,768]{3,2,1,0:T(8,128)(2,1)S(1)} %pad_maximum_fusion.1.refs_5_), channel_id=1, source_target_pairs={{0,8},{8,0},{16,24},{24,16},{1,9},{9,1},{17,25},{25,17},{2,10},{10... | collective-permute-start | bytes 3538952 | tf_op jit(solution)/shard_map/ppermute | solution.py:849
  96.9 25.6 %collective-permute-start.18 = (bf16[2,2,192,768]{3,2,1,0:T(8,128)(2,1)S(1)}, bf16[2,2,192,768]{3,2,1,0:T(8,128)(2,1)S(1)}, u32[]{:S(2)}, u32[]{:S(2)}) collective-permute-start(bf16[2,2,192,768]{3,2,1,0:T(8,128)(2,1)S(1)} %pad_maximum_fusion.1.refs_5_), channel_id=1, source_target_pairs={{0,16},{8,24},{16,0},{24,8},{1,17},{9,25},{17,1},{25,9},{2,18},{10... | collective-permute-start | bytes 3538952 | tf_op jit(solution)/shard_map/ppermute | solution.py:849
  98.7 25.2 %collective-permute-start.22 = (bf16[48,1536]{1,0:T(8,128)(2,1)S(1)}, bf16[48,1536]{1,0:T(8,128)(2,1)S(1)}, u32[]{:S(2)}, u32[]{:S(2)}) collective-permute-start(bf16[48,1536]{1,0:T(8,128)(2,1)S(1)} %maximum_maximum_fusion.1), channel_id=1, source_target_pairs={{0,2},{2,0},{4,6},{6,4},{1,3},{3,1},{5,7},{7,5},{8,10},{10,8},{12,... | collective-permute-start | bytes 442376 | tf_op jit(solution)/shard_map/ppermute | solution.py:849
  98.7 26.6 %collective-permute-start.23 = (bf16[48,1536]{1,0:T(8,128)(2,1)S(1)}, bf16[48,1536]{1,0:T(8,128)(2,1)S(1)}, u32[]{:S(2)}, u32[]{:S(2)}) collective-permute-start(bf16[48,1536]{1,0:T(8,128)(2,1)S(1)} %maximum_maximum_fusion.1), channel_id=1, source_target_pairs={{0,4},{2,6},{4,0},{6,2},{1,5},{3,7},{5,1},{7,3},{8,12},{10,14},{12... | collective-permute-start | bytes 442376 | tf_op jit(solution)/shard_map/ppermute | solution.py:849
  100.7 24.7 %collective-permute-start.24 = (bf16[48,1536]{1,0:T(8,128)(2,1)S(1)}, bf16[48,1536]{1,0:T(8,128)(2,1)S(1)}, u32[]{:S(2)}, u32[]{:S(2)}) collective-permute-start(bf16[48,1536]{1,0:T(8,128)(2,1)S(1)} %maximum_maximum_fusion.1), channel_id=1, source_target_pairs={{0,6},{2,4},{4,2},{6,0},{1,7},{3,5},{5,3},{7,1},{8,14},{10,12},{12... | collective-permute-start | bytes 442376 | tf_op jit(solution)/shard_map/ppermute | solution.py:849
  122.3 18.2 %collective-permute-start.12 = (bf16[320,768]{1,0:T(8,128)(2,1)S(1)}, bf16[320,768]{1,0:T(8,128)(2,1)S(1)}, u32[]{:S(2)}, u32[]{:S(2)}) collective-permute-start(bf16[320,768]{1,0:T(8,128)(2,1)S(1)} %get-tuple-element.149), channel_id=1, source_target_pairs={{0,1},{1,0},{2,3},{3,2},{4,5},{5,4},{6,7},{7,6},{8,9},{9,8},{10,11... | collective-permute-start | bytes 1474568 | tf_op jit(solution)/shard_map/ppermute | solution.py:849
  122.6 15.6 %collective-permute-start.19 = (bf16[2,192,768]{2,1,0:T(8,128)(2,1)S(1)}, bf16[2,192,768]{2,1,0:T(8,128)(2,1)S(1)}, u32[]{:S(2)}, u32[]{:S(2)}) collective-permute-start(bf16[2,192,768]{2,1,0:T(8,128)(2,1)S(1)} %slice_bitcast_fusion.1), channel_id=1, source_target_pairs={{0,16},{8,24},{16,0},{24,8},{1,17},{9,25},{17,1},{25,9},{2,18},{10... | collective-permute-start | bytes 1769480 | tf_op jit(solution)/shard_map/ppermute | solution.py:849
  123.9 15.2 %collective-permute-start.20 = (bf16[2,192,768]{2,1,0:T(8,128)(2,1)S(1)}, bf16[2,192,768]{2,1,0:T(8,128)(2,1)S(1)}, u32[]{:S(2)}, u32[]{:S(2)}) collective-permute-start(bf16[2,192,768]{2,1,0:T(8,128)(2,1)S(1)} %slice_bitcast_fusion), channel_id=1, source_target_pairs={{0,8},{8,0},{16,24},{24,16},{1,9},{9,1},{17,25},{25,17},{2,10},{10... | collective-permute-start | bytes 1769480 | tf_op jit(solution)/shard_map/ppermute | solution.py:849
  139.1 14.3 %collective-permute-start.25 = (bf16[768,384]{1,0:T(8,128)(2,1)S(1)}, bf16[768,384]{1,0:T(8,128)(2,1)S(1)}, u32[]{:S(2)}, u32[]{:S(2)}) collective-permute-start(bf16[768,384]{1,0:T(8,128)(2,1)S(1)} %constant_dynamic-update-slice_fusion.7.refs_2_), channel_id=1, source_target_pairs={{0,8},{8,0},{16,24},{24,16},{1,9},{9,1},{17,25},{25,17},{2,10},{10... | collective-permute-start | bytes 1769480 | tf_op jit(solution)/shard_map/ppermute | solution.py:849
  139.7 13.7 %collective-permute-start.26 = (bf16[768,384]{1,0:T(8,128)(2,1)S(1)}, bf16[768,384]{1,0:T(8,128)(2,1)S(1)}, u32[]{:S(2)}, u32[]{:S(2)}) collective-permute-start(bf16[768,384]{1,0:T(8,128)(2,1)S(1)} %constant_dynamic-update-slice_fusion.7.refs_2_), channel_id=1, source_target_pairs={{0,16},{8,24},{16,0},{24,8},{1,17},{9,25},{17,1},{25,9},{2,18},{10... | collective-permute-start | bytes 1769480 | tf_op jit(solution)/shard_map/ppermute | solution.py:849
  154.2 16.3 %collective-permute-start.27 = (bf16[384,384]{1,0:T(8,128)(2,1)}, bf16[384,384]{1,0:T(8,128)(2,1)S(1)}, u32[]{:S(2)}, u32[]{:S(2)}) collective-permute-start(bf16[384,384]{1,0:T(8,128)(2,1)} %slice.319), channel_id=1, source_target_pairs={{0,16},{8,24},{16,0},{24,8},{1,17},{9,25},{17,1},{25,9},{2,18},{10... | collective-permute-start | bytes 884744 | tf_op jit(solution)/shard_map/ppermute | solution.py:849
  156.0 15.4 %collective-permute-start.28 = (bf16[384,384]{1,0:T(8,128)(2,1)}, bf16[384,384]{1,0:T(8,128)(2,1)}, u32[]{:S(2)}, u32[]{:S(2)}) collective-permute-start(bf16[384,384]{1,0:T(8,128)(2,1)} %slice.320), channel_id=1, source_target_pairs={{0,8},{8,0},{16,24},{24,16},{1,9},{9,1},{17,25},{25,17},{2,10},{10... | collective-permute-start | bytes 884744 | tf_op jit(solution)/shard_map/ppermute | solution.py:849
  157.8 12.7 %collective-permute-start.30 = (bf16[145,768]{1,0:T(8,128)(2,1)}, bf16[145,768]{1,0:T(8,128)(2,1)S(1)}, u32[]{:S(2)}, u32[]{:S(2)}) collective-permute-start(bf16[145,768]{1,0:T(8,128)(2,1)} %bitcast.213), channel_id=1, source_target_pairs={{0,0},{1,2},{2,1},{3,3},{4,8},{5,10},{6,9},{7,11},{8,4},{9,6},{10,... | collective-permute-start | bytes 668168 | tf_op jit(solution)/shard_map/ppermute | solution.py:845
  185.6 27.2 %collective-permute-start.37 = (bf16[768,1536]{1,0:T(8,128)(2,1)}, bf16[768,1536]{1,0:T(8,128)(2,1)}, u32[]{:S(2)}, u32[]{:S(2)}) collective-permute-start(bf16[768,1536]{1,0:T(8,128)(2,1)} %bitcast.57.refs_4_.refs_1_), channel_id=1, source_target_pairs={{0,1},{1,0},{2,3},{3,2},{4,5},{5,4},{6,7},{7,6},{8,9},{9,8},{10,11... | collective-permute-start | bytes 7077896 | tf_op jit(solution)/shard_map/ppermute | solution.py:849
  185.7 27.1 %collective-permute-start.38 = (bf16[1536,768]{1,0:T(8,128)(2,1)}, bf16[1536,768]{1,0:T(8,128)(2,1)}, u32[]{:S(2)}, u32[]{:S(2)}) collective-permute-start(bf16[1536,768]{1,0:T(8,128)(2,1)} %bitcast.58.refs_5_.refs_2_), channel_id=1, source_target_pairs={{0,1},{1,0},{2,3},{3,2},{4,5},{5,4},{6,7},{7,6},{8,9},{9,8},{10,11... | collective-permute-start | bytes 7077896 | tf_op jit(solution)/shard_map/ppermute | solution.py:849
  196.0 14.8 %collective-permute-start.36 = (bf16[192,768]{1,0:T(8,128)(2,1)S(1)}, bf16[192,768]{1,0:T(8,128)(2,1)S(1)}, u32[]{:S(2)}, u32[]{:S(2)}) collective-permute-start(bf16[192,768]{1,0:T(8,128)(2,1)S(1)} %get-tuple-element.187), channel_id=1, source_target_pairs={{0,24},{8,16},{16,8},{24,0},{1,25},{9,17},{17,9},{25,1},{2,26},{10... | collective-permute-start | bytes 884744 | tf_op jit(solution)/shard_map/ppermute | solution.py:849
  212.8 219.5 %reduce-scatter.3.cloned.1.call-start = ((), (), s32[]{:S(2)}) async-start(), calls=%async_computation.2 | async-start | bytes 2949120 | tf_op jit(solution)/shard_map/reduce_scatter | solution.py:1011
  230.9 14.2 %collective-permute-start.40 = (bf16[192,768]{1,0:T(8,128)(2,1)S(1)}, bf16[192,768]{1,0:T(8,128)(2,1)S(1)}, u32[]{:S(2)}, u32[]{:S(2)}) collective-permute-start(bf16[192,768]{1,0:T(8,128)(2,1)S(1)} %get-tuple-element.194), channel_id=1, source_target_pairs={{0,16},{8,24},{16,0},{24,8},{1,17},{9,25},{17,1},{25,9},{2,18},{10... | collective-permute-start | bytes 884744 | tf_op jit(solution)/shard_map/ppermute | solution.py:849
  231.8 13.3 %collective-permute-start.41 = (bf16[192,768]{1,0:T(8,128)(2,1)S(1)}, bf16[192,768]{1,0:T(8,128)(2,1)S(1)}, u32[]{:S(2)}, u32[]{:S(2)}) collective-permute-start(bf16[192,768]{1,0:T(8,128)(2,1)S(1)} %get-tuple-element.195), channel_id=1, source_target_pairs={{0,24},{8,16},{16,8},{24,0},{1,25},{9,17},{17,9},{25,1},{2,26},{10... | collective-permute-start | bytes 884744 | tf_op jit(solution)/shard_map/ppermute | solution.py:849
  256.9 13.3 %collective-permute-start.43 = (bf16[320,768]{1,0:T(8,128)(2,1)S(1)}, bf16[320,768]{1,0:T(8,128)(2,1)S(1)}, u32[]{:S(2)}, u32[]{:S(2)}) collective-permute-start(bf16[320,768]{1,0:T(8,128)(2,1)S(1)} %get-tuple-element.210), channel_id=1, source_target_pairs={{0,8},{8,0},{16,24},{24,16},{1,9},{9,1},{17,25},{25,17},{2,10},{10... | collective-permute-start | bytes 1474568 | tf_op jit(solution)/shard_map/ppermute | solution.py:849
  277.3 31.1 %collective-permute-start.64 = (bf16[2,832,384]{2,1,0:T(8,128)(2,1)}, bf16[2,832,384]{2,1,0:T(8,128)(2,1)S(1)}, u32[]{:S(2)}, u32[]{:S(2)}) collective-permute-start(bf16[2,832,384]{2,1,0:T(8,128)(2,1)} %get-tuple-element.252), channel_id=1, source_target_pairs={{0,16},{8,24},{16,0},{24,8},{1,17},{9,25},{17,1},{25,9},{2,18},{10... | collective-permute-start | bytes 3833864 | tf_op jit(solution)/shard_map/ppermute | solution.py:849
  293.1 40.3 %collective-permute-start.56 = (bf16[2,2,192,768]{3,2,1,0:T(8,128)(2,1)}, bf16[2,2,192,768]{3,2,1,0:T(8,128)(2,1)}, u32[]{:S(2)}, u32[]{:S(2)}) collective-permute-start(bf16[2,2,192,768]{3,2,1,0:T(8,128)(2,1)} %get-tuple-element.242), channel_id=1, source_target_pairs={{0,16},{8,24},{16,0},{24,8},{1,17},{9,25},{17,1},{25,9},{2,18},{10... | collective-permute-start | bytes 3538952 | tf_op jit(solution)/shard_map/ppermute | solution.py:849
  304.2 14.4 %collective-permute-start.46 = (bf16[320,768]{1,0:T(8,128)(2,1)}, bf16[320,768]{1,0:T(8,128)(2,1)}, u32[]{:S(2)}, u32[]{:S(2)}) collective-permute-start(bf16[320,768]{1,0:T(8,128)(2,1)} %get-tuple-element.228), channel_id=1, source_target_pairs={{0,8},{8,0},{16,24},{24,16},{1,9},{9,1},{17,25},{25,17},{2,10},{10... | collective-permute-start | bytes 1474568 | tf_op jit(solution)/shard_map/ppermute | solution.py:849
  310.3 31.7 %collective-permute-start.65 = (bf16[832,384]{1,0:T(8,128)(2,1)}, bf16[832,384]{1,0:T(8,128)(2,1)}, u32[]{:S(2)}, u32[]{:S(2)}) collective-permute-start(bf16[832,384]{1,0:T(8,128)(2,1)} %fusion.10), channel_id=1, source_target_pairs={{0,8},{8,0},{16,24},{24,16},{1,9},{9,1},{17,25},{25,17},{2,10},{10... | collective-permute-start | bytes 1916936 | tf_op jit(solution)/shard_map/ppermute | solution.py:849
  324.3 13.0 %collective-permute-start.47 = (bf16[160,768]{1,0:T(8,128)(2,1)S(1)}, bf16[160,768]{1,0:T(8,128)(2,1)S(1)}, u32[]{:S(2)}, u32[]{:S(2)}) collective-permute-start(bf16[160,768]{1,0:T(8,128)(2,1)S(1)} %get-tuple-element.233), channel_id=1, source_target_pairs={{0,1},{1,0},{2,3},{3,2},{4,5},{5,4},{6,7},{7,6},{8,9},{9,8},{10,11... | collective-permute-start | bytes 737288 | tf_op jit(solution)/shard_map/ppermute | solution.py:849
  324.4 44.2 %collective-permute-start.49 = (bf16[2,768,384]{2,1,0:T(8,128)(2,1)}, bf16[2,768,384]{2,1,0:T(8,128)(2,1)}, u32[]{:S(2)}, u32[]{:S(2)}) collective-permute-start(bf16[2,768,384]{2,1,0:T(8,128)(2,1)} %get-tuple-element.235), channel_id=1, source_target_pairs={{0,8},{8,0},{16,24},{24,16},{1,9},{9,1},{17,25},{25,17},{2,10},{10... | collective-permute-start | bytes 3538952 | tf_op jit(solution)/shard_map/ppermute | solution.py:849
  336.5 40.6 %collective-permute-start.57 = (bf16[2,192,768]{2,1,0:T(8,128)(2,1)}, bf16[2,192,768]{2,1,0:T(8,128)(2,1)S(1)}, u32[]{:S(2)}, u32[]{:S(2)}) collective-permute-start(bf16[2,192,768]{2,1,0:T(8,128)(2,1)} %fusion.12.refs_5_), channel_id=1, source_target_pairs={{0,8},{8,0},{16,24},{24,16},{1,9},{9,1},{17,25},{25,17},{2,10},{10... | collective-permute-start | bytes 1769480 | tf_op jit(solution)/shard_map/ppermute | solution.py:849
  339.1 57.9 %collective-permute-start.48 = (bf16[2,145,768]{2,1,0:T(8,128)(2,1)}, bf16[2,145,768]{2,1,0:T(8,128)(2,1)S(1)}, u32[]{:S(2)}, u32[]{:S(2)}) collective-permute-start(bf16[2,145,768]{2,1,0:T(8,128)(2,1)} %pad_maximum_fusion.6), channel_id=1, source_target_pairs={{0,0},{1,2},{2,1},{3,3},{4,8},{5,10},{6,9},{7,11},{8,4},{9,6},{10,... | collective-permute-start | bytes 1336328 | tf_op jit(solution)/shard_map/ppermute | solution.py:845
  344.5 132.3 %reduce-scatter.5.cloned.1.call-start = ((), (), s32[]{:S(2)}) async-start(), calls=%async_computation.3 | async-start | bytes 798720 | tf_op jit(solution)/shard_map/reduce_scatter | solution.py:977
  370.3 38.7 %collective-permute-start.50 = (bf16[768,384]{1,0:T(8,128)(2,1)S(1)}, bf16[768,384]{1,0:T(8,128)(2,1)S(1)}, u32[]{:S(2)}, u32[]{:S(2)}) collective-permute-start(bf16[768,384]{1,0:T(8,128)(2,1)S(1)} %fusion.11.refs_7_), channel_id=1, source_target_pairs={{0,16},{8,24},{16,0},{24,8},{1,17},{9,25},{17,1},{25,9},{2,18},{10... | collective-permute-start | bytes 1769480 | tf_op jit(solution)/shard_map/ppermute | solution.py:849
  377.3 22.2 %collective-permute-start.58 = (bf16[2,48,768]{2,1,0:T(8,128)(2,1)S(1)}, bf16[2,48,768]{2,1,0:T(8,128)(2,1)S(1)}, u32[]{:S(2)}, u32[]{:S(2)}) collective-permute-start(bf16[2,48,768]{2,1,0:T(8,128)(2,1)S(1)} %get-tuple-element.365), channel_id=1, source_target_pairs={{0,2},{2,0},{4,6},{6,4},{1,3},{3,1},{5,7},{7,5},{8,10},{10,8},{12,... | collective-permute-start | bytes 442376 | tf_op jit(solution)/shard_map/ppermute | solution.py:849
  379.7 23.1 %collective-permute-start.59 = (bf16[2,48,768]{2,1,0:T(8,128)(2,1)S(1)}, bf16[2,48,768]{2,1,0:T(8,128)(2,1)S(1)}, u32[]{:S(2)}, u32[]{:S(2)}) collective-permute-start(bf16[2,48,768]{2,1,0:T(8,128)(2,1)S(1)} %get-tuple-element.364), channel_id=1, source_target_pairs={{0,4},{2,6},{4,0},{6,2},{1,5},{3,7},{5,1},{7,3},{8,12},{10,14},{12... | collective-permute-start | bytes 442376 | tf_op jit(solution)/shard_map/ppermute | solution.py:849
  379.7 29.4 %collective-permute-start.60 = (bf16[2,48,768]{2,1,0:T(8,128)(2,1)S(1)}, bf16[2,48,768]{2,1,0:T(8,128)(2,1)S(1)}, u32[]{:S(2)}, u32[]{:S(2)}) collective-permute-start(bf16[2,48,768]{2,1,0:T(8,128)(2,1)S(1)} %get-tuple-element.363), channel_id=1, source_target_pairs={{0,6},{2,4},{4,2},{6,0},{1,7},{3,5},{5,3},{7,1},{8,14},{10,12},{12... | collective-permute-start | bytes 442376 | tf_op jit(solution)/shard_map/ppermute | solution.py:849
  399.5 49.6 %collective-permute-start.68 = (bf16[768,1536]{1,0:T(8,128)(2,1)}, bf16[768,1536]{1,0:T(8,128)(2,1)}, u32[]{:S(2)}, u32[]{:S(2)}) collective-permute-start(bf16[768,1536]{1,0:T(8,128)(2,1)} %get-tuple-element.236), channel_id=1, source_target_pairs={{0,1},{1,0},{2,3},{3,2},{4,5},{5,4},{6,7},{7,6},{8,9},{9,8},{10,11... | collective-permute-start | bytes 7077896 | tf_op jit(solution)/shard_map/ppermute | solution.py:849
  399.5 49.6 %collective-permute-start.69 = (bf16[1536,768]{1,0:T(8,128)(2,1)}, bf16[1536,768]{1,0:T(8,128)(2,1)}, u32[]{:S(2)}, u32[]{:S(2)}) collective-permute-start(bf16[1536,768]{1,0:T(8,128)(2,1)} %get-tuple-element.256), channel_id=1, source_target_pairs={{0,1},{1,0},{2,3},{3,2},{4,5},{5,4},{6,7},{7,6},{8,9},{9,8},{10,11... | collective-permute-start | bytes 7077896 | tf_op jit(solution)/shard_map/ppermute | solution.py:849
  409.7 13.4 %collective-permute-start.52 = (bf16[48,1536]{1,0:T(8,128)(2,1)S(1)}, bf16[48,1536]{1,0:T(8,128)(2,1)S(1)}, u32[]{:S(2)}, u32[]{:S(2)}) collective-permute-start(bf16[48,1536]{1,0:T(8,128)(2,1)S(1)} %get-tuple-element.367), channel_id=1, source_target_pairs={{0,4},{2,6},{4,0},{6,2},{1,5},{3,7},{5,1},{7,3},{8,12},{10,14},{12... | collective-permute-start | bytes 442376 | tf_op jit(solution)/shard_map/ppermute | solution.py:849
  448.9 25.9 %collective-permute-start.63 = (f32[24,1536]{1,0:T(8,128)S(1)}, f32[24,1536]{1,0:T(8,128)S(1)}, u32[]{:S(2)}, u32[]{:S(2)}) collective-permute-start(f32[24,1536]{1,0:T(8,128)S(1)} %get-tuple-element.388), channel_id=1, source_target_pairs={{0,1},{1,0},{2,3},{3,2},{4,5},{5,4},{6,7},{7,6},{8,9},{9,8},{10,11... | collective-permute-start | bytes 442376 | tf_op jit(solution)/shard_map/ppermute | solution.py:849
  (100 other events, 651.1 us)
Sparse Core Ops, SparseCore 0:
  212.9 86.4 all-gather.2
  343.8 77.2 reduce-scatter.2
  444.5 20.7 reduce-scatter.4

commit v4 on v3

--- a/solution.py
+++ b/solution.py
@@ -227,7 +227,7 @@
         c.wait()
 
 
-def attend_copies(e, refs, w_ref, p_ref, small_ref, sems):
+def attend_copies(e, refs, w_ref, p_ref, small_ref, sems, skip):
     copies = []
 
     def add(src, dst):
@@ -239,7 +239,7 @@
     for j in range(4):
         to = e ^ j
         rows, prows = pl.ds(pl.multiple_of(to * n, 16), n), pl.ds(pl.multiple_of(to * m, 16), m)
-        a, b, at = (refs[j], refs[j], 2 * n) if j < 3 else (refs[3], refs[4], 0)
+        a, b, at = (refs[j], refs[j], 2 * n + skip) if j < 3 else (refs[3], refs[4], 0)
         for g in range(2):
             add(a.at[pl.ds(g * n, n)], w_ref.at[rows, pl.ds(g * half, half)])
         add(b.at[pl.ds(at, n)], w_ref.at[rows, pl.ds(2 * half, half)])
@@ -252,7 +252,7 @@
     return copies
 
 
-def attend_first(where, tokens, small_rows, blocks, rows, after=()):
+def attend_first(where, tokens, small_rows, blocks, rows, skip, after=()):
     blk_len, feat = tokens[0].shape
     half = feat // 2
     r2 = 2 * rows
@@ -262,7 +262,7 @@
         take = lambda n: [refs.pop(0) for _ in range(n)]
         tok, block_refs = take(4), take(5)
         x_ref, normed_ref, q_ref, kv_ref, far_ref, w_ref, p_ref, small_ref, rows_ref, all_ref, sems = take(11)
-        copies = attend_copies(where_ref[1], block_refs, w_ref, p_ref, small_ref, sems)
+        copies = attend_copies(where_ref[1], block_refs, w_ref, p_ref, small_ref, sems, skip)
         start_all(copies)
         all_ref[...] = jnp.zeros_like(all_ref)
         for j in range(4):
@@ -314,33 +314,42 @@
     )
 
 
-def attend_next(where, normed, blocks, after=()):
+def attend_next(where, normed, source, after=()):
     r2, feat = normed.shape
     half = feat // 2
-
-    def kernel(where_ref, normed_ref, *refs):
-        refs = list(refs)
-        take = lambda n: [refs.pop(0) for _ in range(n)]
-        block_refs = take(5)
-        q_ref, kv_ref, w_ref, p_ref, sems = take(5)
-        copies = attend_copies(where_ref[1], block_refs, w_ref, p_ref, None, sems)
-        start_all(copies)
-        wait_all(copies)
+    packed = source.ndim == 4
+
+    def kernel(where_ref, normed_ref, source_ref, q_ref, kv_ref, *more):
+        if packed:
+            w_ref, sems = more
+            r = source_ref.shape[2] // 4
+            copies = []
+            for c in range(4):
+                for j in range(4):
+                    at = pl.multiple_of((where_ref[1] ^ j) * (feat // 4) + c * r, 16)
+                    for g in range(3):
+                        copies.append(pltpu.make_async_copy(
+                            source_ref.at[c, j, pl.ds(g * r, r)],
+                            w_ref.at[pl.ds(at, r), pl.ds(g * half, half)], sems.at[len(copies)],
+                        ))
+            start_all(copies)
+            wait_all(copies)
+        else:
+            w_ref = source_ref
         normed = normed_ref[...]
         q_ref[...] = dot(normed, w_ref[:, :half]).astype(BF)
         kv_ref[...] = dot(normed, w_ref[:, half:]).astype(BF)
 
-    return call(
+    out = call(
         kernel,
-        [
-            ((r2, half), BF, VM), ((r2, feat), BF, VM), ((feat, 3 * half), BF, VM), ((half, feat), BF, VM),
-        ],
-        [(where, SM), (normed, VM)] + [(t, HB) for t in blocks],
-        scratch=[pltpu.SemaphoreType.DMA((20,))],
+        [((r2, half), BF, VM), ((r2, feat), BF, VM)] + ([((feat, 3 * half), BF, VM)] if packed else []),
+        [(where, SM), (normed, VM), (source, HB if packed else VM)],
+        scratch=[pltpu.SemaphoreType.DMA((48,))] if packed else [],
         after=after,
         flops=2 * r2 * feat * 3 * half,
-        bytes_accessed=5 * 2**20,
-    )
+        bytes_accessed=4 * 2**20,
+    )
+    return out if packed else [*out, source]
 
 
 def widen_forward(where, x, part, got, gains, blocks, rows, after=()):
@@ -461,7 +470,7 @@
     )
 
 
-def attend_proj_back(where, dq, own, got, normed, w, wps, small, first, rows, last, after=()):
+def attend_proj_back(where, dq, own, got, normed, w, wps, small, firsts, rows, last, after=()):
     r2, feat = normed.shape
     half = feat // 2
     n, m = feat // 4, half // 4
@@ -472,7 +481,9 @@
         refs = list(refs)
         take = lambda k: [refs.pop(0) for _ in range(k)]
         small_ref = take(1)[0] if extra else None
-        out_ref, low_ref, keep_ref, send_ref, packed_ref, turned_ref, ws_ref, sm_ref, sems = take(9)
+        out_ref, low_ref = take(2)
+        sides = [take(2) for _ in firsts]
+        packed_ref, turned_ref, ws_ref, sm_ref, sems = take(5)
         packed_ref[:, :half] = dq_ref[...]
         packed_ref[:, half:] = (own_ref[...] + got_ref[...].astype(F32)).astype(BF)
         out = dot_t(packed_ref[...], w_ref[...])
@@ -495,26 +506,35 @@
         def add(src, dst):
             copies.append(pltpu.make_async_copy(src, dst, sems.at[len(copies)]))
 
-        for ref, js in ((keep_ref, (0, 3 - first)), (send_ref, (first, 3))):
-            for i, j in enumerate(js):
-                to = where_ref[1] ^ j
-                at, pat = pl.ds(pl.multiple_of(to * n, 16), n), pl.ds(pl.multiple_of(to * m, 16), m)
-                for g in range(3):
-                    add(ws_ref.at[at, pl.ds(g * half, half)], ref.at[i, pl.ds(g * n, n)])
-                for g in range(2):
-                    add(wps_ref.at[pat, pl.ds(g * half, half)], ref.at[i, pl.ds(3 * n + g * m, m)])
-                if extra:
+        for lane, first in enumerate(firsts):
+            one = len(firsts) == 1
+            skip = 2 * n if lane == 1 else 0
+            for ref, js in zip(sides[lane], ((0, 3 - first), (first, 3))):
+                for i, j in enumerate(js):
+                    to = where_ref[1] ^ j
+                    at, pat = pl.ds(pl.multiple_of(to * n, 16), n), pl.ds(pl.multiple_of(to * m, 16), m)
                     for g in range(3):
-                        sat = pl.ds(pl.multiple_of(to * n + g * extra, 16), extra)
-                        add(sm_ref.at[sat], ref.at[i, pl.ds(3 * n + 2 * m, extra), pl.ds(128 * g, 128)])
+                        if one or (g == 2) == (lane == 1):
+                            add(ws_ref.at[at, pl.ds(g * half, half)], ref.at[i, pl.ds(g * n - skip, n)])
+                    for g in range(2):
+                        if one or lane == 1:
+                            add(
+                                wps_ref.at[pat, pl.ds(g * half, half)],
+                                ref.at[i, pl.ds(3 * n + g * m - skip, m)],
+                            )
+                    if extra:
+                        for g in range(3):
+                            sat = pl.ds(pl.multiple_of(to * n + g * extra, 16), extra)
+                            add(sm_ref.at[sat], ref.at[i, pl.ds(3 * n + 2 * m, extra), pl.ds(128 * g, 128)])
         start_all(copies)
         wait_all(copies)
 
     n_out = rows if last else r2
-    block = ((2, 3 * n + 2 * m + extra, half), BF, HB)
+    deep = 3 * n + 2 * m + extra
+    deeps = [deep] * 2 if len(firsts) == 1 else [2 * n] * 2 + [n + 2 * m] * 2
     return call(
         kernel,
-        [((n_out, feat), F32, VM), ((n_out, feat), BF, VM), block, block],
+        [((n_out, feat), F32, VM), ((n_out, feat), BF, VM)] + [((2, k, half), BF, HB) for k in deeps],
         [(where, SM), (dq, VM), (own, VM), (got, VM), (normed, VM), (w, VM), (wps, VM)]
         + ([(small, VM)] if extra else []),
         scratch=[
@@ -632,22 +652,18 @@
     )
 
 
-def expert_half(blocks, w_in, w_out, acc, cap_rows, after=()):
-    feat = w_in.shape[0]
-    wide = w_in.shape[1]
+def experts_forward(blocks, own, sib, cap_rows, after=()):
+    feat, wide = own[0].shape
     tile = 512 if wide % 512 == 0 else wide
     n = len(blocks) * cap_rows
     steps = wide // tile
-    final = acc is not None
 
     def kernel(*refs):
         refs = list(refs)
         take = lambda k: [refs.pop(0) for _ in range(k)]
-        ins = take(len(blocks))
-        wi_ref, wo_ref = take(2)
-        before = take(2) if final else None
+        ins, weights = take(len(blocks)), take(4)
         take(len(after))
-        outs = take(len(blocks)) if final else take(2)
+        outs = take(len(blocks))
         rows_ref, slope_ref, res_ref, back_ref = take(4)
         t = pl.program_id(0)
 
@@ -657,46 +673,44 @@
                 at = pl.ds(j * cap_rows, cap_rows)
                 rows_ref[at, :] = ref[pl.ds(0, cap_rows), :]
                 slope_ref[at, :] = ref[pl.ds(cap_rows, cap_rows), :]
-            if final:
-                res_ref[...] = before[0][...]
-                back_ref[...] = before[1][...]
-            else:
-                res_ref[...] = jnp.zeros_like(res_ref)
-                back_ref[...] = jnp.zeros_like(back_ref)
-
-        act, dact = gelu_both(dot(rows_ref[...], wi_ref[...]))
-        hs = (dact * dot_t(slope_ref[...], wo_ref[...])).astype(BF)
-        res_ref[...] += dot(act.astype(BF), wo_ref[...])
-        back_ref[...] += dot_t(hs, wi_ref[...])
-
-        @pl.when(t == steps - 1)
+            res_ref[...] = jnp.zeros_like(res_ref)
+            back_ref[...] = jnp.zeros_like(back_ref)
+
+        def step(wi_ref, wo_ref):
+            act, dact = gelu_both(dot(rows_ref[...], wi_ref[...]))
+            hs = (dact * dot_t(slope_ref[...], wo_ref[...])).astype(BF)
+            res_ref[...] += dot(act.astype(BF), wo_ref[...])
+            back_ref[...] += dot_t(hs, wi_ref[...])
+
+        @pl.when(t < steps)
         def _():
-            if final:
-                for j, ref in enumerate(outs):
-                    at = pl.ds(j * cap_rows, cap_rows)
-                    ref[pl.ds(0, cap_rows), :] = res_ref[at, :].astype(BF)
-                    ref[pl.ds(cap_rows, cap_rows), :] = back_ref[at, :].astype(BF)
-            else:
-                outs[0][...] = res_ref[...]
-                outs[1][...] = back_ref[...]
-
-    whole = lambda shape: pl.BlockSpec(shape, lambda t: (0,) * len(shape))
+            step(*weights[:2])
+
+        @pl.when(t >= steps)
+        def _():
+            step(*weights[2:])
+
+        @pl.when(t == 2 * steps - 1)
+        def _():
+            for j, ref in enumerate(outs):
+                at = pl.ds(j * cap_rows, cap_rows)
+                ref[pl.ds(0, cap_rows), :] = res_ref[at, :].astype(BF)
+                ref[pl.ds(cap_rows, cap_rows), :] = back_ref[at, :].astype(BF)
+
     blk = (2 * cap_rows, feat)
-    ins = [*blocks, w_in, w_out] + (list(acc) if final else []) + list(after)
-    in_specs = [whole(blk)] * len(blocks) + [
-        pl.BlockSpec((feat, tile), lambda t: (0, t)), pl.BlockSpec((tile, feat), lambda t: (t, 0))
-    ]
-    in_specs += [whole((n, feat))] * (2 if final else 0) + [HB] * len(after)
-    if final:
-        shapes, specs = [jax.ShapeDtypeStruct(blk, BF)] * len(blocks), [whole(blk)] * len(blocks)
-    else:
-        shapes, specs = [jax.ShapeDtypeStruct((n, feat), F32)] * 2, [whole((n, feat))] * 2
+    whole = pl.BlockSpec(blk, lambda t: (0, 0))
+    first = lambda t: jnp.minimum(t, steps - 1)
+    later = lambda t: jnp.maximum(t - steps, 0)
+    specs = []
+    for place in (first, later):
+        specs.append(pl.BlockSpec((feat, tile), lambda t, place=place: (0, place(t))))
+        specs.append(pl.BlockSpec((tile, feat), lambda t, place=place: (place(t), 0)))
     return pl.pallas_call(
         kernel,
-        grid=(steps,),
-        out_shape=shapes,
-        in_specs=in_specs,
-        out_specs=specs,
+        grid=(2 * steps,),
+        out_shape=[jax.ShapeDtypeStruct(blk, BF)] * len(blocks),
+        in_specs=[whole] * len(blocks) + specs + [HB] * len(after),
+        out_specs=[whole] * len(blocks),
         scratch_shapes=[
             pltpu.VMEM((n, feat), BF), pltpu.VMEM((n, feat), BF),
             pltpu.VMEM((n, feat), F32), pltpu.VMEM((n, feat), F32),
@@ -705,14 +719,14 @@
             vmem_limit_bytes=50 * 2**20, dimension_semantics=("arbitrary",)
         ),
         cost_estimate=pl.CostEstimate(
-            flops=8 * n * feat * wide, bytes_accessed=10 * 2**20, transcendentals=0
+            flops=16 * n * feat * wide, bytes_accessed=20 * 2**20, transcendentals=0
         ),
-    )(*ins)
+    )(*blocks, *own, *sib, *after)
 
 
 def expert_slopes(every, w_in, w_out, got, after=()):
     feat, wide = w_in.shape
-    tile = 256 if wide % 256 == 0 else wide
+    tile = 512 if wide % 512 == 0 else wide
     steps = wide // tile
     groups, experts, cap_rows = every.shape[0], every.shape[1], every.shape[2] // 2
     total = groups * experts * cap_rows
@@ -738,8 +752,11 @@
                             sems.at[len(copies)],
                         ))
             start_all(copies)
-            wait_all(copies)
-            turned_ref[...] = rows_ref[...].T
+            per = total // groups
+            for k in range(groups):
+                wait_all(copies[k * 2 * experts : (k + 1) * 2 * experts])
+                at = pl.ds(k * per, per)
+                turned_ref[:, at] = rows_ref[at, :].T
 
         act, dact = gelu_both(dot(rows_ref[...], wi_ref[...]))
         hs = (dact * dot_t(slope_ref[...], wo_ref[...])).astype(BF)
@@ -899,7 +916,6 @@
     def __init__(self, links, rdev, feat, ff):
         self.links, self.rdev, self.feat, self.ff = links, rdev, feat, ff
         self.d = lax.axis_index("dp")
-        self.given = []
         self.half = feat // 2
 
     def split_attend(self, w):
@@ -928,12 +944,14 @@
     def cut(self, x):
         return x if self.links.fast else x.reshape(4, -1, x.shape[-1])
 
-    def pack_block(self, quad):
+    def pack_block(self, quad, between):
         f, h, r = self.feat, self.half, self.rdev
         n = quad.shape[0]
         p = quad[..., f + h : 2 * f].reshape(n, 2, r, h)
         parts = [quad[..., i * h : (i + 1) * h] for i in range(3)] + [p[:, 0], p[:, 1]]
         parts = [self.cut(t.reshape(-1, h)) for t in parts]
+        if self.links.fast:
+            parts.insert(2, between)
         if quad.shape[2] > 2 * f:
             small = self.cut(quad[..., 2 * f :].reshape(-1, 128))
             small = small.reshape(small.shape[:-2] + (3, -1, 128))
@@ -955,8 +973,8 @@
         x1, x2 = tie([to(x, 1), to(x, 2)], *hold)
         return [x, x1, x2, to(cuts[0](x1), 2), to(cuts[1](x2), 1)]
 
-    def spread_attend(self, x, *hold):
-        n = self.feat // 2
+    def spread_attend(self, x, skip, *hold):
+        n = self.feat // 2 + skip
         return self.spread(x, (lambda t: t[:n], lambda t: t[n:]), *hold)
 
     def spread_pair(self, x, *hold):
@@ -964,17 +982,13 @@
 
     def total(self, keep, send, first, hold):
         if self.links.fast:
-            out, give = self.links.plane_sum(keep, send, first, hold)
-            self.given.append(give)
+            out, _ = self.links.plane_sum(keep, send, first, hold)
             return out
         blk = {0: keep[0], 3 - first: keep[1], first: send[0], 3: send[1]}
         return jnp.stack([blk[j] for j in range(4)])
 
-    def column_sum(self, buf, hold):
-        if self.links.fast and hold is not None:
-            return self.links.column_sum(buf, *hold)
-        axes = "context" if self.links.fast else CHIPS
-        return lax.psum_scatter(buf.astype(BF), axes, scatter_dimension=0, tiled=False).astype(F32)
+    def all_sum(self, buf):
+        return lax.psum_scatter(buf.astype(BF), CHIPS, scatter_dimension=0, tiled=False).astype(F32)
 
     def exchange(self, w):
         w = w.reshape(2, self.rdev, -1)
@@ -982,51 +996,37 @@
         got = self.links.sib(lax.dynamic_index_in_dim(w, 1 - self.d, 0, False))
         return in_order(self.d, mine, got)
 
-    def owner_attend(self, keep, send, first, hold, after=()):
-        f, h, r = self.feat, self.half, self.rdev
-        t = self.total(keep, send, first, hold)
-        n, m = f // 4, h // 4
+    def to_columns(self, t):
+        n, m = self.feat // 4, self.half // 4
+        r = self.rdev
         cut = lambda t, k: t.reshape(-1, k * r, t.shape[-1])
         parts = [cut(t[..., g * n : (g + 1) * n, :], 2) for g in range(3)]
         p = [cut(t[..., 3 * n + g * m : 3 * n + (g + 1) * m, :], 1) for g in range(2)]
         parts.append(jnp.concatenate(p, 1))
-        small = t.shape[-2] > 3 * n + 2 * m
-        if small:
+        if t.shape[-2] > 3 * n + 2 * m:
             sm = t[..., 3 * n + 2 * m :, :]
             sm = jnp.stack([sm[..., 128 * g : 128 * (g + 1)] for g in range(3)], -3)
             parts.append(sm.reshape(-1, 2 * r, 128))
-        (buf,) = tie([jnp.concatenate(parts, 2)], *after)
-        buf = self.column_sum(buf, hold[2])
+        return jnp.concatenate(parts, 2)
+
+    def owner_attend(self, buf):
+        f, h, r = self.feat, self.half, self.rdev
         p = jnp.concatenate([buf[:r, f + h : 2 * f], buf[r:, f + h : 2 * f]], 1)
         p = lax.ppermute(p, ALL, self.links.from_lane)
         w = buf[:, : f + h]
-        if small:
+        if buf.shape[1] > 2 * f:
             w = jnp.concatenate([w, buf[:, 2 * f :]], 1)
         w = self.exchange(w)
         extra = w[0, :, f + h :] + w[1, :, f + h :]
         w = w[..., : f + h].reshape(2, r, 3, h).transpose(1, 2, 0, 3).reshape(r, 3 * f)
         return w, p, extra
 
-    def reduce_column(self, by_context):
-        t = lax.psum_scatter(by_context, "context", scatter_dimension=0, tiled=False)
-        return t[:2], t[2:]
-
-    def owner_wide(self, slopes, first, hold):
-        f, r = self.feat, self.rdev
-        a = self.total(*slopes[:2], first, hold[0])
-        if self.links.fast:
-            a = jnp.moveaxis(a.reshape(2, 4, 2 * r, f), 1, 0)
-            a = self.column_sum(a, hold[0][2])
-            b = self.total(*slopes[2:], first, hold[1])
-            w = jnp.concatenate([a[0], b[0]], 1)
-            w_out = jnp.concatenate([a[1], b[1]], 0)
-        else:
-            b = self.total(*slopes[2:], first, hold[1])
-            hid = self.ff // (4 * self.links.chips)
-            w = [t[..., 0, :, :].reshape(-1, 2 * r, f) for t in (a, b)]
-            w_out = [t[..., 1, :, :].reshape(-1, hid, f) for t in (a, b)]
-            w, w_out = [self.column_sum(jnp.concatenate(t, 2), None) for t in (w, w_out)]
-            w_out = jnp.concatenate([w_out[:, :f], w_out[:, f:]], 0)
+    def pair_columns(self, t):
+        t = t.reshape(2, 4, 2 * self.rdev, self.feat)
+        return jnp.concatenate([t[0], t[1]], 2)
+
+    def owner_wide(self, w, w_out):
+        r = self.rdev
         w = self.exchange(w).reshape(2, r, 2, self.links.chips, -1)
         return w.transpose(1, 3, 0, 2, 4).reshape(r, self.ff), w_out
 
@@ -1059,84 +1059,124 @@
     lane1 = lane_rows(links, lane1, d)
     buf1 = wt.pack_attend(lane1[:, : 3 * half], ps[:rdev], lane1[:, 3 * half :])
     quad1 = wt.column(buf1)
-    tok_pair = jnp.stack([tok, links.partner(tok)])
-    tok_sib = links.sib(tok_pair)
-    toks = [tok_pair[0], tok_sib[0], tok_pair[1], tok_sib[1]]
-    blocks1 = wt.spread_attend(wt.pack_block(quad1))
-
     later = jnp.concatenate([wt.split_widen(win), wt.split_attend(w3)], 2)
     later = lane_rows(links, later, d)
     w_in, w_out = later[:, : ff // 2], wt.pack_wide(wout)
-    buf3 = wt.pack_attend(later[:, ff // 2 :], ps[rdev:], None)
-
-    x0, normed1, q1, kv1, far1, wa1, wp1, small, gains = attend_first(where, toks, small_rows, blocks1, rows)
-    part, low, blend1, lse1 = attend_core(where, q1, kv1, far1, wp1, solo=False, **img)
+    w3_lane, p3_lane = later[:, ff // 2 :], ps[rdev:]
+    block3 = jnp.concatenate(
+        [w3_lane[:, g * half : (g + 1) * half] for g in range(3)] + [p3_lane[:, :half], p3_lane[:, half:]], 0
+    )
+    skip = block3.shape[0] if links.fast else 0
+    tok_pair = jnp.stack([tok, links.partner(tok)])
+    block1 = wt.pack_block(tie([quad1], tok_pair)[0], block3)
     if links.fast:
         (buf2,) = tie([jnp.concatenate([w_in, w_out], 1)], quad1)
-        quad2 = wt.column(buf2, part)
-        quad2 = quad2[..., : ff // 2], quad2[..., ff // 2 :]
+        quad2 = wt.column(buf2)
+        blocks1 = wt.spread_attend(block1, skip, quad2)
+        (tok_pair,) = tie([tok_pair], *blocks1[1:3])
     else:
-        quad2 = wt.column(w_in), wt.column(w_out)
-    pair2 = wt.pack_pair(*quad2)
-    blocks2 = wt.spread_pair(pair2)
-    quad3 = wt.column(tie([buf3], pair2)[0], *blocks2[1:3])
-    cot, raw = tie([cotangent[0].astype(BF), jnp.concatenate([routes[0], slots[0]], 1)], quad3)
-    raw, cot = tie([links.move(raw), links.move(cot)], blocks2[3])
+        quad2 = None
+        blocks1 = wt.spread_attend(block1, skip)
+    tok_sib = links.sib(tok_pair)
+    toks = [tok_pair[0], tok_sib[0], tok_pair[1], tok_sib[1]]
+    cot, raw = tie([cotangent[0].astype(BF), jnp.concatenate([routes[0], slots[0]], 1)], *blocks1[1:3])
+    raw, cot = links.move(raw), links.move(cot)
     index = jnp.pad(raw, ((0, rows - blk_len), (0, 0)), constant_values=cap)
+    if links.fast:
+        (quad2,) = tie([quad2], *blocks1[3:], *toks, cot, index)
+        pair2 = wt.pack_pair(quad2[..., : ff // 2], quad2[..., ff // 2 :])
+        q, n = feat // 2, block3.shape[0]
+        place3 = jnp.stack([t[q : q + n] for t in blocks1[:4]])
+        source3 = lax.all_gather(place3, "context", axis=0, tiled=False)
+        p3 = source3[:, :, 6 * rdev :].reshape(4, 4, 2, rdev, half)
+        p3 = jnp.stack([lax.dynamic_index_in_dim(p3, e ^ k, 1, False) for k in range(4)])
+        wp3 = p3.transpose(0, 1, 3, 2, 4).reshape(half, feat)
+    else:
+        pair2 = wt.pack_pair(wt.column(w_in), wt.column(w_out))
+        all3 = lax.all_gather(block3, CHIPS, axis=0, tiled=False)
+        source3 = all3[:, : 6 * rdev].reshape(links.chips, 3, 2 * rdev, half)
+        source3 = source3.transpose(0, 2, 1, 3).reshape(feat, 3 * half)
+        wp3 = all3[:, 6 * rdev :].reshape(links.chips, 2, rdev, half)
+        wp3 = wp3.transpose(0, 2, 1, 3).reshape(half, feat)
+
+    x0, normed1, q1, kv1, far1, wa1, wp1, small, gains = attend_first(
+        where, toks, small_rows, blocks1, rows, skip
+    )
+    part, low, blend1, lse1 = attend_core(
+        where, q1, kv1, far1, wp1, solo=False, **img
+    )
+    blocks2 = wt.spread_pair(pair2, part)
     x1, normed2, hidden, part2, low2, wi, wo = widen_forward(
         where, x0, part, links.sib(low), gains, blocks2, rows
     )
-    blocks3 = wt.spread_attend(tie([wt.pack_block(quad3)], *blocks2[3:])[0], x1)
     x2, normed3, own3 = norm_next(x1, part2, links.sib(low2), gains, 2, rows)
+    ein_own, eout_own = ein[0], eout[0]
+    ein_sib, eout_sib = [links.sib(t) for t in tie([ein_own, eout_own], x1)]
     far_own = links.partner(own3)
-    q3, kv3, wa3, wp3 = attend_next(where, normed3, blocks3, after=(cot, index))
+    q3, kv3, wa3 = attend_next(where, normed3, source3)
     (far_own,) = tie([far_own], q3)
     part3, low3, blend3, lse3, far3 = attend_core(
-        where, q3, kv3, None, wp3, solo=True, far=(far_own, links.sib(far_own), wa3), **img
+        where, q3, kv3, None, wp3, solo=True, far=(far_own, links.sib(far_own), wa3),
+        after=(ein_sib, eout_sib), **img
     )
     moe_args = dict(experts=experts, cap=cap, fast=links.fast, **img)
     x3, moe, gates, up, *sent = route(
         where, x2, part3, links.sib(low3), gains, small, cot, index, **moe_args
     )
-    ein_own, eout_own = ein[0], eout[0]
-    ein_sib, eout_sib = [links.sib(t) for t in tie([ein_own, eout_own], low3)]
     came = links.swap_blocks(sent)
     every = lax.all_gather(jnp.stack(came), "context", axis=0, tiled=False)
-    sums = expert_half(came, ein_sib, eout_sib, None, up16(cap))
-    answer = links.swap_blocks(expert_half(came, ein_own, eout_own, sums, up16(cap)))
+    answer = experts_forward(came, (ein_own, eout_own), (ein_sib, eout_sib), up16(cap))
+    answer = links.swap_blocks(answer)
     acts, u, u_low, small_slopes = combine(
         where, answer, x3, moe, gates, up, index, small, gains, small_rows, **moe_args
     )
 
     u, u_low = join_upstream(u, links.sib(u_low), rows)
     dq, own, far, wps = attend_core_back(where, u_low, wp3, blend3, q3, kv3, far3, lse3, **img)
-    first3, first2, first1 = 2, 2, 1
+    first3, first2, first1 = (1,), 2, (1, 2)
     part, low, *slopes3 = attend_proj_back(
         where, dq, own, links.partner(far), normed3, wa3, wps, small_slopes, first3, rows, False
     )
     u, part, low, *slopes2 = widen_back(
-        where, u, x2, gains, part, links.sib(low), normed2, hidden, wi, wo, first2, rows, links.fast
+        where, u, x2, gains, part, links.sib(low), normed2, hidden, wi, wo, first2, rows, False
     )
     u1, u_low = norm_step(u, x1, gains, 1, part, links.sib(low), rows, 0)
     dq1, own, far, wps = attend_core_back(where, u_low, wp1, blend1, q1, kv1, far1, lse1, **img)
     part, low, *slopes1 = attend_proj_back(
-        where, dq1, own, links.partner(far), normed1, wa1, wps, None, first1, rows, True
+        where, dq1, own, links.partner(far), normed1, wa1, wps, None, first1, rows, True, after=(every,)
     )
     (u2,) = norm_step(u1, x0, gains, 0, part, links.sib(low), rows, blk_len)
     moved = links.move(jnp.stack([acts, u2]))
     acts, token_slope = moved[0], moved[1]
+    e_sib = expert_slopes(every, ein_sib, eout_sib, None, after=(u2,))
+    sum3 = wt.total(*slopes3, first3[0], ((low,), (e_sib[0],)))
+    sum2a = wt.total(*slopes2[:2], first2, ((low,), (e_sib[0],)))
+    sum2b = wt.total(*slopes2[2:], first2, ((e_sib[0],), ()))
+    sum1 = [wt.total(*slopes1[2 * i : 2 * i + 2], first1[i], ((e_sib[0],), ())) for i in range(2)]
+    col3, col1 = wt.to_columns(sum3), wt.to_columns(jnp.concatenate(sum1, -2))
     if links.fast:
-        (by_context,) = tie(slopes2[2:], every)
-        slopes2 = slopes2[:2] + list(wt.reduce_column(by_context))
-        after3 = slopes2[2:]
+        col2a, col2b = wt.pair_columns(sum2a), wt.pair_columns(sum2b)
+        early = jnp.concatenate([col3, col2a], 2).astype(BF)
+        early = lax.psum_scatter(tie([early], every)[0], "context", scatter_dimension=0, tiled=False)
+        early = early.astype(F32)
+        col3, col2a = early[:, : col3.shape[2]], early[:, col3.shape[2] :]
+        late = jnp.concatenate([col2b, col1], 2)
+        e_slopes = expert_slopes(every, ein_own, eout_own, [links.sib(t) for t in e_sib], after=(late,))
+        late = links.column_sum(late, e_slopes[0])
+        col2b, col1 = late[:, : 2 * feat], late[:, 2 * feat :]
+        w2 = jnp.concatenate([col2a[:, :feat], col2b[:, :feat]], 1)
+        w2_out = jnp.concatenate([col2a[:, feat:], col2b[:, feat:]], 0)
     else:
-        after3 = ()
-    e_sib = expert_slopes(every, ein_sib, eout_sib, None, after=(u2,))
-    w3_out, p3_out, extra = wt.owner_attend(*slopes3, first3, ((u,), (dq1,), None), after=after3)
-    wt.given = []
-    win_out, wout_out = wt.owner_wide(slopes2, first2, (((dq1,), (e_sib[0],), ()), ((e_sib[0],), (), ())))
-    w1_out, p1_out, _ = wt.owner_attend(*slopes1, first1, ((e_sib[0],), (), ()))
-    e_slopes = expert_slopes(every, ein_own, eout_own, [links.sib(t) for t in e_sib], after=wt.given)
+        e_slopes = expert_slopes(every, ein_own, eout_own, [links.sib(t) for t in e_sib])
+        col3, col1 = wt.all_sum(col3), wt.all_sum(col1)
+        hid = ff // (4 * links.chips)
+        w2 = [t[..., 0, :, :].reshape(-1, 2 * rdev, feat) for t in (sum2a, sum2b)]
+        w2_out = [t[..., 1, :, :].reshape(-1, hid, feat) for t in (sum2a, sum2b)]
+        w2, w2_out = [wt.all_sum(jnp.concatenate(t, 2)) for t in (w2, w2_out)]
+        w2_out = jnp.concatenate([w2_out[:, :feat], w2_out[:, feat:]], 0)
+    w3_out, p3_out, extra = wt.owner_attend(col3)
+    win_out, wout_out = wt.owner_wide(w2, w2_out)
+    w1_out, p1_out, _ = wt.owner_attend(col1)
 
     def gain_slope(w, slope, gain):
         return jnp.sum(w.astype(F32) * slope, 1) / gain.astype(F32)

time: 503 us -> 465 us (0.924)
  waiting for transfers between devices: 215 us -> 168 us
  other arithmetic: 16.1 us -> 30.5 us
  Pallas kernels: 140 us -> 132 us
  starting transfers between devices: 75.8 us -> 67.8 us
  local copies, waits for them, and re-layouts: 35.9 us -> 43.7 us
    ppermute x63 -> x55, waiting for transfers between devices: 183 us -> 136 us  [xor(): return lax.ppermute(x, axis, [(i, i ^ j) for i in range(n)])]
    ppermute x63 -> x55, starting transfers between devices: 49.9 us -> 40.4 us  [xor(): return lax.ppermute(x, axis, [(i, i ^ j) for i in range(n)])]
    ppermute x4, starting transfers between devices: 12.1 us -> 18.1 us  [move(): return lax.ppermute(x, ALL, self.team)]
    ppermute x4, waiting for transfers between devices: 18.6 us -> 13.2 us  [move(): return lax.ppermute(x, ALL, self.team)]
    unnamed x169 -> x203, local copies, waits for them, and re-layouts: 23.8 us -> 27.2 us
    pallas_call x2 -> x1, Pallas kernels: 13.7 us -> 12 us  [experts_forward(): pl.pallas_call(kernel, grid=(2 * steps,), out_shape=[jax.ShapeDtypeStruct...]
  transfers between devices with their start and end apart: 73 -> 65, of which waited for: 40 -> 31; matrix products, arithmetic and copies ran while one was open for 6% -> 10% of each run, Pallas kernels for 27% -> 27%
where the time goes in v4:
time: 465 us; the launch traced here: 459 us
  waiting for transfers between devices  168 us (36%)
  Pallas kernels  132 us (28%)
  starting transfers between devices  67.8 us (15%)
  local copies, waits for them, and re-layouts  43.7 us (9%)
  other arithmetic  30.5 us (7%)
  between operations  16.3 us (4%)
    ppermute x55, waiting for transfers between devices, xor(): return lax.ppermute(x, axis, [(i, i ^ j) for i in range(n)])  136 us
    pallas_call x16, Pallas kernels, call(): pl.pallas_call(run, out_shape=[jax.ShapeDtypeStruct(s, t) for s, t, _ in...  76.2 us
    pallas_call x2, Pallas kernels, expert_slopes(): pl.pallas_call(kernel, grid=(steps,), out_shape=[jax.ShapeDtypeStruct((fe...  44.2 us
    ppermute x55, starting transfers between devices, xor(): return lax.ppermute(x, axis, [(i, i ^ j) for i in range(n)])  40.4 us
    unnamed x203, local copies, waits for them, and re-layouts  27.2 us
    ppermute x4, starting transfers between devices, move(): return lax.ppermute(x, ALL, self.team)  18.1 us
    ppermute x4, waiting for transfers between devices, move(): return lax.ppermute(x, ALL, self.team)  13.2 us
    ppermute x2, waiting for transfers between devices, owner_attend(): p = lax.ppermute(p, ALL, self.links.from_lane)  12.8 us
  transfers between devices with their start and end apart: 65, of which 31 were waited for; matrix products, arithmetic and copies ran while one was open for 10% of the time, Pallas kernels for 27%

profile of v4, /device:TPU:10, one launch (start us, length us, event | category | flops | bytes accessed | tf_op | source)
XLA Modules:
  0.0 458.6 jit_solution(16245605928947515430)
XLA Ops:
  7.2 2.9 collective-permute-start
  14.2 4.0 collective-permute-start.3
  18.3 6.1 %collective-permute-done.3 = bf16[48,768]{1,0:T(8,128)(2,1)S(1)} collective-permute-done((bf16[48,768]{1,0:T(8,128)(2,1)S(1)}, bf16[48,768]{1,0:T(8,128)(2,1)S(1)}, u32[]{:S(2)}, u32[]{:S(2)}) %collective-permute-start.3) | collective-permute-done | bytes 73760 | tf_op jit(solution)/shard_map/ppermute | solution.py:1053
  28.2 3.7 collective-permute-done.4
  31.9 5.7 %collective-permute-done.5 = bf16[48,1664]{1,0:T(8,128)(2,1)S(1)} collective-permute-done((bf16[48,1664]{1,0:T(8,128)(2,1)S(1)}, bf16[48,1664]{1,0:T(8,128)(2,1)S(1)}, u32[]{:S(2)}, u32[]{:S(2)}) %collective-permute-start.5) | collective-permute-done | bytes 159776 | tf_op jit(solution)/shard_map/ppermute | solution.py:866
  37.7 5.4 %collective-permute-done.6 = bf16[48,1664]{1,0:T(8,128)(2,1)S(1)} collective-permute-done((bf16[48,1664]{1,0:T(8,128)(2,1)S(1)}, bf16[48,1664]{1,0:T(8,128)(2,1)S(1)}, u32[]{:S(2)}, u32[]{:S(2)}) %collective-permute-start.6) | collective-permute-done | bytes 159776 | tf_op jit(solution)/shard_map/ppermute | solution.py:866
  49.2 5.9 %collective-permute-done.10 = bf16[48,3072]{1,0:T(8,128)(2,1)S(1)} collective-permute-done((bf16[48,3072]{1,0:T(8,128)(2,1)S(1)}, bf16[48,3072]{1,0:T(8,128)(2,1)S(1)}, u32[]{:S(2)}, u32[]{:S(2)}) %collective-permute-start.10) | collective-permute-done | bytes 294944 | tf_op jit(solution)/shard_map/ppermute | solution.py:866
  55.0 10.3 %collective-permute-done.11 = bf16[48,3072]{1,0:T(8,128)(2,1)S(1)} collective-permute-done((bf16[48,3072]{1,0:T(8,128)(2,1)S(1)}, bf16[48,3072]{1,0:T(8,128)(2,1)S(1)}, u32[]{:S(2)}, u32[]{:S(2)}) %collective-permute-start.11) | collective-permute-done | bytes 294944 | tf_op jit(solution)/shard_map/ppermute | solution.py:866
  65.4 7.0 %collective-permute-done.12 = bf16[48,3072]{1,0:T(8,128)(2,1)S(1)} collective-permute-done((bf16[48,3072]{1,0:T(8,128)(2,1)S(1)}, bf16[48,3072]{1,0:T(8,128)(2,1)S(1)}, u32[]{:S(2)}, u32[]{:S(2)}) %collective-permute-start.12) | collective-permute-done | bytes 294944 | tf_op jit(solution)/shard_map/ppermute | solution.py:866
  75.8 2.5 collective-permute-start.18
  78.3 4.0 collective-permute-start.17
  84.4 8.8 %collective-permute-done.17.refs_6_ = bf16[145,768]{1,0:T(8,128)(2,1)S(1)} collective-permute-done((bf16[145,768]{1,0:T(8,128)(2,1)S(1)}, bf16[145,768]{1,0:T(8,128)(2,1)S(1)}, u32[]{:S(2)}, u32[]{:S(2)}) %collective-permute-start.17) | collective-permute-done | bytes 222752 | tf_op jit(solution)/shard_map/ppermute | solution.py:862
  99.3 5.0 %shard_map.280 = (f32[320,768]{1,0:T(8,128)}, bf16[320,768]{1,0:T(8,128)(2,1)S(1)}, bf16[320,384]{1,0:T(8,128)(2,1)S(1)}, bf16[320,768]{1,0:T(8,128)(2,1)S(1)}, ...) custom-call(s32[2]{0:T(128)S(1)} %pad_add_fusion.1.refs_0_, ...), custom_call_target="tpu_custom_call" | custom-call | flops 943718400 | bytes 6291456 | tf_op jit(solution)/shard_map/pallas_call | solution.py:45
  105.9 4.2 shard_map.281
  110.2 11.1 %collective-permute-done.19.refs_6_ = bf16[2,2,192,768]{3,2,1,0:T(8,128)(2,1)} collective-permute-done((bf16[2,2,192,768]{3,2,1,0:T(8,128)(2,1)}, bf16[2,2,192,768]{3,2,1,0:T(8,128)(2,1)}, u32[]{:S(2)}, u32[]{:S(2)}) %collective-permute-start.19) | collective-permute-done | bytes 1179680 | tf_op jit(solution)/shard_map/ppermute | solution.py:866
  128.6 6.3 %collective-permute-done.21.refs_8_ = bf16[2,192,768]{2,1,0:T(8,128)(2,1)S(1)} collective-permute-done((bf16[2,192,768]{2,1,0:T(8,128)(2,1)S(1)}, bf16[2,192,768]{2,1,0:T(8,128)(2,1)S(1)}, u32[]{:S(2)}, u32[]{:S(2)}) %collective-permute-start.21) | collective-permute-done | bytes 589856 | tf_op jit(solution)/shard_map/ppermute | solution.py:866
  136.4 9.8 %shard_map.282 = (f32[320,768]{1,0:T(8,128)S(1)}, bf16[320,768]{1,0:T(8,128)(2,1)S(1)}, f32[320,1536]{1,0:T(8,128)}, f32[320,768]{1,0:T(8,128)}, bf16[320,768]{1...) custom-call(s32[2]{0:T(128)S(1)} %pad_add_fusion.1.refs_0_, ...), custom_call_target="tpu_custom_call" | custom-call | flops 1509949440 | bytes 16777216 | tf_op jit(solution)/shard_map/pallas_call | solution.py:45
  147.5 5.4 %collective-permute-done.23.refs_2_ = bf16[320,768]{1,0:T(8,128)(2,1)S(1)} collective-permute-done((bf16[320,768]{1,0:T(8,128)(2,1)S(1)}, bf16[320,768]{1,0:T(8,128)(2,1)S(1)}, u32[]{:S(2)}, u32[]{:S(2)}) %collective-permute-start.23) | collective-permute-done | bytes 491552 | tf_op jit(solution)/shard_map/ppermute | solution.py:866
  153.0 2.2 shard_map.283
  158.7 3.2 shard_map.284
  162.0 2.4 collective-permute-done.24.refs_3_
  166.1 5.6 %shard_map.285 = (f32[320,768]{1,0:T(8,128)S(1)}, bf16[160,768]{1,0:T(8,128)(2,1)S(1)}, bf16[384,320]{1,0:T(8,128)(2,1)S(1)}, f32[8,320]{1,0:T(8,128)S(1)}, bf16[320,768]{1,0:T(8,128)(2,1)S(1)}) custom-call(s32[2]{0:T(128)S(1)} %pad_add_fusion.1.refs_0_, bf16[320,384]{1,0:T(8,128)(2,1)S(1)} %get-tuple-element.158.refs_1_.refs_4_, ...), custom_call_target="tpu_custom_call" | custom-call | flops 503316480 | bytes 4194304 | tf_op jit(solution)/shard_map/pallas_call | solution.py:45
  175.1 2.9 shard_map.286
  183.8 6.3 %collective-permute-done.29.refs_1_ = bf16[192,768]{1,0:T(8,128)(2,1)S(1)} collective-permute-done((bf16[192,768]{1,0:T(8,128)(2,1)S(1)}, bf16[192,768]{1,0:T(8,128)(2,1)S(1)}, u32[]{:S(2)}, u32[]{:S(2)}) %collective-permute-start.29) | collective-permute-done | bytes 294944 | tf_op jit(solution)/shard_map/ppermute | solution.py:866
  190.1 6.9 %collective-permute-done.30.refs_2_ = bf16[192,768]{1,0:T(8,128)(2,1)S(1)} collective-permute-done((bf16[192,768]{1,0:T(8,128)(2,1)S(1)}, bf16[192,768]{1,0:T(8,128)(2,1)S(1)}, u32[]{:S(2)}, u32[]{:S(2)}) %collective-permute-start.30) | collective-permute-done | bytes 294944 | tf_op jit(solution)/shard_map/ppermute | solution.py:866
  201.7 12.0 %shard_map.287 = (bf16[192,768]{1,0:T(8,128)(2,1)S(1)}, bf16[192,768]{1,0:T(8,128)(2,1)S(1)}, bf16[192,768]{1,0:T(8,128)(2,1)S(1)}, bf16[192,768]{1,0:T(8,128)(2,1)S(1)}) custom-call(bf16[192,768]{1,0:T(8,128)(2,1)S(1)} %get-tuple-element.168.refs_0_, bf16[192,768]{1,0:T(8,128)(2,1)S(1)} %collective-permute-done.29.refs_1_, bf16[192,768]{1,0:T(8,128)(2,1)S(1)} %copy-done.18, ...), custom_call_target="tpu_custom_call" | custom-call | flops 7247757312 | bytes 20971520 | tf_op jit(solution)/shard_map/pallas_call | solution.py:708
  217.3 6.5 %collective-permute-done.32.refs_2_ = bf16[192,768]{1,0:T(8,128)(2,1)S(1)} collective-permute-done((bf16[192,768]{1,0:T(8,128)(2,1)S(1)}, bf16[192,768]{1,0:T(8,128)(2,1)S(1)}, u32[]{:S(2)}, u32[]{:S(2)}) %collective-permute-start.32) | collective-permute-done | bytes 294944 | tf_op jit(solution)/shard_map/ppermute | solution.py:866
  223.7 5.7 %collective-permute-done.33.refs_3_ = bf16[192,768]{1,0:T(8,128)(2,1)S(1)} collective-permute-done((bf16[192,768]{1,0:T(8,128)(2,1)S(1)}, bf16[192,768]{1,0:T(8,128)(2,1)S(1)}, u32[]{:S(2)}, u32[]{:S(2)}) %collective-permute-start.33) | collective-permute-done | bytes 294944 | tf_op jit(solution)/shard_map/ppermute | solution.py:866
  229.5 2.0 shard_map.288
  233.2 6.9 %shard_map.290 = (bf16[320,384]{1,0:T(8,128)(2,1)S(1)}, f32[320,768]{1,0:T(8,128)}, bf16[320,768]{1,0:T(8,128)(2,1)S(1)}, bf16[384,768]{1,0:T(8,128)(2,1)S(1)}) custom-call(s32[2]{0:T(128)S(1)} %pad_add_fusion.1.refs_0_, bf16[320,768]{1,0:T(8,128)(2,1)S(1)} %get-tuple-element.184.refs_1_, bf16[384,768]{1,0:T(8,128)(2,1)S(1)} %bitcast.208, ...), custom_call_target="tpu_custom_call" | custom-call | flops 1163919360 | bytes 6291456 | tf_op jit(solution)/shard_map/pallas_call | solution.py:45
  240.7 12.7 %collective-permute-done.36.refs_3_ = bf16[320,768]{1,0:T(8,128)(2,1)S(1)} collective-permute-done((bf16[320,768]{1,0:T(8,128)(2,1)S(1)}, bf16[320,768]{1,0:T(8,128)(2,1)S(1)}, u32[]{:S(2)}, u32[]{:S(2)}) %collective-permute-start.36) | collective-permute-done | bytes 491552 | tf_op jit(solution)/shard_map/ppermute | solution.py:866
  253.4 6.2 %shard_map.291 = (f32[320,768]{1,0:T(8,128)S(1)}, bf16[320,768]{1,0:T(8,128)(2,1)S(1)}, bf16[2,832,384]{2,1,0:T(8,128)(2,1)}, bf16[2,832,384]{2,1,0:T(8,128)(2,1)}) custom-call(s32[2]{0:T(128)S(1)} %pad_add_fusion.1.refs_0_, bf16[320,384]{1,0:T(8,128)(2,1)S(1)} %get-tuple-element.188.refs_1_, f32[320,768]{1,0:T(8,128)} %get-tuple-element.189.refs_2_, ...), custom_call_target="tpu_custom_call" | custom-call | flops 1132462080 | bytes 10485760 | tf_op jit(solution)/shard_map/pallas_call | solution.py:45
  262.4 12.8 %shard_map.292 = (f32[320,768]{1,0:T(8,128)S(1)}, f32[320,768]{1,0:T(8,128)S(1)}, bf16[320,768]{1,0:T(8,128)(2,1)S(1)}, bf16[2,2,192,768]{3,2,1,0:T(8,128)(2,1)}...) custom-call(s32[2]{0:T(128)S(1)} %pad_add_fusion.1.refs_0_, ...), custom_call_target="tpu_custom_call" | custom-call | flops 3774873600 | bytes 25165824 | tf_op jit(solution)/shard_map/pallas_call | solution.py:45
  278.1 2.1 shard_map.293
  280.2 7.0 %shard_map.294 = (bf16[320,384]{1,0:T(8,128)(2,1)S(1)}, f32[320,768]{1,0:T(8,128)}, bf16[320,768]{1,0:T(8,128)(2,1)S(1)}, bf16[384,768]{1,0:T(8,128)(2,1)S(1)}) custom-call(s32[2]{0:T(128)S(1)} %pad_add_fusion.1.refs_0_, bf16[320,768]{1,0:T(8,128)(2,1)S(1)} %get-tuple-element.203.refs_1_, bf16[384,768]{1,0:T(8,128)(2,1)S(1)} %copy-done.30, ...), custom_call_target="tpu_custom_call" | custom-call | flops 1163919360 | bytes 6291456 | tf_op jit(solution)/shard_map/pallas_call | solution.py:45
  290.0 11.8 %collective-permute-done.39.refs_3_ = bf16[320,768]{1,0:T(8,128)(2,1)S(1)} collective-permute-done((bf16[320,768]{1,0:T(8,128)(2,1)S(1)}, bf16[320,768]{1,0:T(8,128)(2,1)S(1)}, u32[]{:S(2)}, u32[]{:S(2)}) %collective-permute-start.39) | collective-permute-done | bytes 491552 | tf_op jit(solution)/shard_map/ppermute | solution.py:866
  303.6 5.8 %shard_map.295 = (f32[160,768]{1,0:T(8,128)S(1)}, bf16[160,768]{1,0:T(8,128)(2,1)S(1)}, bf16[2,384,384]{2,1,0:T(8,128)(2,1)S(1)}, bf16[2,384,384]{2,1,0:T(8,128)...) custom-call(s32[2]{0:T(128)S(1)} %pad_add_fusion.1.refs_0_, ...), custom_call_target="tpu_custom_call" | custom-call | flops 1132462080 | bytes 10485760 | tf_op jit(solution)/shard_map/pallas_call | solution.py:45
  319.7 21.5 %shard_map.297 = (bf16[768,1536]{1,0:T(8,128)(2,1)}, bf16[1536,768]{1,0:T(8,128)(2,1)}) custom-call(bf16[4,4,192,768]{3,2,1,0:T(8,128)(2,1)} %bitcast.216, bf16[768,1536]{1,0:T(8,128)(2,1)} %collective-permute-done.26.refs_7_.refs_6_.refs_1_, bf16[1536,768]{1,0:T(8,128)(2,1)} %collective-permute-done.27.refs_8_.refs_7_.refs_2_, bf16[145,768]{1,0:T(8,128)(2,1)} %copy-done.6), custom_call_target="tpu_custom_call" | custom-call | flops 14495514624 | bytes 20971520 | tf_op jit(solution)/shard_map/pallas_call | solution.py:772
  344.8 8.7 %collective-permute-start.41 = (bf16[2,145,768]{2,1,0:T(8,128)(2,1)}, bf16[2,145,768]{2,1,0:T(8,128)(2,1)}, u32[]{:S(2)}, u32[]{:S(2)}) collective-permute-start(bf16[2,145,768]{2,1,0:T(8,128)(2,1)} %pad_maximum_fusion.7), channel_id=1, source_target_pairs={{0,0},{1,2},{2,1},{3,3},{4,8},{5,10},{6,9},{7,11},{8,4},{9,6},{10,... | collective-permute-start | bytes 1336328 | tf_op jit(solution)/shard_map/ppermute | solution.py:862
  367.1 3.5 collective-permute-done.41
  374.3 3.8 collective-permute-done.43
  379.6 2.3 collective-permute-done.47
  386.1 4.9 %collective-permute-start.49 = (bf16[48,3072]{1,0:T(8,128)(2,1)S(1)}, bf16[48,3072]{1,0:T(8,128)(2,1)S(1)}, u32[]{:S(2)}, u32[]{:S(2)}) collective-permute-start(bf16[48,3072]{1,0:T(8,128)(2,1)S(1)} %get-tuple-element.315), channel_id=1, source_target_pairs={{0,4},{2,6},{4,0},{6,2},{1,5},{3,7},{5,1},{7,3},{8,12},{10,14},{12... | collective-permute-start | bytes 884744 | tf_op jit(solution)/shard_map/ppermute | solution.py:866
  391.0 22.6 %shard_map.298 = (f32[768,1536]{1,0:T(8,128)}, f32[1536,768]{1,0:T(8,128)}) custom-call(bf16[4,4,192,768]{3,2,1,0:T(8,128)(2,1)} %bitcast.217, bf16[768,1536]{1,0:T(8,128)(2,1)} %bitcast.60.refs_4_.refs_1_, bf16[1536,768]{1,0:T(8,128)(2,1)} %bitcast.61.refs_5_.refs_2_, bf16[768,1536]{1,0:T(8,128)(2,1)} %collective-permute-done.51.refs_3_, ...), custom_call_target="tpu_custom_call" | custom-call | flops 14495514624 | bytes 20971520 | tf_op jit(solution)/shard_map/pallas_call | solution.py:772
  413.8 8.0 %collective-permute-done.50 = bf16[48,3072]{1,0:T(8,128)(2,1)S(1)} collective-permute-done((bf16[48,3072]{1,0:T(8,128)(2,1)S(1)}, bf16[48,3072]{1,0:T(8,128)(2,1)S(1)}, u32[]{:S(2)}, u32[]{:S(2)}) %collective-permute-start.50) | collective-permute-done | bytes 294944 | tf_op jit(solution)/shard_map/ppermute | solution.py:866
  423.1 3.1 collective-permute-start.54
  426.3 6.6 %collective-permute-done.54 = f32[24,768]{1,0:T(8,128)S(1)} collective-permute-done((f32[24,768]{1,0:T(8,128)S(1)}, f32[24,768]{1,0:T(8,128)S(1)}, u32[]{:S(2)}, u32[]{:S(2)}) %collective-permute-start.54) | collective-permute-done | bytes 73760 | tf_op jit(solution)/shard_map/ppermute | solution.py:1015
  439.0 6.2 %collective-permute-done.61 = f32[24,768]{1,0:T(8,128)S(1)} collective-permute-done((f32[24,768]{1,0:T(8,128)S(1)}, f32[24,768]{1,0:T(8,128)S(1)}, u32[]{:S(2)}, u32[]{:S(2)}) %collective-permute-start.61) | collective-permute-done | bytes 73760 | tf_op jit(solution)/shard_map/ppermute | solution.py:1015
  (440 shorter events, 121.8 us)
Async XLA Ops:
  7.2 150.4 %all-gather.5.cloned.1.call-start = ((), (), s32[]{:S(2)}) async-start(), calls=%async_computation.2 | async-start | bytes 2949120 | tf_op jit(solution)/shard_map/all_gather | solution.py:1090
  7.2 20.9 %collective-permute-start = (bf16[145,768]{1,0:T(8,128)(2,1)}, bf16[145,768]{1,0:T(8,128)(2,1)S(1)}, u32[]{:S(2)}, u32[]{:S(2)}) collective-permute-start(bf16[145,768]{1,0:T(8,128)(2,1)} %bitcast.270), channel_id=1, source_target_pairs={{0,0},{1,2},{2,1},{3,3},{4,8},{5,10},{6,9},{7,11},{8,4},{9,6},{10,... | collective-permute-start | bytes 668168 | tf_op jit(solution)/shard_map/ppermute | solution.py:862
  12.5 15.6 %collective-permute-start.7 = (bf16[24,2688]{1,0:T(8,128)(2,1)S(1)}, bf16[24,2688]{1,0:T(8,128)(2,1)S(1)}, u32[]{:S(2)}, u32[]{:S(2)}) collective-permute-start(bf16[24,2688]{1,0:T(8,128)(2,1)S(1)} %get-tuple-element.376), channel_id=1, source_target_pairs={{0,1},{1,0},{2,3},{3,2},{4,5},{5,4},{6,7},{7,6},{8,9},{9,8},{10,11... | collective-permute-start | bytes 387080 | tf_op jit(solution)/shard_map/ppermute | solution.py:866
  14.2 10.3 %collective-permute-start.3 = (bf16[48,768]{1,0:T(8,128)(2,1)S(1)}, bf16[48,768]{1,0:T(8,128)(2,1)S(1)}, u32[]{:S(2)}, u32[]{:S(2)}) collective-permute-start(bf16[48,768]{1,0:T(8,128)(2,1)S(1)} %pad_maximum_fusion.12), channel_id=1, source_target_pairs={{0,0},{1,2},{2,4},{3,6},{4,8},{5,10},{6,12},{7,14},{8,16},{9,18},{... | collective-permute-start | bytes 221192 | tf_op jit(solution)/shard_map/ppermute | solution.py:1053
  26.5 11.2 %collective-permute-start.5 = (bf16[48,1664]{1,0:T(8,128)(2,1)S(1)}, bf16[48,1664]{1,0:T(8,128)(2,1)S(1)}, u32[]{:S(2)}, u32[]{:S(2)}) collective-permute-start(bf16[48,1664]{1,0:T(8,128)(2,1)S(1)} %fusion.28), channel_id=1, source_target_pairs={{0,4},{2,6},{4,0},{6,2},{1,5},{3,7},{5,1},{7,3},{8,12},{10,14},{12... | collective-permute-start | bytes 479240 | tf_op jit(solution)/shard_map/ppermute | solution.py:866
  26.5 16.6 %collective-permute-start.6 = (bf16[48,1664]{1,0:T(8,128)(2,1)S(1)}, bf16[48,1664]{1,0:T(8,128)(2,1)S(1)}, u32[]{:S(2)}, u32[]{:S(2)}) collective-permute-start(bf16[48,1664]{1,0:T(8,128)(2,1)S(1)} %fusion.28), channel_id=1, source_target_pairs={{0,6},{2,4},{4,2},{6,0},{1,7},{3,5},{5,3},{7,1},{8,14},{10,12},{12... | collective-permute-start | bytes 479240 | tf_op jit(solution)/shard_map/ppermute | solution.py:866
  28.1 18.7 %collective-permute-start.1 = (bf16[145,768]{1,0:T(8,128)(2,1)S(1)}, bf16[145,768]{1,0:T(8,128)(2,1)S(1)}, u32[]{:S(2)}, u32[]{:S(2)}) collective-permute-start(bf16[145,768]{1,0:T(8,128)(2,1)S(1)} %collective-permute-done), channel_id=1, source_target_pairs={{0,8},{8,0},{16,24},{24,16},{1,9},{9,1},{17,25},{25,17},{2,10},{10... | collective-permute-start | bytes 668168 | tf_op jit(solution)/shard_map/ppermute | solution.py:866
  43.3 11.7 %collective-permute-start.10 = (bf16[48,3072]{1,0:T(8,128)(2,1)S(1)}, bf16[48,3072]{1,0:T(8,128)(2,1)S(1)}, u32[]{:S(2)}, u32[]{:S(2)}) collective-permute-start(bf16[48,3072]{1,0:T(8,128)(2,1)S(1)} %pad_maximum_fusion.8), channel_id=1, source_target_pairs={{0,2},{2,0},{4,6},{6,4},{1,3},{3,1},{5,7},{7,5},{8,10},{10,8},{12,... | collective-permute-start | bytes 884744 | tf_op jit(solution)/shard_map/ppermute | solution.py:866
  43.4 22.0 %collective-permute-start.11 = (bf16[48,3072]{1,0:T(8,128)(2,1)S(1)}, bf16[48,3072]{1,0:T(8,128)(2,1)S(1)}, u32[]{:S(2)}, u32[]{:S(2)}) collective-permute-start(bf16[48,3072]{1,0:T(8,128)(2,1)S(1)} %pad_maximum_fusion.8), channel_id=1, source_target_pairs={{0,4},{2,6},{4,0},{6,2},{1,5},{3,7},{5,1},{7,3},{8,12},{10,14},{12... | collective-permute-start | bytes 884744 | tf_op jit(solution)/shard_map/ppermute | solution.py:866
  45.3 27.1 %collective-permute-start.12 = (bf16[48,3072]{1,0:T(8,128)(2,1)S(1)}, bf16[48,3072]{1,0:T(8,128)(2,1)S(1)}, u32[]{:S(2)}, u32[]{:S(2)}) collective-permute-start(bf16[48,3072]{1,0:T(8,128)(2,1)S(1)} %pad_maximum_fusion.8), channel_id=1, source_target_pairs={{0,6},{2,4},{4,2},{6,0},{1,7},{3,5},{5,3},{7,1},{8,14},{10,12},{12... | collective-permute-start | bytes 884744 | tf_op jit(solution)/shard_map/ppermute | solution.py:866
  47.9 24.8 %collective-permute-start.8 = (bf16[1024,384]{1,0:T(8,128)(2,1)S(1)}, bf16[1024,384]{1,0:T(8,128)(2,1)S(1)}, u32[]{:S(2)}, u32[]{:S(2)}) collective-permute-start(bf16[1024,384]{1,0:T(8,128)(2,1)S(1)} %constant_dynamic-update-slice_fusion.2.refs_5_), channel_id=1, source_target_pairs={{0,8},{8,0},{16,24},{24,16},{1,9},{9,1},{17,25},{25,17},{2,10},{10... | collective-permute-start | bytes 2359304 | tf_op jit(solution)/shard_map/ppermute | solution.py:866
  47.9 24.8 %collective-permute-start.9 = (bf16[1024,384]{1,0:T(8,128)(2,1)S(1)}, bf16[1024,384]{1,0:T(8,128)(2,1)S(1)}, u32[]{:S(2)}, u32[]{:S(2)}) collective-permute-start(bf16[1024,384]{1,0:T(8,128)(2,1)S(1)} %constant_dynamic-update-slice_fusion.2.refs_5_), channel_id=1, source_target_pairs={{0,16},{8,24},{16,0},{24,8},{1,17},{9,25},{17,1},{25,9},{2,18},{10... | collective-permute-start | bytes 2359304 | tf_op jit(solution)/shard_map/ppermute | solution.py:866
  72.7 10.5 %collective-permute-start.13 = (bf16[2,145,768]{2,1,0:T(8,128)(2,1)S(1)}, bf16[2,145,768]{2,1,0:T(8,128)(2,1)}, u32[]{:S(2)}, u32[]{:S(2)}) collective-permute-start(bf16[2,145,768]{2,1,0:T(8,128)(2,1)S(1)} %pad_maximum_fusion.6), channel_id=1, source_target_pairs={{0,1},{1,0},{2,3},{3,2},{4,5},{5,4},{6,7},{7,6},{8,9},{9,8},{10,11... | collective-permute-start | bytes 1336328 | tf_op jit(solution)/shard_map/ppermute | solution.py:866
  75.1 18.1 %collective-permute-start.14 = (bf16[576,384]{1,0:T(8,128)(2,1)}, bf16[576,384]{1,0:T(8,128)(2,1)S(1)}, u32[]{:S(2)}, u32[]{:S(2)}) collective-permute-start(bf16[576,384]{1,0:T(8,128)(2,1)} %slice.354), channel_id=1, source_target_pairs={{0,16},{8,24},{16,0},{24,8},{1,17},{9,25},{17,1},{25,9},{2,18},{10... | collective-permute-start | bytes 1327112 | tf_op jit(solution)/shard_map/ppermute | solution.py:866
  75.2 18.1 %collective-permute-start.15 = (bf16[448,384]{1,0:T(8,128)(2,1)}, bf16[448,384]{1,0:T(8,128)(2,1)S(1)}, u32[]{:S(2)}, u32[]{:S(2)}) collective-permute-start(bf16[448,384]{1,0:T(8,128)(2,1)} %slice.355), channel_id=1, source_target_pairs={{0,8},{8,0},{16,24},{24,16},{1,9},{9,1},{17,25},{25,17},{2,10},{10... | collective-permute-start | bytes 1032200 | tf_op jit(solution)/shard_map/ppermute | solution.py:866
  78.3 14.9 %collective-permute-start.17 = (bf16[145,768]{1,0:T(8,128)(2,1)S(1)}, bf16[145,768]{1,0:T(8,128)(2,1)S(1)}, u32[]{:S(2)}, u32[]{:S(2)}) collective-permute-start(bf16[145,768]{1,0:T(8,128)(2,1)S(1)} %bitcast.260), channel_id=1, source_target_pairs={{0,0},{1,2},{2,1},{3,3},{4,8},{5,10},{6,9},{7,11},{8,4},{9,6},{10,... | collective-permute-start | bytes 668168 | tf_op jit(solution)/shard_map/ppermute | solution.py:862
  95.0 26.2 %collective-permute-start.19 = (bf16[2,2,192,768]{3,2,1,0:T(8,128)(2,1)}, bf16[2,2,192,768]{3,2,1,0:T(8,128)(2,1)}, u32[]{:S(2)}, u32[]{:S(2)}) collective-permute-start(bf16[2,2,192,768]{3,2,1,0:T(8,128)(2,1)} %pad_maximum_fusion.1.refs_5_), channel_id=1, source_target_pairs={{0,8},{8,0},{16,24},{24,16},{1,9},{9,1},{17,25},{25,17},{2,10},{10... | collective-permute-start | bytes 3538952 | tf_op jit(solution)/shard_map/ppermute | solution.py:866
  95.0 26.2 %collective-permute-start.20 = (bf16[2,2,192,768]{3,2,1,0:T(8,128)(2,1)}, bf16[2,2,192,768]{3,2,1,0:T(8,128)(2,1)}, u32[]{:S(2)}, u32[]{:S(2)}) collective-permute-start(bf16[2,2,192,768]{3,2,1,0:T(8,128)(2,1)} %pad_maximum_fusion.1.refs_5_), channel_id=1, source_target_pairs={{0,16},{8,24},{16,0},{24,8},{1,17},{9,25},{17,1},{25,9},{2,18},{10... | collective-permute-start | bytes 3538952 | tf_op jit(solution)/shard_map/ppermute | solution.py:866
  99.0 203.6 %all-gather.7.cloned.1.call-start = ((), (), s32[]{:S(2)}) async-start(), calls=%async_computation.3 | async-start | bytes 5898240 | tf_op jit(solution)/shard_map/all_gather | solution.py:1127
  122.4 12.4 %collective-permute-start.21 = (bf16[2,192,768]{2,1,0:T(8,128)(2,1)S(1)}, bf16[2,192,768]{2,1,0:T(8,128)(2,1)S(1)}, u32[]{:S(2)}, u32[]{:S(2)}) collective-permute-start(bf16[2,192,768]{2,1,0:T(8,128)(2,1)S(1)} %slice_bitcast_fusion.1), channel_id=1, source_target_pairs={{0,16},{8,24},{16,0},{24,8},{1,17},{9,25},{17,1},{25,9},{2,18},{10... | collective-permute-start | bytes 1769480 | tf_op jit(solution)/shard_map/ppermute | solution.py:866
  124.9 11.5 %collective-permute-start.22 = (bf16[2,192,768]{2,1,0:T(8,128)(2,1)S(1)}, bf16[2,192,768]{2,1,0:T(8,128)(2,1)S(1)}, u32[]{:S(2)}, u32[]{:S(2)}) collective-permute-start(bf16[2,192,768]{2,1,0:T(8,128)(2,1)S(1)} %slice_bitcast_fusion), channel_id=1, source_target_pairs={{0,8},{8,0},{16,24},{24,16},{1,9},{9,1},{17,25},{25,17},{2,10},{10... | collective-permute-start | bytes 1769480 | tf_op jit(solution)/shard_map/ppermute | solution.py:866
  147.0 19.1 %collective-permute-start.26 = (bf16[768,1536]{1,0:T(8,128)(2,1)}, bf16[768,1536]{1,0:T(8,128)(2,1)}, u32[]{:S(2)}, u32[]{:S(2)}) collective-permute-start(bf16[768,1536]{1,0:T(8,128)(2,1)} %bitcast.60.refs_4_.refs_1_), channel_id=1, source_target_pairs={{0,1},{1,0},{2,3},{3,2},{4,5},{5,4},{6,7},{7,6},{8,9},{9,8},{10,11... | collective-permute-start | bytes 7077896 | tf_op jit(solution)/shard_map/ppermute | solution.py:866
  147.0 19.1 %collective-permute-start.27 = (bf16[1536,768]{1,0:T(8,128)(2,1)}, bf16[1536,768]{1,0:T(8,128)(2,1)}, u32[]{:S(2)}, u32[]{:S(2)}) collective-permute-start(bf16[1536,768]{1,0:T(8,128)(2,1)} %bitcast.61.refs_5_.refs_2_), channel_id=1, source_target_pairs={{0,1},{1,0},{2,3},{3,2},{4,5},{5,4},{6,7},{7,6},{8,9},{9,8},{10,11... | collective-permute-start | bytes 7077896 | tf_op jit(solution)/shard_map/ppermute | solution.py:866
  181.7 15.3 %collective-permute-start.30 = (bf16[192,768]{1,0:T(8,128)(2,1)S(1)}, bf16[192,768]{1,0:T(8,128)(2,1)S(1)}, u32[]{:S(2)}, u32[]{:S(2)}) collective-permute-start(bf16[192,768]{1,0:T(8,128)(2,1)S(1)} %get-tuple-element.170), channel_id=1, source_target_pairs={{0,16},{8,24},{16,0},{24,8},{1,17},{9,25},{17,1},{25,9},{2,18},{10... | collective-permute-start | bytes 884744 | tf_op jit(solution)/shard_map/ppermute | solution.py:866
  183.1 13.9 %collective-permute-start.31 = (bf16[192,768]{1,0:T(8,128)(2,1)S(1)}, bf16[192,768]{1,0:T(8,128)(2,1)S(1)}, u32[]{:S(2)}, u32[]{:S(2)}) collective-permute-start(bf16[192,768]{1,0:T(8,128)(2,1)S(1)} %get-tuple-element.171), channel_id=1, source_target_pairs={{0,24},{8,16},{16,8},{24,0},{1,25},{9,17},{17,9},{25,1},{2,26},{10... | collective-permute-start | bytes 884744 | tf_op jit(solution)/shard_map/ppermute | solution.py:866
  199.7 234.6 %reduce-scatter.2.cloned.1.call-start = ((), (), s32[]{:S(2)}) async-start(), calls=%async_computation.1 | async-start | bytes 1536000 | tf_op jit(solution)/shard_map/reduce_scatter | solution.py:1160
  213.7 10.0 %collective-permute-start.32 = (bf16[192,768]{1,0:T(8,128)(2,1)S(1)}, bf16[192,768]{1,0:T(8,128)(2,1)S(1)}, u32[]{:S(2)}, u32[]{:S(2)}) collective-permute-start(bf16[192,768]{1,0:T(8,128)(2,1)S(1)} %get-tuple-element.173), channel_id=1, source_target_pairs={{0,8},{8,0},{16,24},{24,16},{1,9},{9,1},{17,25},{25,17},{2,10},{10... | collective-permute-start | bytes 884744 | tf_op jit(solution)/shard_map/ppermute | solution.py:866
  214.9 14.5 %collective-permute-start.33 = (bf16[192,768]{1,0:T(8,128)(2,1)S(1)}, bf16[192,768]{1,0:T(8,128)(2,1)S(1)}, u32[]{:S(2)}, u32[]{:S(2)}) collective-permute-start(bf16[192,768]{1,0:T(8,128)(2,1)S(1)} %get-tuple-element.174), channel_id=1, source_target_pairs={{0,16},{8,24},{16,0},{24,8},{1,17},{9,25},{17,1},{25,9},{2,18},{10... | collective-permute-start | bytes 884744 | tf_op jit(solution)/shard_map/ppermute | solution.py:866
  215.7 13.7 %collective-permute-start.34 = (bf16[192,768]{1,0:T(8,128)(2,1)S(1)}, bf16[192,768]{1,0:T(8,128)(2,1)S(1)}, u32[]{:S(2)}, u32[]{:S(2)}) collective-permute-start(bf16[192,768]{1,0:T(8,128)(2,1)S(1)} %get-tuple-element.175), channel_id=1, source_target_pairs={{0,24},{8,16},{16,8},{24,0},{1,25},{9,17},{17,9},{25,1},{2,26},{10... | collective-permute-start | bytes 884744 | tf_op jit(solution)/shard_map/ppermute | solution.py:866
  240.1 13.3 %collective-permute-start.36 = (bf16[320,768]{1,0:T(8,128)(2,1)S(1)}, bf16[320,768]{1,0:T(8,128)(2,1)S(1)}, u32[]{:S(2)}, u32[]{:S(2)}) collective-permute-start(bf16[320,768]{1,0:T(8,128)(2,1)S(1)} %get-tuple-element.190), channel_id=1, source_target_pairs={{0,8},{8,0},{16,24},{24,16},{1,9},{9,1},{17,25},{25,17},{2,10},{10... | collective-permute-start | bytes 1474568 | tf_op jit(solution)/shard_map/ppermute | solution.py:866
  260.5 49.7 %collective-permute-start.55 = (bf16[2,832,384]{2,1,0:T(8,128)(2,1)}, bf16[2,832,384]{2,1,0:T(8,128)(2,1)}, u32[]{:S(2)}, u32[]{:S(2)}) collective-permute-start(bf16[2,832,384]{2,1,0:T(8,128)(2,1)} %get-tuple-element.230), channel_id=1, source_target_pairs={{0,8},{8,0},{16,24},{24,16},{1,9},{9,1},{17,25},{25,17},{2,10},{10... | collective-permute-start | bytes 3833864 | tf_op jit(solution)/shard_map/ppermute | solution.py:866
  276.4 37.8 %collective-permute-start.57 = (bf16[2,2,192,768]{3,2,1,0:T(8,128)(2,1)}, bf16[2,2,192,768]{3,2,1,0:T(8,128)(2,1)}, u32[]{:S(2)}, u32[]{:S(2)}) collective-permute-start(bf16[2,2,192,768]{3,2,1,0:T(8,128)(2,1)} %get-tuple-element.234), channel_id=1, source_target_pairs={{0,16},{8,24},{16,0},{24,8},{1,17},{9,25},{17,1},{25,9},{2,18},{10... | collective-permute-start | bytes 3538952 | tf_op jit(solution)/shard_map/ppermute | solution.py:866
  288.0 13.8 %collective-permute-start.39 = (bf16[320,768]{1,0:T(8,128)(2,1)S(1)}, bf16[320,768]{1,0:T(8,128)(2,1)S(1)}, u32[]{:S(2)}, u32[]{:S(2)}) collective-permute-start(bf16[320,768]{1,0:T(8,128)(2,1)S(1)} %get-tuple-element.208), channel_id=1, source_target_pairs={{0,8},{8,0},{16,24},{24,16},{1,9},{9,1},{17,25},{25,17},{2,10},{10... | collective-permute-start | bytes 1474568 | tf_op jit(solution)/shard_map/ppermute | solution.py:866
  288.6 52.7 %collective-permute-start.42 = (bf16[2,2,192,768]{3,2,1,0:T(8,128)(2,1)}, bf16[2,2,192,768]{3,2,1,0:T(8,128)(2,1)}, u32[]{:S(2)}, u32[]{:S(2)}) collective-permute-start(bf16[2,2,192,768]{3,2,1,0:T(8,128)(2,1)} %get-tuple-element.215), channel_id=1, source_target_pairs={{0,16},{8,24},{16,0},{24,8},{1,17},{9,25},{17,1},{25,9},{2,18},{10... | collective-permute-start | bytes 3538952 | tf_op jit(solution)/shard_map/ppermute | solution.py:866
  309.6 35.3 %collective-permute-start.44 = (bf16[2,384,384]{2,1,0:T(8,128)(2,1)S(1)}, bf16[2,384,384]{2,1,0:T(8,128)(2,1)}, u32[]{:S(2)}, u32[]{:S(2)}) collective-permute-start(bf16[2,384,384]{2,1,0:T(8,128)(2,1)S(1)} %get-tuple-element.219), channel_id=1, source_target_pairs={{0,8},{8,0},{16,24},{24,16},{1,9},{9,1},{17,25},{25,17},{2,10},{10... | collective-permute-start | bytes 1769480 | tf_op jit(solution)/shard_map/ppermute | solution.py:866
  310.2 44.7 %collective-permute-start.46 = (bf16[2,384,384]{2,1,0:T(8,128)(2,1)}, bf16[2,384,384]{2,1,0:T(8,128)(2,1)}, u32[]{:S(2)}, u32[]{:S(2)}) collective-permute-start(bf16[2,384,384]{2,1,0:T(8,128)(2,1)} %get-tuple-element.222), channel_id=1, source_target_pairs={{0,16},{8,24},{16,0},{24,8},{1,17},{9,25},{17,1},{25,9},{2,18},{10... | collective-permute-start | bytes 1769480 | tf_op jit(solution)/shard_map/ppermute | solution.py:866
  314.1 45.4 %collective-permute-start.56 = (bf16[832,384]{1,0:T(8,128)(2,1)}, bf16[832,384]{1,0:T(8,128)(2,1)}, u32[]{:S(2)}, u32[]{:S(2)}) collective-permute-start(bf16[832,384]{1,0:T(8,128)(2,1)} %fusion.12), channel_id=1, source_target_pairs={{0,16},{8,24},{16,0},{24,8},{1,17},{9,25},{17,1},{25,9},{2,18},{10... | collective-permute-start | bytes 1916936 | tf_op jit(solution)/shard_map/ppermute | solution.py:866
  317.2 39.0 %collective-permute-start.58 = (bf16[2,192,768]{2,1,0:T(8,128)(2,1)}, bf16[2,192,768]{2,1,0:T(8,128)(2,1)}, u32[]{:S(2)}, u32[]{:S(2)}) collective-permute-start(bf16[2,192,768]{2,1,0:T(8,128)(2,1)} %fusion.14), channel_id=1, source_target_pairs={{0,8},{8,0},{16,24},{24,16},{1,9},{9,1},{17,25},{25,17},{2,10},{10... | collective-permute-start | bytes 1769480 | tf_op jit(solution)/shard_map/ppermute | solution.py:866
  341.2 49.8 %collective-permute-start.51 = (bf16[768,1536]{1,0:T(8,128)(2,1)}, bf16[768,1536]{1,0:T(8,128)(2,1)}, u32[]{:S(2)}, u32[]{:S(2)}) collective-permute-start(bf16[768,1536]{1,0:T(8,128)(2,1)} %get-tuple-element.216), channel_id=1, source_target_pairs={{0,1},{1,0},{2,3},{3,2},{4,5},{5,4},{6,7},{7,6},{8,9},{9,8},{10,11... | collective-permute-start | bytes 7077896 | tf_op jit(solution)/shard_map/ppermute | solution.py:866
  344.8 25.7 %collective-permute-start.41 = (bf16[2,145,768]{2,1,0:T(8,128)(2,1)}, bf16[2,145,768]{2,1,0:T(8,128)(2,1)}, u32[]{:S(2)}, u32[]{:S(2)}) collective-permute-start(bf16[2,145,768]{2,1,0:T(8,128)(2,1)} %pad_maximum_fusion.7), channel_id=1, source_target_pairs={{0,0},{1,2},{2,1},{3,3},{4,8},{5,10},{6,9},{7,11},{8,4},{9,6},{10,... | collective-permute-start | bytes 1336328 | tf_op jit(solution)/shard_map/ppermute | solution.py:862
  354.9 23.1 %collective-permute-start.43 = (bf16[2,192,768]{2,1,0:T(8,128)(2,1)}, bf16[2,192,768]{2,1,0:T(8,128)(2,1)S(1)}, u32[]{:S(2)}, u32[]{:S(2)}) collective-permute-start(bf16[2,192,768]{2,1,0:T(8,128)(2,1)} %fusion.13), channel_id=1, source_target_pairs={{0,8},{8,0},{16,24},{24,16},{1,9},{9,1},{17,25},{25,17},{2,10},{10... | collective-permute-start | bytes 1769480 | tf_op jit(solution)/shard_map/ppermute | solution.py:866
  356.2 34.8 %collective-permute-start.52 = (bf16[1536,768]{1,0:T(8,128)(2,1)}, bf16[1536,768]{1,0:T(8,128)(2,1)}, u32[]{:S(2)}, u32[]{:S(2)}) collective-permute-start(bf16[1536,768]{1,0:T(8,128)(2,1)} %get-tuple-element.224), channel_id=1, source_target_pairs={{0,1},{1,0},{2,3},{3,2},{4,5},{5,4},{6,7},{7,6},{8,9},{9,8},{10,11... | collective-permute-start | bytes 7077896 | tf_op jit(solution)/shard_map/ppermute | solution.py:866
  359.5 22.4 %collective-permute-start.45 = (bf16[384,384]{1,0:T(8,128)(2,1)}, bf16[384,384]{1,0:T(8,128)(2,1)}, u32[]{:S(2)}, u32[]{:S(2)}) collective-permute-start(bf16[384,384]{1,0:T(8,128)(2,1)} %fusion.24), channel_id=1, source_target_pairs={{0,16},{8,24},{16,0},{24,8},{1,17},{9,25},{17,1},{25,9},{2,18},{10... | collective-permute-start | bytes 884744 | tf_op jit(solution)/shard_map/ppermute | solution.py:866
  370.5 11.3 %collective-permute-start.47 = (bf16[384,384]{1,0:T(8,128)(2,1)}, bf16[384,384]{1,0:T(8,128)(2,1)S(1)}, u32[]{:S(2)}, u32[]{:S(2)}) collective-permute-start(bf16[384,384]{1,0:T(8,128)(2,1)} %fusion.25), channel_id=1, source_target_pairs={{0,8},{8,0},{16,24},{24,16},{1,9},{9,1},{17,25},{25,17},{2,10},{10... | collective-permute-start | bytes 884744 | tf_op jit(solution)/shard_map/ppermute | solution.py:866
  386.0 27.7 %collective-permute-start.48 = (bf16[48,3072]{1,0:T(8,128)(2,1)S(1)}, bf16[48,3072]{1,0:T(8,128)(2,1)S(1)}, u32[]{:S(2)}, u32[]{:S(2)}) collective-permute-start(bf16[48,3072]{1,0:T(8,128)(2,1)S(1)} %get-tuple-element.316), channel_id=1, source_target_pairs={{0,2},{2,0},{4,6},{6,4},{1,3},{3,1},{5,7},{7,5},{8,10},{10,8},{12,... | collective-permute-start | bytes 884744 | tf_op jit(solution)/shard_map/ppermute | solution.py:866
  386.1 27.7 %collective-permute-start.49 = (bf16[48,3072]{1,0:T(8,128)(2,1)S(1)}, bf16[48,3072]{1,0:T(8,128)(2,1)S(1)}, u32[]{:S(2)}, u32[]{:S(2)}) collective-permute-start(bf16[48,3072]{1,0:T(8,128)(2,1)S(1)} %get-tuple-element.315), channel_id=1, source_target_pairs={{0,4},{2,6},{4,0},{6,2},{1,5},{3,7},{5,1},{7,3},{8,12},{10,14},{12... | collective-permute-start | bytes 884744 | tf_op jit(solution)/shard_map/ppermute | solution.py:866
  391.0 30.7 %collective-permute-start.50 = (bf16[48,3072]{1,0:T(8,128)(2,1)S(1)}, bf16[48,3072]{1,0:T(8,128)(2,1)S(1)}, u32[]{:S(2)}, u32[]{:S(2)}) collective-permute-start(bf16[48,3072]{1,0:T(8,128)(2,1)S(1)} %get-tuple-element.314), channel_id=1, source_target_pairs={{0,6},{2,4},{4,2},{6,0},{1,7},{3,5},{5,3},{7,1},{8,14},{10,12},{12... | collective-permute-start | bytes 884744 | tf_op jit(solution)/shard_map/ppermute | solution.py:866
  435.4 12.4 %collective-permute-start.59 = (f32[24,1536]{1,0:T(8,128)S(1)}, f32[24,1536]{1,0:T(8,128)S(1)}, u32[]{:S(2)}, u32[]{:S(2)}) collective-permute-start(f32[24,1536]{1,0:T(8,128)S(1)} %get-tuple-element.368), channel_id=1, source_target_pairs={{0,1},{1,0},{2,3},{3,2},{4,5},{5,4},{6,7},{7,6},{8,9},{9,8},{10,11... | collective-permute-start | bytes 442376 | tf_op jit(solution)/shard_map/ppermute | solution.py:866
  (107 other events, 574.4 us)
Sparse Core Ops, SparseCore 0:
  99.1 47.6 all-gather.4
  199.8 91.4 all-gather.6
  367.2 38.6 reduce-scatter.1

commit v5 on v4

--- a/solution.py
+++ b/solution.py
@@ -36,7 +36,7 @@
     return lax.dot_general(a, b, (((0,), (0,)), ((), ())), preferred_element_type=F32)
 
 
-def call(kernel, outs, ins, scratch=(), after=(), flops=0, bytes_accessed=0):
+def call(kernel, outs, ins, scratch=(), after=(), flops=0, bytes_accessed=0, grid=()):
     n_in, n_after = len(ins), len(after)
 
     def run(*refs):
@@ -44,6 +44,7 @@
 
     return pl.pallas_call(
         run,
+        grid=grid,
         out_shape=[jax.ShapeDtypeStruct(s, t) for s, t, _ in outs],
         in_specs=[s for _, s in ins] + [HB] * n_after,
         out_specs=[s for _, _, s in outs],
@@ -547,6 +548,86 @@
     )
 
 
+def spread_attend_rows(t, store):
+    half = t.shape[1]
+    n, m = half // 2, half // 4
+    r = n // 4
+    for z in range(4):
+        for g in range(3):
+            store(z, g * half, t[g * n + z * r : g * n + (z + 1) * r])
+        at = 3 * n + z * (m // 4)
+        p = [t[at + g * m : at + g * m + m // 4] for g in range(2)]
+        store(z, 3 * half, jnp.concatenate(p, 0))
+    if t.shape[0] > 3 * n + 2 * m:
+        sm = t[3 * n + 2 * m :]
+        sm = jnp.concatenate([sm[:, 128 * g : 128 * (g + 1)] for g in range(3)], 0)
+        for z in range(4):
+            store(z, 4 * half, sm[z * r : (z + 1) * r])
+
+
+def spread_pair_rows(t, first, store):
+    r = t.shape[1] // 4
+    for i in range(2):
+        for z in range(4):
+            store(z, first + i * t.shape[2], t[i, z * r : (z + 1) * r])
+
+
+def columns_of(groups, after=()):
+    wide = 0
+    for t in groups:
+        wide += 2 * t.shape[2] if t.ndim == 3 else 4 * t.shape[1] + (128 if t.shape[0] > 2 * t.shape[1] else 0)
+    r = groups[0].shape[1] // 4 if groups[0].ndim == 3 else groups[0].shape[1] // 8
+
+    def kernel(*refs):
+        out = refs[len(groups)]
+
+        def store(z, lane, value):
+            out[z, :, pl.ds(lane, value.shape[1])] = value.astype(BF)
+
+        at = 0
+        for ref in refs[: len(groups)]:
+            t = ref[...]
+            if t.ndim == 3:
+                spread_pair_rows(t, at, store)
+                at += 2 * t.shape[2]
+            else:
+                spread_attend_rows(t, lambda z, lane, value, at=at: store(z, at + lane, value))
+                at += 4 * t.shape[1] + (128 if t.shape[0] > 2 * t.shape[1] else 0)
+
+    return call(
+        kernel, [((4, r, wide), BF, VM)], [(t, VM) for t in groups], after=after,
+        bytes_accessed=3 * 2**20,
+    )[0]
+
+
+def last_columns(where, upper, lower, pair, after=()):
+    half = upper.shape[1]
+    r = half // 8
+    wide = 4 * half + 2 * pair.shape[2]
+
+    def kernel(where_ref, upper_ref, lower_ref, pair_ref, *refs):
+        outs, scratch = refs[:4], refs[4]
+
+        def store(z, lane, value):
+            scratch[z, :, pl.ds(lane, value.shape[1])] = value
+
+        spread_attend_rows(jnp.concatenate([upper_ref[...], lower_ref[...]], 0), store)
+        spread_pair_rows(pair_ref[...], 4 * half, store)
+        c = where_ref[2]
+        outs[0][...] = scratch[c]
+        for j in range(1, 4):
+            outs[j][...] = scratch[c ^ j].astype(BF)
+
+    return call(
+        kernel,
+        [((r, wide), F32, VM)] + [((r, wide), BF, VM)] * 3,
+        [(where, SM), (upper, VM), (lower, VM), (pair, VM)],
+        scratch=[pltpu.VMEM((4, r, wide), F32)],
+        after=after,
+        bytes_accessed=6 * 2**20,
+    )
+
+
 def join_upstream(u_own, u_sib, rows):
     feat = u_own.shape[1]
 
@@ -716,7 +797,7 @@
             pltpu.VMEM((n, feat), F32), pltpu.VMEM((n, feat), F32),
         ],
         compiler_params=pltpu.CompilerParams(
-            vmem_limit_bytes=50 * 2**20, dimension_semantics=("arbitrary",)
+            vmem_limit_bytes=62 * 2**20, dimension_semantics=("arbitrary",)
         ),
         cost_estimate=pl.CostEstimate(
             flops=16 * n * feat * wide, bytes_accessed=20 * 2**20, transcendentals=0
@@ -1009,26 +1090,20 @@
             parts.append(sm.reshape(-1, 2 * r, 128))
         return jnp.concatenate(parts, 2)
 
-    def owner_attend(self, buf):
+    def owners(self, col1, col3, w2):
         f, h, r = self.feat, self.half, self.rdev
-        p = jnp.concatenate([buf[:r, f + h : 2 * f], buf[r:, f + h : 2 * f]], 1)
-        p = lax.ppermute(p, ALL, self.links.from_lane)
-        w = buf[:, : f + h]
-        if buf.shape[1] > 2 * f:
-            w = jnp.concatenate([w, buf[:, 2 * f :]], 1)
-        w = self.exchange(w)
-        extra = w[0, :, f + h :] + w[1, :, f + h :]
-        w = w[..., : f + h].reshape(2, r, 3, h).transpose(1, 2, 0, 3).reshape(r, 3 * f)
-        return w, p, extra
-
-    def pair_columns(self, t):
-        t = t.reshape(2, 4, 2 * self.rdev, self.feat)
-        return jnp.concatenate([t[0], t[1]], 2)
-
-    def owner_wide(self, w, w_out):
-        r = self.rdev
-        w = self.exchange(w).reshape(2, r, 2, self.links.chips, -1)
-        return w.transpose(1, 3, 0, 2, 4).reshape(r, self.ff), w_out
+        w = f + h
+        p = [jnp.concatenate([c[:r, w : 2 * f], c[r:, w : 2 * f]], 1) for c in (col1, col3)]
+        p = lax.ppermute(jnp.concatenate(p, 0), ALL, self.links.from_lane)
+        t = self.exchange(jnp.concatenate([col1[:, :w], col3[:, :w], col3[:, 2 * f :], w2], 1))
+
+        def attend(t):
+            return t.reshape(2, r, 3, h).transpose(1, 2, 0, 3).reshape(r, 3 * f)
+
+        small = t[..., 2 * w : 2 * w + 128]
+        win = t[..., 2 * w + 128 :].reshape(2, r, 2, self.links.chips, -1)
+        win = win.transpose(1, 3, 0, 2, 4).reshape(r, self.ff)
+        return attend(t[..., :w]), p[:r], attend(t[..., w : 2 * w]), p[r:], small[0] + small[1], win
 
 
 def body(links, *args):
@@ -1042,10 +1117,11 @@
     ff = win.shape[1]
     longest = LEN - (blk_len - 1) * links.C
     experts = router.shape[1]
+    assert experts <= 128
     small_rows = (4 + experts + 7) // 8 * 8
     cap = max(2, (5 * TOP * blk_len + 4 * experts - 1) // (4 * experts))
     blk = 2 * (e % 2) + d
-    where = jnp.stack([blk, e if links.fast else 0 * e]).astype(jnp.int32)
+    where = jnp.stack([blk, e if links.fast else 0 * e, lax.axis_index("context")]).astype(jnp.int32)
     wt = Weights(links, rdev, feat, ff)
     img = dict(rows=rows, blk_len=blk_len, longest=longest)
 
@@ -1079,11 +1155,11 @@
         blocks1 = wt.spread_attend(block1, skip)
     tok_sib = links.sib(tok_pair)
     toks = [tok_pair[0], tok_sib[0], tok_pair[1], tok_sib[1]]
-    cot, raw = tie([cotangent[0].astype(BF), jnp.concatenate([routes[0], slots[0]], 1)], *blocks1[1:3])
-    raw, cot = links.move(raw), links.move(cot)
-    index = jnp.pad(raw, ((0, rows - blk_len), (0, 0)), constant_values=cap)
+    raw = jnp.concatenate([routes[0], slots[0]], 1).astype(BF)
+    cot = jnp.concatenate([cotangent[0].astype(BF), jnp.pad(raw, ((0, 0), (0, 128 - 2 * TOP)))], 1)
+    cot = links.move(tie([cot], *blocks1[1:3])[0])
     if links.fast:
-        (quad2,) = tie([quad2], *blocks1[3:], *toks, cot, index)
+        (quad2,) = tie([quad2], *blocks1[3:], *toks, cot)
         pair2 = wt.pack_pair(quad2[..., : ff // 2], quad2[..., ff // 2 :])
         q, n = feat // 2, block3.shape[0]
         place3 = jnp.stack([t[q : q + n] for t in blocks1[:4]])
@@ -1111,17 +1187,19 @@
     )
     x2, normed3, own3 = norm_next(x1, part2, links.sib(low2), gains, 2, rows)
     ein_own, eout_own = ein[0], eout[0]
-    ein_sib, eout_sib = [links.sib(t) for t in tie([ein_own, eout_own], x1)]
+    ein_sib, eout_sib = [links.sib(t) for t in tie([ein_own, eout_own], own3)]
     far_own = links.partner(own3)
     q3, kv3, wa3 = attend_next(where, normed3, source3)
     (far_own,) = tie([far_own], q3)
     part3, low3, blend3, lse3, far3 = attend_core(
-        where, q3, kv3, None, wp3, solo=True, far=(far_own, links.sib(far_own), wa3),
-        after=(ein_sib, eout_sib), **img
+        where, q3, kv3, None, wp3, solo=True, far=(far_own, links.sib(far_own), wa3), **img
     )
     moe_args = dict(experts=experts, cap=cap, fast=links.fast, **img)
+    index = cot[:, feat : feat + 2 * TOP].astype(jnp.int32)
+    index = jnp.pad(index, ((0, rows - blk_len), (0, 0)), constant_values=cap)
     x3, moe, gates, up, *sent = route(
-        where, x2, part3, links.sib(low3), gains, small, cot, index, **moe_args
+        where, x2, part3, links.sib(low3), gains, small, cot[:, :feat], index,
+        after=(ein_sib, eout_sib), **moe_args
     )
     came = links.swap_blocks(sent)
     every = lax.all_gather(jnp.stack(came), "context", axis=0, tiled=False)
@@ -1153,30 +1231,28 @@
     sum2a = wt.total(*slopes2[:2], first2, ((low,), (e_sib[0],)))
     sum2b = wt.total(*slopes2[2:], first2, ((e_sib[0],), ()))
     sum1 = [wt.total(*slopes1[2 * i : 2 * i + 2], first1[i], ((e_sib[0],), ())) for i in range(2)]
-    col3, col1 = wt.to_columns(sum3), wt.to_columns(jnp.concatenate(sum1, -2))
     if links.fast:
-        col2a, col2b = wt.pair_columns(sum2a), wt.pair_columns(sum2b)
-        early = jnp.concatenate([col3, col2a], 2).astype(BF)
+        early = columns_of([sum3, sum2a])
         early = lax.psum_scatter(tie([early], every)[0], "context", scatter_dimension=0, tiled=False)
-        early = early.astype(F32)
-        col3, col2a = early[:, : col3.shape[2]], early[:, col3.shape[2] :]
-        late = jnp.concatenate([col2b, col1], 2)
-        e_slopes = expert_slopes(every, ein_own, eout_own, [links.sib(t) for t in e_sib], after=(late,))
-        late = links.column_sum(late, e_slopes[0])
-        col2b, col1 = late[:, : 2 * feat], late[:, 2 * feat :]
+        own, *away = last_columns(where, *sum1, sum2b, after=(moved,))
+        e_slopes = expert_slopes(every, ein_own, eout_own, [links.sib(t) for t in e_sib], after=(own,))
+        for t in tie([links.xor(t, "context", j + 1) for j, t in enumerate(away)], e_slopes[0]):
+            own = own + t.astype(F32)
+        early = tie([early], e_slopes[0])[0].astype(F32)
+        col1, col2b = own[:, : 2 * feat], own[:, 2 * feat :]
+        col3, col2a = early[:, : early.shape[1] - 2 * feat], early[:, early.shape[1] - 2 * feat :]
         w2 = jnp.concatenate([col2a[:, :feat], col2b[:, :feat]], 1)
-        w2_out = jnp.concatenate([col2a[:, feat:], col2b[:, feat:]], 0)
+        wout_out = jnp.concatenate([col2a[:, feat:], col2b[:, feat:]], 0)
     else:
         e_slopes = expert_slopes(every, ein_own, eout_own, [links.sib(t) for t in e_sib])
+        col3, col1 = wt.to_columns(sum3), wt.to_columns(jnp.concatenate(sum1, -2))
         col3, col1 = wt.all_sum(col3), wt.all_sum(col1)
         hid = ff // (4 * links.chips)
         w2 = [t[..., 0, :, :].reshape(-1, 2 * rdev, feat) for t in (sum2a, sum2b)]
         w2_out = [t[..., 1, :, :].reshape(-1, hid, feat) for t in (sum2a, sum2b)]
         w2, w2_out = [wt.all_sum(jnp.concatenate(t, 2)) for t in (w2, w2_out)]
-        w2_out = jnp.concatenate([w2_out[:, :feat], w2_out[:, feat:]], 0)
-    w3_out, p3_out, extra = wt.owner_attend(col3)
-    win_out, wout_out = wt.owner_wide(w2, w2_out)
-    w1_out, p1_out, _ = wt.owner_attend(col1)
+        wout_out = jnp.concatenate([w2_out[:, :feat], w2_out[:, feat:]], 0)
+    w1_out, p1_out, w3_out, p3_out, extra, win_out = wt.owners(col1, col3, w2)
 
     def gain_slope(w, slope, gain):
         return jnp.sum(w.astype(F32) * slope, 1) / gain.astype(F32)

time: 465 us -> 455 us (0.978)
  starting transfers between devices: 67.8 us -> 60.6 us
  other arithmetic: 30.5 us -> 25.1 us
  Pallas kernels: 132 us -> 137 us
    ppermute x55 -> x53, waiting for transfers between devices: 136 us -> 144 us  [xor(): return lax.ppermute(x, axis, [(i, i ^ j) for i in range(n)])]
    ppermute x4 -> x3, starting transfers between devices: 18.1 us -> 11.5 us  [move(): return lax.ppermute(x, ALL, self.team)]
    ppermute x2 -> x1, waiting for transfers between devices: 12.8 us -> 6.32 us  [owners(): p = lax.ppermute(jnp.concatenate(p, 0), ALL, self.links.from_lane)]
    pallas_call x16 -> x18, Pallas kernels: 76.2 us -> 78.9 us  [call(): pl.pallas_call(run, grid=grid, out_shape=[jax.ShapeDtypeStruct(s, t) for...]
    ppermute x4 -> x3, waiting for transfers between devices: 13.2 us -> 10.8 us  [move(): return lax.ppermute(x, ALL, self.team)]
    ppermute x55 -> x53, starting transfers between devices: 40.4 us -> 42.2 us  [xor(): return lax.ppermute(x, axis, [(i, i ^ j) for i in range(n)])]
    unnamed x203 -> x193, local copies, waits for them, and re-layouts: 27.2 us -> 26.3 us
  transfers between devices with their start and end apart: 65 -> 61, of which waited for: 31 -> 32; matrix products, arithmetic and copies ran while one was open for 10% -> 8% of each run, Pallas kernels for 27% -> 30%
where the time goes in v5:
time: 455 us; the launch traced here: 449 us
  waiting for transfers between devices  167 us (37%)
  Pallas kernels  137 us (30%)
  starting transfers between devices  60.6 us (13%)
  local copies, waits for them, and re-layouts  43.6 us (10%)
  other arithmetic  25.1 us (6%)
  between operations  16 us (4%)
    ppermute x53, waiting for transfers between devices, xor(): return lax.ppermute(x, axis, [(i, i ^ j) for i in range(n)])  144 us
    pallas_call x18, Pallas kernels, call(): pl.pallas_call(run, grid=grid, out_shape=[jax.ShapeDtypeStruct(s, t) for...  78.9 us
    pallas_call x2, Pallas kernels, expert_slopes(): pl.pallas_call(kernel, grid=(steps,), out_shape=[jax.ShapeDtypeStruct((fe...  44.1 us
    ppermute x53, starting transfers between devices, xor(): return lax.ppermute(x, axis, [(i, i ^ j) for i in range(n)])  42.2 us
    unnamed x193, local copies, waits for them, and re-layouts  26.3 us
    pallas_call x1, Pallas kernels, experts_forward(): pl.pallas_call(kernel, grid=(2 * steps,), out_shape=[jax.ShapeDtypeStruct...  13.8 us
    ppermute x3, starting transfers between devices, move(): return lax.ppermute(x, ALL, self.team)  11.5 us
    ppermute x3, waiting for transfers between devices, move(): return lax.ppermute(x, ALL, self.team)  10.8 us
  transfers between devices with their start and end apart: 61, of which 32 were waited for; matrix products, arithmetic and copies ran while one was open for 8% of the time, Pallas kernels for 30%

profile of v5, /device:TPU:10, one launch (start us, length us, event | category | flops | bytes accessed | tf_op | source)
XLA Modules:
  0.0 448.8 jit_solution(9763495101564064853)
XLA Ops:
  7.2 2.9 collective-permute-start
  14.2 4.0 collective-permute-start.3
  18.4 6.0 %collective-permute-done.3 = bf16[48,768]{1,0:T(8,128)(2,1)S(1)} collective-permute-done((bf16[48,768]{1,0:T(8,128)(2,1)S(1)}, bf16[48,768]{1,0:T(8,128)(2,1)S(1)}, u32[]{:S(2)}, u32[]{:S(2)}) %collective-permute-start.3) | collective-permute-done | bytes 73760 | tf_op jit(solution)/shard_map/ppermute | solution.py:1129
  28.2 3.7 collective-permute-done.4
  31.9 5.7 %collective-permute-done.5 = bf16[48,1664]{1,0:T(8,128)(2,1)S(1)} collective-permute-done((bf16[48,1664]{1,0:T(8,128)(2,1)S(1)}, bf16[48,1664]{1,0:T(8,128)(2,1)S(1)}, u32[]{:S(2)}, u32[]{:S(2)}) %collective-permute-start.5) | collective-permute-done | bytes 159776 | tf_op jit(solution)/shard_map/ppermute | solution.py:947
  37.7 5.4 %collective-permute-done.6 = bf16[48,1664]{1,0:T(8,128)(2,1)S(1)} collective-permute-done((bf16[48,1664]{1,0:T(8,128)(2,1)S(1)}, bf16[48,1664]{1,0:T(8,128)(2,1)S(1)}, u32[]{:S(2)}, u32[]{:S(2)}) %collective-permute-start.6) | collective-permute-done | bytes 159776 | tf_op jit(solution)/shard_map/ppermute | solution.py:947
  49.2 5.9 %collective-permute-done.10 = bf16[48,3072]{1,0:T(8,128)(2,1)S(1)} collective-permute-done((bf16[48,3072]{1,0:T(8,128)(2,1)S(1)}, bf16[48,3072]{1,0:T(8,128)(2,1)S(1)}, u32[]{:S(2)}, u32[]{:S(2)}) %collective-permute-start.10) | collective-permute-done | bytes 294944 | tf_op jit(solution)/shard_map/ppermute | solution.py:947
  55.0 10.3 %collective-permute-done.11 = bf16[48,3072]{1,0:T(8,128)(2,1)S(1)} collective-permute-done((bf16[48,3072]{1,0:T(8,128)(2,1)S(1)}, bf16[48,3072]{1,0:T(8,128)(2,1)S(1)}, u32[]{:S(2)}, u32[]{:S(2)}) %collective-permute-start.11) | collective-permute-done | bytes 294944 | tf_op jit(solution)/shard_map/ppermute | solution.py:947
  65.4 7.0 %collective-permute-done.12 = bf16[48,3072]{1,0:T(8,128)(2,1)S(1)} collective-permute-done((bf16[48,3072]{1,0:T(8,128)(2,1)S(1)}, bf16[48,3072]{1,0:T(8,128)(2,1)S(1)}, u32[]{:S(2)}, u32[]{:S(2)}) %collective-permute-start.12) | collective-permute-done | bytes 294944 | tf_op jit(solution)/shard_map/ppermute | solution.py:947
  75.1 2.8 collective-permute-start.17
  79.1 10.8 %collective-permute-done.17 = bf16[145,896]{1,0:T(8,128)(2,1)S(1)} collective-permute-done((bf16[145,896]{1,0:T(8,128)(2,1)S(1)}, bf16[145,896]{1,0:T(8,128)(2,1)S(1)}, u32[]{:S(2)}, u32[]{:S(2)}) %collective-permute-start.17) | collective-permute-done | bytes 259872 | tf_op jit(solution)/shard_map/ppermute | solution.py:943
  96.0 5.1 %shard_map.280 = (f32[320,768]{1,0:T(8,128)}, bf16[320,768]{1,0:T(8,128)(2,1)S(1)}, bf16[320,384]{1,0:T(8,128)(2,1)S(1)}, bf16[320,768]{1,0:T(8,128)(2,1)S(1)}, ...) custom-call(s32[3]{0:T(128)S(1)} %pad_add_fusion.refs_0_, ...), custom_call_target="tpu_custom_call" | custom-call | flops 943718400 | bytes 6291456 | tf_op jit(solution)/shard_map/pallas_call | solution.py:45
  103.4 4.2 shard_map.281
  107.7 10.6 %collective-permute-done.18.refs_6_ = bf16[2,2,192,768]{3,2,1,0:T(8,128)(2,1)} collective-permute-done((bf16[2,2,192,768]{3,2,1,0:T(8,128)(2,1)S(1)}, bf16[2,2,192,768]{3,2,1,0:T(8,128)(2,1)}, u32[]{:S(2)}, u32[]{:S(2)}) %collective-permute-start.18) | collective-permute-done | bytes 1179680 | tf_op jit(solution)/shard_map/ppermute | solution.py:947
  125.7 7.3 %collective-permute-done.20.refs_8_ = bf16[2,192,768]{2,1,0:T(8,128)(2,1)S(1)} collective-permute-done((bf16[2,192,768]{2,1,0:T(8,128)(2,1)S(1)}, bf16[2,192,768]{2,1,0:T(8,128)(2,1)S(1)}, u32[]{:S(2)}, u32[]{:S(2)}) %collective-permute-start.20) | collective-permute-done | bytes 589856 | tf_op jit(solution)/shard_map/ppermute | solution.py:947
  133.0 2.2 collective-permute-done.21.refs_9_
  135.3 9.8 %shard_map.282 = (f32[320,768]{1,0:T(8,128)S(1)}, bf16[320,768]{1,0:T(8,128)(2,1)S(1)}, f32[320,1536]{1,0:T(8,128)}, f32[320,768]{1,0:T(8,128)}, bf16[320,768]{1...) custom-call(s32[3]{0:T(128)S(1)} %pad_add_fusion.refs_0_, ...), custom_call_target="tpu_custom_call" | custom-call | flops 1509949440 | bytes 16777216 | tf_op jit(solution)/shard_map/pallas_call | solution.py:45
  147.7 2.2 shard_map.283
  154.0 3.2 shard_map.284
  157.2 2.4 collective-permute-done.23.refs_3_
  161.5 5.6 %shard_map.285 = (f32[320,768]{1,0:T(8,128)S(1)}, bf16[160,768]{1,0:T(8,128)(2,1)S(1)}, bf16[384,320]{1,0:T(8,128)(2,1)S(1)}, f32[8,320]{1,0:T(8,128)S(1)}, bf16[320,768]{1,0:T(8,128)(2,1)S(1)}) custom-call(s32[3]{0:T(128)S(1)} %pad_add_fusion.refs_0_, bf16[320,384]{1,0:T(8,128)(2,1)S(1)} %get-tuple-element.161.refs_1_.refs_4_, ...), custom_call_target="tpu_custom_call" | custom-call | flops 503316480 | bytes 4194304 | tf_op jit(solution)/shard_map/pallas_call | solution.py:45
  170.4 2.9 shard_map.286
  179.1 6.3 %collective-permute-done.28.refs_1_ = bf16[192,768]{1,0:T(8,128)(2,1)S(1)} collective-permute-done((bf16[192,768]{1,0:T(8,128)(2,1)S(1)}, bf16[192,768]{1,0:T(8,128)(2,1)S(1)}, u32[]{:S(2)}, u32[]{:S(2)}) %collective-permute-start.28) | collective-permute-done | bytes 294944 | tf_op jit(solution)/shard_map/ppermute | solution.py:947
  185.5 6.9 %collective-permute-done.29.refs_2_ = bf16[192,768]{1,0:T(8,128)(2,1)S(1)} collective-permute-done((bf16[192,768]{1,0:T(8,128)(2,1)S(1)}, bf16[192,768]{1,0:T(8,128)(2,1)S(1)}, u32[]{:S(2)}, u32[]{:S(2)}) %collective-permute-start.29) | collective-permute-done | bytes 294944 | tf_op jit(solution)/shard_map/ppermute | solution.py:947
  194.4 13.8 %shard_map.287 = (bf16[192,768]{1,0:T(8,128)(2,1)}, bf16[192,768]{1,0:T(8,128)(2,1)}, bf16[192,768]{1,0:T(8,128)(2,1)}, bf16[192,768]{1,0:T(8,128)(2,1)}) custom-call(bf16[192,768]{1,0:T(8,128)(2,1)} %copy-done.23, bf16[192,768]{1,0:T(8,128)(2,1)} %copy-done.73, bf16[192,768]{1,0:T(8,128)(2,1)} %copy-done.74, bf16[192,768]{1,0:T(8,128)(2,1)} %copy-done.75, ...), custom_call_target="tpu_custom_call" | custom-call | flops 7247757312 | bytes 20971520 | tf_op jit(solution)/shard_map/pallas_call | solution.py:789
  211.7 6.7 %collective-permute-done.31.refs_2_ = bf16[192,768]{1,0:T(8,128)(2,1)S(1)} collective-permute-done((bf16[192,768]{1,0:T(8,128)(2,1)}, bf16[192,768]{1,0:T(8,128)(2,1)S(1)}, u32[]{:S(2)}, u32[]{:S(2)}) %collective-permute-start.31) | collective-permute-done | bytes 294944 | tf_op jit(solution)/shard_map/ppermute | solution.py:947
  218.4 4.9 %collective-permute-done.32.refs_3_ = bf16[192,768]{1,0:T(8,128)(2,1)S(1)} collective-permute-done((bf16[192,768]{1,0:T(8,128)(2,1)}, bf16[192,768]{1,0:T(8,128)(2,1)S(1)}, u32[]{:S(2)}, u32[]{:S(2)}) %collective-permute-start.32) | collective-permute-done | bytes 294944 | tf_op jit(solution)/shard_map/ppermute | solution.py:947
  227.3 2.0 shard_map.288
  232.1 7.0 %shard_map.290 = (bf16[320,384]{1,0:T(8,128)(2,1)S(1)}, f32[320,768]{1,0:T(8,128)}, bf16[320,768]{1,0:T(8,128)(2,1)S(1)}, bf16[384,768]{1,0:T(8,128)(2,1)S(1)}) custom-call(s32[3]{0:T(128)S(1)} %pad_add_fusion.refs_0_, bf16[320,768]{1,0:T(8,128)(2,1)S(1)} %get-tuple-element.187.refs_1_, bf16[384,768]{1,0:T(8,128)(2,1)S(1)} %bitcast.164, ...), custom_call_target="tpu_custom_call" | custom-call | flops 1163919360 | bytes 6291456 | tf_op jit(solution)/shard_map/pallas_call | solution.py:45
  240.0 12.3 %collective-permute-done.35.refs_3_ = bf16[320,768]{1,0:T(8,128)(2,1)S(1)} collective-permute-done((bf16[320,768]{1,0:T(8,128)(2,1)S(1)}, bf16[320,768]{1,0:T(8,128)(2,1)S(1)}, u32[]{:S(2)}, u32[]{:S(2)}) %collective-permute-start.35) | collective-permute-done | bytes 491552 | tf_op jit(solution)/shard_map/ppermute | solution.py:947
  252.3 6.2 %shard_map.291 = (f32[320,768]{1,0:T(8,128)S(1)}, bf16[320,768]{1,0:T(8,128)(2,1)S(1)}, bf16[2,832,384]{2,1,0:T(8,128)(2,1)}, bf16[2,832,384]{2,1,0:T(8,128)(2,1)}) custom-call(s32[3]{0:T(128)S(1)} %pad_add_fusion.refs_0_, bf16[320,384]{1,0:T(8,128)(2,1)S(1)} %get-tuple-element.191.refs_1_, f32[320,768]{1,0:T(8,128)} %get-tuple-element.192.refs_2_, ...), custom_call_target="tpu_custom_call" | custom-call | flops 1132462080 | bytes 10485760 | tf_op jit(solution)/shard_map/pallas_call | solution.py:45
  261.3 12.8 %shard_map.292 = (f32[320,768]{1,0:T(8,128)S(1)}, f32[320,768]{1,0:T(8,128)S(1)}, bf16[320,768]{1,0:T(8,128)(2,1)S(1)}, bf16[2,2,192,768]{3,2,1,0:T(8,128)(2,1)}...) custom-call(s32[3]{0:T(128)S(1)} %pad_add_fusion.refs_0_, ...), custom_call_target="tpu_custom_call" | custom-call | flops 3774873600 | bytes 25165824 | tf_op jit(solution)/shard_map/pallas_call | solution.py:45
  276.9 2.0 shard_map.293
  279.0 7.0 %shard_map.294 = (bf16[320,384]{1,0:T(8,128)(2,1)S(1)}, f32[320,768]{1,0:T(8,128)}, bf16[320,768]{1,0:T(8,128)(2,1)S(1)}, bf16[384,768]{1,0:T(8,128)(2,1)S(1)}) custom-call(s32[3]{0:T(128)S(1)} %pad_add_fusion.refs_0_, bf16[320,768]{1,0:T(8,128)(2,1)S(1)} %get-tuple-element.206.refs_1_, bf16[384,768]{1,0:T(8,128)(2,1)S(1)} %copy-done.34, ...), custom_call_target="tpu_custom_call" | custom-call | flops 1163919360 | bytes 6291456 | tf_op jit(solution)/shard_map/pallas_call | solution.py:45
  288.7 11.9 %collective-permute-done.38.refs_3_ = bf16[320,768]{1,0:T(8,128)(2,1)S(1)} collective-permute-done((bf16[320,768]{1,0:T(8,128)(2,1)S(1)}, bf16[320,768]{1,0:T(8,128)(2,1)S(1)}, u32[]{:S(2)}, u32[]{:S(2)}) %collective-permute-start.38) | collective-permute-done | bytes 491552 | tf_op jit(solution)/shard_map/ppermute | solution.py:947
  302.5 5.8 %shard_map.295 = (f32[160,768]{1,0:T(8,128)S(1)}, bf16[160,768]{1,0:T(8,128)(2,1)S(1)}, bf16[2,384,384]{2,1,0:T(8,128)(2,1)S(1)}, bf16[2,384,384]{2,1,0:T(8,128)...) custom-call(s32[3]{0:T(128)S(1)} %pad_add_fusion.refs_0_, ...), custom_call_target="tpu_custom_call" | custom-call | flops 1132462080 | bytes 10485760 | tf_op jit(solution)/shard_map/pallas_call | solution.py:45
  318.9 21.5 %shard_map.297 = (bf16[768,1536]{1,0:T(8,128)(2,1)}, bf16[1536,768]{1,0:T(8,128)(2,1)}) custom-call(bf16[4,4,192,768]{3,2,1,0:T(8,128)(2,1)} %bitcast.169, bf16[768,1536]{1,0:T(8,128)(2,1)} %collective-permute-done.26.refs_8_.refs_6_.refs_1_, bf16[1536,768]{1,0:T(8,128)(2,1)} %collective-permute-done.27.refs_9_.refs_7_.refs_2_, bf16[145,768]{1,0:T(8,128)(2,1)} %copy-done.8), custom_call_target="tpu_custom_call" | custom-call | flops 14495514624 | bytes 20971520 | tf_op jit(solution)/shard_map/pallas_call | solution.py:853
  350.0 5.8 %collective-permute-start.40 = (bf16[2,145,768]{2,1,0:T(8,128)(2,1)}, bf16[2,145,768]{2,1,0:T(8,128)(2,1)S(1)}, u32[]{:S(2)}, u32[]{:S(2)}) collective-permute-start(bf16[2,145,768]{2,1,0:T(8,128)(2,1)} %pad_maximum_fusion.8), channel_id=1, source_target_pairs={{0,0},{1,2},{2,1},{3,3},{4,8},{5,10},{6,9},{7,11},{8,4},{9,6},{10,... | collective-permute-start | bytes 1336328 | tf_op jit(solution)/shard_map/ppermute | solution.py:943
  357.8 3.6 collective-permute-done.53
  363.6 8.6 %collective-permute-done.46 = bf16[2,192,768]{2,1,0:T(8,128)(2,1)} collective-permute-done((bf16[2,192,768]{2,1,0:T(8,128)(2,1)}, bf16[2,192,768]{2,1,0:T(8,128)(2,1)}, u32[]{:S(2)}, u32[]{:S(2)}) %collective-permute-start.46) | collective-permute-done | bytes 589856 | tf_op jit(solution)/shard_map/ppermute | solution.py:947
  372.2 2.8 fusion.8.refs_3_
  375.0 4.4 collective-permute-done.44
  382.0 5.2 %collective-permute-start.48 = (bf16[48,3072]{1,0:T(8,128)(2,1)S(1)}, bf16[48,3072]{1,0:T(8,128)(2,1)S(1)}, u32[]{:S(2)}, u32[]{:S(2)}) collective-permute-start(bf16[48,3072]{1,0:T(8,128)(2,1)S(1)} %get-tuple-element.229), channel_id=1, source_target_pairs={{0,4},{2,6},{4,0},{6,2},{1,5},{3,7},{5,1},{7,3},{8,12},{10,14},{12... | collective-permute-start | bytes 884744 | tf_op jit(solution)/shard_map/ppermute | solution.py:947
  387.2 22.6 %shard_map.299 = (f32[768,1536]{1,0:T(8,128)}, f32[1536,768]{1,0:T(8,128)}) custom-call(bf16[4,4,192,768]{3,2,1,0:T(8,128)(2,1)} %bitcast.170, bf16[768,1536]{1,0:T(8,128)(2,1)} %bitcast.61.refs_4_.refs_1_, bf16[1536,768]{1,0:T(8,128)(2,1)} %bitcast.62.refs_5_.refs_2_, bf16[768,1536]{1,0:T(8,128)(2,1)} %collective-permute-done.50.refs_3_, ...), custom_call_target="tpu_custom_call" | custom-call | flops 14495514624 | bytes 20971520 | tf_op jit(solution)/shard_map/pallas_call | solution.py:853
  409.9 2.0 collective-permute-done.48
  411.9 6.8 %collective-permute-done.49 = bf16[48,3072]{1,0:T(8,128)(2,1)S(1)} collective-permute-done((bf16[48,3072]{1,0:T(8,128)(2,1)S(1)}, bf16[48,3072]{1,0:T(8,128)(2,1)S(1)}, u32[]{:S(2)}, u32[]{:S(2)}) %collective-permute-start.49) | collective-permute-done | bytes 294944 | tf_op jit(solution)/shard_map/ppermute | solution.py:947
  421.7 2.5 collective-permute-start.57
  428.4 6.3 %collective-permute-done.57 = f32[48,768]{1,0:T(8,128)S(1)} collective-permute-done((f32[48,768]{1,0:T(8,128)S(1)}, f32[48,768]{1,0:T(8,128)S(1)}, u32[]{:S(2)}, u32[]{:S(2)}) %collective-permute-start.57) | collective-permute-done | bytes 147488 | tf_op jit(solution)/shard_map/ppermute | solution.py:1097
  (409 shorter events, 114.8 us)
Async XLA Ops:
  7.2 145.7 %all-gather.5.cloned.1.call-start = ((), (), s32[]{:S(2)}) async-start(), calls=%async_computation.2 | async-start | bytes 2949120 | tf_op jit(solution)/shard_map/all_gather | solution.py:1166
  7.2 20.9 %collective-permute-start = (bf16[145,768]{1,0:T(8,128)(2,1)}, bf16[145,768]{1,0:T(8,128)(2,1)S(1)}, u32[]{:S(2)}, u32[]{:S(2)}) collective-permute-start(bf16[145,768]{1,0:T(8,128)(2,1)} %bitcast.213), channel_id=1, source_target_pairs={{0,0},{1,2},{2,1},{3,3},{4,8},{5,10},{6,9},{7,11},{8,4},{9,6},{10,... | collective-permute-start | bytes 668168 | tf_op jit(solution)/shard_map/ppermute | solution.py:943
  12.5 15.5 %collective-permute-start.7 = (bf16[24,2688]{1,0:T(8,128)(2,1)S(1)}, bf16[24,2688]{1,0:T(8,128)(2,1)S(1)}, u32[]{:S(2)}, u32[]{:S(2)}) collective-permute-start(bf16[24,2688]{1,0:T(8,128)(2,1)S(1)} %get-tuple-element.365), channel_id=1, source_target_pairs={{0,1},{1,0},{2,3},{3,2},{4,5},{5,4},{6,7},{7,6},{8,9},{9,8},{10,11... | collective-permute-start | bytes 387080 | tf_op jit(solution)/shard_map/ppermute | solution.py:947
  14.2 10.2 %collective-permute-start.3 = (bf16[48,768]{1,0:T(8,128)(2,1)S(1)}, bf16[48,768]{1,0:T(8,128)(2,1)S(1)}, u32[]{:S(2)}, u32[]{:S(2)}) collective-permute-start(bf16[48,768]{1,0:T(8,128)(2,1)S(1)} %pad_maximum_fusion.11), channel_id=1, source_target_pairs={{0,0},{1,2},{2,4},{3,6},{4,8},{5,10},{6,12},{7,14},{8,16},{9,18},{... | collective-permute-start | bytes 221192 | tf_op jit(solution)/shard_map/ppermute | solution.py:1129
  26.5 11.2 %collective-permute-start.5 = (bf16[48,1664]{1,0:T(8,128)(2,1)S(1)}, bf16[48,1664]{1,0:T(8,128)(2,1)S(1)}, u32[]{:S(2)}, u32[]{:S(2)}) collective-permute-start(bf16[48,1664]{1,0:T(8,128)(2,1)S(1)} %fusion.24), channel_id=1, source_target_pairs={{0,4},{2,6},{4,0},{6,2},{1,5},{3,7},{5,1},{7,3},{8,12},{10,14},{12... | collective-permute-start | bytes 479240 | tf_op jit(solution)/shard_map/ppermute | solution.py:947
  26.5 16.6 %collective-permute-start.6 = (bf16[48,1664]{1,0:T(8,128)(2,1)S(1)}, bf16[48,1664]{1,0:T(8,128)(2,1)S(1)}, u32[]{:S(2)}, u32[]{:S(2)}) collective-permute-start(bf16[48,1664]{1,0:T(8,128)(2,1)S(1)} %fusion.24), channel_id=1, source_target_pairs={{0,6},{2,4},{4,2},{6,0},{1,7},{3,5},{5,3},{7,1},{8,14},{10,12},{12... | collective-permute-start | bytes 479240 | tf_op jit(solution)/shard_map/ppermute | solution.py:947
  28.1 18.7 %collective-permute-start.1 = (bf16[145,768]{1,0:T(8,128)(2,1)S(1)}, bf16[145,768]{1,0:T(8,128)(2,1)S(1)}, u32[]{:S(2)}, u32[]{:S(2)}) collective-permute-start(bf16[145,768]{1,0:T(8,128)(2,1)S(1)} %collective-permute-done), channel_id=1, source_target_pairs={{0,8},{8,0},{16,24},{24,16},{1,9},{9,1},{17,25},{25,17},{2,10},{10... | collective-permute-start | bytes 668168 | tf_op jit(solution)/shard_map/ppermute | solution.py:947
  43.3 11.7 %collective-permute-start.10 = (bf16[48,3072]{1,0:T(8,128)(2,1)S(1)}, bf16[48,3072]{1,0:T(8,128)(2,1)S(1)}, u32[]{:S(2)}, u32[]{:S(2)}) collective-permute-start(bf16[48,3072]{1,0:T(8,128)(2,1)S(1)} %pad_maximum_fusion.9), channel_id=1, source_target_pairs={{0,2},{2,0},{4,6},{6,4},{1,3},{3,1},{5,7},{7,5},{8,10},{10,8},{12,... | collective-permute-start | bytes 884744 | tf_op jit(solution)/shard_map/ppermute | solution.py:947
  43.4 22.0 %collective-permute-start.11 = (bf16[48,3072]{1,0:T(8,128)(2,1)S(1)}, bf16[48,3072]{1,0:T(8,128)(2,1)S(1)}, u32[]{:S(2)}, u32[]{:S(2)}) collective-permute-start(bf16[48,3072]{1,0:T(8,128)(2,1)S(1)} %pad_maximum_fusion.9), channel_id=1, source_target_pairs={{0,4},{2,6},{4,0},{6,2},{1,5},{3,7},{5,1},{7,3},{8,12},{10,14},{12... | collective-permute-start | bytes 884744 | tf_op jit(solution)/shard_map/ppermute | solution.py:947
  45.3 27.1 %collective-permute-start.12 = (bf16[48,3072]{1,0:T(8,128)(2,1)S(1)}, bf16[48,3072]{1,0:T(8,128)(2,1)S(1)}, u32[]{:S(2)}, u32[]{:S(2)}) collective-permute-start(bf16[48,3072]{1,0:T(8,128)(2,1)S(1)} %pad_maximum_fusion.9), channel_id=1, source_target_pairs={{0,6},{2,4},{4,2},{6,0},{1,7},{3,5},{5,3},{7,1},{8,14},{10,12},{12... | collective-permute-start | bytes 884744 | tf_op jit(solution)/shard_map/ppermute | solution.py:947
  47.9 24.8 %collective-permute-start.8 = (bf16[1024,384]{1,0:T(8,128)(2,1)S(1)}, bf16[1024,384]{1,0:T(8,128)(2,1)S(1)}, u32[]{:S(2)}, u32[]{:S(2)}) collective-permute-start(bf16[1024,384]{1,0:T(8,128)(2,1)S(1)} %maximum_dynamic-update-slice_fusion.refs_5_), channel_id=1, source_target_pairs={{0,8},{8,0},{16,24},{24,16},{1,9},{9,1},{17,25},{25,17},{2,10},{10... | collective-permute-start | bytes 2359304 | tf_op jit(solution)/shard_map/ppermute | solution.py:947
  47.9 24.8 %collective-permute-start.9 = (bf16[1024,384]{1,0:T(8,128)(2,1)S(1)}, bf16[1024,384]{1,0:T(8,128)(2,1)S(1)}, u32[]{:S(2)}, u32[]{:S(2)}) collective-permute-start(bf16[1024,384]{1,0:T(8,128)(2,1)S(1)} %maximum_dynamic-update-slice_fusion.refs_5_), channel_id=1, source_target_pairs={{0,16},{8,24},{16,0},{24,8},{1,17},{9,25},{17,1},{25,9},{2,18},{10... | collective-permute-start | bytes 2359304 | tf_op jit(solution)/shard_map/ppermute | solution.py:947
  74.4 16.2 %collective-permute-start.14 = (bf16[576,384]{1,0:T(8,128)(2,1)S(1)}, bf16[576,384]{1,0:T(8,128)(2,1)S(1)}, u32[]{:S(2)}, u32[]{:S(2)}) collective-permute-start(bf16[576,384]{1,0:T(8,128)(2,1)S(1)} %slice.305), channel_id=1, source_target_pairs={{0,16},{8,24},{16,0},{24,8},{1,17},{9,25},{17,1},{25,9},{2,18},{10... | collective-permute-start | bytes 1327112 | tf_op jit(solution)/shard_map/ppermute | solution.py:947
  74.5 16.1 %collective-permute-start.15 = (bf16[448,384]{1,0:T(8,128)(2,1)S(1)}, bf16[448,384]{1,0:T(8,128)(2,1)S(1)}, u32[]{:S(2)}, u32[]{:S(2)}) collective-permute-start(bf16[448,384]{1,0:T(8,128)(2,1)S(1)} %slice.306), channel_id=1, source_target_pairs={{0,8},{8,0},{16,24},{24,16},{1,9},{9,1},{17,25},{25,17},{2,10},{10... | collective-permute-start | bytes 1032200 | tf_op jit(solution)/shard_map/ppermute | solution.py:947
  75.1 14.8 %collective-permute-start.17 = (bf16[145,896]{1,0:T(8,128)(2,1)S(1)}, bf16[145,896]{1,0:T(8,128)(2,1)S(1)}, u32[]{:S(2)}, u32[]{:S(2)}) collective-permute-start(bf16[145,896]{1,0:T(8,128)(2,1)S(1)} %fusion.22), channel_id=1, source_target_pairs={{0,0},{1,2},{2,1},{3,3},{4,8},{5,10},{6,9},{7,11},{8,4},{9,6},{10,... | collective-permute-start | bytes 779528 | tf_op jit(solution)/shard_map/ppermute | solution.py:943
  90.9 27.3 %collective-permute-start.18 = (bf16[2,2,192,768]{3,2,1,0:T(8,128)(2,1)S(1)}, bf16[2,2,192,768]{3,2,1,0:T(8,128)(2,1)}, u32[]{:S(2)}, u32[]{:S(2)}) collective-permute-start(bf16[2,2,192,768]{3,2,1,0:T(8,128)(2,1)S(1)} %pad_maximum_fusion.1.refs_5_), channel_id=1, source_target_pairs={{0,8},{8,0},{16,24},{24,16},{1,9},{9,1},{17,25},{25,17},{2,10},{10... | collective-permute-start | bytes 3538952 | tf_op jit(solution)/shard_map/ppermute | solution.py:947
  91.0 27.3 %collective-permute-start.19 = (bf16[2,2,192,768]{3,2,1,0:T(8,128)(2,1)S(1)}, bf16[2,2,192,768]{3,2,1,0:T(8,128)(2,1)}, u32[]{:S(2)}, u32[]{:S(2)}) collective-permute-start(bf16[2,2,192,768]{3,2,1,0:T(8,128)(2,1)S(1)} %pad_maximum_fusion.1.refs_5_), channel_id=1, source_target_pairs={{0,16},{8,24},{16,0},{24,8},{1,17},{9,25},{17,1},{25,9},{2,18},{10... | collective-permute-start | bytes 3538952 | tf_op jit(solution)/shard_map/ppermute | solution.py:947
  95.8 205.7 %all-gather.7.cloned.1.call-start = ((), (), s32[]{:S(2)}) async-start(), calls=%async_computation.3 | async-start | bytes 5898240 | tf_op jit(solution)/shard_map/all_gather | solution.py:1205
  119.5 13.6 %collective-permute-start.20 = (bf16[2,192,768]{2,1,0:T(8,128)(2,1)S(1)}, bf16[2,192,768]{2,1,0:T(8,128)(2,1)S(1)}, u32[]{:S(2)}, u32[]{:S(2)}) collective-permute-start(bf16[2,192,768]{2,1,0:T(8,128)(2,1)S(1)} %slice_bitcast_fusion.1), channel_id=1, source_target_pairs={{0,16},{8,24},{16,0},{24,8},{1,17},{9,25},{17,1},{25,9},{2,18},{10... | collective-permute-start | bytes 1769480 | tf_op jit(solution)/shard_map/ppermute | solution.py:947
  122.1 13.1 %collective-permute-start.21 = (bf16[2,192,768]{2,1,0:T(8,128)(2,1)S(1)}, bf16[2,192,768]{2,1,0:T(8,128)(2,1)S(1)}, u32[]{:S(2)}, u32[]{:S(2)}) collective-permute-start(bf16[2,192,768]{2,1,0:T(8,128)(2,1)S(1)} %slice_bitcast_fusion), channel_id=1, source_target_pairs={{0,8},{8,0},{16,24},{24,16},{1,9},{9,1},{17,25},{25,17},{2,10},{10... | collective-permute-start | bytes 1769480 | tf_op jit(solution)/shard_map/ppermute | solution.py:947
  150.9 19.5 %collective-permute-start.26 = (bf16[768,1536]{1,0:T(8,128)(2,1)}, bf16[768,1536]{1,0:T(8,128)(2,1)}, u32[]{:S(2)}, u32[]{:S(2)}) collective-permute-start(bf16[768,1536]{1,0:T(8,128)(2,1)} %bitcast.61.refs_4_.refs_1_), channel_id=1, source_target_pairs={{0,1},{1,0},{2,3},{3,2},{4,5},{5,4},{6,7},{7,6},{8,9},{9,8},{10,11... | collective-permute-start | bytes 7077896 | tf_op jit(solution)/shard_map/ppermute | solution.py:947
  151.1 19.3 %collective-permute-start.27 = (bf16[1536,768]{1,0:T(8,128)(2,1)}, bf16[1536,768]{1,0:T(8,128)(2,1)}, u32[]{:S(2)}, u32[]{:S(2)}) collective-permute-start(bf16[1536,768]{1,0:T(8,128)(2,1)} %bitcast.62.refs_5_.refs_2_), channel_id=1, source_target_pairs={{0,1},{1,0},{2,3},{3,2},{4,5},{5,4},{6,7},{7,6},{8,9},{9,8},{10,11... | collective-permute-start | bytes 7077896 | tf_op jit(solution)/shard_map/ppermute | solution.py:947
  175.6 9.8 %collective-permute-start.28 = (bf16[192,768]{1,0:T(8,128)(2,1)S(1)}, bf16[192,768]{1,0:T(8,128)(2,1)S(1)}, u32[]{:S(2)}, u32[]{:S(2)}) collective-permute-start(bf16[192,768]{1,0:T(8,128)(2,1)S(1)} %get-tuple-element.172), channel_id=1, source_target_pairs={{0,8},{8,0},{16,24},{24,16},{1,9},{9,1},{17,25},{25,17},{2,10},{10... | collective-permute-start | bytes 884744 | tf_op jit(solution)/shard_map/ppermute | solution.py:947
  177.0 15.3 %collective-permute-start.29 = (bf16[192,768]{1,0:T(8,128)(2,1)S(1)}, bf16[192,768]{1,0:T(8,128)(2,1)S(1)}, u32[]{:S(2)}, u32[]{:S(2)}) collective-permute-start(bf16[192,768]{1,0:T(8,128)(2,1)S(1)} %get-tuple-element.173), channel_id=1, source_target_pairs={{0,16},{8,24},{16,0},{24,8},{1,17},{9,25},{17,1},{25,9},{2,18},{10... | collective-permute-start | bytes 884744 | tf_op jit(solution)/shard_map/ppermute | solution.py:947
  177.8 14.6 %collective-permute-start.30 = (bf16[192,768]{1,0:T(8,128)(2,1)S(1)}, bf16[192,768]{1,0:T(8,128)(2,1)S(1)}, u32[]{:S(2)}, u32[]{:S(2)}) collective-permute-start(bf16[192,768]{1,0:T(8,128)(2,1)S(1)} %get-tuple-element.174), channel_id=1, source_target_pairs={{0,24},{8,16},{16,8},{24,0},{1,25},{9,17},{17,9},{25,1},{2,26},{10... | collective-permute-start | bytes 884744 | tf_op jit(solution)/shard_map/ppermute | solution.py:947
  194.4 224.5 %reduce-scatter.2.cloned.1.call-start = ((), (), s32[]{:S(2)}) async-start(), calls=%async_computation.1 | async-start | bytes 1536000 | tf_op jit(solution)/shard_map/reduce_scatter | solution.py:1236
  208.2 10.2 %collective-permute-start.31 = (bf16[192,768]{1,0:T(8,128)(2,1)}, bf16[192,768]{1,0:T(8,128)(2,1)S(1)}, u32[]{:S(2)}, u32[]{:S(2)}) collective-permute-start(bf16[192,768]{1,0:T(8,128)(2,1)} %get-tuple-element.176), channel_id=1, source_target_pairs={{0,8},{8,0},{16,24},{24,16},{1,9},{9,1},{17,25},{25,17},{2,10},{10... | collective-permute-start | bytes 884744 | tf_op jit(solution)/shard_map/ppermute | solution.py:947
  208.9 14.5 %collective-permute-start.32 = (bf16[192,768]{1,0:T(8,128)(2,1)}, bf16[192,768]{1,0:T(8,128)(2,1)S(1)}, u32[]{:S(2)}, u32[]{:S(2)}) collective-permute-start(bf16[192,768]{1,0:T(8,128)(2,1)} %get-tuple-element.177), channel_id=1, source_target_pairs={{0,16},{8,24},{16,0},{24,8},{1,17},{9,25},{17,1},{25,9},{2,18},{10... | collective-permute-start | bytes 884744 | tf_op jit(solution)/shard_map/ppermute | solution.py:947
  209.9 13.5 %collective-permute-start.33 = (bf16[192,768]{1,0:T(8,128)(2,1)}, bf16[192,768]{1,0:T(8,128)(2,1)S(1)}, u32[]{:S(2)}, u32[]{:S(2)}) collective-permute-start(bf16[192,768]{1,0:T(8,128)(2,1)} %get-tuple-element.178), channel_id=1, source_target_pairs={{0,24},{8,16},{16,8},{24,0},{1,25},{9,17},{17,9},{25,1},{2,26},{10... | collective-permute-start | bytes 884744 | tf_op jit(solution)/shard_map/ppermute | solution.py:947
  239.0 13.3 %collective-permute-start.35 = (bf16[320,768]{1,0:T(8,128)(2,1)S(1)}, bf16[320,768]{1,0:T(8,128)(2,1)S(1)}, u32[]{:S(2)}, u32[]{:S(2)}) collective-permute-start(bf16[320,768]{1,0:T(8,128)(2,1)S(1)} %get-tuple-element.193), channel_id=1, source_target_pairs={{0,8},{8,0},{16,24},{24,16},{1,9},{9,1},{17,25},{25,17},{2,10},{10... | collective-permute-start | bytes 1474568 | tf_op jit(solution)/shard_map/ppermute | solution.py:947
  259.4 50.0 %collective-permute-start.52 = (bf16[2,832,384]{2,1,0:T(8,128)(2,1)}, bf16[2,832,384]{2,1,0:T(8,128)(2,1)}, u32[]{:S(2)}, u32[]{:S(2)}) collective-permute-start(bf16[2,832,384]{2,1,0:T(8,128)(2,1)} %get-tuple-element.237), channel_id=1, source_target_pairs={{0,8},{8,0},{16,24},{24,16},{1,9},{9,1},{17,25},{25,17},{2,10},{10... | collective-permute-start | bytes 3833864 | tf_op jit(solution)/shard_map/ppermute | solution.py:947
  275.1 36.8 %collective-permute-start.54 = (bf16[2,2,192,768]{3,2,1,0:T(8,128)(2,1)}, bf16[2,2,192,768]{3,2,1,0:T(8,128)(2,1)}, u32[]{:S(2)}, u32[]{:S(2)}) collective-permute-start(bf16[2,2,192,768]{3,2,1,0:T(8,128)(2,1)} %get-tuple-element.241), channel_id=1, source_target_pairs={{0,16},{8,24},{16,0},{24,8},{1,17},{9,25},{17,1},{25,9},{2,18},{10... | collective-permute-start | bytes 3538952 | tf_op jit(solution)/shard_map/ppermute | solution.py:947
  286.7 13.9 %collective-permute-start.38 = (bf16[320,768]{1,0:T(8,128)(2,1)S(1)}, bf16[320,768]{1,0:T(8,128)(2,1)S(1)}, u32[]{:S(2)}, u32[]{:S(2)}) collective-permute-start(bf16[320,768]{1,0:T(8,128)(2,1)S(1)} %get-tuple-element.211), channel_id=1, source_target_pairs={{0,8},{8,0},{16,24},{24,16},{1,9},{9,1},{17,25},{25,17},{2,10},{10... | collective-permute-start | bytes 1474568 | tf_op jit(solution)/shard_map/ppermute | solution.py:947
  287.7 52.7 %collective-permute-start.45 = (bf16[2,2,192,768]{3,2,1,0:T(8,128)(2,1)}, bf16[2,2,192,768]{3,2,1,0:T(8,128)(2,1)}, u32[]{:S(2)}, u32[]{:S(2)}) collective-permute-start(bf16[2,2,192,768]{3,2,1,0:T(8,128)(2,1)} %get-tuple-element.225), channel_id=1, source_target_pairs={{0,16},{8,24},{16,0},{24,8},{1,17},{9,25},{17,1},{25,9},{2,18},{10... | collective-permute-start | bytes 3538952 | tf_op jit(solution)/shard_map/ppermute | solution.py:947
  308.4 38.6 %collective-permute-start.41 = (bf16[2,384,384]{2,1,0:T(8,128)(2,1)S(1)}, bf16[2,384,384]{2,1,0:T(8,128)(2,1)}, u32[]{:S(2)}, u32[]{:S(2)}) collective-permute-start(bf16[2,384,384]{2,1,0:T(8,128)(2,1)S(1)} %get-tuple-element.218), channel_id=1, source_target_pairs={{0,8},{8,0},{16,24},{24,16},{1,9},{9,1},{17,25},{25,17},{2,10},{10... | collective-permute-start | bytes 1769480 | tf_op jit(solution)/shard_map/ppermute | solution.py:947
  309.4 40.6 %collective-permute-start.43 = (bf16[2,384,384]{2,1,0:T(8,128)(2,1)}, bf16[2,384,384]{2,1,0:T(8,128)(2,1)}, u32[]{:S(2)}, u32[]{:S(2)}) collective-permute-start(bf16[2,384,384]{2,1,0:T(8,128)(2,1)} %get-tuple-element.222), channel_id=1, source_target_pairs={{0,16},{8,24},{16,0},{24,8},{1,17},{9,25},{17,1},{25,9},{2,18},{10... | collective-permute-start | bytes 1769480 | tf_op jit(solution)/shard_map/ppermute | solution.py:947
  315.1 30.0 %collective-permute-start.55 = (bf16[2,192,768]{2,1,0:T(8,128)(2,1)}, bf16[2,192,768]{2,1,0:T(8,128)(2,1)}, u32[]{:S(2)}, u32[]{:S(2)}) collective-permute-start(bf16[2,192,768]{2,1,0:T(8,128)(2,1)} %fusion.11), channel_id=1, source_target_pairs={{0,8},{8,0},{16,24},{24,16},{1,9},{9,1},{17,25},{25,17},{2,10},{10... | collective-permute-start | bytes 1769480 | tf_op jit(solution)/shard_map/ppermute | solution.py:947
  340.4 46.8 %collective-permute-start.50 = (bf16[768,1536]{1,0:T(8,128)(2,1)}, bf16[768,1536]{1,0:T(8,128)(2,1)}, u32[]{:S(2)}, u32[]{:S(2)}) collective-permute-start(bf16[768,1536]{1,0:T(8,128)(2,1)} %get-tuple-element.219), channel_id=1, source_target_pairs={{0,1},{1,0},{2,3},{3,2},{4,5},{5,4},{6,7},{7,6},{8,9},{9,8},{10,11... | collective-permute-start | bytes 7077896 | tf_op jit(solution)/shard_map/ppermute | solution.py:947
  342.1 45.1 %collective-permute-start.51 = (bf16[1536,768]{1,0:T(8,128)(2,1)}, bf16[1536,768]{1,0:T(8,128)(2,1)}, u32[]{:S(2)}, u32[]{:S(2)}) collective-permute-start(bf16[1536,768]{1,0:T(8,128)(2,1)} %get-tuple-element.231), channel_id=1, source_target_pairs={{0,1},{1,0},{2,3},{3,2},{4,5},{5,4},{6,7},{7,6},{8,9},{9,8},{10,11... | collective-permute-start | bytes 7077896 | tf_op jit(solution)/shard_map/ppermute | solution.py:947
  345.0 16.4 %collective-permute-start.53 = (bf16[832,384]{1,0:T(8,128)(2,1)S(1)}, bf16[832,384]{1,0:T(8,128)(2,1)S(1)}, u32[]{:S(2)}, u32[]{:S(2)}) collective-permute-start(bf16[832,384]{1,0:T(8,128)(2,1)S(1)} %copy-done.67), channel_id=1, source_target_pairs={{0,16},{8,24},{16,0},{24,8},{1,17},{9,25},{17,1},{25,9},{2,18},{10... | collective-permute-start | bytes 1916936 | tf_op jit(solution)/shard_map/ppermute | solution.py:947
  347.0 25.2 %collective-permute-start.46 = (bf16[2,192,768]{2,1,0:T(8,128)(2,1)}, bf16[2,192,768]{2,1,0:T(8,128)(2,1)}, u32[]{:S(2)}, u32[]{:S(2)}) collective-permute-start(bf16[2,192,768]{2,1,0:T(8,128)(2,1)} %fusion.10), channel_id=1, source_target_pairs={{0,8},{8,0},{16,24},{24,16},{1,9},{9,1},{17,25},{25,17},{2,10},{10... | collective-permute-start | bytes 1769480 | tf_op jit(solution)/shard_map/ppermute | solution.py:947
  350.0 29.6 %collective-permute-start.40 = (bf16[2,145,768]{2,1,0:T(8,128)(2,1)}, bf16[2,145,768]{2,1,0:T(8,128)(2,1)S(1)}, u32[]{:S(2)}, u32[]{:S(2)}) collective-permute-start(bf16[2,145,768]{2,1,0:T(8,128)(2,1)} %pad_maximum_fusion.8), channel_id=1, source_target_pairs={{0,0},{1,2},{2,1},{3,3},{4,8},{5,10},{6,9},{7,11},{8,4},{9,6},{10,... | collective-permute-start | bytes 1336328 | tf_op jit(solution)/shard_map/ppermute | solution.py:943
  361.4 13.6 %collective-permute-start.42 = (bf16[384,384]{1,0:T(8,128)(2,1)}, bf16[384,384]{1,0:T(8,128)(2,1)S(1)}, u32[]{:S(2)}, u32[]{:S(2)}) collective-permute-start(bf16[384,384]{1,0:T(8,128)(2,1)} %fusion.20), channel_id=1, source_target_pairs={{0,16},{8,24},{16,0},{24,8},{1,17},{9,25},{17,1},{25,9},{2,18},{10... | collective-permute-start | bytes 884744 | tf_op jit(solution)/shard_map/ppermute | solution.py:947
  382.0 27.8 %collective-permute-start.47 = (bf16[48,3072]{1,0:T(8,128)(2,1)S(1)}, bf16[48,3072]{1,0:T(8,128)(2,1)S(1)}, u32[]{:S(2)}, u32[]{:S(2)}) collective-permute-start(bf16[48,3072]{1,0:T(8,128)(2,1)S(1)} %get-tuple-element.228), channel_id=1, source_target_pairs={{0,2},{2,0},{4,6},{6,4},{1,3},{3,1},{5,7},{7,5},{8,10},{10,8},{12,... | collective-permute-start | bytes 884744 | tf_op jit(solution)/shard_map/ppermute | solution.py:947
  382.0 29.9 %collective-permute-start.48 = (bf16[48,3072]{1,0:T(8,128)(2,1)S(1)}, bf16[48,3072]{1,0:T(8,128)(2,1)S(1)}, u32[]{:S(2)}, u32[]{:S(2)}) collective-permute-start(bf16[48,3072]{1,0:T(8,128)(2,1)S(1)} %get-tuple-element.229), channel_id=1, source_target_pairs={{0,4},{2,6},{4,0},{6,2},{1,5},{3,7},{5,1},{7,3},{8,12},{10,14},{12... | collective-permute-start | bytes 884744 | tf_op jit(solution)/shard_map/ppermute | solution.py:947
  387.2 31.5 %collective-permute-start.49 = (bf16[48,3072]{1,0:T(8,128)(2,1)S(1)}, bf16[48,3072]{1,0:T(8,128)(2,1)S(1)}, u32[]{:S(2)}, u32[]{:S(2)}) collective-permute-start(bf16[48,3072]{1,0:T(8,128)(2,1)S(1)} %get-tuple-element.230), channel_id=1, source_target_pairs={{0,6},{2,4},{4,2},{6,0},{1,7},{3,5},{5,3},{7,1},{8,14},{10,12},{12... | collective-permute-start | bytes 884744 | tf_op jit(solution)/shard_map/ppermute | solution.py:947
  421.6 13.8 %collective-permute-start.56 = (f32[24,3968]{1,0:T(8,128)S(1)}, f32[24,3968]{1,0:T(8,128)S(1)}, u32[]{:S(2)}, u32[]{:S(2)}) collective-permute-start(f32[24,3968]{1,0:T(8,128)S(1)} %get-tuple-element.333), channel_id=1, source_target_pairs={{0,1},{1,0},{2,3},{3,2},{4,5},{5,4},{6,7},{7,6},{8,9},{9,8},{10,11... | collective-permute-start | bytes 1142792 | tf_op jit(solution)/shard_map/ppermute | solution.py:947
  421.7 13.0 %collective-permute-start.57 = (f32[48,768]{1,0:T(8,128)S(1)}, f32[48,768]{1,0:T(8,128)S(1)}, u32[]{:S(2)}, u32[]{:S(2)}) collective-permute-start(f32[48,768]{1,0:T(8,128)S(1)} %maximum_maximum_fusion), channel_id=1, source_target_pairs={{0,0},{2,1},{4,2},{6,3},{8,4},{10,5},{12,6},{14,7},{16,8},{18,9},{... | collective-permute-start | bytes 442376 | tf_op jit(solution)/shard_map/ppermute | solution.py:1097
  (104 other events, 495.3 us)
Sparse Core Ops, SparseCore 0:
  95.9 47.9 all-gather.4
  194.5 88.3 all-gather.6
  363.7 39.6 reduce-scatter.1

commit v6 on v5

--- a/solution.py
+++ b/solution.py
@@ -353,6 +353,22 @@
     return out if packed else [*out, source]
 
 
+def widen_copies(e, blocks, wi_ref, wo_ref, sems):
+    copies = []
+    feat = wo_ref.shape[1]
+    n = feat // 4
+    for h in range(2):
+        for j in range(4):
+            src = blocks[j].at[h] if j < 3 else blocks[3 + h]
+            at = (e ^ j) * n
+            for part, dst in (
+                (0, wi_ref.at[pl.ds(pl.multiple_of(at, 16), n), pl.ds(h * feat, feat)]),
+                (1, wo_ref.at[pl.ds(pl.multiple_of(at + h * feat, 16), n)]),
+            ):
+                copies.append(pltpu.make_async_copy(src.at[part], dst, sems.at[len(copies)]))
+    return copies
+
+
 def widen_forward(where, x, part, got, gains, blocks, rows, after=()):
     r2, feat = x.shape
     wide = 2 * feat
@@ -362,58 +378,53 @@
         where_ref, x_ref, part_ref, got_ref, gains_ref, z0, z1, z2, a3, b3,
         x1_ref, normed_ref, hidden_ref, out_ref, low_ref, wi_ref, wo_ref, sems,
     ):
-        n = feat // 4
-        copies = []
-        for h, last in enumerate((a3, b3)):
-            pairs = [z0.at[h], z1.at[h], z2.at[h], last]
-            for j in range(4):
-                at = (where_ref[1] ^ j) * n
-                for src, dst in (
-                    (pairs[j].at[0], wi_ref.at[pl.ds(pl.multiple_of(at, 16), n), pl.ds(h * feat, feat)]),
-                    (pairs[j].at[1], wo_ref.at[pl.ds(pl.multiple_of(at + h * feat, 16), n)]),
-                ):
-                    copies.append(pltpu.make_async_copy(src, dst, sems.at[len(copies)]))
+        copies = widen_copies(where_ref[1], (z0, z1, z2, a3, b3), wi_ref, wo_ref, sems)
         start_all(copies)
         x1 = add_both(x_ref[...] + part_ref[...], got_ref[...], rows)
         x1_ref[...] = x1
         normed_ref[...] = layer_norm(x1, gains_ref[pl.ds(1, 1), :])
-        wait_all(copies)
         out_ref[...] = jnp.zeros_like(out_ref)
-
-        @pl.loop(0, wide // tile)
-        def _(t):
-            at = pl.ds(pl.multiple_of(t * tile, 128), tile)
-            h = dot(normed_ref[...], wi_ref[:, at])
-            hidden_ref[:, at] = h
-            out_ref[...] += dot(gelu_both(h)[0].astype(BF), wo_ref[at, :])
+        for half in range(2):
+            wait_all(copies[8 * half : 8 * half + 8])
+
+            @pl.loop(half * (feat // tile), (half + 1) * (feat // tile))
+            def _(t):
+                at = pl.ds(pl.multiple_of(t * tile, 128), tile)
+                h = dot(normed_ref[...], wi_ref[:, at])
+                hidden_ref[:, at] = h.astype(BF)
+                out_ref[...] += dot(gelu_both(h)[0].astype(BF), wo_ref[at, :])
 
         low_ref[...] = out_ref[...].astype(BF)
 
     return call(
         kernel,
         [
-            ((r2, feat), F32, VM), ((r2, feat), BF, VM), ((r2, wide), F32, VM), ((r2, feat), F32, VM),
-            ((r2, feat), BF, VM), ((feat, wide), BF, VM), ((wide, feat), BF, VM),
+            ((r2, feat), F32, VM), ((r2, feat), BF, VM), ((r2, wide), BF, VM), ((r2, feat), F32, VM),
+            ((r2, feat), BF, VM),
         ],
         [(where, SM), (x, VM), (part, VM), (got, VM), (gains, VM)] + [(t, HB) for t in blocks],
-        scratch=[pltpu.SemaphoreType.DMA((16,))],
+        scratch=[
+            pltpu.VMEM((feat, wide), BF), pltpu.VMEM((wide, feat), BF), pltpu.SemaphoreType.DMA((16,)),
+        ],
         after=after,
         flops=4 * r2 * feat * wide,
         bytes_accessed=16 * 2**20,
     )
 
 
-def widen_back(where, u, x, gains, part, got, normed, hidden, wi, wo, first, rows, columns, after=()):
+def widen_back(where, u, x, gains, part, got, normed, hidden, blocks, first, rows, columns, after=()):
     r2, feat = u.shape
     wide = 2 * feat
     tile = 384
     n = feat // 4
 
     def kernel(
-        where_ref, u_ref, x_ref, gains_ref, part_ref, got_ref, normed_ref, hidden_ref, wi_ref, wo_ref,
-        u2_ref, out_ref, low_ref, *more,
+        where_ref, u_ref, x_ref, gains_ref, part_ref, got_ref, normed_ref, hidden_ref,
+        z0, z1, z2, a3, b3, u2_ref, out_ref, low_ref, *more,
     ):
-        outs, (ulow_ref, turned_ref, wis_ref, wos_ref, sems) = more[:-5], more[-5:]
+        outs, (ulow_ref, turned_ref, wis_ref, wos_ref, wi_ref, wo_ref, in_sems, sems) = more[:-8], more[-8:]
+        arriving = widen_copies(where_ref[1], (z0, z1, z2, a3, b3), wi_ref, wo_ref, in_sems)
+        start_all(arriving)
         slope = add_both(part_ref[...], got_ref[...], rows)
         u2 = u_ref[...] + norm_back(x_ref[...], gains_ref[pl.ds(2, 1), :], slope)[0]
         u2_ref[...] = u2
@@ -421,16 +432,6 @@
         turned_ref[...] = normed_ref[...].T
         out_ref[...] = jnp.zeros_like(out_ref)
 
-        @pl.loop(0, wide // tile)
-        def _(t):
-            at = pl.ds(pl.multiple_of(t * tile, 128), tile)
-            ulow = ulow_ref[...]
-            act, dact = gelu_both(hidden_ref[:, at])
-            hs = (dact * dot_t(ulow, wo_ref[at, :])).astype(BF)
-            wos_ref[at, :] = t_dot(act.astype(BF), ulow).astype(BF)
-            wis_ref[:, at] = dot(turned_ref[...], hs).astype(BF)
-            out_ref[...] += dot_t(hs, wi_ref[:, at])
-
         copies = []
         slots = (0, 3 - first, first, 3)
 
@@ -439,16 +440,29 @@
             deep_at = pl.ds(pl.multiple_of(at + h * feat, 16), size)
             for i, src in enumerate((wis_ref.at[wide_at, pl.ds(h * feat, feat)], wos_ref.at[deep_at])):
                 copies.append(pltpu.make_async_copy(src, dst.at[i], sems.at[len(copies)]))
-
-        for i, j in enumerate(slots):
-            to = (where_ref[1] ^ j) * n
-            add(0, to, n, outs[i // 2].at[i % 2])
-            if columns:
-                for c in range(4):
-                    add(1, to + c * (n // 4), n // 4, outs[2].at[c, i])
-            else:
-                add(1, to, n, outs[2 + i // 2].at[i % 2])
-        start_all(copies)
+                copies[-1].start()
+
+        for h in range(2):
+            wait_all(arriving[8 * h : 8 * h + 8])
+
+            @pl.loop(h * (feat // tile), (h + 1) * (feat // tile))
+            def _(t):
+                at = pl.ds(pl.multiple_of(t * tile, 128), tile)
+                ulow = ulow_ref[...]
+                act, dact = gelu_both(hidden_ref[:, at].astype(F32))
+                hs = (dact * dot_t(ulow, wo_ref[at, :])).astype(BF)
+                wos_ref[at, :] = t_dot(act.astype(BF), ulow).astype(BF)
+                wis_ref[:, at] = dot(turned_ref[...], hs).astype(BF)
+                out_ref[...] += dot_t(hs, wi_ref[:, at])
+
+            for i, j in enumerate(slots):
+                to = (where_ref[1] ^ j) * n
+                if h == 1 and columns:
+                    for c in range(4):
+                        add(1, to + c * (n // 4), n // 4, outs[2].at[c, i])
+                else:
+                    add(h, to, n, outs[2 * h + i // 2].at[i % 2])
+
         low_ref[...] = out_ref[...].astype(BF)
         wait_all(copies)
 
@@ -459,11 +473,13 @@
         [((r2, feat), F32, VM), ((r2, feat), F32, VM), ((r2, feat), BF, VM)] + [block] * 2 + more,
         [
             (where, SM), (u, VM), (x, VM), (gains, VM), (part, VM), (got, VM), (normed, VM),
-            (hidden, VM), (wi, VM), (wo, VM),
-        ],
+            (hidden, VM),
+        ]
+        + [(t, HB) for t in blocks],
         scratch=[
             pltpu.VMEM((r2, feat), BF), pltpu.VMEM((feat, r2), BF), pltpu.VMEM((feat, wide), BF),
-            pltpu.VMEM((wide, feat), BF), pltpu.SemaphoreType.DMA((40,)),
+            pltpu.VMEM((wide, feat), BF), pltpu.VMEM((feat, wide), BF), pltpu.VMEM((wide, feat), BF),
+            pltpu.SemaphoreType.DMA((16,)), pltpu.SemaphoreType.DMA((40,)),
         ],
         after=after,
         flops=10 * r2 * feat * wide,
@@ -1182,7 +1198,7 @@
         where, q1, kv1, far1, wp1, solo=False, **img
     )
     blocks2 = wt.spread_pair(pair2, part)
-    x1, normed2, hidden, part2, low2, wi, wo = widen_forward(
+    x1, normed2, hidden, part2, low2 = widen_forward(
         where, x0, part, links.sib(low), gains, blocks2, rows
     )
     x2, normed3, own3 = norm_next(x1, part2, links.sib(low2), gains, 2, rows)
@@ -1216,7 +1232,7 @@
         where, dq, own, links.partner(far), normed3, wa3, wps, small_slopes, first3, rows, False
     )
     u, part, low, *slopes2 = widen_back(
-        where, u, x2, gains, part, links.sib(low), normed2, hidden, wi, wo, first2, rows, False
+        where, u, x2, gains, part, links.sib(low), normed2, hidden, blocks2, first2, rows, False
     )
     u1, u_low = norm_step(u, x1, gains, 1, part, links.sib(low), rows, 0)
     dq1, own, far, wps = attend_core_back(where, u_low, wp1, blend1, q1, kv1, far1, lse1, **img)

time: 455 us -> 453 us (level)
    unnamed x193 -> x199, local copies, waits for them, and re-layouts: 26.3 us -> 25.5 us
  transfers between devices with their start and end apart: 61 -> 61, of which waited for: 32 -> 32; matrix products, arithmetic and copies ran while one was open for 8% -> 8% of each run, Pallas kernels for 30% -> 29%
where the time goes in v6:
time: 453 us; the launch traced here: 447 us
  waiting for transfers between devices  168 us (37%)
  Pallas kernels  134 us (30%)
  starting transfers between devices  60.6 us (13%)
  local copies, waits for them, and re-layouts  42.8 us (9%)
  other arithmetic  24.9 us (5%)
  between operations  16 us (4%)
    ppermute x53, waiting for transfers between devices, xor(): return lax.ppermute(x, axis, [(i, i ^ j) for i in range(n)])  145 us
    pallas_call x18, Pallas kernels, call(): pl.pallas_call(run, grid=grid, out_shape=[jax.ShapeDtypeStruct(s, t) for...  76.4 us
    pallas_call x2, Pallas kernels, expert_slopes(): pl.pallas_call(kernel, grid=(steps,), out_shape=[jax.ShapeDtypeStruct((fe...  44.1 us
    ppermute x53, starting transfers between devices, xor(): return lax.ppermute(x, axis, [(i, i ^ j) for i in range(n)])  42.2 us
    unnamed x199, local copies, waits for them, and re-layouts  25.5 us
    pallas_call x1, Pallas kernels, experts_forward(): pl.pallas_call(kernel, grid=(2 * steps,), out_shape=[jax.ShapeDtypeStruct...  13.8 us
    ppermute x3, starting transfers between devices, move(): return lax.ppermute(x, ALL, self.team)  11.5 us
    ppermute x3, waiting for transfers between devices, move(): return lax.ppermute(x, ALL, self.team)  10.8 us
  transfers between devices with their start and end apart: 61, of which 32 were waited for; matrix products, arithmetic and copies ran while one was open for 8% of the time, Pallas kernels for 29%

profile of v6, /device:TPU:10, one launch (start us, length us, event | category | flops | bytes accessed | tf_op | source)
XLA Modules:
  0.0 446.9 jit_solution(1401835700049872552)
XLA Ops:
  7.2 2.9 collective-permute-start
  14.2 4.0 collective-permute-start.3
  18.4 6.0 %collective-permute-done.3 = bf16[48,768]{1,0:T(8,128)(2,1)S(1)} collective-permute-done((bf16[48,768]{1,0:T(8,128)(2,1)S(1)}, bf16[48,768]{1,0:T(8,128)(2,1)S(1)}, u32[]{:S(2)}, u32[]{:S(2)}) %collective-permute-start.3) | collective-permute-done | bytes 73760 | tf_op jit(solution)/shard_map/ppermute | solution.py:1145
  28.2 3.7 collective-permute-done.4
  31.9 5.7 %collective-permute-done.5 = bf16[48,1664]{1,0:T(8,128)(2,1)S(1)} collective-permute-done((bf16[48,1664]{1,0:T(8,128)(2,1)S(1)}, bf16[48,1664]{1,0:T(8,128)(2,1)S(1)}, u32[]{:S(2)}, u32[]{:S(2)}) %collective-permute-start.5) | collective-permute-done | bytes 159776 | tf_op jit(solution)/shard_map/ppermute | solution.py:963
  37.7 5.4 %collective-permute-done.6 = bf16[48,1664]{1,0:T(8,128)(2,1)S(1)} collective-permute-done((bf16[48,1664]{1,0:T(8,128)(2,1)S(1)}, bf16[48,1664]{1,0:T(8,128)(2,1)S(1)}, u32[]{:S(2)}, u32[]{:S(2)}) %collective-permute-start.6) | collective-permute-done | bytes 159776 | tf_op jit(solution)/shard_map/ppermute | solution.py:963
  49.2 5.9 %collective-permute-done.10 = bf16[48,3072]{1,0:T(8,128)(2,1)S(1)} collective-permute-done((bf16[48,3072]{1,0:T(8,128)(2,1)S(1)}, bf16[48,3072]{1,0:T(8,128)(2,1)S(1)}, u32[]{:S(2)}, u32[]{:S(2)}) %collective-permute-start.10) | collective-permute-done | bytes 294944 | tf_op jit(solution)/shard_map/ppermute | solution.py:963
  55.0 10.3 %collective-permute-done.11 = bf16[48,3072]{1,0:T(8,128)(2,1)S(1)} collective-permute-done((bf16[48,3072]{1,0:T(8,128)(2,1)S(1)}, bf16[48,3072]{1,0:T(8,128)(2,1)S(1)}, u32[]{:S(2)}, u32[]{:S(2)}) %collective-permute-start.11) | collective-permute-done | bytes 294944 | tf_op jit(solution)/shard_map/ppermute | solution.py:963
  65.4 7.0 %collective-permute-done.12 = bf16[48,3072]{1,0:T(8,128)(2,1)S(1)} collective-permute-done((bf16[48,3072]{1,0:T(8,128)(2,1)S(1)}, bf16[48,3072]{1,0:T(8,128)(2,1)S(1)}, u32[]{:S(2)}, u32[]{:S(2)}) %collective-permute-start.12) | collective-permute-done | bytes 294944 | tf_op jit(solution)/shard_map/ppermute | solution.py:963
  75.1 2.8 collective-permute-start.17
  79.1 10.8 %collective-permute-done.17 = bf16[145,896]{1,0:T(8,128)(2,1)S(1)} collective-permute-done((bf16[145,896]{1,0:T(8,128)(2,1)S(1)}, bf16[145,896]{1,0:T(8,128)(2,1)S(1)}, u32[]{:S(2)}, u32[]{:S(2)}) %collective-permute-start.17) | collective-permute-done | bytes 259872 | tf_op jit(solution)/shard_map/ppermute | solution.py:959
  96.0 5.0 %shard_map.280 = (f32[320,768]{1,0:T(8,128)}, bf16[320,768]{1,0:T(8,128)(2,1)S(1)}, bf16[320,384]{1,0:T(8,128)(2,1)S(1)}, bf16[320,768]{1,0:T(8,128)(2,1)S(1)}, ...) custom-call(s32[3]{0:T(128)S(1)} %pad_add_fusion.refs_0_, ...), custom_call_target="tpu_custom_call" | custom-call | flops 943718400 | bytes 6291456 | tf_op jit(solution)/shard_map/pallas_call | solution.py:45
  103.3 4.2 shard_map.281
  107.6 10.7 %collective-permute-done.18.refs_6_.refs_9_ = bf16[2,2,192,768]{3,2,1,0:T(8,128)(2,1)} collective-permute-done((bf16[2,2,192,768]{3,2,1,0:T(8,128)(2,1)S(1)}, bf16[2,2,192,768]{3,2,1,0:T(8,128)(2,1)}, u32[]{:S(2)}, u32[]{:S(2)}) %collective-permute-start.18) | collective-permute-done | bytes 1179680 | tf_op jit(solution)/shard_map/ppermute | solution.py:963
  125.7 7.3 %collective-permute-done.20.refs_8_.refs_11_ = bf16[2,192,768]{2,1,0:T(8,128)(2,1)S(1)} collective-permute-done((bf16[2,192,768]{2,1,0:T(8,128)(2,1)S(1)}, bf16[2,192,768]{2,1,0:T(8,128)(2,1)S(1)}, u32[]{:S(2)}, u32[]{:S(2)}) %collective-permute-start.20) | collective-permute-done | bytes 589856 | tf_op jit(solution)/shard_map/ppermute | solution.py:963
  133.0 2.2 collective-permute-done.21.refs_9_.refs_12_
  135.3 7.8 %shard_map.282 = (f32[320,768]{1,0:T(8,128)S(1)}, bf16[320,768]{1,0:T(8,128)(2,1)S(1)}, bf16[320,1536]{1,0:T(8,128)(2,1)}, f32[320,768]{1,0:T(8,128)}, bf16[320,768]{1,0:T(8,128)(2,1)S(1)}) custom-call(s32[3]{0:T(128)S(1)} %pad_add_fusion.refs_0_, f32[320,768]{1,0:T(8,128)} %get-tuple-element.142.refs_1_, f32[320,768]{1,0:T(8,128)} %copy-done.5, ...), custom_call_target="tpu_custom_call" | custom-call | flops 1509949440 | bytes 16777216 | tf_op jit(solution)/shard_map/pallas_call | solution.py:45
  145.7 2.2 shard_map.283
  151.9 3.2 shard_map.284
  155.2 2.4 collective-permute-done.23.refs_3_
  159.4 5.6 %shard_map.285 = (f32[320,768]{1,0:T(8,128)S(1)}, bf16[160,768]{1,0:T(8,128)(2,1)S(1)}, bf16[384,320]{1,0:T(8,128)(2,1)S(1)}, f32[8,320]{1,0:T(8,128)S(1)}, bf16[320,768]{1,0:T(8,128)(2,1)S(1)}) custom-call(s32[3]{0:T(128)S(1)} %pad_add_fusion.refs_0_, bf16[320,384]{1,0:T(8,128)(2,1)S(1)} %get-tuple-element.159.refs_1_.refs_4_, ...), custom_call_target="tpu_custom_call" | custom-call | flops 503316480 | bytes 4194304 | tf_op jit(solution)/shard_map/pallas_call | solution.py:45
  168.4 2.9 shard_map.286
  177.1 6.3 %collective-permute-done.28.refs_1_ = bf16[192,768]{1,0:T(8,128)(2,1)S(1)} collective-permute-done((bf16[192,768]{1,0:T(8,128)(2,1)S(1)}, bf16[192,768]{1,0:T(8,128)(2,1)S(1)}, u32[]{:S(2)}, u32[]{:S(2)}) %collective-permute-start.28) | collective-permute-done | bytes 294944 | tf_op jit(solution)/shard_map/ppermute | solution.py:963
  183.4 6.9 %collective-permute-done.29.refs_2_ = bf16[192,768]{1,0:T(8,128)(2,1)S(1)} collective-permute-done((bf16[192,768]{1,0:T(8,128)(2,1)S(1)}, bf16[192,768]{1,0:T(8,128)(2,1)S(1)}, u32[]{:S(2)}, u32[]{:S(2)}) %collective-permute-start.29) | collective-permute-done | bytes 294944 | tf_op jit(solution)/shard_map/ppermute | solution.py:963
  192.4 13.8 %shard_map.287 = (bf16[192,768]{1,0:T(8,128)(2,1)}, bf16[192,768]{1,0:T(8,128)(2,1)}, bf16[192,768]{1,0:T(8,128)(2,1)}, bf16[192,768]{1,0:T(8,128)(2,1)}) custom-call(bf16[192,768]{1,0:T(8,128)(2,1)} %copy-done.26, bf16[192,768]{1,0:T(8,128)(2,1)} %copy-done.76, bf16[192,768]{1,0:T(8,128)(2,1)} %copy-done.77, bf16[192,768]{1,0:T(8,128)(2,1)} %copy-done.78, ...), custom_call_target="tpu_custom_call" | custom-call | flops 7247757312 | bytes 20971520 | tf_op jit(solution)/shard_map/pallas_call | solution.py:805
  209.7 6.7 %collective-permute-done.31.refs_2_ = bf16[192,768]{1,0:T(8,128)(2,1)S(1)} collective-permute-done((bf16[192,768]{1,0:T(8,128)(2,1)}, bf16[192,768]{1,0:T(8,128)(2,1)S(1)}, u32[]{:S(2)}, u32[]{:S(2)}) %collective-permute-start.31) | collective-permute-done | bytes 294944 | tf_op jit(solution)/shard_map/ppermute | solution.py:963
  216.4 4.9 %collective-permute-done.32.refs_3_ = bf16[192,768]{1,0:T(8,128)(2,1)S(1)} collective-permute-done((bf16[192,768]{1,0:T(8,128)(2,1)}, bf16[192,768]{1,0:T(8,128)(2,1)S(1)}, u32[]{:S(2)}, u32[]{:S(2)}) %collective-permute-start.32) | collective-permute-done | bytes 294944 | tf_op jit(solution)/shard_map/ppermute | solution.py:963
  225.3 2.0 shard_map.288
  230.1 6.9 %shard_map.290 = (bf16[320,384]{1,0:T(8,128)(2,1)S(1)}, f32[320,768]{1,0:T(8,128)}, bf16[320,768]{1,0:T(8,128)(2,1)S(1)}, bf16[384,768]{1,0:T(8,128)(2,1)S(1)}) custom-call(s32[3]{0:T(128)S(1)} %pad_add_fusion.refs_0_, bf16[320,768]{1,0:T(8,128)(2,1)S(1)} %get-tuple-element.185.refs_1_, bf16[384,768]{1,0:T(8,128)(2,1)S(1)} %bitcast.164, ...), custom_call_target="tpu_custom_call" | custom-call | flops 1163919360 | bytes 6291456 | tf_op jit(solution)/shard_map/pallas_call | solution.py:45
  237.9 12.3 %collective-permute-done.35.refs_3_ = bf16[320,768]{1,0:T(8,128)(2,1)S(1)} collective-permute-done((bf16[320,768]{1,0:T(8,128)(2,1)S(1)}, bf16[320,768]{1,0:T(8,128)(2,1)S(1)}, u32[]{:S(2)}, u32[]{:S(2)}) %collective-permute-start.35) | collective-permute-done | bytes 491552 | tf_op jit(solution)/shard_map/ppermute | solution.py:963
  250.2 6.2 %shard_map.291 = (f32[320,768]{1,0:T(8,128)S(1)}, bf16[320,768]{1,0:T(8,128)(2,1)S(1)}, bf16[2,832,384]{2,1,0:T(8,128)(2,1)}, bf16[2,832,384]{2,1,0:T(8,128)(2,1)}) custom-call(s32[3]{0:T(128)S(1)} %pad_add_fusion.refs_0_, bf16[320,384]{1,0:T(8,128)(2,1)S(1)} %get-tuple-element.189.refs_1_, f32[320,768]{1,0:T(8,128)} %get-tuple-element.190.refs_2_, ...), custom_call_target="tpu_custom_call" | custom-call | flops 1132462080 | bytes 10485760 | tf_op jit(solution)/shard_map/pallas_call | solution.py:45
  259.3 12.3 %shard_map.292 = (f32[320,768]{1,0:T(8,128)S(1)}, f32[320,768]{1,0:T(8,128)}, bf16[320,768]{1,0:T(8,128)(2,1)S(1)}, bf16[2,2,192,768]{3,2,1,0:T(8,128)(2,1)}, bf...) custom-call(s32[3]{0:T(128)S(1)} %pad_add_fusion.refs_0_, ...), custom_call_target="tpu_custom_call" | custom-call | flops 3774873600 | bytes 25165824 | tf_op jit(solution)/shard_map/pallas_call | solution.py:45
  273.5 2.0 shard_map.293
  275.6 7.0 %shard_map.294 = (bf16[320,384]{1,0:T(8,128)(2,1)S(1)}, f32[320,768]{1,0:T(8,128)}, bf16[320,768]{1,0:T(8,128)(2,1)S(1)}, bf16[384,768]{1,0:T(8,128)(2,1)S(1)}) custom-call(s32[3]{0:T(128)S(1)} %pad_add_fusion.refs_0_, bf16[320,768]{1,0:T(8,128)(2,1)S(1)} %get-tuple-element.202.refs_1_, bf16[384,768]{1,0:T(8,128)(2,1)S(1)} %copy-done.37, ...), custom_call_target="tpu_custom_call" | custom-call | flops 1163919360 | bytes 6291456 | tf_op jit(solution)/shard_map/pallas_call | solution.py:45
  285.4 13.2 %collective-permute-done.38.refs_3_ = bf16[320,768]{1,0:T(8,128)(2,1)S(1)} collective-permute-done((bf16[320,768]{1,0:T(8,128)(2,1)S(1)}, bf16[320,768]{1,0:T(8,128)(2,1)S(1)}, u32[]{:S(2)}, u32[]{:S(2)}) %collective-permute-start.38) | collective-permute-done | bytes 491552 | tf_op jit(solution)/shard_map/ppermute | solution.py:963
  300.4 5.9 %shard_map.295 = (f32[160,768]{1,0:T(8,128)S(1)}, bf16[160,768]{1,0:T(8,128)(2,1)S(1)}, bf16[2,384,384]{2,1,0:T(8,128)(2,1)S(1)}, bf16[2,384,384]{2,1,0:T(8,128)...) custom-call(s32[3]{0:T(128)S(1)} %pad_add_fusion.refs_0_, ...), custom_call_target="tpu_custom_call" | custom-call | flops 1132462080 | bytes 10485760 | tf_op jit(solution)/shard_map/pallas_call | solution.py:45
  316.9 21.5 %shard_map.297 = (bf16[768,1536]{1,0:T(8,128)(2,1)}, bf16[1536,768]{1,0:T(8,128)(2,1)}) custom-call(bf16[4,4,192,768]{3,2,1,0:T(8,128)(2,1)} %bitcast.169, bf16[768,1536]{1,0:T(8,128)(2,1)} %collective-permute-done.26.refs_8_.refs_6_.refs_1_, bf16[1536,768]{1,0:T(8,128)(2,1)} %collective-permute-done.27.refs_9_.refs_7_.refs_2_, bf16[145,768]{1,0:T(8,128)(2,1)} %copy-done.7), custom_call_target="tpu_custom_call" | custom-call | flops 14495514624 | bytes 20971520 | tf_op jit(solution)/shard_map/pallas_call | solution.py:869
  348.0 5.8 %collective-permute-start.40 = (bf16[2,145,768]{2,1,0:T(8,128)(2,1)}, bf16[2,145,768]{2,1,0:T(8,128)(2,1)S(1)}, u32[]{:S(2)}, u32[]{:S(2)}) collective-permute-start(bf16[2,145,768]{2,1,0:T(8,128)(2,1)} %pad_maximum_fusion.8), channel_id=1, source_target_pairs={{0,0},{1,2},{2,1},{3,3},{4,8},{5,10},{6,9},{7,11},{8,4},{9,6},{10,... | collective-permute-start | bytes 1336328 | tf_op jit(solution)/shard_map/ppermute | solution.py:959
  355.8 3.6 collective-permute-done.53
  361.6 8.6 %collective-permute-done.46 = bf16[2,192,768]{2,1,0:T(8,128)(2,1)} collective-permute-done((bf16[2,192,768]{2,1,0:T(8,128)(2,1)}, bf16[2,192,768]{2,1,0:T(8,128)(2,1)}, u32[]{:S(2)}, u32[]{:S(2)}) %collective-permute-start.46) | collective-permute-done | bytes 589856 | tf_op jit(solution)/shard_map/ppermute | solution.py:963
  370.2 2.8 fusion.8.refs_3_
  373.0 4.4 collective-permute-done.44
  380.0 5.1 %collective-permute-start.48 = (bf16[48,3072]{1,0:T(8,128)(2,1)S(1)}, bf16[48,3072]{1,0:T(8,128)(2,1)S(1)}, u32[]{:S(2)}, u32[]{:S(2)}) collective-permute-start(bf16[48,3072]{1,0:T(8,128)(2,1)S(1)} %get-tuple-element.225), channel_id=1, source_target_pairs={{0,4},{2,6},{4,0},{6,2},{1,5},{3,7},{5,1},{7,3},{8,12},{10,14},{12... | collective-permute-start | bytes 884744 | tf_op jit(solution)/shard_map/ppermute | solution.py:963
  385.2 22.6 %shard_map.299 = (f32[768,1536]{1,0:T(8,128)}, f32[1536,768]{1,0:T(8,128)}) custom-call(bf16[4,4,192,768]{3,2,1,0:T(8,128)(2,1)} %bitcast.170, bf16[768,1536]{1,0:T(8,128)(2,1)} %bitcast.61.refs_4_.refs_1_, bf16[1536,768]{1,0:T(8,128)(2,1)} %bitcast.62.refs_5_.refs_2_, bf16[768,1536]{1,0:T(8,128)(2,1)} %collective-permute-done.50.refs_3_, ...), custom_call_target="tpu_custom_call" | custom-call | flops 14495514624 | bytes 20971520 | tf_op jit(solution)/shard_map/pallas_call | solution.py:869
  407.8 2.1 collective-permute-done.48
  409.9 6.8 %collective-permute-done.49 = bf16[48,3072]{1,0:T(8,128)(2,1)S(1)} collective-permute-done((bf16[48,3072]{1,0:T(8,128)(2,1)S(1)}, bf16[48,3072]{1,0:T(8,128)(2,1)S(1)}, u32[]{:S(2)}, u32[]{:S(2)}) %collective-permute-start.49) | collective-permute-done | bytes 294944 | tf_op jit(solution)/shard_map/ppermute | solution.py:963
  419.7 2.5 collective-permute-start.57
  426.4 6.3 %collective-permute-done.57 = f32[48,768]{1,0:T(8,128)S(1)} collective-permute-done((f32[48,768]{1,0:T(8,128)S(1)}, f32[48,768]{1,0:T(8,128)S(1)}, u32[]{:S(2)}, u32[]{:S(2)}) %collective-permute-start.57) | collective-permute-done | bytes 147488 | tf_op jit(solution)/shard_map/ppermute | solution.py:1113
  (415 shorter events, 114.1 us)
Async XLA Ops:
  7.2 143.6 %all-gather.5.cloned.1.call-start = ((), (), s32[]{:S(2)}) async-start(), calls=%async_computation.2 | async-start | bytes 2949120 | tf_op jit(solution)/shard_map/all_gather | solution.py:1182
  7.2 20.9 %collective-permute-start = (bf16[145,768]{1,0:T(8,128)(2,1)}, bf16[145,768]{1,0:T(8,128)(2,1)S(1)}, u32[]{:S(2)}, u32[]{:S(2)}) collective-permute-start(bf16[145,768]{1,0:T(8,128)(2,1)} %bitcast.213), channel_id=1, source_target_pairs={{0,0},{1,2},{2,1},{3,3},{4,8},{5,10},{6,9},{7,11},{8,4},{9,6},{10,... | collective-permute-start | bytes 668168 | tf_op jit(solution)/shard_map/ppermute | solution.py:959
  12.5 15.5 %collective-permute-start.7 = (bf16[24,2688]{1,0:T(8,128)(2,1)S(1)}, bf16[24,2688]{1,0:T(8,128)(2,1)S(1)}, u32[]{:S(2)}, u32[]{:S(2)}) collective-permute-start(bf16[24,2688]{1,0:T(8,128)(2,1)S(1)} %get-tuple-element.361), channel_id=1, source_target_pairs={{0,1},{1,0},{2,3},{3,2},{4,5},{5,4},{6,7},{7,6},{8,9},{9,8},{10,11... | collective-permute-start | bytes 387080 | tf_op jit(solution)/shard_map/ppermute | solution.py:963
  14.2 10.2 %collective-permute-start.3 = (bf16[48,768]{1,0:T(8,128)(2,1)S(1)}, bf16[48,768]{1,0:T(8,128)(2,1)S(1)}, u32[]{:S(2)}, u32[]{:S(2)}) collective-permute-start(bf16[48,768]{1,0:T(8,128)(2,1)S(1)} %pad_maximum_fusion.11), channel_id=1, source_target_pairs={{0,0},{1,2},{2,4},{3,6},{4,8},{5,10},{6,12},{7,14},{8,16},{9,18},{... | collective-permute-start | bytes 221192 | tf_op jit(solution)/shard_map/ppermute | solution.py:1145
  26.5 11.2 %collective-permute-start.5 = (bf16[48,1664]{1,0:T(8,128)(2,1)S(1)}, bf16[48,1664]{1,0:T(8,128)(2,1)S(1)}, u32[]{:S(2)}, u32[]{:S(2)}) collective-permute-start(bf16[48,1664]{1,0:T(8,128)(2,1)S(1)} %fusion.24), channel_id=1, source_target_pairs={{0,4},{2,6},{4,0},{6,2},{1,5},{3,7},{5,1},{7,3},{8,12},{10,14},{12... | collective-permute-start | bytes 479240 | tf_op jit(solution)/shard_map/ppermute | solution.py:963
  26.5 16.6 %collective-permute-start.6 = (bf16[48,1664]{1,0:T(8,128)(2,1)S(1)}, bf16[48,1664]{1,0:T(8,128)(2,1)S(1)}, u32[]{:S(2)}, u32[]{:S(2)}) collective-permute-start(bf16[48,1664]{1,0:T(8,128)(2,1)S(1)} %fusion.24), channel_id=1, source_target_pairs={{0,6},{2,4},{4,2},{6,0},{1,7},{3,5},{5,3},{7,1},{8,14},{10,12},{12... | collective-permute-start | bytes 479240 | tf_op jit(solution)/shard_map/ppermute | solution.py:963
  28.1 18.7 %collective-permute-start.1 = (bf16[145,768]{1,0:T(8,128)(2,1)S(1)}, bf16[145,768]{1,0:T(8,128)(2,1)S(1)}, u32[]{:S(2)}, u32[]{:S(2)}) collective-permute-start(bf16[145,768]{1,0:T(8,128)(2,1)S(1)} %collective-permute-done), channel_id=1, source_target_pairs={{0,8},{8,0},{16,24},{24,16},{1,9},{9,1},{17,25},{25,17},{2,10},{10... | collective-permute-start | bytes 668168 | tf_op jit(solution)/shard_map/ppermute | solution.py:963
  43.3 11.7 %collective-permute-start.10 = (bf16[48,3072]{1,0:T(8,128)(2,1)S(1)}, bf16[48,3072]{1,0:T(8,128)(2,1)S(1)}, u32[]{:S(2)}, u32[]{:S(2)}) collective-permute-start(bf16[48,3072]{1,0:T(8,128)(2,1)S(1)} %pad_maximum_fusion.9), channel_id=1, source_target_pairs={{0,2},{2,0},{4,6},{6,4},{1,3},{3,1},{5,7},{7,5},{8,10},{10,8},{12,... | collective-permute-start | bytes 884744 | tf_op jit(solution)/shard_map/ppermute | solution.py:963
  43.4 22.0 %collective-permute-start.11 = (bf16[48,3072]{1,0:T(8,128)(2,1)S(1)}, bf16[48,3072]{1,0:T(8,128)(2,1)S(1)}, u32[]{:S(2)}, u32[]{:S(2)}) collective-permute-start(bf16[48,3072]{1,0:T(8,128)(2,1)S(1)} %pad_maximum_fusion.9), channel_id=1, source_target_pairs={{0,4},{2,6},{4,0},{6,2},{1,5},{3,7},{5,1},{7,3},{8,12},{10,14},{12... | collective-permute-start | bytes 884744 | tf_op jit(solution)/shard_map/ppermute | solution.py:963
  45.3 27.1 %collective-permute-start.12 = (bf16[48,3072]{1,0:T(8,128)(2,1)S(1)}, bf16[48,3072]{1,0:T(8,128)(2,1)S(1)}, u32[]{:S(2)}, u32[]{:S(2)}) collective-permute-start(bf16[48,3072]{1,0:T(8,128)(2,1)S(1)} %pad_maximum_fusion.9), channel_id=1, source_target_pairs={{0,6},{2,4},{4,2},{6,0},{1,7},{3,5},{5,3},{7,1},{8,14},{10,12},{12... | collective-permute-start | bytes 884744 | tf_op jit(solution)/shard_map/ppermute | solution.py:963
  47.9 24.8 %collective-permute-start.8 = (bf16[1024,384]{1,0:T(8,128)(2,1)S(1)}, bf16[1024,384]{1,0:T(8,128)(2,1)S(1)}, u32[]{:S(2)}, u32[]{:S(2)}) collective-permute-start(bf16[1024,384]{1,0:T(8,128)(2,1)S(1)} %maximum_dynamic-update-slice_fusion.refs_5_), channel_id=1, source_target_pairs={{0,8},{8,0},{16,24},{24,16},{1,9},{9,1},{17,25},{25,17},{2,10},{10... | collective-permute-start | bytes 2359304 | tf_op jit(solution)/shard_map/ppermute | solution.py:963
  47.9 24.8 %collective-permute-start.9 = (bf16[1024,384]{1,0:T(8,128)(2,1)S(1)}, bf16[1024,384]{1,0:T(8,128)(2,1)S(1)}, u32[]{:S(2)}, u32[]{:S(2)}) collective-permute-start(bf16[1024,384]{1,0:T(8,128)(2,1)S(1)} %maximum_dynamic-update-slice_fusion.refs_5_), channel_id=1, source_target_pairs={{0,16},{8,24},{16,0},{24,8},{1,17},{9,25},{17,1},{25,9},{2,18},{10... | collective-permute-start | bytes 2359304 | tf_op jit(solution)/shard_map/ppermute | solution.py:963
  74.4 16.2 %collective-permute-start.14 = (bf16[576,384]{1,0:T(8,128)(2,1)S(1)}, bf16[576,384]{1,0:T(8,128)(2,1)S(1)}, u32[]{:S(2)}, u32[]{:S(2)}) collective-permute-start(bf16[576,384]{1,0:T(8,128)(2,1)S(1)} %slice.305), channel_id=1, source_target_pairs={{0,16},{8,24},{16,0},{24,8},{1,17},{9,25},{17,1},{25,9},{2,18},{10... | collective-permute-start | bytes 1327112 | tf_op jit(solution)/shard_map/ppermute | solution.py:963
  74.5 16.1 %collective-permute-start.15 = (bf16[448,384]{1,0:T(8,128)(2,1)S(1)}, bf16[448,384]{1,0:T(8,128)(2,1)S(1)}, u32[]{:S(2)}, u32[]{:S(2)}) collective-permute-start(bf16[448,384]{1,0:T(8,128)(2,1)S(1)} %slice.306), channel_id=1, source_target_pairs={{0,8},{8,0},{16,24},{24,16},{1,9},{9,1},{17,25},{25,17},{2,10},{10... | collective-permute-start | bytes 1032200 | tf_op jit(solution)/shard_map/ppermute | solution.py:963
  75.1 14.8 %collective-permute-start.17 = (bf16[145,896]{1,0:T(8,128)(2,1)S(1)}, bf16[145,896]{1,0:T(8,128)(2,1)S(1)}, u32[]{:S(2)}, u32[]{:S(2)}) collective-permute-start(bf16[145,896]{1,0:T(8,128)(2,1)S(1)} %fusion.22), channel_id=1, source_target_pairs={{0,0},{1,2},{2,1},{3,3},{4,8},{5,10},{6,9},{7,11},{8,4},{9,6},{10,... | collective-permute-start | bytes 779528 | tf_op jit(solution)/shard_map/ppermute | solution.py:959
  90.9 27.3 %collective-permute-start.18 = (bf16[2,2,192,768]{3,2,1,0:T(8,128)(2,1)S(1)}, bf16[2,2,192,768]{3,2,1,0:T(8,128)(2,1)}, u32[]{:S(2)}, u32[]{:S(2)}) collective-permute-start(bf16[2,2,192,768]{3,2,1,0:T(8,128)(2,1)S(1)} %pad_maximum_fusion.1.refs_5_.refs_8_), channel_id=1, source_target_pairs={{0,8},{8,0},{16,24},{24,16},{1,9},{9,1},{17,25},{25,17},{2,10},{10... | collective-permute-start | bytes 3538952 | tf_op jit(solution)/shard_map/ppermute | solution.py:963
  91.0 27.3 %collective-permute-start.19 = (bf16[2,2,192,768]{3,2,1,0:T(8,128)(2,1)S(1)}, bf16[2,2,192,768]{3,2,1,0:T(8,128)(2,1)}, u32[]{:S(2)}, u32[]{:S(2)}) collective-permute-start(bf16[2,2,192,768]{3,2,1,0:T(8,128)(2,1)S(1)} %pad_maximum_fusion.1.refs_5_.refs_8_), channel_id=1, source_target_pairs={{0,16},{8,24},{16,0},{24,8},{1,17},{9,25},{17,1},{25,9},{2,18},{10... | collective-permute-start | bytes 3538952 | tf_op jit(solution)/shard_map/ppermute | solution.py:963
  95.7 203.7 %all-gather.7.cloned.1.call-start = ((), (), s32[]{:S(2)}) async-start(), calls=%async_computation.3 | async-start | bytes 5898240 | tf_op jit(solution)/shard_map/all_gather | solution.py:1221
  119.4 13.6 %collective-permute-start.20 = (bf16[2,192,768]{2,1,0:T(8,128)(2,1)S(1)}, bf16[2,192,768]{2,1,0:T(8,128)(2,1)S(1)}, u32[]{:S(2)}, u32[]{:S(2)}) collective-permute-start(bf16[2,192,768]{2,1,0:T(8,128)(2,1)S(1)} %slice_bitcast_fusion.1), channel_id=1, source_target_pairs={{0,16},{8,24},{16,0},{24,8},{1,17},{9,25},{17,1},{25,9},{2,18},{10... | collective-permute-start | bytes 1769480 | tf_op jit(solution)/shard_map/ppermute | solution.py:963
  122.1 13.1 %collective-permute-start.21 = (bf16[2,192,768]{2,1,0:T(8,128)(2,1)S(1)}, bf16[2,192,768]{2,1,0:T(8,128)(2,1)S(1)}, u32[]{:S(2)}, u32[]{:S(2)}) collective-permute-start(bf16[2,192,768]{2,1,0:T(8,128)(2,1)S(1)} %slice_bitcast_fusion), channel_id=1, source_target_pairs={{0,8},{8,0},{16,24},{24,16},{1,9},{9,1},{17,25},{25,17},{2,10},{10... | collective-permute-start | bytes 1769480 | tf_op jit(solution)/shard_map/ppermute | solution.py:963
  148.9 19.5 %collective-permute-start.26 = (bf16[768,1536]{1,0:T(8,128)(2,1)}, bf16[768,1536]{1,0:T(8,128)(2,1)}, u32[]{:S(2)}, u32[]{:S(2)}) collective-permute-start(bf16[768,1536]{1,0:T(8,128)(2,1)} %bitcast.61.refs_4_.refs_1_), channel_id=1, source_target_pairs={{0,1},{1,0},{2,3},{3,2},{4,5},{5,4},{6,7},{7,6},{8,9},{9,8},{10,11... | collective-permute-start | bytes 7077896 | tf_op jit(solution)/shard_map/ppermute | solution.py:963
  149.0 19.3 %collective-permute-start.27 = (bf16[1536,768]{1,0:T(8,128)(2,1)}, bf16[1536,768]{1,0:T(8,128)(2,1)}, u32[]{:S(2)}, u32[]{:S(2)}) collective-permute-start(bf16[1536,768]{1,0:T(8,128)(2,1)} %bitcast.62.refs_5_.refs_2_), channel_id=1, source_target_pairs={{0,1},{1,0},{2,3},{3,2},{4,5},{5,4},{6,7},{7,6},{8,9},{9,8},{10,11... | collective-permute-start | bytes 7077896 | tf_op jit(solution)/shard_map/ppermute | solution.py:963
  173.6 9.8 %collective-permute-start.28 = (bf16[192,768]{1,0:T(8,128)(2,1)S(1)}, bf16[192,768]{1,0:T(8,128)(2,1)S(1)}, u32[]{:S(2)}, u32[]{:S(2)}) collective-permute-start(bf16[192,768]{1,0:T(8,128)(2,1)S(1)} %get-tuple-element.170), channel_id=1, source_target_pairs={{0,8},{8,0},{16,24},{24,16},{1,9},{9,1},{17,25},{25,17},{2,10},{10... | collective-permute-start | bytes 884744 | tf_op jit(solution)/shard_map/ppermute | solution.py:963
  175.0 15.3 %collective-permute-start.29 = (bf16[192,768]{1,0:T(8,128)(2,1)S(1)}, bf16[192,768]{1,0:T(8,128)(2,1)S(1)}, u32[]{:S(2)}, u32[]{:S(2)}) collective-permute-start(bf16[192,768]{1,0:T(8,128)(2,1)S(1)} %get-tuple-element.171), channel_id=1, source_target_pairs={{0,16},{8,24},{16,0},{24,8},{1,17},{9,25},{17,1},{25,9},{2,18},{10... | collective-permute-start | bytes 884744 | tf_op jit(solution)/shard_map/ppermute | solution.py:963
  175.7 14.6 %collective-permute-start.30 = (bf16[192,768]{1,0:T(8,128)(2,1)S(1)}, bf16[192,768]{1,0:T(8,128)(2,1)S(1)}, u32[]{:S(2)}, u32[]{:S(2)}) collective-permute-start(bf16[192,768]{1,0:T(8,128)(2,1)S(1)} %get-tuple-element.172), channel_id=1, source_target_pairs={{0,24},{8,16},{16,8},{24,0},{1,25},{9,17},{17,9},{25,1},{2,26},{10... | collective-permute-start | bytes 884744 | tf_op jit(solution)/shard_map/ppermute | solution.py:963
  192.3 224.6 %reduce-scatter.2.cloned.1.call-start = ((), (), s32[]{:S(2)}) async-start(), calls=%async_computation.1 | async-start | bytes 1536000 | tf_op jit(solution)/shard_map/reduce_scatter | solution.py:1252
  206.2 10.2 %collective-permute-start.31 = (bf16[192,768]{1,0:T(8,128)(2,1)}, bf16[192,768]{1,0:T(8,128)(2,1)S(1)}, u32[]{:S(2)}, u32[]{:S(2)}) collective-permute-start(bf16[192,768]{1,0:T(8,128)(2,1)} %get-tuple-element.174), channel_id=1, source_target_pairs={{0,8},{8,0},{16,24},{24,16},{1,9},{9,1},{17,25},{25,17},{2,10},{10... | collective-permute-start | bytes 884744 | tf_op jit(solution)/shard_map/ppermute | solution.py:963
  206.9 14.5 %collective-permute-start.32 = (bf16[192,768]{1,0:T(8,128)(2,1)}, bf16[192,768]{1,0:T(8,128)(2,1)S(1)}, u32[]{:S(2)}, u32[]{:S(2)}) collective-permute-start(bf16[192,768]{1,0:T(8,128)(2,1)} %get-tuple-element.175), channel_id=1, source_target_pairs={{0,16},{8,24},{16,0},{24,8},{1,17},{9,25},{17,1},{25,9},{2,18},{10... | collective-permute-start | bytes 884744 | tf_op jit(solution)/shard_map/ppermute | solution.py:963
  207.9 13.5 %collective-permute-start.33 = (bf16[192,768]{1,0:T(8,128)(2,1)}, bf16[192,768]{1,0:T(8,128)(2,1)S(1)}, u32[]{:S(2)}, u32[]{:S(2)}) collective-permute-start(bf16[192,768]{1,0:T(8,128)(2,1)} %get-tuple-element.176), channel_id=1, source_target_pairs={{0,24},{8,16},{16,8},{24,0},{1,25},{9,17},{17,9},{25,1},{2,26},{10... | collective-permute-start | bytes 884744 | tf_op jit(solution)/shard_map/ppermute | solution.py:963
  236.9 13.3 %collective-permute-start.35 = (bf16[320,768]{1,0:T(8,128)(2,1)S(1)}, bf16[320,768]{1,0:T(8,128)(2,1)S(1)}, u32[]{:S(2)}, u32[]{:S(2)}) collective-permute-start(bf16[320,768]{1,0:T(8,128)(2,1)S(1)} %get-tuple-element.191), channel_id=1, source_target_pairs={{0,8},{8,0},{16,24},{24,16},{1,9},{9,1},{17,25},{25,17},{2,10},{10... | collective-permute-start | bytes 1474568 | tf_op jit(solution)/shard_map/ppermute | solution.py:963
  257.4 50.0 %collective-permute-start.52 = (bf16[2,832,384]{2,1,0:T(8,128)(2,1)}, bf16[2,832,384]{2,1,0:T(8,128)(2,1)}, u32[]{:S(2)}, u32[]{:S(2)}) collective-permute-start(bf16[2,832,384]{2,1,0:T(8,128)(2,1)} %get-tuple-element.233), channel_id=1, source_target_pairs={{0,8},{8,0},{16,24},{24,16},{1,9},{9,1},{17,25},{25,17},{2,10},{10... | collective-permute-start | bytes 3833864 | tf_op jit(solution)/shard_map/ppermute | solution.py:963
  271.7 38.2 %collective-permute-start.54 = (bf16[2,2,192,768]{3,2,1,0:T(8,128)(2,1)}, bf16[2,2,192,768]{3,2,1,0:T(8,128)(2,1)}, u32[]{:S(2)}, u32[]{:S(2)}) collective-permute-start(bf16[2,2,192,768]{3,2,1,0:T(8,128)(2,1)} %get-tuple-element.237), channel_id=1, source_target_pairs={{0,16},{8,24},{16,0},{24,8},{1,17},{9,25},{17,1},{25,9},{2,18},{10... | collective-permute-start | bytes 3538952 | tf_op jit(solution)/shard_map/ppermute | solution.py:963
  283.5 15.2 %collective-permute-start.38 = (bf16[320,768]{1,0:T(8,128)(2,1)S(1)}, bf16[320,768]{1,0:T(8,128)(2,1)S(1)}, u32[]{:S(2)}, u32[]{:S(2)}) collective-permute-start(bf16[320,768]{1,0:T(8,128)(2,1)S(1)} %get-tuple-element.207), channel_id=1, source_target_pairs={{0,8},{8,0},{16,24},{24,16},{1,9},{9,1},{17,25},{25,17},{2,10},{10... | collective-permute-start | bytes 1474568 | tf_op jit(solution)/shard_map/ppermute | solution.py:963
  284.4 54.0 %collective-permute-start.45 = (bf16[2,2,192,768]{3,2,1,0:T(8,128)(2,1)}, bf16[2,2,192,768]{3,2,1,0:T(8,128)(2,1)}, u32[]{:S(2)}, u32[]{:S(2)}) collective-permute-start(bf16[2,2,192,768]{3,2,1,0:T(8,128)(2,1)} %get-tuple-element.221), channel_id=1, source_target_pairs={{0,16},{8,24},{16,0},{24,8},{1,17},{9,25},{17,1},{25,9},{2,18},{10... | collective-permute-start | bytes 3538952 | tf_op jit(solution)/shard_map/ppermute | solution.py:963
  306.4 38.6 %collective-permute-start.41 = (bf16[2,384,384]{2,1,0:T(8,128)(2,1)S(1)}, bf16[2,384,384]{2,1,0:T(8,128)(2,1)}, u32[]{:S(2)}, u32[]{:S(2)}) collective-permute-start(bf16[2,384,384]{2,1,0:T(8,128)(2,1)S(1)} %get-tuple-element.214), channel_id=1, source_target_pairs={{0,8},{8,0},{16,24},{24,16},{1,9},{9,1},{17,25},{25,17},{2,10},{10... | collective-permute-start | bytes 1769480 | tf_op jit(solution)/shard_map/ppermute | solution.py:963
  307.4 40.6 %collective-permute-start.43 = (bf16[2,384,384]{2,1,0:T(8,128)(2,1)}, bf16[2,384,384]{2,1,0:T(8,128)(2,1)}, u32[]{:S(2)}, u32[]{:S(2)}) collective-permute-start(bf16[2,384,384]{2,1,0:T(8,128)(2,1)} %get-tuple-element.218), channel_id=1, source_target_pairs={{0,16},{8,24},{16,0},{24,8},{1,17},{9,25},{17,1},{25,9},{2,18},{10... | collective-permute-start | bytes 1769480 | tf_op jit(solution)/shard_map/ppermute | solution.py:963
  313.1 30.0 %collective-permute-start.55 = (bf16[2,192,768]{2,1,0:T(8,128)(2,1)}, bf16[2,192,768]{2,1,0:T(8,128)(2,1)}, u32[]{:S(2)}, u32[]{:S(2)}) collective-permute-start(bf16[2,192,768]{2,1,0:T(8,128)(2,1)} %fusion.11), channel_id=1, source_target_pairs={{0,8},{8,0},{16,24},{24,16},{1,9},{9,1},{17,25},{25,17},{2,10},{10... | collective-permute-start | bytes 1769480 | tf_op jit(solution)/shard_map/ppermute | solution.py:963
  338.4 46.8 %collective-permute-start.50 = (bf16[768,1536]{1,0:T(8,128)(2,1)}, bf16[768,1536]{1,0:T(8,128)(2,1)}, u32[]{:S(2)}, u32[]{:S(2)}) collective-permute-start(bf16[768,1536]{1,0:T(8,128)(2,1)} %get-tuple-element.215), channel_id=1, source_target_pairs={{0,1},{1,0},{2,3},{3,2},{4,5},{5,4},{6,7},{7,6},{8,9},{9,8},{10,11... | collective-permute-start | bytes 7077896 | tf_op jit(solution)/shard_map/ppermute | solution.py:963
  340.1 45.0 %collective-permute-start.51 = (bf16[1536,768]{1,0:T(8,128)(2,1)}, bf16[1536,768]{1,0:T(8,128)(2,1)}, u32[]{:S(2)}, u32[]{:S(2)}) collective-permute-start(bf16[1536,768]{1,0:T(8,128)(2,1)} %get-tuple-element.227), channel_id=1, source_target_pairs={{0,1},{1,0},{2,3},{3,2},{4,5},{5,4},{6,7},{7,6},{8,9},{9,8},{10,11... | collective-permute-start | bytes 7077896 | tf_op jit(solution)/shard_map/ppermute | solution.py:963
  343.0 16.4 %collective-permute-start.53 = (bf16[832,384]{1,0:T(8,128)(2,1)S(1)}, bf16[832,384]{1,0:T(8,128)(2,1)S(1)}, u32[]{:S(2)}, u32[]{:S(2)}) collective-permute-start(bf16[832,384]{1,0:T(8,128)(2,1)S(1)} %copy-done.70), channel_id=1, source_target_pairs={{0,16},{8,24},{16,0},{24,8},{1,17},{9,25},{17,1},{25,9},{2,18},{10... | collective-permute-start | bytes 1916936 | tf_op jit(solution)/shard_map/ppermute | solution.py:963
  345.0 25.2 %collective-permute-start.46 = (bf16[2,192,768]{2,1,0:T(8,128)(2,1)}, bf16[2,192,768]{2,1,0:T(8,128)(2,1)}, u32[]{:S(2)}, u32[]{:S(2)}) collective-permute-start(bf16[2,192,768]{2,1,0:T(8,128)(2,1)} %fusion.10), channel_id=1, source_target_pairs={{0,8},{8,0},{16,24},{24,16},{1,9},{9,1},{17,25},{25,17},{2,10},{10... | collective-permute-start | bytes 1769480 | tf_op jit(solution)/shard_map/ppermute | solution.py:963
  348.0 29.6 %collective-permute-start.40 = (bf16[2,145,768]{2,1,0:T(8,128)(2,1)}, bf16[2,145,768]{2,1,0:T(8,128)(2,1)S(1)}, u32[]{:S(2)}, u32[]{:S(2)}) collective-permute-start(bf16[2,145,768]{2,1,0:T(8,128)(2,1)} %pad_maximum_fusion.8), channel_id=1, source_target_pairs={{0,0},{1,2},{2,1},{3,3},{4,8},{5,10},{6,9},{7,11},{8,4},{9,6},{10,... | collective-permute-start | bytes 1336328 | tf_op jit(solution)/shard_map/ppermute | solution.py:959
  359.5 13.5 %collective-permute-start.42 = (bf16[384,384]{1,0:T(8,128)(2,1)}, bf16[384,384]{1,0:T(8,128)(2,1)S(1)}, u32[]{:S(2)}, u32[]{:S(2)}) collective-permute-start(bf16[384,384]{1,0:T(8,128)(2,1)} %fusion.20), channel_id=1, source_target_pairs={{0,16},{8,24},{16,0},{24,8},{1,17},{9,25},{17,1},{25,9},{2,18},{10... | collective-permute-start | bytes 884744 | tf_op jit(solution)/shard_map/ppermute | solution.py:963
  380.0 27.8 %collective-permute-start.47 = (bf16[48,3072]{1,0:T(8,128)(2,1)S(1)}, bf16[48,3072]{1,0:T(8,128)(2,1)S(1)}, u32[]{:S(2)}, u32[]{:S(2)}) collective-permute-start(bf16[48,3072]{1,0:T(8,128)(2,1)S(1)} %get-tuple-element.224), channel_id=1, source_target_pairs={{0,2},{2,0},{4,6},{6,4},{1,3},{3,1},{5,7},{7,5},{8,10},{10,8},{12,... | collective-permute-start | bytes 884744 | tf_op jit(solution)/shard_map/ppermute | solution.py:963
  380.0 29.9 %collective-permute-start.48 = (bf16[48,3072]{1,0:T(8,128)(2,1)S(1)}, bf16[48,3072]{1,0:T(8,128)(2,1)S(1)}, u32[]{:S(2)}, u32[]{:S(2)}) collective-permute-start(bf16[48,3072]{1,0:T(8,128)(2,1)S(1)} %get-tuple-element.225), channel_id=1, source_target_pairs={{0,4},{2,6},{4,0},{6,2},{1,5},{3,7},{5,1},{7,3},{8,12},{10,14},{12... | collective-permute-start | bytes 884744 | tf_op jit(solution)/shard_map/ppermute | solution.py:963
  385.1 31.6 %collective-permute-start.49 = (bf16[48,3072]{1,0:T(8,128)(2,1)S(1)}, bf16[48,3072]{1,0:T(8,128)(2,1)S(1)}, u32[]{:S(2)}, u32[]{:S(2)}) collective-permute-start(bf16[48,3072]{1,0:T(8,128)(2,1)S(1)} %get-tuple-element.226), channel_id=1, source_target_pairs={{0,6},{2,4},{4,2},{6,0},{1,7},{3,5},{5,3},{7,1},{8,14},{10,12},{12... | collective-permute-start | bytes 884744 | tf_op jit(solution)/shard_map/ppermute | solution.py:963
  419.6 13.8 %collective-permute-start.56 = (f32[24,3968]{1,0:T(8,128)S(1)}, f32[24,3968]{1,0:T(8,128)S(1)}, u32[]{:S(2)}, u32[]{:S(2)}) collective-permute-start(f32[24,3968]{1,0:T(8,128)S(1)} %get-tuple-element.329), channel_id=1, source_target_pairs={{0,1},{1,0},{2,3},{3,2},{4,5},{5,4},{6,7},{7,6},{8,9},{9,8},{10,11... | collective-permute-start | bytes 1142792 | tf_op jit(solution)/shard_map/ppermute | solution.py:963
  419.7 13.0 %collective-permute-start.57 = (f32[48,768]{1,0:T(8,128)S(1)}, f32[48,768]{1,0:T(8,128)S(1)}, u32[]{:S(2)}, u32[]{:S(2)}) collective-permute-start(f32[48,768]{1,0:T(8,128)S(1)} %maximum_maximum_fusion), channel_id=1, source_target_pairs={{0,0},{2,1},{4,2},{6,3},{8,4},{10,5},{12,6},{14,7},{16,8},{18,9},{... | collective-permute-start | bytes 442376 | tf_op jit(solution)/shard_map/ppermute | solution.py:1113
  (107 other events, 532.3 us)
Sparse Core Ops, SparseCore 0:
  95.9 47.9 all-gather.4
  192.5 88.3 all-gather.6
  361.8 39.6 reduce-scatter.1

commit v7 on v6

--- a/solution.py
+++ b/solution.py
@@ -503,9 +503,6 @@
         packed_ref, turned_ref, ws_ref, sm_ref, sems = take(5)
         packed_ref[:, :half] = dq_ref[...]
         packed_ref[:, half:] = (own_ref[...] + got_ref[...].astype(F32)).astype(BF)
-        out = dot_t(packed_ref[...], w_ref[...])
-        out_ref[...] = out[: out_ref.shape[0]]
-        low_ref[...] = (out[rows:] if last else out).astype(BF)
         turned_ref[...] = normed_ref[...].T
 
         @pl.loop(0, 3 * half // tile)
@@ -544,6 +541,9 @@
                             sat = pl.ds(pl.multiple_of(to * n + g * extra, 16), extra)
                             add(sm_ref.at[sat], ref.at[i, pl.ds(3 * n + 2 * m, extra), pl.ds(128 * g, 128)])
         start_all(copies)
+        out = dot_t(packed_ref[...], w_ref[...])
+        out_ref[...] = out[: out_ref.shape[0]]
+        low_ref[...] = (out[rows:] if last else out).astype(BF)
         wait_all(copies)
 
     n_out = rows if last else r2

time: 453 us -> 452 us (level)
  no operation moved by 1% of the time
where the time goes in v7:
time: 452 us; the launch traced here: 447 us
  waiting for transfers between devices  168 us (37%)
  Pallas kernels  134 us (30%)
  starting transfers between devices  60.5 us (13%)
  local copies, waits for them, and re-layouts  42.8 us (9%)
  other arithmetic  24.9 us (6%)
  between operations  16 us (4%)
    ppermute x53, waiting for transfers between devices, xor(): return lax.ppermute(x, axis, [(i, i ^ j) for i in range(n)])  145 us
    pallas_call x18, Pallas kernels, call(): pl.pallas_call(run, grid=grid, out_shape=[jax.ShapeDtypeStruct(s, t) for...  76 us
    pallas_call x2, Pallas kernels, expert_slopes(): pl.pallas_call(kernel, grid=(steps,), out_shape=[jax.ShapeDtypeStruct((fe...  44.1 us
    ppermute x53, starting transfers between devices, xor(): return lax.ppermute(x, axis, [(i, i ^ j) for i in range(n)])  42.1 us
    unnamed x199, local copies, waits for them, and re-layouts  25.5 us
    pallas_call x1, Pallas kernels, experts_forward(): pl.pallas_call(kernel, grid=(2 * steps,), out_shape=[jax.ShapeDtypeStruct...  13.8 us
    ppermute x3, starting transfers between devices, move(): return lax.ppermute(x, ALL, self.team)  11.5 us
    ppermute x3, waiting for transfers between devices, move(): return lax.ppermute(x, ALL, self.team)  10.8 us
  transfers between devices with their start and end apart: 61, of which 32 were waited for; matrix products, arithmetic and copies ran while one was open for 8% of the time, Pallas kernels for 29%

profile of v7, /device:TPU:10, one launch (start us, length us, event | category | flops | bytes accessed | tf_op | source)
XLA Modules:
  0.0 446.5 jit_solution(13086436742902101296)
XLA Ops:
  7.2 2.9 collective-permute-start
  14.2 4.0 collective-permute-start.3
  18.4 6.0 %collective-permute-done.3 = bf16[48,768]{1,0:T(8,128)(2,1)S(1)} collective-permute-done((bf16[48,768]{1,0:T(8,128)(2,1)S(1)}, bf16[48,768]{1,0:T(8,128)(2,1)S(1)}, u32[]{:S(2)}, u32[]{:S(2)}) %collective-permute-start.3) | collective-permute-done | bytes 73760 | tf_op jit(solution)/shard_map/ppermute | solution.py:1145
  28.2 3.7 collective-permute-done.4
  31.9 5.7 %collective-permute-done.5 = bf16[48,1664]{1,0:T(8,128)(2,1)S(1)} collective-permute-done((bf16[48,1664]{1,0:T(8,128)(2,1)S(1)}, bf16[48,1664]{1,0:T(8,128)(2,1)S(1)}, u32[]{:S(2)}, u32[]{:S(2)}) %collective-permute-start.5) | collective-permute-done | bytes 159776 | tf_op jit(solution)/shard_map/ppermute | solution.py:963
  37.7 5.4 %collective-permute-done.6 = bf16[48,1664]{1,0:T(8,128)(2,1)S(1)} collective-permute-done((bf16[48,1664]{1,0:T(8,128)(2,1)S(1)}, bf16[48,1664]{1,0:T(8,128)(2,1)S(1)}, u32[]{:S(2)}, u32[]{:S(2)}) %collective-permute-start.6) | collective-permute-done | bytes 159776 | tf_op jit(solution)/shard_map/ppermute | solution.py:963
  49.2 5.9 %collective-permute-done.10 = bf16[48,3072]{1,0:T(8,128)(2,1)S(1)} collective-permute-done((bf16[48,3072]{1,0:T(8,128)(2,1)S(1)}, bf16[48,3072]{1,0:T(8,128)(2,1)S(1)}, u32[]{:S(2)}, u32[]{:S(2)}) %collective-permute-start.10) | collective-permute-done | bytes 294944 | tf_op jit(solution)/shard_map/ppermute | solution.py:963
  55.0 10.3 %collective-permute-done.11 = bf16[48,3072]{1,0:T(8,128)(2,1)S(1)} collective-permute-done((bf16[48,3072]{1,0:T(8,128)(2,1)S(1)}, bf16[48,3072]{1,0:T(8,128)(2,1)S(1)}, u32[]{:S(2)}, u32[]{:S(2)}) %collective-permute-start.11) | collective-permute-done | bytes 294944 | tf_op jit(solution)/shard_map/ppermute | solution.py:963
  65.4 7.0 %collective-permute-done.12 = bf16[48,3072]{1,0:T(8,128)(2,1)S(1)} collective-permute-done((bf16[48,3072]{1,0:T(8,128)(2,1)S(1)}, bf16[48,3072]{1,0:T(8,128)(2,1)S(1)}, u32[]{:S(2)}, u32[]{:S(2)}) %collective-permute-start.12) | collective-permute-done | bytes 294944 | tf_op jit(solution)/shard_map/ppermute | solution.py:963
  75.1 2.8 collective-permute-start.17
  79.1 10.8 %collective-permute-done.17 = bf16[145,896]{1,0:T(8,128)(2,1)S(1)} collective-permute-done((bf16[145,896]{1,0:T(8,128)(2,1)S(1)}, bf16[145,896]{1,0:T(8,128)(2,1)S(1)}, u32[]{:S(2)}, u32[]{:S(2)}) %collective-permute-start.17) | collective-permute-done | bytes 259872 | tf_op jit(solution)/shard_map/ppermute | solution.py:959
  96.0 5.0 %shard_map.280 = (f32[320,768]{1,0:T(8,128)}, bf16[320,768]{1,0:T(8,128)(2,1)S(1)}, bf16[320,384]{1,0:T(8,128)(2,1)S(1)}, bf16[320,768]{1,0:T(8,128)(2,1)S(1)}, ...) custom-call(s32[3]{0:T(128)S(1)} %pad_add_fusion.refs_0_, ...), custom_call_target="tpu_custom_call" | custom-call | flops 943718400 | bytes 6291456 | tf_op jit(solution)/shard_map/pallas_call | solution.py:45
  103.3 4.2 shard_map.281
  107.6 10.7 %collective-permute-done.18.refs_6_.refs_9_ = bf16[2,2,192,768]{3,2,1,0:T(8,128)(2,1)} collective-permute-done((bf16[2,2,192,768]{3,2,1,0:T(8,128)(2,1)S(1)}, bf16[2,2,192,768]{3,2,1,0:T(8,128)(2,1)}, u32[]{:S(2)}, u32[]{:S(2)}) %collective-permute-start.18) | collective-permute-done | bytes 1179680 | tf_op jit(solution)/shard_map/ppermute | solution.py:963
  125.7 7.3 %collective-permute-done.20.refs_8_.refs_11_ = bf16[2,192,768]{2,1,0:T(8,128)(2,1)S(1)} collective-permute-done((bf16[2,192,768]{2,1,0:T(8,128)(2,1)S(1)}, bf16[2,192,768]{2,1,0:T(8,128)(2,1)S(1)}, u32[]{:S(2)}, u32[]{:S(2)}) %collective-permute-start.20) | collective-permute-done | bytes 589856 | tf_op jit(solution)/shard_map/ppermute | solution.py:963
  133.0 2.2 collective-permute-done.21.refs_9_.refs_12_
  135.3 7.8 %shard_map.282 = (f32[320,768]{1,0:T(8,128)S(1)}, bf16[320,768]{1,0:T(8,128)(2,1)S(1)}, bf16[320,1536]{1,0:T(8,128)(2,1)}, f32[320,768]{1,0:T(8,128)}, bf16[320,768]{1,0:T(8,128)(2,1)S(1)}) custom-call(s32[3]{0:T(128)S(1)} %pad_add_fusion.refs_0_, f32[320,768]{1,0:T(8,128)} %get-tuple-element.142.refs_1_, f32[320,768]{1,0:T(8,128)} %copy-done.5, ...), custom_call_target="tpu_custom_call" | custom-call | flops 1509949440 | bytes 16777216 | tf_op jit(solution)/shard_map/pallas_call | solution.py:45
  145.7 2.2 shard_map.283
  151.9 3.2 shard_map.284
  155.2 2.4 collective-permute-done.23.refs_3_
  159.4 5.6 %shard_map.285 = (f32[320,768]{1,0:T(8,128)S(1)}, bf16[160,768]{1,0:T(8,128)(2,1)S(1)}, bf16[384,320]{1,0:T(8,128)(2,1)S(1)}, f32[8,320]{1,0:T(8,128)S(1)}, bf16[320,768]{1,0:T(8,128)(2,1)S(1)}) custom-call(s32[3]{0:T(128)S(1)} %pad_add_fusion.refs_0_, bf16[320,384]{1,0:T(8,128)(2,1)S(1)} %get-tuple-element.159.refs_1_.refs_4_, ...), custom_call_target="tpu_custom_call" | custom-call | flops 503316480 | bytes 4194304 | tf_op jit(solution)/shard_map/pallas_call | solution.py:45
  168.4 2.9 shard_map.286
  177.1 6.3 %collective-permute-done.28.refs_1_ = bf16[192,768]{1,0:T(8,128)(2,1)S(1)} collective-permute-done((bf16[192,768]{1,0:T(8,128)(2,1)S(1)}, bf16[192,768]{1,0:T(8,128)(2,1)S(1)}, u32[]{:S(2)}, u32[]{:S(2)}) %collective-permute-start.28) | collective-permute-done | bytes 294944 | tf_op jit(solution)/shard_map/ppermute | solution.py:963
  183.4 6.9 %collective-permute-done.29.refs_2_ = bf16[192,768]{1,0:T(8,128)(2,1)S(1)} collective-permute-done((bf16[192,768]{1,0:T(8,128)(2,1)S(1)}, bf16[192,768]{1,0:T(8,128)(2,1)S(1)}, u32[]{:S(2)}, u32[]{:S(2)}) %collective-permute-start.29) | collective-permute-done | bytes 294944 | tf_op jit(solution)/shard_map/ppermute | solution.py:963
  192.4 13.8 %shard_map.287 = (bf16[192,768]{1,0:T(8,128)(2,1)}, bf16[192,768]{1,0:T(8,128)(2,1)}, bf16[192,768]{1,0:T(8,128)(2,1)}, bf16[192,768]{1,0:T(8,128)(2,1)}) custom-call(bf16[192,768]{1,0:T(8,128)(2,1)} %copy-done.26, bf16[192,768]{1,0:T(8,128)(2,1)} %copy-done.76, bf16[192,768]{1,0:T(8,128)(2,1)} %copy-done.77, bf16[192,768]{1,0:T(8,128)(2,1)} %copy-done.78, ...), custom_call_target="tpu_custom_call" | custom-call | flops 7247757312 | bytes 20971520 | tf_op jit(solution)/shard_map/pallas_call | solution.py:805
  209.7 6.7 %collective-permute-done.31.refs_2_ = bf16[192,768]{1,0:T(8,128)(2,1)S(1)} collective-permute-done((bf16[192,768]{1,0:T(8,128)(2,1)}, bf16[192,768]{1,0:T(8,128)(2,1)S(1)}, u32[]{:S(2)}, u32[]{:S(2)}) %collective-permute-start.31) | collective-permute-done | bytes 294944 | tf_op jit(solution)/shard_map/ppermute | solution.py:963
  216.4 4.9 %collective-permute-done.32.refs_3_ = bf16[192,768]{1,0:T(8,128)(2,1)S(1)} collective-permute-done((bf16[192,768]{1,0:T(8,128)(2,1)}, bf16[192,768]{1,0:T(8,128)(2,1)S(1)}, u32[]{:S(2)}, u32[]{:S(2)}) %collective-permute-start.32) | collective-permute-done | bytes 294944 | tf_op jit(solution)/shard_map/ppermute | solution.py:963
  225.3 2.0 shard_map.288
  230.1 6.9 %shard_map.290 = (bf16[320,384]{1,0:T(8,128)(2,1)S(1)}, f32[320,768]{1,0:T(8,128)}, bf16[320,768]{1,0:T(8,128)(2,1)S(1)}, bf16[384,768]{1,0:T(8,128)(2,1)S(1)}) custom-call(s32[3]{0:T(128)S(1)} %pad_add_fusion.refs_0_, bf16[320,768]{1,0:T(8,128)(2,1)S(1)} %get-tuple-element.185.refs_1_, bf16[384,768]{1,0:T(8,128)(2,1)S(1)} %bitcast.164, ...), custom_call_target="tpu_custom_call" | custom-call | flops 1163919360 | bytes 6291456 | tf_op jit(solution)/shard_map/pallas_call | solution.py:45
  237.9 12.3 %collective-permute-done.35.refs_3_ = bf16[320,768]{1,0:T(8,128)(2,1)S(1)} collective-permute-done((bf16[320,768]{1,0:T(8,128)(2,1)S(1)}, bf16[320,768]{1,0:T(8,128)(2,1)S(1)}, u32[]{:S(2)}, u32[]{:S(2)}) %collective-permute-start.35) | collective-permute-done | bytes 491552 | tf_op jit(solution)/shard_map/ppermute | solution.py:963
  250.2 6.2 %shard_map.291 = (f32[320,768]{1,0:T(8,128)S(1)}, bf16[320,768]{1,0:T(8,128)(2,1)S(1)}, bf16[2,832,384]{2,1,0:T(8,128)(2,1)}, bf16[2,832,384]{2,1,0:T(8,128)(2,1)}) custom-call(s32[3]{0:T(128)S(1)} %pad_add_fusion.refs_0_, bf16[320,384]{1,0:T(8,128)(2,1)S(1)} %get-tuple-element.189.refs_1_, f32[320,768]{1,0:T(8,128)} %get-tuple-element.190.refs_2_, ...), custom_call_target="tpu_custom_call" | custom-call | flops 1132462080 | bytes 10485760 | tf_op jit(solution)/shard_map/pallas_call | solution.py:45
  259.3 12.2 %shard_map.292 = (f32[320,768]{1,0:T(8,128)S(1)}, f32[320,768]{1,0:T(8,128)}, bf16[320,768]{1,0:T(8,128)(2,1)S(1)}, bf16[2,2,192,768]{3,2,1,0:T(8,128)(2,1)}, bf...) custom-call(s32[3]{0:T(128)S(1)} %pad_add_fusion.refs_0_, ...), custom_call_target="tpu_custom_call" | custom-call | flops 3774873600 | bytes 25165824 | tf_op jit(solution)/shard_map/pallas_call | solution.py:45
  273.5 2.0 shard_map.293
  275.6 7.0 %shard_map.294 = (bf16[320,384]{1,0:T(8,128)(2,1)S(1)}, f32[320,768]{1,0:T(8,128)}, bf16[320,768]{1,0:T(8,128)(2,1)S(1)}, bf16[384,768]{1,0:T(8,128)(2,1)S(1)}) custom-call(s32[3]{0:T(128)S(1)} %pad_add_fusion.refs_0_, bf16[320,768]{1,0:T(8,128)(2,1)S(1)} %get-tuple-element.202.refs_1_, bf16[384,768]{1,0:T(8,128)(2,1)S(1)} %copy-done.37, ...), custom_call_target="tpu_custom_call" | custom-call | flops 1163919360 | bytes 6291456 | tf_op jit(solution)/shard_map/pallas_call | solution.py:45
  285.4 13.2 %collective-permute-done.38.refs_3_ = bf16[320,768]{1,0:T(8,128)(2,1)S(1)} collective-permute-done((bf16[320,768]{1,0:T(8,128)(2,1)S(1)}, bf16[320,768]{1,0:T(8,128)(2,1)S(1)}, u32[]{:S(2)}, u32[]{:S(2)}) %collective-permute-start.38) | collective-permute-done | bytes 491552 | tf_op jit(solution)/shard_map/ppermute | solution.py:963
  300.4 5.5 %shard_map.295 = (f32[160,768]{1,0:T(8,128)S(1)}, bf16[160,768]{1,0:T(8,128)(2,1)S(1)}, bf16[2,384,384]{2,1,0:T(8,128)(2,1)S(1)}, bf16[2,384,384]{2,1,0:T(8,128)...) custom-call(s32[3]{0:T(128)S(1)} %pad_add_fusion.refs_0_, ...), custom_call_target="tpu_custom_call" | custom-call | flops 1132462080 | bytes 10485760 | tf_op jit(solution)/shard_map/pallas_call | solution.py:45
  316.6 21.5 %shard_map.297 = (bf16[768,1536]{1,0:T(8,128)(2,1)}, bf16[1536,768]{1,0:T(8,128)(2,1)}) custom-call(bf16[4,4,192,768]{3,2,1,0:T(8,128)(2,1)} %bitcast.169, bf16[768,1536]{1,0:T(8,128)(2,1)} %collective-permute-done.26.refs_8_.refs_6_.refs_1_, bf16[1536,768]{1,0:T(8,128)(2,1)} %collective-permute-done.27.refs_9_.refs_7_.refs_2_, bf16[145,768]{1,0:T(8,128)(2,1)} %copy-done.7), custom_call_target="tpu_custom_call" | custom-call | flops 14495514624 | bytes 20971520 | tf_op jit(solution)/shard_map/pallas_call | solution.py:869
  347.7 5.8 %collective-permute-start.40 = (bf16[2,145,768]{2,1,0:T(8,128)(2,1)}, bf16[2,145,768]{2,1,0:T(8,128)(2,1)S(1)}, u32[]{:S(2)}, u32[]{:S(2)}) collective-permute-start(bf16[2,145,768]{2,1,0:T(8,128)(2,1)} %pad_maximum_fusion.8), channel_id=1, source_target_pairs={{0,0},{1,2},{2,1},{3,3},{4,8},{5,10},{6,9},{7,11},{8,4},{9,6},{10,... | collective-permute-start | bytes 1336328 | tf_op jit(solution)/shard_map/ppermute | solution.py:959
  355.5 3.6 collective-permute-done.53
  361.3 8.6 %collective-permute-done.46 = bf16[2,192,768]{2,1,0:T(8,128)(2,1)} collective-permute-done((bf16[2,192,768]{2,1,0:T(8,128)(2,1)}, bf16[2,192,768]{2,1,0:T(8,128)(2,1)}, u32[]{:S(2)}, u32[]{:S(2)}) %collective-permute-start.46) | collective-permute-done | bytes 589856 | tf_op jit(solution)/shard_map/ppermute | solution.py:963
  369.9 2.8 fusion.8.refs_3_
  372.7 4.4 collective-permute-done.44
  379.7 5.1 %collective-permute-start.48 = (bf16[48,3072]{1,0:T(8,128)(2,1)S(1)}, bf16[48,3072]{1,0:T(8,128)(2,1)S(1)}, u32[]{:S(2)}, u32[]{:S(2)}) collective-permute-start(bf16[48,3072]{1,0:T(8,128)(2,1)S(1)} %get-tuple-element.225), channel_id=1, source_target_pairs={{0,4},{2,6},{4,0},{6,2},{1,5},{3,7},{5,1},{7,3},{8,12},{10,14},{12... | collective-permute-start | bytes 884744 | tf_op jit(solution)/shard_map/ppermute | solution.py:963
  384.8 22.6 %shard_map.299 = (f32[768,1536]{1,0:T(8,128)}, f32[1536,768]{1,0:T(8,128)}) custom-call(bf16[4,4,192,768]{3,2,1,0:T(8,128)(2,1)} %bitcast.170, bf16[768,1536]{1,0:T(8,128)(2,1)} %bitcast.61.refs_4_.refs_1_, bf16[1536,768]{1,0:T(8,128)(2,1)} %bitcast.62.refs_5_.refs_2_, bf16[768,1536]{1,0:T(8,128)(2,1)} %collective-permute-done.50.refs_3_, ...), custom_call_target="tpu_custom_call" | custom-call | flops 14495514624 | bytes 20971520 | tf_op jit(solution)/shard_map/pallas_call | solution.py:869
  407.5 2.2 collective-permute-done.48
  409.6 6.8 %collective-permute-done.49 = bf16[48,3072]{1,0:T(8,128)(2,1)S(1)} collective-permute-done((bf16[48,3072]{1,0:T(8,128)(2,1)S(1)}, bf16[48,3072]{1,0:T(8,128)(2,1)S(1)}, u32[]{:S(2)}, u32[]{:S(2)}) %collective-permute-start.49) | collective-permute-done | bytes 294944 | tf_op jit(solution)/shard_map/ppermute | solution.py:963
  419.4 2.5 collective-permute-start.57
  426.1 6.3 %collective-permute-done.57 = f32[48,768]{1,0:T(8,128)S(1)} collective-permute-done((f32[48,768]{1,0:T(8,128)S(1)}, f32[48,768]{1,0:T(8,128)S(1)}, u32[]{:S(2)}, u32[]{:S(2)}) %collective-permute-start.57) | collective-permute-done | bytes 147488 | tf_op jit(solution)/shard_map/ppermute | solution.py:1113
  (415 shorter events, 114.1 us)
Async XLA Ops:
  7.2 143.6 %all-gather.5.cloned.1.call-start = ((), (), s32[]{:S(2)}) async-start(), calls=%async_computation.2 | async-start | bytes 2949120 | tf_op jit(solution)/shard_map/all_gather | solution.py:1182
  7.2 20.9 %collective-permute-start = (bf16[145,768]{1,0:T(8,128)(2,1)}, bf16[145,768]{1,0:T(8,128)(2,1)S(1)}, u32[]{:S(2)}, u32[]{:S(2)}) collective-permute-start(bf16[145,768]{1,0:T(8,128)(2,1)} %bitcast.213), channel_id=1, source_target_pairs={{0,0},{1,2},{2,1},{3,3},{4,8},{5,10},{6,9},{7,11},{8,4},{9,6},{10,... | collective-permute-start | bytes 668168 | tf_op jit(solution)/shard_map/ppermute | solution.py:959
  12.5 15.5 %collective-permute-start.7 = (bf16[24,2688]{1,0:T(8,128)(2,1)S(1)}, bf16[24,2688]{1,0:T(8,128)(2,1)S(1)}, u32[]{:S(2)}, u32[]{:S(2)}) collective-permute-start(bf16[24,2688]{1,0:T(8,128)(2,1)S(1)} %get-tuple-element.361), channel_id=1, source_target_pairs={{0,1},{1,0},{2,3},{3,2},{4,5},{5,4},{6,7},{7,6},{8,9},{9,8},{10,11... | collective-permute-start | bytes 387080 | tf_op jit(solution)/shard_map/ppermute | solution.py:963
  14.2 10.2 %collective-permute-start.3 = (bf16[48,768]{1,0:T(8,128)(2,1)S(1)}, bf16[48,768]{1,0:T(8,128)(2,1)S(1)}, u32[]{:S(2)}, u32[]{:S(2)}) collective-permute-start(bf16[48,768]{1,0:T(8,128)(2,1)S(1)} %pad_maximum_fusion.11), channel_id=1, source_target_pairs={{0,0},{1,2},{2,4},{3,6},{4,8},{5,10},{6,12},{7,14},{8,16},{9,18},{... | collective-permute-start | bytes 221192 | tf_op jit(solution)/shard_map/ppermute | solution.py:1145
  26.5 11.2 %collective-permute-start.5 = (bf16[48,1664]{1,0:T(8,128)(2,1)S(1)}, bf16[48,1664]{1,0:T(8,128)(2,1)S(1)}, u32[]{:S(2)}, u32[]{:S(2)}) collective-permute-start(bf16[48,1664]{1,0:T(8,128)(2,1)S(1)} %fusion.24), channel_id=1, source_target_pairs={{0,4},{2,6},{4,0},{6,2},{1,5},{3,7},{5,1},{7,3},{8,12},{10,14},{12... | collective-permute-start | bytes 479240 | tf_op jit(solution)/shard_map/ppermute | solution.py:963
  26.5 16.6 %collective-permute-start.6 = (bf16[48,1664]{1,0:T(8,128)(2,1)S(1)}, bf16[48,1664]{1,0:T(8,128)(2,1)S(1)}, u32[]{:S(2)}, u32[]{:S(2)}) collective-permute-start(bf16[48,1664]{1,0:T(8,128)(2,1)S(1)} %fusion.24), channel_id=1, source_target_pairs={{0,6},{2,4},{4,2},{6,0},{1,7},{3,5},{5,3},{7,1},{8,14},{10,12},{12... | collective-permute-start | bytes 479240 | tf_op jit(solution)/shard_map/ppermute | solution.py:963
  28.1 18.7 %collective-permute-start.1 = (bf16[145,768]{1,0:T(8,128)(2,1)S(1)}, bf16[145,768]{1,0:T(8,128)(2,1)S(1)}, u32[]{:S(2)}, u32[]{:S(2)}) collective-permute-start(bf16[145,768]{1,0:T(8,128)(2,1)S(1)} %collective-permute-done), channel_id=1, source_target_pairs={{0,8},{8,0},{16,24},{24,16},{1,9},{9,1},{17,25},{25,17},{2,10},{10... | collective-permute-start | bytes 668168 | tf_op jit(solution)/shard_map/ppermute | solution.py:963
  43.3 11.7 %collective-permute-start.10 = (bf16[48,3072]{1,0:T(8,128)(2,1)S(1)}, bf16[48,3072]{1,0:T(8,128)(2,1)S(1)}, u32[]{:S(2)}, u32[]{:S(2)}) collective-permute-start(bf16[48,3072]{1,0:T(8,128)(2,1)S(1)} %pad_maximum_fusion.9), channel_id=1, source_target_pairs={{0,2},{2,0},{4,6},{6,4},{1,3},{3,1},{5,7},{7,5},{8,10},{10,8},{12,... | collective-permute-start | bytes 884744 | tf_op jit(solution)/shard_map/ppermute | solution.py:963
  43.4 22.0 %collective-permute-start.11 = (bf16[48,3072]{1,0:T(8,128)(2,1)S(1)}, bf16[48,3072]{1,0:T(8,128)(2,1)S(1)}, u32[]{:S(2)}, u32[]{:S(2)}) collective-permute-start(bf16[48,3072]{1,0:T(8,128)(2,1)S(1)} %pad_maximum_fusion.9), channel_id=1, source_target_pairs={{0,4},{2,6},{4,0},{6,2},{1,5},{3,7},{5,1},{7,3},{8,12},{10,14},{12... | collective-permute-start | bytes 884744 | tf_op jit(solution)/shard_map/ppermute | solution.py:963
  45.3 27.1 %collective-permute-start.12 = (bf16[48,3072]{1,0:T(8,128)(2,1)S(1)}, bf16[48,3072]{1,0:T(8,128)(2,1)S(1)}, u32[]{:S(2)}, u32[]{:S(2)}) collective-permute-start(bf16[48,3072]{1,0:T(8,128)(2,1)S(1)} %pad_maximum_fusion.9), channel_id=1, source_target_pairs={{0,6},{2,4},{4,2},{6,0},{1,7},{3,5},{5,3},{7,1},{8,14},{10,12},{12... | collective-permute-start | bytes 884744 | tf_op jit(solution)/shard_map/ppermute | solution.py:963
  47.9 24.8 %collective-permute-start.8 = (bf16[1024,384]{1,0:T(8,128)(2,1)S(1)}, bf16[1024,384]{1,0:T(8,128)(2,1)S(1)}, u32[]{:S(2)}, u32[]{:S(2)}) collective-permute-start(bf16[1024,384]{1,0:T(8,128)(2,1)S(1)} %maximum_dynamic-update-slice_fusion.refs_5_), channel_id=1, source_target_pairs={{0,8},{8,0},{16,24},{24,16},{1,9},{9,1},{17,25},{25,17},{2,10},{10... | collective-permute-start | bytes 2359304 | tf_op jit(solution)/shard_map/ppermute | solution.py:963
  47.9 24.8 %collective-permute-start.9 = (bf16[1024,384]{1,0:T(8,128)(2,1)S(1)}, bf16[1024,384]{1,0:T(8,128)(2,1)S(1)}, u32[]{:S(2)}, u32[]{:S(2)}) collective-permute-start(bf16[1024,384]{1,0:T(8,128)(2,1)S(1)} %maximum_dynamic-update-slice_fusion.refs_5_), channel_id=1, source_target_pairs={{0,16},{8,24},{16,0},{24,8},{1,17},{9,25},{17,1},{25,9},{2,18},{10... | collective-permute-start | bytes 2359304 | tf_op jit(solution)/shard_map/ppermute | solution.py:963
  74.4 16.2 %collective-permute-start.14 = (bf16[576,384]{1,0:T(8,128)(2,1)S(1)}, bf16[576,384]{1,0:T(8,128)(2,1)S(1)}, u32[]{:S(2)}, u32[]{:S(2)}) collective-permute-start(bf16[576,384]{1,0:T(8,128)(2,1)S(1)} %slice.305), channel_id=1, source_target_pairs={{0,16},{8,24},{16,0},{24,8},{1,17},{9,25},{17,1},{25,9},{2,18},{10... | collective-permute-start | bytes 1327112 | tf_op jit(solution)/shard_map/ppermute | solution.py:963
  74.5 16.1 %collective-permute-start.15 = (bf16[448,384]{1,0:T(8,128)(2,1)S(1)}, bf16[448,384]{1,0:T(8,128)(2,1)S(1)}, u32[]{:S(2)}, u32[]{:S(2)}) collective-permute-start(bf16[448,384]{1,0:T(8,128)(2,1)S(1)} %slice.306), channel_id=1, source_target_pairs={{0,8},{8,0},{16,24},{24,16},{1,9},{9,1},{17,25},{25,17},{2,10},{10... | collective-permute-start | bytes 1032200 | tf_op jit(solution)/shard_map/ppermute | solution.py:963
  75.1 14.8 %collective-permute-start.17 = (bf16[145,896]{1,0:T(8,128)(2,1)S(1)}, bf16[145,896]{1,0:T(8,128)(2,1)S(1)}, u32[]{:S(2)}, u32[]{:S(2)}) collective-permute-start(bf16[145,896]{1,0:T(8,128)(2,1)S(1)} %fusion.22), channel_id=1, source_target_pairs={{0,0},{1,2},{2,1},{3,3},{4,8},{5,10},{6,9},{7,11},{8,4},{9,6},{10,... | collective-permute-start | bytes 779528 | tf_op jit(solution)/shard_map/ppermute | solution.py:959
  90.9 27.3 %collective-permute-start.18 = (bf16[2,2,192,768]{3,2,1,0:T(8,128)(2,1)S(1)}, bf16[2,2,192,768]{3,2,1,0:T(8,128)(2,1)}, u32[]{:S(2)}, u32[]{:S(2)}) collective-permute-start(bf16[2,2,192,768]{3,2,1,0:T(8,128)(2,1)S(1)} %pad_maximum_fusion.1.refs_5_.refs_8_), channel_id=1, source_target_pairs={{0,8},{8,0},{16,24},{24,16},{1,9},{9,1},{17,25},{25,17},{2,10},{10... | collective-permute-start | bytes 3538952 | tf_op jit(solution)/shard_map/ppermute | solution.py:963
  91.0 27.3 %collective-permute-start.19 = (bf16[2,2,192,768]{3,2,1,0:T(8,128)(2,1)S(1)}, bf16[2,2,192,768]{3,2,1,0:T(8,128)(2,1)}, u32[]{:S(2)}, u32[]{:S(2)}) collective-permute-start(bf16[2,2,192,768]{3,2,1,0:T(8,128)(2,1)S(1)} %pad_maximum_fusion.1.refs_5_.refs_8_), channel_id=1, source_target_pairs={{0,16},{8,24},{16,0},{24,8},{1,17},{9,25},{17,1},{25,9},{2,18},{10... | collective-permute-start | bytes 3538952 | tf_op jit(solution)/shard_map/ppermute | solution.py:963
  95.7 203.7 %all-gather.7.cloned.1.call-start = ((), (), s32[]{:S(2)}) async-start(), calls=%async_computation.3 | async-start | bytes 5898240 | tf_op jit(solution)/shard_map/all_gather | solution.py:1221
  119.4 13.6 %collective-permute-start.20 = (bf16[2,192,768]{2,1,0:T(8,128)(2,1)S(1)}, bf16[2,192,768]{2,1,0:T(8,128)(2,1)S(1)}, u32[]{:S(2)}, u32[]{:S(2)}) collective-permute-start(bf16[2,192,768]{2,1,0:T(8,128)(2,1)S(1)} %slice_bitcast_fusion.1), channel_id=1, source_target_pairs={{0,16},{8,24},{16,0},{24,8},{1,17},{9,25},{17,1},{25,9},{2,18},{10... | collective-permute-start | bytes 1769480 | tf_op jit(solution)/shard_map/ppermute | solution.py:963
  122.1 13.1 %collective-permute-start.21 = (bf16[2,192,768]{2,1,0:T(8,128)(2,1)S(1)}, bf16[2,192,768]{2,1,0:T(8,128)(2,1)S(1)}, u32[]{:S(2)}, u32[]{:S(2)}) collective-permute-start(bf16[2,192,768]{2,1,0:T(8,128)(2,1)S(1)} %slice_bitcast_fusion), channel_id=1, source_target_pairs={{0,8},{8,0},{16,24},{24,16},{1,9},{9,1},{17,25},{25,17},{2,10},{10... | collective-permute-start | bytes 1769480 | tf_op jit(solution)/shard_map/ppermute | solution.py:963
  148.9 19.5 %collective-permute-start.26 = (bf16[768,1536]{1,0:T(8,128)(2,1)}, bf16[768,1536]{1,0:T(8,128)(2,1)}, u32[]{:S(2)}, u32[]{:S(2)}) collective-permute-start(bf16[768,1536]{1,0:T(8,128)(2,1)} %bitcast.61.refs_4_.refs_1_), channel_id=1, source_target_pairs={{0,1},{1,0},{2,3},{3,2},{4,5},{5,4},{6,7},{7,6},{8,9},{9,8},{10,11... | collective-permute-start | bytes 7077896 | tf_op jit(solution)/shard_map/ppermute | solution.py:963
  149.0 19.3 %collective-permute-start.27 = (bf16[1536,768]{1,0:T(8,128)(2,1)}, bf16[1536,768]{1,0:T(8,128)(2,1)}, u32[]{:S(2)}, u32[]{:S(2)}) collective-permute-start(bf16[1536,768]{1,0:T(8,128)(2,1)} %bitcast.62.refs_5_.refs_2_), channel_id=1, source_target_pairs={{0,1},{1,0},{2,3},{3,2},{4,5},{5,4},{6,7},{7,6},{8,9},{9,8},{10,11... | collective-permute-start | bytes 7077896 | tf_op jit(solution)/shard_map/ppermute | solution.py:963
  173.6 9.8 %collective-permute-start.28 = (bf16[192,768]{1,0:T(8,128)(2,1)S(1)}, bf16[192,768]{1,0:T(8,128)(2,1)S(1)}, u32[]{:S(2)}, u32[]{:S(2)}) collective-permute-start(bf16[192,768]{1,0:T(8,128)(2,1)S(1)} %get-tuple-element.170), channel_id=1, source_target_pairs={{0,8},{8,0},{16,24},{24,16},{1,9},{9,1},{17,25},{25,17},{2,10},{10... | collective-permute-start | bytes 884744 | tf_op jit(solution)/shard_map/ppermute | solution.py:963
  175.0 15.3 %collective-permute-start.29 = (bf16[192,768]{1,0:T(8,128)(2,1)S(1)}, bf16[192,768]{1,0:T(8,128)(2,1)S(1)}, u32[]{:S(2)}, u32[]{:S(2)}) collective-permute-start(bf16[192,768]{1,0:T(8,128)(2,1)S(1)} %get-tuple-element.171), channel_id=1, source_target_pairs={{0,16},{8,24},{16,0},{24,8},{1,17},{9,25},{17,1},{25,9},{2,18},{10... | collective-permute-start | bytes 884744 | tf_op jit(solution)/shard_map/ppermute | solution.py:963
  175.7 14.6 %collective-permute-start.30 = (bf16[192,768]{1,0:T(8,128)(2,1)S(1)}, bf16[192,768]{1,0:T(8,128)(2,1)S(1)}, u32[]{:S(2)}, u32[]{:S(2)}) collective-permute-start(bf16[192,768]{1,0:T(8,128)(2,1)S(1)} %get-tuple-element.172), channel_id=1, source_target_pairs={{0,24},{8,16},{16,8},{24,0},{1,25},{9,17},{17,9},{25,1},{2,26},{10... | collective-permute-start | bytes 884744 | tf_op jit(solution)/shard_map/ppermute | solution.py:963
  192.3 224.3 %reduce-scatter.2.cloned.1.call-start = ((), (), s32[]{:S(2)}) async-start(), calls=%async_computation.1 | async-start | bytes 1536000 | tf_op jit(solution)/shard_map/reduce_scatter | solution.py:1252
  206.2 10.2 %collective-permute-start.31 = (bf16[192,768]{1,0:T(8,128)(2,1)}, bf16[192,768]{1,0:T(8,128)(2,1)S(1)}, u32[]{:S(2)}, u32[]{:S(2)}) collective-permute-start(bf16[192,768]{1,0:T(8,128)(2,1)} %get-tuple-element.174), channel_id=1, source_target_pairs={{0,8},{8,0},{16,24},{24,16},{1,9},{9,1},{17,25},{25,17},{2,10},{10... | collective-permute-start | bytes 884744 | tf_op jit(solution)/shard_map/ppermute | solution.py:963
  206.9 14.5 %collective-permute-start.32 = (bf16[192,768]{1,0:T(8,128)(2,1)}, bf16[192,768]{1,0:T(8,128)(2,1)S(1)}, u32[]{:S(2)}, u32[]{:S(2)}) collective-permute-start(bf16[192,768]{1,0:T(8,128)(2,1)} %get-tuple-element.175), channel_id=1, source_target_pairs={{0,16},{8,24},{16,0},{24,8},{1,17},{9,25},{17,1},{25,9},{2,18},{10... | collective-permute-start | bytes 884744 | tf_op jit(solution)/shard_map/ppermute | solution.py:963
  207.9 13.5 %collective-permute-start.33 = (bf16[192,768]{1,0:T(8,128)(2,1)}, bf16[192,768]{1,0:T(8,128)(2,1)S(1)}, u32[]{:S(2)}, u32[]{:S(2)}) collective-permute-start(bf16[192,768]{1,0:T(8,128)(2,1)} %get-tuple-element.176), channel_id=1, source_target_pairs={{0,24},{8,16},{16,8},{24,0},{1,25},{9,17},{17,9},{25,1},{2,26},{10... | collective-permute-start | bytes 884744 | tf_op jit(solution)/shard_map/ppermute | solution.py:963
  236.9 13.3 %collective-permute-start.35 = (bf16[320,768]{1,0:T(8,128)(2,1)S(1)}, bf16[320,768]{1,0:T(8,128)(2,1)S(1)}, u32[]{:S(2)}, u32[]{:S(2)}) collective-permute-start(bf16[320,768]{1,0:T(8,128)(2,1)S(1)} %get-tuple-element.191), channel_id=1, source_target_pairs={{0,8},{8,0},{16,24},{24,16},{1,9},{9,1},{17,25},{25,17},{2,10},{10... | collective-permute-start | bytes 1474568 | tf_op jit(solution)/shard_map/ppermute | solution.py:963
  257.4 49.7 %collective-permute-start.52 = (bf16[2,832,384]{2,1,0:T(8,128)(2,1)}, bf16[2,832,384]{2,1,0:T(8,128)(2,1)}, u32[]{:S(2)}, u32[]{:S(2)}) collective-permute-start(bf16[2,832,384]{2,1,0:T(8,128)(2,1)} %get-tuple-element.233), channel_id=1, source_target_pairs={{0,8},{8,0},{16,24},{24,16},{1,9},{9,1},{17,25},{25,17},{2,10},{10... | collective-permute-start | bytes 3833864 | tf_op jit(solution)/shard_map/ppermute | solution.py:963
  271.7 37.9 %collective-permute-start.54 = (bf16[2,2,192,768]{3,2,1,0:T(8,128)(2,1)}, bf16[2,2,192,768]{3,2,1,0:T(8,128)(2,1)}, u32[]{:S(2)}, u32[]{:S(2)}) collective-permute-start(bf16[2,2,192,768]{3,2,1,0:T(8,128)(2,1)} %get-tuple-element.237), channel_id=1, source_target_pairs={{0,16},{8,24},{16,0},{24,8},{1,17},{9,25},{17,1},{25,9},{2,18},{10... | collective-permute-start | bytes 3538952 | tf_op jit(solution)/shard_map/ppermute | solution.py:963
  283.5 15.2 %collective-permute-start.38 = (bf16[320,768]{1,0:T(8,128)(2,1)S(1)}, bf16[320,768]{1,0:T(8,128)(2,1)S(1)}, u32[]{:S(2)}, u32[]{:S(2)}) collective-permute-start(bf16[320,768]{1,0:T(8,128)(2,1)S(1)} %get-tuple-element.207), channel_id=1, source_target_pairs={{0,8},{8,0},{16,24},{24,16},{1,9},{9,1},{17,25},{25,17},{2,10},{10... | collective-permute-start | bytes 1474568 | tf_op jit(solution)/shard_map/ppermute | solution.py:963
  284.4 53.7 %collective-permute-start.45 = (bf16[2,2,192,768]{3,2,1,0:T(8,128)(2,1)}, bf16[2,2,192,768]{3,2,1,0:T(8,128)(2,1)}, u32[]{:S(2)}, u32[]{:S(2)}) collective-permute-start(bf16[2,2,192,768]{3,2,1,0:T(8,128)(2,1)} %get-tuple-element.221), channel_id=1, source_target_pairs={{0,16},{8,24},{16,0},{24,8},{1,17},{9,25},{17,1},{25,9},{2,18},{10... | collective-permute-start | bytes 3538952 | tf_op jit(solution)/shard_map/ppermute | solution.py:963
  306.1 38.6 %collective-permute-start.41 = (bf16[2,384,384]{2,1,0:T(8,128)(2,1)S(1)}, bf16[2,384,384]{2,1,0:T(8,128)(2,1)}, u32[]{:S(2)}, u32[]{:S(2)}) collective-permute-start(bf16[2,384,384]{2,1,0:T(8,128)(2,1)S(1)} %get-tuple-element.214), channel_id=1, source_target_pairs={{0,8},{8,0},{16,24},{24,16},{1,9},{9,1},{17,25},{25,17},{2,10},{10... | collective-permute-start | bytes 1769480 | tf_op jit(solution)/shard_map/ppermute | solution.py:963
  307.1 40.6 %collective-permute-start.43 = (bf16[2,384,384]{2,1,0:T(8,128)(2,1)}, bf16[2,384,384]{2,1,0:T(8,128)(2,1)}, u32[]{:S(2)}, u32[]{:S(2)}) collective-permute-start(bf16[2,384,384]{2,1,0:T(8,128)(2,1)} %get-tuple-element.218), channel_id=1, source_target_pairs={{0,16},{8,24},{16,0},{24,8},{1,17},{9,25},{17,1},{25,9},{2,18},{10... | collective-permute-start | bytes 1769480 | tf_op jit(solution)/shard_map/ppermute | solution.py:963
  312.8 30.0 %collective-permute-start.55 = (bf16[2,192,768]{2,1,0:T(8,128)(2,1)}, bf16[2,192,768]{2,1,0:T(8,128)(2,1)}, u32[]{:S(2)}, u32[]{:S(2)}) collective-permute-start(bf16[2,192,768]{2,1,0:T(8,128)(2,1)} %fusion.11), channel_id=1, source_target_pairs={{0,8},{8,0},{16,24},{24,16},{1,9},{9,1},{17,25},{25,17},{2,10},{10... | collective-permute-start | bytes 1769480 | tf_op jit(solution)/shard_map/ppermute | solution.py:963
  338.1 46.7 %collective-permute-start.50 = (bf16[768,1536]{1,0:T(8,128)(2,1)}, bf16[768,1536]{1,0:T(8,128)(2,1)}, u32[]{:S(2)}, u32[]{:S(2)}) collective-permute-start(bf16[768,1536]{1,0:T(8,128)(2,1)} %get-tuple-element.215), channel_id=1, source_target_pairs={{0,1},{1,0},{2,3},{3,2},{4,5},{5,4},{6,7},{7,6},{8,9},{9,8},{10,11... | collective-permute-start | bytes 7077896 | tf_op jit(solution)/shard_map/ppermute | solution.py:963
  339.8 45.0 %collective-permute-start.51 = (bf16[1536,768]{1,0:T(8,128)(2,1)}, bf16[1536,768]{1,0:T(8,128)(2,1)}, u32[]{:S(2)}, u32[]{:S(2)}) collective-permute-start(bf16[1536,768]{1,0:T(8,128)(2,1)} %get-tuple-element.227), channel_id=1, source_target_pairs={{0,1},{1,0},{2,3},{3,2},{4,5},{5,4},{6,7},{7,6},{8,9},{9,8},{10,11... | collective-permute-start | bytes 7077896 | tf_op jit(solution)/shard_map/ppermute | solution.py:963
  342.7 16.4 %collective-permute-start.53 = (bf16[832,384]{1,0:T(8,128)(2,1)S(1)}, bf16[832,384]{1,0:T(8,128)(2,1)S(1)}, u32[]{:S(2)}, u32[]{:S(2)}) collective-permute-start(bf16[832,384]{1,0:T(8,128)(2,1)S(1)} %copy-done.70), channel_id=1, source_target_pairs={{0,16},{8,24},{16,0},{24,8},{1,17},{9,25},{17,1},{25,9},{2,18},{10... | collective-permute-start | bytes 1916936 | tf_op jit(solution)/shard_map/ppermute | solution.py:963
  344.7 25.2 %collective-permute-start.46 = (bf16[2,192,768]{2,1,0:T(8,128)(2,1)}, bf16[2,192,768]{2,1,0:T(8,128)(2,1)}, u32[]{:S(2)}, u32[]{:S(2)}) collective-permute-start(bf16[2,192,768]{2,1,0:T(8,128)(2,1)} %fusion.10), channel_id=1, source_target_pairs={{0,8},{8,0},{16,24},{24,16},{1,9},{9,1},{17,25},{25,17},{2,10},{10... | collective-permute-start | bytes 1769480 | tf_op jit(solution)/shard_map/ppermute | solution.py:963
  347.7 29.6 %collective-permute-start.40 = (bf16[2,145,768]{2,1,0:T(8,128)(2,1)}, bf16[2,145,768]{2,1,0:T(8,128)(2,1)S(1)}, u32[]{:S(2)}, u32[]{:S(2)}) collective-permute-start(bf16[2,145,768]{2,1,0:T(8,128)(2,1)} %pad_maximum_fusion.8), channel_id=1, source_target_pairs={{0,0},{1,2},{2,1},{3,3},{4,8},{5,10},{6,9},{7,11},{8,4},{9,6},{10,... | collective-permute-start | bytes 1336328 | tf_op jit(solution)/shard_map/ppermute | solution.py:959
  359.1 13.5 %collective-permute-start.42 = (bf16[384,384]{1,0:T(8,128)(2,1)}, bf16[384,384]{1,0:T(8,128)(2,1)S(1)}, u32[]{:S(2)}, u32[]{:S(2)}) collective-permute-start(bf16[384,384]{1,0:T(8,128)(2,1)} %fusion.20), channel_id=1, source_target_pairs={{0,16},{8,24},{16,0},{24,8},{1,17},{9,25},{17,1},{25,9},{2,18},{10... | collective-permute-start | bytes 884744 | tf_op jit(solution)/shard_map/ppermute | solution.py:963
  379.7 27.7 %collective-permute-start.47 = (bf16[48,3072]{1,0:T(8,128)(2,1)S(1)}, bf16[48,3072]{1,0:T(8,128)(2,1)S(1)}, u32[]{:S(2)}, u32[]{:S(2)}) collective-permute-start(bf16[48,3072]{1,0:T(8,128)(2,1)S(1)} %get-tuple-element.224), channel_id=1, source_target_pairs={{0,2},{2,0},{4,6},{6,4},{1,3},{3,1},{5,7},{7,5},{8,10},{10,8},{12,... | collective-permute-start | bytes 884744 | tf_op jit(solution)/shard_map/ppermute | solution.py:963
  379.7 29.9 %collective-permute-start.48 = (bf16[48,3072]{1,0:T(8,128)(2,1)S(1)}, bf16[48,3072]{1,0:T(8,128)(2,1)S(1)}, u32[]{:S(2)}, u32[]{:S(2)}) collective-permute-start(bf16[48,3072]{1,0:T(8,128)(2,1)S(1)} %get-tuple-element.225), channel_id=1, source_target_pairs={{0,4},{2,6},{4,0},{6,2},{1,5},{3,7},{5,1},{7,3},{8,12},{10,14},{12... | collective-permute-start | bytes 884744 | tf_op jit(solution)/shard_map/ppermute | solution.py:963
  384.8 31.6 %collective-permute-start.49 = (bf16[48,3072]{1,0:T(8,128)(2,1)S(1)}, bf16[48,3072]{1,0:T(8,128)(2,1)S(1)}, u32[]{:S(2)}, u32[]{:S(2)}) collective-permute-start(bf16[48,3072]{1,0:T(8,128)(2,1)S(1)} %get-tuple-element.226), channel_id=1, source_target_pairs={{0,6},{2,4},{4,2},{6,0},{1,7},{3,5},{5,3},{7,1},{8,14},{10,12},{12... | collective-permute-start | bytes 884744 | tf_op jit(solution)/shard_map/ppermute | solution.py:963
  419.3 13.8 %collective-permute-start.56 = (f32[24,3968]{1,0:T(8,128)S(1)}, f32[24,3968]{1,0:T(8,128)S(1)}, u32[]{:S(2)}, u32[]{:S(2)}) collective-permute-start(f32[24,3968]{1,0:T(8,128)S(1)} %get-tuple-element.329), channel_id=1, source_target_pairs={{0,1},{1,0},{2,3},{3,2},{4,5},{5,4},{6,7},{7,6},{8,9},{9,8},{10,11... | collective-permute-start | bytes 1142792 | tf_op jit(solution)/shard_map/ppermute | solution.py:963
  419.4 13.0 %collective-permute-start.57 = (f32[48,768]{1,0:T(8,128)S(1)}, f32[48,768]{1,0:T(8,128)S(1)}, u32[]{:S(2)}, u32[]{:S(2)}) collective-permute-start(f32[48,768]{1,0:T(8,128)S(1)} %maximum_maximum_fusion), channel_id=1, source_target_pairs={{0,0},{2,1},{4,2},{6,3},{8,4},{10,5},{12,6},{14,7},{16,8},{18,9},{... | collective-permute-start | bytes 442376 | tf_op jit(solution)/shard_map/ppermute | solution.py:1113
  (107 other events, 532.3 us)
Sparse Core Ops, SparseCore 0:
  95.9 47.9 all-gather.4
  192.5 88.3 all-gather.6
  361.4 39.6 reduce-scatter.1
